TPU v7x, 32 devices: a whole 2x2x4 slice. The times are simulated.
32 devices in a mesh: section: 2 (over y), dp: 16 (over z, x, core).
Axes of the slice: x: 2, y: 2, z: 4, core: 2. Of those that a mesh axis runs over, the one named last changes fastest.
Arguments:
- base: bfloat16 [6144, 8192], P('dp'), may hold values from -6 to 6
- cotangent: bfloat16 [6144, 8192], P('dp'), may hold values from -6 to 6
- gain: float32 [2, 8192], P('section'), may hold values from 0.1 to 1.9
- weight_in: bfloat16 [2, 8192, 128], P('section', 'dp'), may hold values from -0.0625 to 0.0625
- weight_out: bfloat16 [2, 8192, 128], P('section', 'dp'), may hold values from -0.5 to 0.5
- subspace: bfloat16 [8192, 256], P('dp'), may hold values from -0.0625 to 0.0625
Outputs:
- codes: bfloat16 [2, 6144, 256], P('section', 'dp')
- grad_in: float32 [2, 8192, 128], P('section', 'dp')
- grad_out: float32 [2, 8192, 128], P('section', 'dp')
All inputs are finite; a program needn't handle non-finite values.
Results may differ from a plain program's by a relative error of at most 0.0076.
Values may be sent and summed in bfloat16 or wider, within the bound.
No kernel may reach another device: no remote copies, remote signals or barrier semaphores. Data moves between devices by JAX's collectives and lax.ppermute only.
A program may use at most 128 MiB of HBM per device.

v0:
```python
import jax
import jax.numpy as jnp
from jax import lax
from jax.sharding import PartitionSpec as P

MICRO = 3


def from_behind(value, axis, by):
    peers = lax.axis_size(axis)
    pairs = [(i, i + by) for i in range(peers) if 0 <= i + by < peers]
    return lax.ppermute(value, axis, pairs)


def rebuild(base_rows, coded, subspace):
    return (
        base_rows.astype(jnp.float32)
        + jnp.dot(coded, subspace.T, preferred_element_type=jnp.float32)
    ).astype(jnp.bfloat16)


def branch_parts(residual, gain_row, weight_in):
    residual_f = residual.astype(jnp.float32)
    inverse = lax.rsqrt(jnp.mean(residual_f * residual_f, axis=-1, keepdims=True) + 1e-05)
    normed = (residual_f * inverse * gain_row).astype(jnp.bfloat16)
    inner_act = jnp.dot(normed, weight_in, preferred_element_type=jnp.float32)
    active = jax.nn.silu(inner_act).astype(jnp.bfloat16)
    return (residual_f, inverse, normed, inner_act, active)


def layer_forward(residual, base_rows, gain_row, weight_in, weight_out, subspace):
    residual_f, inverse, normed, inner_act, active = branch_parts(residual, gain_row, weight_in)
    output = residual_f + jnp.dot(active, weight_out.T, preferred_element_type=jnp.float32)
    offset = (output - base_rows.astype(jnp.float32)).astype(jnp.bfloat16)
    return jnp.dot(offset, subspace, preferred_element_type=jnp.float32).astype(jnp.bfloat16)


def backward_data(residual, grad_y, gain_row, weight_in, weight_out, subspace):
    residual_f, inverse, normed, inner_act, active = branch_parts(residual, gain_row, weight_in)
    grad_half = grad_y.astype(jnp.bfloat16)
    grad_active = jnp.dot(grad_half, weight_out, preferred_element_type=jnp.float32)
    logistic = jax.nn.sigmoid(inner_act)
    grad_inner = (grad_active * logistic * (1.0 + inner_act * (1.0 - logistic))).astype(
        jnp.bfloat16
    )
    grad_normed = jnp.dot(grad_inner, weight_in.T, preferred_element_type=jnp.float32) * gain_row
    grad_resid = (
        grad_y
        + inverse * grad_normed
        - residual_f * inverse**3 * jnp.mean(residual_f * grad_normed, axis=-1, keepdims=True)
    )
    sent_back = jnp.dot(
        grad_resid.astype(jnp.bfloat16), subspace, preferred_element_type=jnp.float32
    ).astype(jnp.bfloat16)
    return (sent_back, grad_half, grad_inner, normed, active)


def pass_back(sent_back):
    return from_behind(sent_back, "section", -1)


def on_device(base, cotangent, gain, weight_in, weight_out, subspace):
    sections = lax.axis_size("section")
    here = lax.axis_index("section")
    full_space = lax.all_gather(subspace, "dp", axis=0, tiled=True)
    gain_row = gain[0]
    fwd_in, fwd_out = (
        lax.all_gather(weight_in, "dp", axis=1, tiled=True),
        lax.all_gather(weight_out, "dp", axis=1, tiled=True),
    )
    fwd_in = fwd_in[0]
    fwd_out = fwd_out[0]
    rows, width = base.shape
    code_size = full_space.shape[1]
    rank_size = fwd_in.shape[1]
    block_count = MICRO
    block_rows = rows // block_count
    base_blocks = base.reshape(block_count, block_rows, width)
    cot_blocks = cotangent.reshape(block_count, block_rows, width)

    def forward_step(tick, carry):
        incoming, saved, code_store = carry
        index_mb = tick - here
        valid = (index_mb >= 0) & (index_mb < block_count)
        slot = jnp.clip(index_mb, 0, block_count - 1)
        base_rows = lax.dynamic_index_in_dim(base_blocks, slot, 0, keepdims=False)

        def forward_working(state):
            residual = jnp.where(here == 0, base_rows, rebuild(base_rows, incoming, full_space))
            coded = layer_forward(residual, base_rows, gain_row, fwd_in, fwd_out, full_space)
            new_saved = lax.dynamic_update_index_in_dim(state[0], residual, slot, 0)
            new_codes = lax.dynamic_update_index_in_dim(state[1], coded, slot, 0)
            return (coded, new_saved, new_codes)

        def forward_waiting(state):
            return (jnp.zeros_like(incoming), state[0], state[1])

        coded, saved, code_store = lax.cond(
            valid, forward_working, forward_waiting, (saved, code_store)
        )
        outgoing = from_behind(coded, "section", 1)
        return (outgoing, saved, code_store)

    start_fwd = (
        jnp.zeros((block_rows, code_size), jnp.bfloat16),
        jnp.zeros((block_count, block_rows, width), jnp.bfloat16),
        jnp.zeros((block_count, block_rows, code_size), jnp.bfloat16),
    )
    ignored, saved, code_store = lax.fori_loop(
        0, sections + block_count - 1, forward_step, start_fwd
    )
    back_in, back_out = (
        lax.all_gather(weight_in, "dp", axis=1, tiled=True),
        lax.all_gather(weight_out, "dp", axis=1, tiled=True),
    )
    back_in = back_in[0]
    back_out = back_out[0]

    def grad_inputs(tick, incoming):
        index_mb = tick - (sections - 1 - here)
        valid = (index_mb >= 0) & (index_mb < block_count)
        slot = jnp.clip(index_mb, 0, block_count - 1)
        residual = lax.dynamic_index_in_dim(saved, slot, 0, keepdims=False)
        cot_rows = lax.dynamic_index_in_dim(cot_blocks, slot, 0, keepdims=False)
        expanded = jnp.dot(incoming, full_space.T, preferred_element_type=jnp.float32)
        grad_y = jnp.where(here == sections - 1, cot_rows.astype(jnp.float32), expanded)
        return (valid, slot, residual, grad_y)

    def backward_step(tick, carry):
        incoming, sum_in, sum_out = carry
        valid, slot, residual, grad_y = grad_inputs(tick, incoming)

        def backward_working(state):
            sent_back, grad_half, grad_inner, normed, active = backward_data(
                residual, grad_y, gain_row, back_in, back_out, full_space
            )
            grad_win = jnp.dot(normed.T, grad_inner, preferred_element_type=jnp.float32)
            grad_wout = jnp.dot(grad_half.T, active, preferred_element_type=jnp.float32)
            return (sent_back, state[0] + grad_win, state[1] + grad_wout)

        def backward_waiting(state):
            return (jnp.zeros_like(incoming), state[0], state[1])

        sent_back, sum_in, sum_out = lax.cond(
            valid, backward_working, backward_waiting, (sum_in, sum_out)
        )
        return (pass_back(sent_back), sum_in, sum_out)

    start_bwd = (
        jnp.zeros((block_rows, code_size), jnp.bfloat16),
        jnp.zeros((width, rank_size), jnp.float32),
        jnp.zeros((width, rank_size), jnp.float32),
    )
    ignored, sum_in, sum_out = lax.fori_loop(
        0, sections + block_count - 1, backward_step, start_bwd
    )
    total_in, total_out = (
        lax.psum_scatter(sum_in, "dp", scatter_dimension=0, tiled=True),
        lax.psum_scatter(sum_out, "dp", scatter_dimension=0, tiled=True),
    )
    return (code_store.reshape(1, rows, code_size), total_in[None], total_out[None])


def solution(mesh):
    placed = (
        P("dp", None),
        P("dp", None),
        P("section", None),
        P("section", "dp", None),
        P("section", "dp", None),
        P("dp", None),
    )
    return jax.shard_map(
        on_device,
        mesh=mesh,
        in_specs=placed,
        out_specs=(P("section", "dp", None), P("section", "dp", None), P("section", "dp", None)),
        check_vma=False,
    )
```

profile of v0, /device:TPU:0, one launch (start us, length us, event | category | flops | bytes accessed | tf_op | source)
XLA Modules:
  0.0 534.3 jit_solution(1484121048455027655)
XLA Ops:
  9.4 44.9 %all-gather.6.cloned.1.call-done = bf16[1,8192,128]{2,1,0:T(8,128)(2,1)} async-done(((bf16[1,512,128]{2,1,0:T(8,128)(2,1)}), bf16[1,8192,128]{2,1,0:T(8,128)(2,1)}) %all-gather.6.cloned.1.call-update) | async-done | bytes 2097168 | tf_op jit(solution)/shard_map/all_gather | solution.py:68
  54.3 42.4 %all-gather.8.cloned.1.call-done = bf16[1,8192,128]{2,1,0:T(8,128)(2,1)} async-done(((bf16[1,512,128]{2,1,0:T(8,128)(2,1)}), bf16[1,8192,128]{2,1,0:T(8,128)(2,1)}) %all-gather.8.cloned.1.call-update) | async-done | bytes 2097168 | tf_op jit(solution)/shard_map/all_gather | solution.py:69
  96.7 51.5 %all-gather.4.cloned.1.call-done = bf16[8192,256]{1,0:T(8,128)(2,1)} async-done(((bf16[512,256]{1,0:T(8,128)(2,1)}), bf16[8192,256]{1,0:T(8,128)(2,1)}) %all-gather.4.cloned.1.call-update) | async-done | bytes 4194320 | tf_op jit(solution)/shard_map/all_gather | solution.py:65
  151.6 81.4 %while.36 = (s32[]{:T(128)}, bf16[128,256]{1,0:T(8,128)(2,1)S(1)}, bf16[3,128,8192]{2,1,0:T(8,128)(2,1)}, bf16[3,128,256]{2,1,0:T(8,128)(2,1)S(1)}, s32[]{:T(128...) while((s32[]{:T(128)}, bf16[128,256]{1,0:T(8,128)(2,1)S(1)}, ...), condition=%wide.region_4.5_spmd, body=%wide.region_0.4_spmd.sunk | while | flops 1627504768 | bytes 44600744 | solution.py:109
  151.6 14.9 %conditional.4 = (bf16[128,256]{1,0:T(8,128)(2,1)S(1)}, bf16[3,128,8192]{2,1,0:T(8,128)(2,1)}, bf16[3,128,256]{2,1,0:T(8,128)(2,1)S(1)}) conditional(s32[]{:T(128)} %convert_element_type.177, (bf16[3,128,8192]{2,1,0:T(8,128)(2,1)}, bf16[3,128,256]{2,1,0:T(8,128)(2,1)S(1)}) %tuple.102, (s32[]{:T(128)}, s32[]{:T(128)}, bf16[3,128,8192]{2,1,0:T(8,128)(2,1)}, ...), branch_computations={%region_1.1_spmd, %region_2.3_spmd} | conditional | flops 1627504768 | bytes 44338300 | solution.py:98
  169.8 14.9 %conditional.4 = (bf16[128,256]{1,0:T(8,128)(2,1)S(1)}, bf16[3,128,8192]{2,1,0:T(8,128)(2,1)}, bf16[3,128,256]{2,1,0:T(8,128)(2,1)S(1)}) conditional(s32[]{:T(128)} %convert_element_type.177, (bf16[3,128,8192]{2,1,0:T(8,128)(2,1)}, bf16[3,128,256]{2,1,0:T(8,128)(2,1)S(1)}) %tuple.102, (s32[]{:T(128)}, s32[]{:T(128)}, bf16[3,128,8192]{2,1,0:T(8,128)(2,1)}, ...), branch_computations={%region_1.1_spmd, %region_2.3_spmd} | conditional | flops 1627504768 | bytes 44338300 | solution.py:98
  191.0 14.9 %conditional.4 = (bf16[128,256]{1,0:T(8,128)(2,1)S(1)}, bf16[3,128,8192]{2,1,0:T(8,128)(2,1)}, bf16[3,128,256]{2,1,0:T(8,128)(2,1)S(1)}) conditional(s32[]{:T(128)} %convert_element_type.177, (bf16[3,128,8192]{2,1,0:T(8,128)(2,1)}, bf16[3,128,256]{2,1,0:T(8,128)(2,1)S(1)}) %tuple.102, (s32[]{:T(128)}, s32[]{:T(128)}, bf16[3,128,8192]{2,1,0:T(8,128)(2,1)}, ...), branch_computations={%region_1.1_spmd, %region_2.3_spmd} | conditional | flops 1627504768 | bytes 44338300 | solution.py:98
  212.0 19.2 %collective-permute-start = (bf16[128,256]{1,0:T(8,128)(2,1)S(1)}, bf16[128,256]{1,0:T(8,128)(2,1)S(1)}, u32[]{:S(2)}, u32[]{:S(2)}) collective-permute-start(bf16[128,256]{1,0:T(8,128)(2,1)S(1)} %get-tuple-element.869), channel_id=1, source_target_pairs={{0,16},{1,17},{2,18},{3,19},{4,20},{5,21},{6,22},{7,23},{8,24},{9,... | collective-permute-start | bytes 196616 | tf_op jit(solution)/shard_map/while/body/eval_jaxpr/ppermute | solution.py:12
  237.6 143.8 %while.37 = (s32[]{:T(128)}, bf16[128,256]{1,0:T(8,128)(2,1)S(1)}, f32[8192,128]{1,0:T(8,128)}, f32[8192,128]{1,0:T(8,128)}, s32[]{:T(128)}, /*index=5*/bf16[819...) while((s32[]{:T(128)}, bf16[128,256]{1,0:T(8,128)(2,1)S(1)}, ...), condition=%wide.region_10.11_spmd, body=%wide.region_5.10_spmd.sunk | while | flops 2445541888 | bytes 135011344 | solution.py:154
  237.6 5.7 %fusion.69 = f32[128,8192]{1,0:T(8,128)} fusion(bf16[128,256]{1,0:T(8,128)(2,1)S(1)} %get-tuple-element.954, bf16[8192,256]{1,0:T(8,128)(2,1)} %get-tuple-element.973), kind=kOutput, calls=%fused_computation.61.clone.1 | convolution fusion | flops 536870912 | bytes 8454144 | tf_op jit(solution)/shard_map/while/body/eval_jaxpr/dot_general | solution.py:125
  244.6 28.7 %collective-permute-done.1 = bf16[128,256]{1,0:T(8,128)(2,1)S(1)} collective-permute-done((bf16[128,256]{1,0:T(8,128)(2,1)S(1)}, bf16[128,256]{1,0:T(8,128)(2,1)S(1)}, u32[]{:S(2)}, u32[]{:S(2)}) %collective-permute-start.1) | collective-permute-done | bytes 65568 | tf_op jit(solution)/shard_map/while/body/eval_jaxpr/ppermute | solution.py:12
  273.3 5.7 %fusion.69 = f32[128,8192]{1,0:T(8,128)} fusion(bf16[128,256]{1,0:T(8,128)(2,1)S(1)} %get-tuple-element.954, bf16[8192,256]{1,0:T(8,128)(2,1)} %get-tuple-element.973), kind=kOutput, calls=%fused_computation.61.clone.1 | convolution fusion | flops 536870912 | bytes 8454144 | tf_op jit(solution)/shard_map/while/body/eval_jaxpr/dot_general | solution.py:125
  279.1 24.1 %conditional.5 = (bf16[128,256]{1,0:T(8,128)(2,1)S(1)}, f32[8192,128]{1,0:T(8,128)}, f32[8192,128]{1,0:T(8,128)}) conditional(s32[]{:T(128)} %convert_element_type.178, (f32[8192,128]{1,0:T(8,128)}, f32[8192,128]{1,0:T(8,128)}) %tuple.105, (pred[]{:T(512)}, s32[]{:T(128)}, bf16[3,128,8192]{2,1,0:T(8,128)(2,1)}, f32[128,8192]{1,0:T(8,128)}, ...), branch_computations={%region_6.6_spmd, %region_7.9_spmd} | conditional | flops 1908670848 | bytes 126294728 | solution.py:144
  287.3 5.5 %convolution_add_fusion.2 = f32[8192,128]{1,0:T(8,128)} fusion(f32[8192,128]{1,0:T(8,128)} %get-tuple-element.661, bf16[128,8192]{1,0:T(8,128)(2,1)S(1)} %fusion.23, f32[128,128]{1,0:T(8,128)S(1)} %fusion.40), kind=kOutput, calls=%fused_computation.21 | convolution fusion | flops 269565952 | bytes 10551296 | tf_op jit(solution)/shard_map/while/body/eval_jaxpr/cond/branch_1_fun/dot_general | solution.py:138
  298.0 5.2 convolution_add_fusion.3
  309.3 5.7 %fusion.69 = f32[128,8192]{1,0:T(8,128)} fusion(bf16[128,256]{1,0:T(8,128)(2,1)S(1)} %get-tuple-element.954, bf16[8192,256]{1,0:T(8,128)(2,1)} %get-tuple-element.973), kind=kOutput, calls=%fused_computation.61.clone.1 | convolution fusion | flops 536870912 | bytes 8454144 | tf_op jit(solution)/shard_map/while/body/eval_jaxpr/dot_general | solution.py:125
  315.1 24.1 %conditional.5 = (bf16[128,256]{1,0:T(8,128)(2,1)S(1)}, f32[8192,128]{1,0:T(8,128)}, f32[8192,128]{1,0:T(8,128)}) conditional(s32[]{:T(128)} %convert_element_type.178, (f32[8192,128]{1,0:T(8,128)}, f32[8192,128]{1,0:T(8,128)}) %tuple.105, (pred[]{:T(512)}, s32[]{:T(128)}, bf16[3,128,8192]{2,1,0:T(8,128)(2,1)}, f32[128,8192]{1,0:T(8,128)}, ...), branch_computations={%region_6.6_spmd, %region_7.9_spmd} | conditional | flops 1908670848 | bytes 126294728 | solution.py:144
  323.3 5.5 %convolution_add_fusion.2 = f32[8192,128]{1,0:T(8,128)} fusion(f32[8192,128]{1,0:T(8,128)} %get-tuple-element.661, bf16[128,8192]{1,0:T(8,128)(2,1)S(1)} %fusion.23, f32[128,128]{1,0:T(8,128)S(1)} %fusion.40), kind=kOutput, calls=%fused_computation.21 | convolution fusion | flops 269565952 | bytes 10551296 | tf_op jit(solution)/shard_map/while/body/eval_jaxpr/cond/branch_1_fun/dot_general | solution.py:138
  334.1 5.2 convolution_add_fusion.3
  345.4 5.7 %fusion.69 = f32[128,8192]{1,0:T(8,128)} fusion(bf16[128,256]{1,0:T(8,128)(2,1)S(1)} %get-tuple-element.954, bf16[8192,256]{1,0:T(8,128)(2,1)} %get-tuple-element.973), kind=kOutput, calls=%fused_computation.61.clone.1 | convolution fusion | flops 536870912 | bytes 8454144 | tf_op jit(solution)/shard_map/while/body/eval_jaxpr/dot_general | solution.py:125
  351.1 24.1 %conditional.5 = (bf16[128,256]{1,0:T(8,128)(2,1)S(1)}, f32[8192,128]{1,0:T(8,128)}, f32[8192,128]{1,0:T(8,128)}) conditional(s32[]{:T(128)} %convert_element_type.178, (f32[8192,128]{1,0:T(8,128)}, f32[8192,128]{1,0:T(8,128)}) %tuple.105, (pred[]{:T(512)}, s32[]{:T(128)}, bf16[3,128,8192]{2,1,0:T(8,128)(2,1)}, f32[128,8192]{1,0:T(8,128)}, ...), branch_computations={%region_6.6_spmd, %region_7.9_spmd} | conditional | flops 1908670848 | bytes 126294728 | solution.py:144
  359.3 5.5 %convolution_add_fusion.2 = f32[8192,128]{1,0:T(8,128)} fusion(f32[8192,128]{1,0:T(8,128)} %get-tuple-element.661, bf16[128,8192]{1,0:T(8,128)(2,1)S(1)} %fusion.23, f32[128,128]{1,0:T(8,128)S(1)} %fusion.40), kind=kOutput, calls=%fused_computation.21 | convolution fusion | flops 269565952 | bytes 10551296 | tf_op jit(solution)/shard_map/while/body/eval_jaxpr/cond/branch_1_fun/dot_general | solution.py:138
  382.0 69.5 %reduce-scatter.3.cloned.1.call-done = f32[512,128]{1,0:T(8,128)} async-done(((f32[8192,128]{1,0:T(8,128)}), f32[512,128]{1,0:T(8,128)}) %reduce-scatter.3.cloned.1.call-update) | async-done | bytes 262160 | tf_op jit(solution)/shard_map/reduce_scatter | solution.py:158
  451.5 76.3 %reduce-scatter.5.cloned.1.call-done = f32[512,128]{1,0:T(8,128)} async-done(((f32[8192,128]{1,0:T(8,128)}), f32[512,128]{1,0:T(8,128)}) %reduce-scatter.5.cloned.1.call-update) | async-done | bytes 262160 | tf_op jit(solution)/shard_map/reduce_scatter | solution.py:159
  (125 shorter events, 138.0 us)
Async XLA Ops:
  7.2 144.5 %copy-start.6 = (f32[1,8192]{1,0:T(1,128)S(1)}, f32[1,8192]{1,0:T(1,128)}, u32[]{:S(2)}) copy-start(f32[1,8192]{1,0:T(1,128)} %param.16) | copy-start | bytes 98308
  7.2 47.1 %all-gather.6.cloned.1.call-start = ((), (), s32[]{:S(2)}) async-start(), calls=%async_computation.3 | async-start | bytes 2228224 | tf_op jit(solution)/shard_map/all_gather | solution.py:68
  7.9 88.8 %all-gather.8.cloned.1.call-start = ((), (), s32[]{:S(2)}) async-start(), calls=%async_computation.4 | async-start | bytes 2228224 | tf_op jit(solution)/shard_map/all_gather | solution.py:69
  8.7 139.5 %all-gather.4.cloned.1.call-start = ((), (), s32[]{:S(2)}) async-start(), calls=%async_computation.2 | async-start | bytes 4456448 | tf_op jit(solution)/shard_map/all_gather | solution.py:65
  9.4 442.1 %reduce-scatter.3.cloned.1.call-start = ((), (), s32[]{:S(2)}) async-start(), calls=%async_computation.5 | async-start | bytes 4456448 | tf_op jit(solution)/shard_map/reduce_scatter | solution.py:158
  96.7 55.0 %copy-start.2 = (bf16[1,8192,128]{2,1,0:T(8,128)(2,1)S(1)}, bf16[1,8192,128]{2,1,0:T(8,128)(2,1)}, u32[]{:S(2)}) copy-start(bf16[1,8192,128]{2,1,0:T(8,128)(2,1)} %all-gather.8.cloned.1.call-done) | copy-start | bytes 6291460
  151.6 6.1 %copy-start.4 = (bf16[8192,128]{1,0:T(8,128)(2,1)S(1)}, bf16[8192,128]{1,0:T(8,128)(2,1)}, u32[]{:S(2)}) copy-start(bf16[8192,128]{1,0:T(8,128)(2,1)} %get-tuple-element.631) | copy-start | bytes 6291460 | tf_op jit(solution)/shard_map/while/body/eval_jaxpr/cond
  166.5 3.3 collective-permute-start
  169.8 6.1 %copy-start.4 = (bf16[8192,128]{1,0:T(8,128)(2,1)S(1)}, bf16[8192,128]{1,0:T(8,128)(2,1)}, u32[]{:S(2)}) copy-start(bf16[8192,128]{1,0:T(8,128)(2,1)} %get-tuple-element.631) | copy-start | bytes 6291460 | tf_op jit(solution)/shard_map/while/body/eval_jaxpr/cond
  184.7 6.3 %collective-permute-start = (bf16[128,256]{1,0:T(8,128)(2,1)S(1)}, bf16[128,256]{1,0:T(8,128)(2,1)S(1)}, u32[]{:S(2)}, u32[]{:S(2)}) collective-permute-start(bf16[128,256]{1,0:T(8,128)(2,1)S(1)} %get-tuple-element.869), channel_id=1, source_target_pairs={{0,16},{1,17},{2,18},{3,19},{4,20},{5,21},{6,22},{7,23},{8,24},{9,... | collective-permute-start | bytes 196616 | tf_op jit(solution)/shard_map/while/body/eval_jaxpr/ppermute | solution.py:12
  191.0 6.0 %copy-start.4 = (bf16[8192,128]{1,0:T(8,128)(2,1)S(1)}, bf16[8192,128]{1,0:T(8,128)(2,1)}, u32[]{:S(2)}) copy-start(bf16[8192,128]{1,0:T(8,128)(2,1)} %get-tuple-element.631) | copy-start | bytes 6291460 | tf_op jit(solution)/shard_map/while/body/eval_jaxpr/cond
  205.9 6.1 %collective-permute-start = (bf16[128,256]{1,0:T(8,128)(2,1)S(1)}, bf16[128,256]{1,0:T(8,128)(2,1)S(1)}, u32[]{:S(2)}, u32[]{:S(2)}) collective-permute-start(bf16[128,256]{1,0:T(8,128)(2,1)S(1)} %get-tuple-element.869), channel_id=1, source_target_pairs={{0,16},{1,17},{2,18},{3,19},{4,20},{5,21},{6,22},{7,23},{8,24},{9,... | collective-permute-start | bytes 196616 | tf_op jit(solution)/shard_map/while/body/eval_jaxpr/ppermute | solution.py:12
  212.0 21.1 %collective-permute-start = (bf16[128,256]{1,0:T(8,128)(2,1)S(1)}, bf16[128,256]{1,0:T(8,128)(2,1)S(1)}, u32[]{:S(2)}, u32[]{:S(2)}) collective-permute-start(bf16[128,256]{1,0:T(8,128)(2,1)S(1)} %get-tuple-element.869), channel_id=1, source_target_pairs={{0,16},{1,17},{2,18},{3,19},{4,20},{5,21},{6,22},{7,23},{8,24},{9,... | collective-permute-start | bytes 196616 | tf_op jit(solution)/shard_map/while/body/eval_jaxpr/ppermute | solution.py:12
  243.3 30.0 %collective-permute-start.1 = (bf16[128,256]{1,0:T(8,128)(2,1)S(1)}, bf16[128,256]{1,0:T(8,128)(2,1)S(1)}, u32[]{:S(2)}, u32[]{:S(2)}) collective-permute-start(bf16[128,256]{1,0:T(8,128)(2,1)S(1)} %get-tuple-element.884), channel_id=1, source_target_pairs={{16,0},{17,1},{18,2},{19,3},{20,4},{21,5},{22,6},{23,7},{24,8},{25... | collective-permute-start | bytes 196616 | tf_op jit(solution)/shard_map/while/body/eval_jaxpr/ppermute | solution.py:12
  286.5 6.3 %slice-start = ((s8[6291456]{0:T(1024)(128)(4,1)}), s8[4194304]{0:T(1024)(128)(4,1)S(1)}, s32[]{:S(2)}) async-start(s8[6291456]{0:T(1024)(128)(4,1)} %bitcast.64), calls=%async_computation.7 | async-start | bytes 8388608 | tf_op jit(solution)/shard_map/while/body/eval_jaxpr/cond
  287.2 5.5 %slice-start.1 = ((s8[6291456]{0:T(1024)(128)(4,1)}), s8[2097152]{0:T(1024)(128)(4,1)S(1)}, s32[]{:S(2)}) async-start(s8[6291456]{0:T(1024)(128)(4,1)} %bitcast.64), calls=%async_computation.8 | async-start | bytes 4194304 | tf_op jit(solution)/shard_map/while/body/eval_jaxpr/cond
  303.2 6.1 %collective-permute-start.1 = (bf16[128,256]{1,0:T(8,128)(2,1)S(1)}, bf16[128,256]{1,0:T(8,128)(2,1)S(1)}, u32[]{:S(2)}, u32[]{:S(2)}) collective-permute-start(bf16[128,256]{1,0:T(8,128)(2,1)S(1)} %get-tuple-element.884), channel_id=1, source_target_pairs={{16,0},{17,1},{18,2},{19,3},{20,4},{21,5},{22,6},{23,7},{24,8},{25... | collective-permute-start | bytes 196616 | tf_op jit(solution)/shard_map/while/body/eval_jaxpr/ppermute | solution.py:12
  322.5 6.3 %slice-start = ((s8[6291456]{0:T(1024)(128)(4,1)}), s8[4194304]{0:T(1024)(128)(4,1)S(1)}, s32[]{:S(2)}) async-start(s8[6291456]{0:T(1024)(128)(4,1)} %bitcast.64), calls=%async_computation.7 | async-start | bytes 8388608 | tf_op jit(solution)/shard_map/while/body/eval_jaxpr/cond
  323.3 5.5 %slice-start.1 = ((s8[6291456]{0:T(1024)(128)(4,1)}), s8[2097152]{0:T(1024)(128)(4,1)S(1)}, s32[]{:S(2)}) async-start(s8[6291456]{0:T(1024)(128)(4,1)} %bitcast.64), calls=%async_computation.8 | async-start | bytes 4194304 | tf_op jit(solution)/shard_map/while/body/eval_jaxpr/cond
  339.2 6.1 %collective-permute-start.1 = (bf16[128,256]{1,0:T(8,128)(2,1)S(1)}, bf16[128,256]{1,0:T(8,128)(2,1)S(1)}, u32[]{:S(2)}, u32[]{:S(2)}) collective-permute-start(bf16[128,256]{1,0:T(8,128)(2,1)S(1)} %get-tuple-element.884), channel_id=1, source_target_pairs={{16,0},{17,1},{18,2},{19,3},{20,4},{21,5},{22,6},{23,7},{24,8},{25... | collective-permute-start | bytes 196616 | tf_op jit(solution)/shard_map/while/body/eval_jaxpr/ppermute | solution.py:12
  358.5 6.3 %slice-start = ((s8[6291456]{0:T(1024)(128)(4,1)}), s8[4194304]{0:T(1024)(128)(4,1)S(1)}, s32[]{:S(2)}) async-start(s8[6291456]{0:T(1024)(128)(4,1)} %bitcast.64), calls=%async_computation.7 | async-start | bytes 8388608 | tf_op jit(solution)/shard_map/while/body/eval_jaxpr/cond
  359.3 5.5 %slice-start.1 = ((s8[6291456]{0:T(1024)(128)(4,1)}), s8[2097152]{0:T(1024)(128)(4,1)S(1)}, s32[]{:S(2)}) async-start(s8[6291456]{0:T(1024)(128)(4,1)} %bitcast.64), calls=%async_computation.8 | async-start | bytes 4194304 | tf_op jit(solution)/shard_map/while/body/eval_jaxpr/cond
  375.2 6.1 %collective-permute-start.1 = (bf16[128,256]{1,0:T(8,128)(2,1)S(1)}, bf16[128,256]{1,0:T(8,128)(2,1)S(1)}, u32[]{:S(2)}, u32[]{:S(2)}) collective-permute-start(bf16[128,256]{1,0:T(8,128)(2,1)S(1)} %get-tuple-element.884), channel_id=1, source_target_pairs={{16,0},{17,1},{18,2},{19,3},{20,4},{21,5},{22,6},{23,7},{24,8},{25... | collective-permute-start | bytes 196616 | tf_op jit(solution)/shard_map/while/body/eval_jaxpr/ppermute | solution.py:12
  381.4 146.4 %reduce-scatter.5.cloned.1.call-start = ((), (), s32[]{:S(2)}) async-start(), calls=%async_computation.6 | async-start | bytes 4456448 | tf_op jit(solution)/shard_map/reduce_scatter | solution.py:159
  (13 other events, 47.5 us)
Sparse Core Ops, SparseCore 0:
  10.2 44.0 all-gather.5
  56.5 40.1 all-gather.7
  98.8 49.3 all-gather.3
  381.5 69.9 reduce-scatter.2
  456.3 71.4 reduce-scatter.4
where the time goes:
time: 535 us; the launch traced here: 534 us
  waiting for transfers between devices  338 us (63%)
  matrix products  109 us (20%)
  starting transfers between devices  34.4 us (6%)
  local copies, waits for them, and re-layouts  25.4 us (5%)
  between operations  13.8 us (3%)
  other arithmetic  13 us (2%)
    reduce_scatter x1, waiting for transfers between devices, on_device(): lax.psum_scatter(sum_out, 'dp', scatter_dimension=0, tiled=True)  76.3 us
    reduce_scatter x1, waiting for transfers between devices, on_device(): lax.psum_scatter(sum_in, 'dp', scatter_dimension=0, tiled=True)  69.5 us
    all_gather x1, waiting for transfers between devices, on_device(): full_space = lax.all_gather(subspace, 'dp', axis=0, tiled=True)  51.5 us
    ppermute x8, waiting for transfers between devices, from_behind(): return lax.ppermute(value, axis, pairs)  50.9 us
    all_gather x1, waiting for transfers between devices, on_device(): lax.all_gather(weight_in, 'dp', axis=1, tiled=True)  44.9 us
    all_gather x1, waiting for transfers between devices, on_device(): lax.all_gather(weight_out, 'dp', axis=1, tiled=True)  42.4 us
    ppermute x8, starting transfers between devices, from_behind(): return lax.ppermute(value, axis, pairs)  34.2 us
    dot_general x4, matrix products, grad_inputs(): jnp.dot(incoming, full_space.T, preferred_element_type=jnp.float32)  23 us
  transfers between devices with their start and end apart: 13, of which 13 were waited for; matrix products, arithmetic and copies ran while one was open for 0% of the time, Pallas kernels for 0%

commit v1 on v0

v1 whole, which is shorter than its diff:
```python
import jax
import jax.numpy as jnp
from jax import lax
from jax.sharding import PartitionSpec as P

F32 = jnp.float32
BF16 = jnp.bfloat16


def mm(a, b, dims=((1,), (0,))):
    return lax.dot_general(a, b, (dims, ((), ())), preferred_element_type=F32)


def exact(a, b, dims=((1,), (0,))):
    return lax.dot_general(
        a.astype(F32),
        b.astype(F32),
        (dims, ((), ())),
        precision=lax.Precision.HIGHEST,
        preferred_element_type=F32,
    )


def swap(value, axis, bit):
    peers = lax.axis_size(axis)
    return lax.ppermute(value, axis, [(i, i ^ bit) for i in range(peers)])


def sum_over(value, axis):
    peers = lax.axis_size(axis)
    bit = 1
    while bit < peers:
        value = value + swap(value, axis, bit)
        bit *= 2
    return value


def share_sections(value):
    sections = lax.axis_size("section")
    here = lax.axis_index("section")
    around = [(i, (i + 1) % sections) for i in range(sections)]
    held = [value]
    for _ in range(sections - 1):
        held.append(lax.ppermute(held[-1], "section", around))
    stacked = jnp.stack(held)
    order = (here - jnp.arange(sections)) % sections
    return [lax.dynamic_index_in_dim(stacked, order[s], 0, keepdims=False) for s in range(sections)]


def pick(values, index):
    return lax.dynamic_index_in_dim(jnp.stack(values), index, 0, keepdims=False)


def chain(squares, based, coted, aux, gram, width, last_rank):
    base_p, base_s = based
    cot_w, cot_s = coted
    sections = len(base_p)
    acts, codes, inners, inverses, resid_s = [], [], [], [], []
    code = None
    for s in range(sections):
        m_s, q_t = aux[s]
        if s == 0:
            total, moved, inner = squares, None, base_p[s]
            resid_s.append(base_s)
        else:
            code_f = code.astype(F32)
            moved = exact(code, gram)
            total = squares + jnp.sum((2.0 * base_s + moved) * code_f, axis=-1, keepdims=True)
            inner = base_p[s] + exact(code, q_t, ((1,), (1,)))
            resid_s.append(base_s + moved)
        inverse = lax.rsqrt(jnp.maximum(total, 0.0) / width + 1e-05)
        inner = inner * inverse
        active = inner * jax.nn.sigmoid(inner)
        grown = exact(active, m_s)
        code = (grown if s == 0 else moved + grown).astype(BF16)
        acts.append(active.astype(BF16))
        codes.append(code)
        inners.append(inner)
        inverses.append(inverse)
    scaled, t_in, t_out = [None] * sections, [None] * sections, [None] * sections
    back = None
    for s in range(sections - 1, -1, -1):
        m_s, q_t = aux[s]
        if s == sections - 1:
            grad_active, grad_y = cot_w, cot_s
            t_out[s] = jnp.zeros((gram.shape[0], acts[s].shape[1]), F32)
        else:
            grad_active, grad_y = exact(back, m_s, ((1,), (1,))), exact(back, gram)
            t_out[s] = mm(back, acts[s], ((0,), (0,)))
        inner, inverse = inners[s], inverses[s]
        logistic = jax.nn.sigmoid(inner)
        grad_inner = grad_active * logistic * (1.0 + inner * (1.0 - logistic))
        scaled[s] = (inverse * grad_inner).astype(BF16)
        if s > 0:
            t_in[s] = mm(codes[s - 1], scaled[s], ((0,), (0,)))
            along = jnp.sum(inner * grad_inner, axis=-1, keepdims=True) * (inverse * inverse / width)
            back = (grad_y + exact(scaled[s], q_t) - resid_s[s] * along).astype(BF16)
        else:
            t_in[s] = jnp.zeros((gram.shape[0], acts[s].shape[1]), F32)
    return codes, acts, scaled, t_in, t_out


def on_device(base, cotangent, gain, weight_in, weight_out, subspace):
    sections = lax.axis_size("section")
    here = lax.axis_index("section")
    spot = lax.axis_index("dp")
    rows, width = base.shape
    part, size = subspace.shape
    rank = weight_in.shape[2]
    last = sections - 1
    own_gain = lax.dynamic_slice_in_dim(gain[0], spot * part, part, 0)[:, None]
    scaled_in = (own_gain * weight_in[0].astype(F32)).astype(BF16)
    out_rows = weight_out[0]
    cut = size - rank // 2
    first_part = jnp.concatenate([scaled_in, subspace[:, :cut]], axis=1)
    last_part = jnp.concatenate([scaled_in, out_rows, subspace[:, cut:]], axis=1)
    mine = jnp.where(here == last, last_part, first_part)
    wide = lax.all_gather(mine, "dp", axis=0, tiled=True)

    small = mm(jnp.concatenate([out_rows, scaled_in, subspace], axis=1), subspace, ((0,), (0,)))
    small = sum_over(small, "dp")
    aux = [(a[:rank], a[rank:]) for a in share_sections(small[: 2 * rank].astype(BF16))]
    gram = small[2 * rank :]

    base_f = base.astype(F32)
    squares = jnp.sum(base_f * base_f, axis=-1, keepdims=True)
    from_base = mm(base, wide)
    from_cot = mm(cotangent, wide[:, rank:])
    projected = share_sections(jnp.concatenate([from_base, from_cot], axis=1).astype(BF16))
    projected = [p.astype(F32) for p in projected]
    base_p = [p[:, :rank] for p in projected]
    ends = rank + cut
    base_s = jnp.concatenate([projected[0][:, rank:ends], projected[last][:, 2 * rank : ends]], axis=1)
    cot_w = projected[last][:, ends : ends + rank]
    cot_s = jnp.concatenate([projected[0][:, ends:], projected[last][:, ends + rank :]], axis=1)
    codes, acts, scaled, t_in, t_out = chain(
        squares, (base_p, base_s), (cot_w, cot_s), aux, gram, width, rank
    )
    my_scaled = pick(scaled, here)
    grad_in = mm(base, my_scaled, ((0,), (0,))).astype(BF16)
    grad_out = mm(cotangent, acts[last], ((0,), (0,))).astype(BF16)
    both = lax.psum_scatter(
        jnp.concatenate([grad_in, grad_out], axis=1), "dp", scatter_dimension=0, tiled=True
    ).astype(F32)
    thin = jnp.concatenate([pick(t_in, here), pick(t_out, here)], axis=1)
    thin = sum_over(thin, "dp")
    lifted = mm(subspace, thin.astype(BF16))
    total_in = own_gain * (both[:, :rank] + lifted[:, :rank])
    total_out = jnp.where(here == last, both[:, rank:], lifted[:, rank:])
    return pick(codes, here)[None], total_in[None], total_out[None]


def solution(mesh):
    placed = (
        P("dp", None),
        P("dp", None),
        P("section", None),
        P("section", "dp", None),
        P("section", "dp", None),
        P("dp", None),
    )
    return jax.shard_map(
        on_device,
        mesh=mesh,
        in_specs=placed,
        out_specs=(P("section", "dp", None), P("section", "dp", None), P("section", "dp", None)),
        check_vma=False,
    )
```

time: 535 us -> 219 us (0.41)
  waiting for transfers between devices: 338 us -> 150 us
  matrix products: 109 us -> 19.1 us
  starting transfers between devices: 34.4 us -> 13.1 us
  local copies, waits for them, and re-layouts: 25.4 us -> 8.9 us
    reduce_scatter x2 -> x1, waiting for transfers between devices: 146 us -> 39.8 us  [on_device(): lax.psum_scatter(jnp.concatenate([grad_in, grad_out], axis=1), 'dp', scat...]
    all_gather x3 -> x1, waiting for transfers between devices: 139 us -> 44.4 us  [on_device(): wide = lax.all_gather(mine, 'dp', axis=0, tiled=True)]
    dot_general x31 -> x14, matrix products: 109 us -> 19.1 us  [the longest x8 17.1 us: mm(): return lax.dot_general(a, b, (dims, ((), ())), preferred_element_type=F32)]
    ppermute x8 -> x10, starting transfers between devices: 34.2 us -> 13 us  [the longest x8 10.9 us: swap(): return lax.ppermute(value, axis, [(i, i ^ bit) for i in range(peers)])]
    ppermute x8 -> x10, waiting for transfers between devices: 50.9 us -> 65.4 us  [the longest x8 58 us: swap(): return lax.ppermute(value, axis, [(i, i ^ bit) for i in range(peers)])]
    dynamic_update_slice x3 -> x0, local copies, waits for them, and re-layouts: 9.34 us -> none  [forward_working(): new_saved = lax.dynamic_update_index_in_dim(state[0], residual, slot, 0)]
    cond x42 -> x0, local copies, waits for them, and re-layouts: 8.04 us -> none
    unnamed x6 -> x21, local copies, waits for them, and re-layouts: 0.01 us -> 7.05 us
  transfers between devices with their start and end apart: 13 -> 12, of which waited for: 13 -> 10; matrix products, arithmetic and copies ran while one was open for 0% -> 10% of each run, Pallas kernels for 0% -> 0%
where the time goes in v1:
time: 219 us; the launch traced here: 218 us
  waiting for transfers between devices  150 us (68%)
  matrix products  19.1 us (9%)
  between operations  18.3 us (8%)
  starting transfers between devices  13.1 us (6%)
  other arithmetic  9.2 us (4%)
  local copies, waits for them, and re-layouts  8.9 us (4%)
    ppermute x8, waiting for transfers between devices, swap(): return lax.ppermute(value, axis, [(i, i ^ bit) for i in range(peers)])  58 us
    all_gather x1, waiting for transfers between devices, on_device(): wide = lax.all_gather(mine, 'dp', axis=0, tiled=True)  44.4 us
    reduce_scatter x1, waiting for transfers between devices, on_device(): lax.psum_scatter(jnp.concatenate([grad_in, grad_out], axis=1), 'dp', scat...  39.8 us
    dot_general x8, matrix products, mm(): return lax.dot_general(a, b, (dims, ((), ())), preferred_element_type=F32)  17.1 us
    ppermute x8, starting transfers between devices, swap(): return lax.ppermute(value, axis, [(i, i ^ bit) for i in range(peers)])  10.9 us
    ppermute x2, waiting for transfers between devices, share_sections(): held.append(lax.ppermute(held[-1], 'section', around))  7.38 us
    unnamed x21, local copies, waits for them, and re-layouts  7.05 us
  transfers between devices with their start and end apart: 12, of which 10 were waited for; matrix products, arithmetic and copies ran while one was open for 10% of the time, Pallas kernels for 0%

profile of v1, /device:TPU:0, one launch (start us, length us, event | category | flops | bytes accessed | tf_op | source)
XLA Modules:
  0.0 218.3 jit_solution(9447593440351084442)
XLA Ops:
  8.2 1.0 copy.10
  10.4 1.1 copy.26
  12.5 1.4 fusion.14
  14.5 1.5 collective-permute-done.1
  16.1 2.9 %collective-permute-start.2 = (f32[512,256]{1,0:T(8,128)S(1)}, f32[512,256]{1,0:T(8,128)S(1)}, u32[]{:S(2)}, u32[]{:S(2)}) collective-permute-start(f32[512,256]{1,0:T(8,128)S(1)} %add.127), channel_id=1, source_target_pairs={{0,2},{1,3},{2,0},{3,1},{4,6},{5,7},{6,4},{7,5},{8,10},{9,11},{10,... | collective-permute-start | bytes 1572872 | tf_op jit(solution)/shard_map/ppermute | solution.py:26
  19.0 15.7 %collective-permute-done.2 = f32[512,256]{1,0:T(8,128)S(1)} collective-permute-done((f32[512,256]{1,0:T(8,128)S(1)}, f32[512,256]{1,0:T(8,128)S(1)}, u32[]{:S(2)}, u32[]{:S(2)}) %collective-permute-start.2) | collective-permute-done | bytes 524320 | tf_op jit(solution)/shard_map/ppermute | solution.py:26
  34.8 1.9 collective-permute-start.3
  36.7 4.1 %multiply_reduce_fusion = f32[384]{0:T(512)S(1)} fusion(bf16[384,8192]{1,0:T(8,128)(2,1)} %param.6), kind=kLoop, calls=%fused_computation | loop fusion | flops 9436800 | bytes 6292992 | tf_op jit(solution)/shard_map/reduce_sum | solution.py:126
  40.8 13.2 %collective-permute-done.3 = f32[512,256]{1,0:T(8,128)S(1)} collective-permute-done((f32[512,256]{1,0:T(8,128)S(1)}, f32[512,256]{1,0:T(8,128)S(1)}, u32[]{:S(2)}, u32[]{:S(2)}) %collective-permute-start.3) | collective-permute-done | bytes 524320 | tf_op jit(solution)/shard_map/ppermute | solution.py:26
  54.1 2.5 %collective-permute-start.4 = (f32[512,256]{1,0:T(8,128)S(1)}, f32[512,256]{1,0:T(8,128)S(1)}, u32[]{:S(2)}, u32[]{:S(2)}) collective-permute-start(f32[512,256]{1,0:T(8,128)S(1)} %add.129), channel_id=1, source_target_pairs={{0,8},{1,9},{2,10},{3,11},{4,12},{5,13},{6,14},{7,15},{8,0},{9,1},... | collective-permute-start | bytes 1572872 | tf_op jit(solution)/shard_map/ppermute | solution.py:26
  56.7 44.4 %all-gather.2.cloned.1.call-done = bf16[8192,320]{0,1:T(8,128)(2,1)} async-done(((bf16[512,320]{0,1:T(8,128)(2,1)}), bf16[8192,320]{0,1:T(8,128)(2,1)}) %all-gather.2.cloned.1.call-update) | async-done | bytes 5242896 | tf_op jit(solution)/shard_map/all_gather | solution.py:118
  101.0 7.4 %convolution_convert_fusion.2 = bf16[320,384]{1,0:T(8,128)(2,1)S(1)} fusion(bf16[8192,320]{0,1:T(8,128)(2,1)} %all-gather.2.cloned.1.call-done, bf16[384,8192]{1,0:T(8,128)(2,1)} %param.6), kind=kOutput, calls=%fused_computation.11 | convolution fusion | flops 2013388800 | bytes 11780096 | tf_op jit(solution)/shard_map/dot_general | solution.py:11
  108.4 5.1 %fusion.5 = bf16[192,384]{1,0:T(8,128)(2,1)S(1)} fusion(bf16[384,8192]{1,0:T(8,128)(2,1)} %param.7, bf16[8192,320]{0,1:T(8,128)(2,1)S(1)} %copy-done.2), kind=kOutput, calls=%fused_computation.14 | convolution fusion | flops 1208033280 | bytes 9584640 | tf_op jit(solution)/shard_map/dot_general | solution.py:11
  113.5 1.6 collective-permute-start
  120.3 7.4 %collective-permute-done.5 = bf16[256,256]{1,0:T(8,128)(2,1)S(1)} collective-permute-done((bf16[256,256]{1,0:T(8,128)(2,1)S(1)}, bf16[256,256]{1,0:T(8,128)(2,1)S(1)}, u32[]{:S(2)}, u32[]{:S(2)}) %collective-permute-start.5) | collective-permute-done | bytes 131104 | tf_op jit(solution)/shard_map/ppermute | solution.py:44
  129.8 1.3 fusion.1
  132.4 1.3 fusion
  133.7 2.4 %pad_maximum_fusion = bf16[8192,256]{0,1:T(8,128)(2,1)} fusion(bf16[8192,128]{0,1:T(8,128)(2,1)S(1)} %fusion.1, bf16[8192,128]{0,1:T(8,128)(2,1)S(1)} %fusion), kind=kLoop, calls=%fused_computation.5 | loop fusion | flops 8388608 | bytes 8388608 | tf_op jit(solution)/shard_map/concatenate | solution.py:143
  136.7 1.5 collective-permute-done.6
  138.2 2.1 collective-permute-start.7
  140.4 6.6 %collective-permute-done.7 = f32[256,256]{0,1:T(8,128)S(1)} collective-permute-done((f32[256,256]{0,1:T(8,128)S(1)}, f32[256,256]{0,1:T(8,128)S(1)}, u32[]{:S(2)}, u32[]{:S(2)}) %collective-permute-start.7) | collective-permute-done | bytes 262176 | tf_op jit(solution)/shard_map/ppermute | solution.py:26
  147.1 7.8 %collective-permute-done.8 = f32[256,256]{0,1:T(8,128)S(1)} collective-permute-done((f32[256,256]{0,1:T(8,128)S(1)}, f32[256,256]{0,1:T(8,128)S(1)}, u32[]{:S(2)}, u32[]{:S(2)}) %collective-permute-start.8) | collective-permute-done | bytes 262176 | tf_op jit(solution)/shard_map/ppermute | solution.py:26
  157.0 11.5 %collective-permute-done.9 = f32[256,256]{0,1:T(8,128)S(1)} collective-permute-done((f32[256,256]{0,1:T(8,128)S(1)}, f32[256,256]{0,1:T(8,128)S(1)}, u32[]{:S(2)}, u32[]{:S(2)}) %collective-permute-start.9) | collective-permute-done | bytes 262176 | tf_op jit(solution)/shard_map/ppermute | solution.py:26
  168.8 39.8 %reduce-scatter.2.cloned.1.call-done = bf16[512,256]{0,1:T(8,128)(2,1)} async-done(((bf16[8192,256]{0,1:T(8,128)(2,1)}), bf16[512,256]{0,1:T(8,128)(2,1)}) %reduce-scatter.2.cloned.1.call-update) | async-done | bytes 262160 | tf_op jit(solution)/shard_map/reduce_scatter | solution.py:142
  (71 shorter events, 14.3 us)
Async XLA Ops:
  7.2 4.3 %copy-start = (f32[1,8192]{1,0:T(1,128)S(1)}, f32[1,8192]{1,0:T(1,128)}, u32[]{:S(2)}) copy-start(f32[1,8192]{1,0:T(1,128)} %param.8) | copy-start | bytes 98308
  7.2 93.8 %all-gather.2.cloned.1.call-start = ((), (), s32[]{:S(2)}) async-start(), calls=%async_computation.1 | async-start | bytes 5570560 | tf_op jit(solution)/shard_map/all_gather | solution.py:118
  12.3 196.3 %reduce-scatter.2.cloned.1.call-start = ((), (), s32[]{:S(2)}) async-start(), calls=%async_computation.2 | async-start | bytes 4456448 | tf_op jit(solution)/shard_map/reduce_scatter | solution.py:142
  14.0 2.1 collective-permute-start.1
  16.1 18.7 %collective-permute-start.2 = (f32[512,256]{1,0:T(8,128)S(1)}, f32[512,256]{1,0:T(8,128)S(1)}, u32[]{:S(2)}, u32[]{:S(2)}) collective-permute-start(f32[512,256]{1,0:T(8,128)S(1)} %add.127), channel_id=1, source_target_pairs={{0,2},{1,3},{2,0},{3,1},{4,6},{5,7},{6,4},{7,5},{8,10},{9,11},{10,... | collective-permute-start | bytes 1572872 | tf_op jit(solution)/shard_map/ppermute | solution.py:26
  34.8 19.2 %collective-permute-start.3 = (f32[512,256]{1,0:T(8,128)S(1)}, f32[512,256]{1,0:T(8,128)S(1)}, u32[]{:S(2)}, u32[]{:S(2)}) collective-permute-start(f32[512,256]{1,0:T(8,128)S(1)} %add.128), channel_id=1, source_target_pairs={{0,4},{1,5},{2,6},{3,7},{4,0},{5,1},{6,2},{7,3},{8,12},{9,13},{10,... | collective-permute-start | bytes 1572872 | tf_op jit(solution)/shard_map/ppermute | solution.py:26
  54.1 65.5 %collective-permute-start.4 = (f32[512,256]{1,0:T(8,128)S(1)}, f32[512,256]{1,0:T(8,128)S(1)}, u32[]{:S(2)}, u32[]{:S(2)}) collective-permute-start(f32[512,256]{1,0:T(8,128)S(1)} %add.129), channel_id=1, source_target_pairs={{0,8},{1,9},{2,10},{3,11},{4,12},{5,13},{6,14},{7,15},{8,0},{9,1},... | collective-permute-start | bytes 1572872 | tf_op jit(solution)/shard_map/ppermute | solution.py:26
  101.0 7.4 %copy-start.2 = (bf16[8192,320]{0,1:T(8,128)(2,1)S(1)}, bf16[8192,320]{0,1:T(8,128)(2,1)}, u32[]{:S(2)}) copy-start(bf16[8192,320]{0,1:T(8,128)(2,1)} %all-gather.2.cloned.1.call-done) | copy-start | bytes 15728644
  113.5 14.2 %collective-permute-start = (bf16[384,512]{0,1:T(8,128)(2,1)S(1)}, bf16[384,512]{0,1:T(8,128)(2,1)S(1)}, u32[]{:S(2)}, u32[]{:S(2)}) collective-permute-start(bf16[384,512]{0,1:T(8,128)(2,1)S(1)} %pad_maximum_fusion.2), channel_id=1, source_target_pairs={{0,16},{16,0},{1,17},{17,1},{2,18},{18,2},{3,19},{19,3},{4,20},{20... | collective-permute-start | bytes 1179656 | tf_op jit(solution)/shard_map/ppermute | solution.py:44
  119.6 10.1 %slice-start.2 = ((s8[6291456]{0:T(1024)(128)(4,1)}), s8[4194304]{0:T(1024)(128)(4,1)S(1)}, s32[]{:S(2)}) async-start(s8[6291456]{0:T(1024)(128)(4,1)} %bitcast.83), calls=%async_computation.5 | async-start | bytes 8388608
  119.7 8.0 %collective-permute-start.5 = (bf16[256,256]{1,0:T(8,128)(2,1)S(1)}, bf16[256,256]{1,0:T(8,128)(2,1)S(1)}, u32[]{:S(2)}, u32[]{:S(2)}) collective-permute-start(bf16[256,256]{1,0:T(8,128)(2,1)S(1)} %slice.156), channel_id=1, source_target_pairs={{0,16},{16,0},{1,17},{17,1},{2,18},{18,2},{3,19},{19,3},{4,20},{20... | collective-permute-start | bytes 393224 | tf_op jit(solution)/shard_map/ppermute | solution.py:44
  128.0 1.8 slice-start.3
  129.5 2.2 %slice-start = ((s8[6291456]{0:T(1024)(128)(4,1)}), s8[4194304]{0:T(1024)(128)(4,1)S(1)}, s32[]{:S(2)}) async-start(s8[6291456]{0:T(1024)(128)(4,1)} %bitcast.81), calls=%async_computation.3 | async-start | bytes 8388608
  129.8 2.6 %slice-start.1 = ((s8[6291456]{0:T(1024)(128)(4,1)}), s8[2097152]{0:T(1024)(128)(4,1)S(1)}, s32[]{:S(2)}) async-start(s8[6291456]{0:T(1024)(128)(4,1)} %bitcast.81), calls=%async_computation.4 | async-start | bytes 4194304
  136.0 32.5 %copy-start.1 = (bf16[512,256]{1,0:T(8,128)(2,1)S(1)}, bf16[512,256]{1,0:T(8,128)(2,1)}, u32[]{:S(2)}) copy-start(bf16[512,256]{1,0:T(8,128)(2,1)} %param.11) | copy-start | bytes 786436
  136.6 1.6 collective-permute-start.6
  138.2 8.8 %collective-permute-start.7 = (f32[256,256]{0,1:T(8,128)S(1)}, f32[256,256]{0,1:T(8,128)S(1)}, u32[]{:S(2)}, u32[]{:S(2)}) collective-permute-start(f32[256,256]{0,1:T(8,128)S(1)} %fusion.54), channel_id=1, source_target_pairs={{0,2},{1,3},{2,0},{3,1},{4,6},{5,7},{6,4},{7,5},{8,10},{9,11},{10,... | collective-permute-start | bytes 786440 | tf_op jit(solution)/shard_map/ppermute | solution.py:26
  147.0 7.9 %collective-permute-start.8 = (f32[256,256]{0,1:T(8,128)S(1)}, f32[256,256]{0,1:T(8,128)S(1)}, u32[]{:S(2)}, u32[]{:S(2)}) collective-permute-start(f32[256,256]{0,1:T(8,128)S(1)} %add.144), channel_id=1, source_target_pairs={{0,4},{1,5},{2,6},{3,7},{4,0},{5,1},{6,2},{7,3},{8,12},{9,13},{10,... | collective-permute-start | bytes 786440 | tf_op jit(solution)/shard_map/ppermute | solution.py:26
  155.0 13.6 %collective-permute-start.9 = (f32[256,256]{0,1:T(8,128)S(1)}, f32[256,256]{0,1:T(8,128)S(1)}, u32[]{:S(2)}, u32[]{:S(2)}) collective-permute-start(f32[256,256]{0,1:T(8,128)S(1)} %add.145), channel_id=1, source_target_pairs={{0,8},{1,9},{2,10},{3,11},{4,12},{5,13},{6,14},{7,15},{8,0},{9,1},... | collective-permute-start | bytes 786440 | tf_op jit(solution)/shard_map/ppermute | solution.py:26
Sparse Core Ops, SparseCore 0:
  12.5 88.5 all-gather.1
  136.2 72.3 reduce-scatter.1

commit v2 on v1

v2 whole, which is shorter than its diff:
```python
import functools

import jax
import jax.numpy as jnp
from jax import lax
from jax.experimental import pallas as pl
from jax.experimental.pallas import tpu as pltpu
from jax.sharding import PartitionSpec as P

F32 = jnp.float32
BF16 = jnp.bfloat16
VMEM_BYTES = 48 * 1024 * 1024


def mm(a, b, dims=((1,), (0,))):
    return lax.dot_general(a, b, (dims, ((), ())), preferred_element_type=F32)


def exact(a, b, dims=((1,), (0,))):
    return lax.dot_general(
        a.astype(F32),
        b.astype(F32),
        (dims, ((), ())),
        precision=lax.Precision.HIGHEST,
        preferred_element_type=F32,
    )


def swap(value, bits, axis="dp"):
    peers = lax.axis_size(axis)
    return lax.ppermute(value, axis, [(i, i ^ bits) for i in range(peers)])


def share_sections(value):
    sections = lax.axis_size("section")
    here = lax.axis_index("section")
    if sections == 2:
        other = swap(value, 1, "section")
        return [jnp.where(here == 0, value, other), jnp.where(here == 0, other, value)]
    around = [(i, (i + 1) % sections) for i in range(sections)]
    held = [value]
    for _ in range(sections - 1):
        held.append(lax.ppermute(held[-1], "section", around))
    stacked = jnp.stack(held)
    order = (here - jnp.arange(sections)) % sections
    return [lax.dynamic_index_in_dim(stacked, order[s], 0, keepdims=False) for s in range(sections)]


def pick(values, index):
    if len(values) == 2:
        return jnp.where(index == 0, values[0], values[1])
    return lax.dynamic_index_in_dim(jnp.stack(values), index, 0, keepdims=False)


def add_first(ids, base_ref, piece_ref, acc_ref, square_ref, out_ref, squares_ref):
    @pl.when(pl.program_id(0) == 0)
    def _():
        out_ref[...] = acc_ref[...]
        squares_ref[...] = square_ref[...]

    out_ref[...] += mm(base_ref[...], piece_ref[0])
    block = base_ref[...].astype(F32)
    block = block * block
    lanes = squares_ref.shape[1]
    total = squares_ref[...]
    for at in range(0, block.shape[1], lanes):
        total = total + block[:, at : at + lanes]
    squares_ref[...] = total


def project_first(ids, base, pieces, acc, squares):
    rows = base.shape[0]
    count, part, rank = pieces.shape
    whole = lambda a: pl.BlockSpec(a.shape, lambda j, ids: (0, 0))
    return pl.pallas_call(
        add_first,
        grid_spec=pltpu.PrefetchScalarGridSpec(
            num_scalar_prefetch=1,
            grid=(count,),
            in_specs=[
                pl.BlockSpec((rows, part), lambda j, ids: (0, ids[j])),
                pl.BlockSpec((1, part, rank), lambda j, ids: (j, 0, 0)),
                whole(acc),
                whole(squares),
            ],
            out_specs=[whole(acc), whole(squares)],
        ),
        out_shape=[jax.ShapeDtypeStruct(acc.shape, F32), jax.ShapeDtypeStruct(squares.shape, F32)],
        compiler_params=pltpu.CompilerParams(vmem_limit_bytes=VMEM_BYTES),
        cost_estimate=pl.CostEstimate(
            flops=2 * rows * count * part * rank,
            bytes_accessed=2 * count * part * (rows + rank),
            transcendentals=0,
        ),
    )(ids, base, pieces, acc, squares)


def add_second(ids, base_ref, cot_ref, piece_ref, acc_b, acc_c, out_b, out_c):
    @pl.when(pl.program_id(0) == 0)
    def _():
        out_b[...] = acc_b[...]
        out_c[...] = acc_c[...]

    part = base_ref.shape[1]
    rank = piece_ref.shape[2]
    half = part // 2
    at = pl.multiple_of(ids[pl.num_programs(0)] * half, half)
    for tokens, out in ((base_ref, out_b), (cot_ref, out_c)):
        out[:, :rank] += mm(tokens[...], piece_ref[0, :part])
        out[:, rank:] += mm(tokens[:, pl.ds(at, half)], piece_ref[0, part:])


def project_second(ids, base, cotangent, pieces, acc_b, acc_c):
    rows = base.shape[0]
    count, tall, rank = pieces.shape
    part = tall * 2 // 3
    whole = lambda a: pl.BlockSpec(a.shape, lambda j, ids: (0, 0))
    block = pl.BlockSpec((rows, part), lambda j, ids: (0, ids[j]))
    return pl.pallas_call(
        add_second,
        grid_spec=pltpu.PrefetchScalarGridSpec(
            num_scalar_prefetch=1,
            grid=(count,),
            in_specs=[
                block,
                block,
                pl.BlockSpec((1, tall, rank), lambda j, ids: (j, 0, 0)),
                whole(acc_b),
                whole(acc_c),
            ],
            out_specs=[whole(acc_b), whole(acc_c)],
        ),
        out_shape=[jax.ShapeDtypeStruct(acc_b.shape, F32)] * 2,
        compiler_params=pltpu.CompilerParams(vmem_limit_bytes=VMEM_BYTES),
        cost_estimate=pl.CostEstimate(
            flops=4 * rows * count * tall * rank,
            bytes_accessed=2 * count * (2 * part * rows + tall * rank),
            transcendentals=0,
        ),
    )(ids, base, cotangent, pieces, acc_b, acc_c)


def outer_block(ids, small_ref, tokens_ref, out_ref):
    out_ref[0] = mm(small_ref[...], tokens_ref[...]).astype(BF16)


def outer_blocks(ids, small_t, tokens, columns):
    rank, rows = small_t.shape
    count = ids.shape[0]
    return pl.pallas_call(
        outer_block,
        grid_spec=pltpu.PrefetchScalarGridSpec(
            num_scalar_prefetch=1,
            grid=(count,),
            in_specs=[
                pl.BlockSpec((rank, rows), lambda j, ids: (0, 0)),
                pl.BlockSpec((rows, columns), lambda j, ids: (0, ids[j])),
            ],
            out_specs=pl.BlockSpec((1, rank, columns), lambda j, ids: (j, 0, 0)),
        ),
        out_shape=jax.ShapeDtypeStruct((count, rank, columns), BF16),
        compiler_params=pltpu.CompilerParams(vmem_limit_bytes=VMEM_BYTES),
        cost_estimate=pl.CostEstimate(
            flops=2 * rows * count * columns * rank,
            bytes_accessed=2 * count * columns * (rows + rank),
            transcendentals=0,
        ),
    )(ids, small_t, tokens)


def gather_chunk(own, spot):
    peers = lax.axis_size("dp")
    across = swap(own, 2)
    held, marks = own[None], [0]
    bit = peers // 2
    while bit > 2:
        held = jnp.concatenate([held, swap(held, bit)])
        marks = marks + [m ^ bit for m in marks]
        bit //= 2
    beside = jnp.concatenate([across[None], swap(held[1:], 2)])
    other = [swap(held, 1), swap(beside, 1)]
    flips = [0, 2, 1, 3]
    return [
        (jnp.stack([spot ^ (m ^ f) for m in marks]).astype(jnp.int32), shards)
        for f, shards in zip(flips, [held, beside, *other])
    ]


def sum_small(local):
    peers = lax.axis_size("dp")
    core = lax.axis_index("dp") % 2
    half = local.shape[0] // 2
    keep = lax.dynamic_slice_in_dim(local, core * half, half, 0)
    give = lax.dynamic_slice_in_dim(local, (1 - core) * half, half, 0)
    keep = keep + swap(give, 1)
    bit = 2
    while bit < peers:
        keep = keep + swap(keep, bit)
        bit *= 2
    other = swap(keep, 1)
    return jnp.where(
        core == 0, jnp.concatenate([keep, other]), jnp.concatenate([other, keep])
    )


def scatter_sum(spot, small_t, tokens, at, columns, per_part):
    peers = lax.axis_size("dp")
    near = [4 * k for k in range(peers // 4)]
    marks = near + [m ^ 2 for m in near]
    to_ids = lambda who: jnp.stack([(who ^ m) * per_part + at for m in marks]).astype(jnp.int32)
    give = outer_blocks(to_ids(spot ^ 1), small_t, tokens, columns)
    got = swap(give, 1)
    keep = outer_blocks(to_ids(spot), small_t, tokens, columns)
    half = len(near)
    summed = (keep[half:].astype(F32) + got[half:].astype(F32)).astype(BF16)
    got_x = swap(summed, 2)
    total = keep[:half].astype(F32) + got[:half].astype(F32) + got_x.astype(F32)
    sent = total[1:].astype(BF16)
    result = total[0]
    for k, m in enumerate(near[1:]):
        result = result + swap(sent[k], m).astype(F32)
    return result


def on_device(base, cotangent, gain, weight_in, weight_out, subspace):
    sections = lax.axis_size("section")
    here = lax.axis_index("section")
    spot = lax.axis_index("dp")
    rows, width = base.shape
    part, size = subspace.shape
    rank = weight_in.shape[2]
    last = sections - 1
    is_last = here == last
    row_gain = lax.dynamic_slice_in_dim(gain, spot * part, part, 1)
    own_in = (row_gain.reshape(part, 1) * weight_in[0].astype(F32)).astype(BF16)
    own_out = weight_out[0]
    own_rest = jnp.where(
        is_last,
        jnp.concatenate([own_out, subspace[part // 2 :, rank:]]),
        jnp.concatenate([subspace[:, :rank], subspace[: part // 2, rank:]]),
    )
    gram_cols = jnp.where(is_last, subspace[:, rank:], subspace[:, :rank])
    local = jnp.concatenate([mm(a, subspace, ((0,), (0,))) for a in (own_out, own_in, gram_cols)])

    first = gather_chunk(own_in, spot)
    second = gather_chunk(own_rest, spot)
    small = sum_small(local)
    smalls = share_sections(small)

    acc = jnp.zeros((rows, rank), F32)
    squares = jnp.zeros((rows, 128), F32)
    for ids, shards in first:
        acc, squares = project_first(ids, base, shards, acc, squares)
    base_p = share_sections(acc.astype(BF16))
    acc_b = jnp.zeros((rows, 2 * rank), F32)
    acc_c = jnp.zeros((rows, 2 * rank), F32)
    flag = is_last.astype(jnp.int32)[None]
    for ids, shards in second:
        acc_b, acc_c = project_second(
            jnp.concatenate([ids, flag]), base, cotangent, shards, acc_b, acc_c
        )
    from_b = share_sections(acc_b.astype(BF16))
    from_c = share_sections(acc_c.astype(BF16))
    base_p = [p.astype(F32) for p in base_p]
    from_b = [p.astype(F32) for p in from_b]
    from_c = [p.astype(F32) for p in from_c]
    spread = lambda parts: jnp.concatenate(
        [parts[0][:, :rank], parts[0][:, rank:] + parts[last][:, rank:]], axis=1
    )
    base_s, cot_s = spread(from_b), spread(from_c)
    cot_w = from_c[last][:, :rank]
    gram = jnp.concatenate([smalls[0][2 * rank :], smalls[last][2 * rank :]])
    square = jnp.sum(squares, axis=1, keepdims=True)

    acts, codes, inners, inverses, resid_s = [], [], [], [], []
    for s in range(sections):
        m_s, q_t = smalls[s][:rank], smalls[s][rank : 2 * rank]
        if s == 0:
            total, moved, inner = square, None, base_p[s]
            resid_s.append(base_s)
        else:
            moved = exact(codes[-1], gram)
            total = square + jnp.sum(
                (2.0 * base_s + moved) * codes[-1].astype(F32), axis=-1, keepdims=True
            )
            inner = base_p[s] + exact(codes[-1], q_t, ((1,), (1,)))
            resid_s.append(base_s + moved)
        inverse = lax.rsqrt(jnp.maximum(total, 0.0) / width + 1e-05)
        inner = inner * inverse
        active = inner * jax.nn.sigmoid(inner)
        grown = exact(active, m_s)
        codes.append((grown if s == 0 else moved + grown).astype(BF16))
        acts.append(active.astype(BF16))
        inners.append(inner)
        inverses.append(inverse)

    if sections == 2:
        half_out = scatter_sum(spot, acts[last].T, cotangent, flag[0], part // 2, 2)
        whole_out = swap(half_out, 1, "section")
        sum_out = jnp.concatenate([whole_out, half_out], axis=1)
    else:
        sum_out = scatter_sum(spot, acts[last].T, cotangent, 0, part, 1)

    scaled, t_in, t_out = [None] * sections, [None] * sections, [None] * sections
    back = None
    for s in range(last, -1, -1):
        m_s, q_t = smalls[s][:rank], smalls[s][rank : 2 * rank]
        if s == last:
            grad_active, grad_y = cot_w, cot_s
            t_out[s] = jnp.zeros((rank, size), F32)
        else:
            grad_active = exact(back, m_s, ((1,), (1,)))
            grad_y = exact(back, gram) if s > 0 else None
            t_out[s] = mm(acts[s], back, ((0,), (0,)))
        inner, inverse = inners[s], inverses[s]
        logistic = jax.nn.sigmoid(inner)
        grad_inner = grad_active * logistic * (1.0 + inner * (1.0 - logistic))
        scaled[s] = (inverse * grad_inner).astype(BF16)
        if s > 0:
            t_in[s] = mm(scaled[s], codes[s - 1], ((0,), (0,)))
            along = jnp.sum(inner * grad_inner, axis=-1, keepdims=True) * (inverse * inverse / width)
            back = (grad_y + exact(scaled[s], q_t) - resid_s[s] * along).astype(BF16)
        else:
            t_in[s] = jnp.zeros((rank, size), F32)
    scaled_t = pick(scaled, here).T
    halves = [
        scatter_sum(spot, scaled_t, base, k, part // 2, 2) for k in range(2)
    ]
    sum_in = jnp.concatenate(halves, axis=1)
    lift = lambda thin: exact(thin, subspace, ((1,), (1,)))
    if sections == 2:
        lifted = lift(sum_small(jnp.where(is_last, t_in[1], t_out[0])))
        lift_in = jnp.where(is_last, lifted, 0.0)
        lift_out = lifted
    else:
        lift_in = lift(sum_small(pick(t_in, here)))
        lift_out = lift(sum_small(pick(t_out, here)))
    grad_in = (row_gain * (sum_in + lift_in)).T
    grad_out = jnp.where(is_last, sum_out, lift_out).T
    return pick(codes, here)[None], grad_in[None], grad_out[None]


def solution(mesh):
    placed = (
        P("dp", None),
        P("dp", None),
        P("section", None),
        P("section", "dp", None),
        P("section", "dp", None),
        P("dp", None),
    )
    return jax.shard_map(
        on_device,
        mesh=mesh,
        in_specs=placed,
        out_specs=(P("section", "dp", None), P("section", "dp", None), P("section", "dp", None)),
        check_vma=False,
    )
```

time: 219 us -> 208 us (0.950)
  waiting for transfers between devices: 150 us -> 53.1 us
  Pallas kernels: 0 us -> 64.3 us
  starting transfers between devices: 13.1 us -> 46.9 us
  between operations: 18.3 us -> 1.37 us
  matrix products: 19.1 us -> 10.9 us
  other arithmetic: 9.2 us -> 16.6 us
  local copies, waits for them, and re-layouts: 8.9 us -> 12.7 us
    pallas_call x0 -> x14, Pallas kernels: none -> 64.3 us  [the longest x6 31.9 us: outer_blocks(): pl.pallas_call(outer_block, grid_spec=pltpu.PrefetchScalarGridSpec(num_sc...]
    all_gather x1 -> x0, waiting for transfers between devices: 44.4 us -> none  [on_device(): wide = lax.all_gather(mine, 'dp', axis=0, tiled=True)]
    reduce_scatter x1 -> x0, waiting for transfers between devices: 39.8 us -> none  [on_device(): lax.psum_scatter(jnp.concatenate([grad_in, grad_out], axis=1), 'dp', scat...]
    ppermute x10 -> x42, starting transfers between devices: 13 us -> 46.9 us  [swap(): return lax.ppermute(value, axis, [(i, i ^ bits) for i in range(peers)])]
    ppermute x10 -> x42, waiting for transfers between devices: 65.4 us -> 53.1 us  [swap(): return lax.ppermute(value, axis, [(i, i ^ bits) for i in range(peers)])]
    dot_general x8 -> x5, matrix products: 17.1 us -> 5.22 us  [mm(): return lax.dot_general(a, b, (dims, ((), ())), preferred_element_type=F32)]
    select_n x2 -> x5, other arithmetic: 0.79 us -> 6.19 us  [the longest x2 2.6 us: on_device(): jnp.where(is_last, jnp.concatenate([own_out, subspace[part // 2:, rank:]]...]
    reduce_sum x1 -> x2, other arithmetic: 4.1 us -> 0.27 us  [the longest x1 0.14 us: on_device(): square = jnp.sum(squares, axis=1, keepdims=True)]
  transfers between devices with their start and end apart: 12 -> 42, of which waited for: 10 -> 15; matrix products, arithmetic and copies ran while one was open for 10% -> 14% of each run, Pallas kernels for 0% -> 29%
where the time goes in v2:
time: 208 us; the launch traced here: 206 us
  Pallas kernels  64.3 us (31%)
  waiting for transfers between devices  53.1 us (26%)
  starting transfers between devices  46.9 us (23%)
  other arithmetic  16.6 us (8%)
  local copies, waits for them, and re-layouts  12.7 us (6%)
  matrix products  10.9 us (5%)
    ppermute x42, waiting for transfers between devices, swap(): return lax.ppermute(value, axis, [(i, i ^ bits) for i in range(peers)])  53.1 us
    ppermute x42, starting transfers between devices, swap(): return lax.ppermute(value, axis, [(i, i ^ bits) for i in range(peers)])  46.9 us
    pallas_call x6, Pallas kernels, outer_blocks(): pl.pallas_call(outer_block, grid_spec=pltpu.PrefetchScalarGridSpec(num_sc...  31.9 us
    pallas_call x4, Pallas kernels, project_second(): pl.pallas_call(add_second, grid_spec=pltpu.PrefetchScalarGridSpec(num_sca...  17.6 us
    pallas_call x4, Pallas kernels, project_first(): pl.pallas_call(add_first, grid_spec=pltpu.PrefetchScalarGridSpec(num_scal...  14.8 us
    unnamed x29, local copies, waits for them, and re-layouts  6.7 us
    dot_general x7, matrix products, exact(): lax.dot_general(a.astype(F32), b.astype(F32), (dims, ((), ())), precision...  5.64 us
    dot_general x5, matrix products, mm(): return lax.dot_general(a, b, (dims, ((), ())), preferred_element_type=F32)  5.22 us
  transfers between devices with their start and end apart: 42, of which 15 were waited for; matrix products, arithmetic and copies ran while one was open for 14% of the time, Pallas kernels for 29%

profile of v2, /device:TPU:0, one launch (start us, length us, event | category | flops | bytes accessed | tf_op | source)
XLA Modules:
  0.0 205.9 jit_solution(2239698658727882538)
XLA Ops:
  3.5 4.1 %collective-permute-start.14 = (bf16[1,768,128]{2,1,0:T(8,128)(2,1)S(1)}, bf16[1,768,128]{2,1,0:T(8,128)(2,1)S(1)}, u32[]{:S(2)}, u32[]{:S(2)}) collective-permute-start(bf16[1,768,128]{2,1,0:T(8,128)(2,1)S(1)} %maximum_select_fusion.3), channel_id=1, source_target_pairs={{0,8},{1,9},{2,10},{3,11},{4,12},{5,13},{6,14},{7,15},{8,0},{9,1},... | collective-permute-start | bytes 589832 | tf_op jit(solution)/shard_map/ppermute | solution.py:31
  17.6 4.7 %collective-permute-done.1 = bf16[1,512,128]{2,1,0:T(8,128)(2,1)S(1)} collective-permute-done((bf16[1,512,128]{2,1,0:T(8,128)(2,1)S(1)}, bf16[1,512,128]{2,1,0:T(8,128)(2,1)S(1)}, u32[]{:S(2)}, u32[]{:S(2)}) %collective-permute-start.1) | collective-permute-done | bytes 131104 | tf_op jit(solution)/shard_map/ppermute | solution.py:31
  27.0 4.7 %collective-permute-done.2 = bf16[2,512,128]{2,1,0:T(8,128)(2,1)S(1)} collective-permute-done((bf16[2,512,128]{2,1,0:T(8,128)(2,1)S(1)}, bf16[2,512,128]{2,1,0:T(8,128)(2,1)S(1)}, u32[]{:S(2)}, u32[]{:S(2)}) %collective-permute-start.2) | collective-permute-done | bytes 262176 | tf_op jit(solution)/shard_map/ppermute | solution.py:31
  34.9 5.2 %collective-permute-done.15 = bf16[2,768,128]{2,1,0:T(8,128)(2,1)S(1)} collective-permute-done((bf16[2,768,128]{2,1,0:T(8,128)(2,1)}, bf16[2,768,128]{2,1,0:T(8,128)(2,1)S(1)}, u32[]{:S(2)}, u32[]{:S(2)}) %collective-permute-start.15) | collective-permute-done | bytes 393248 | tf_op jit(solution)/shard_map/ppermute | solution.py:31
  47.7 3.8 %shard_map.85 = (f32[384,128]{1,0:T(8,128)S(1)}, f32[384,128]{1,0:T(8,128)S(1)}) custom-call(s32[4]{0:T(128)S(1)} %pad_add_fusion.3.ids, bf16[384,8192]{1,0:T(8,128)(2,1)} %tokens_ref.9, bf16[4,512,128]{2,1,0:T(8,128)(2,1)S(1)} %pad_maximum_fusion.4.piece_ref, f32[384,128]{1,0:T(8,128)S(1)} %broadcast_11_acc_ref_square_ref.2.acc_ref.square_ref, ...), custom_call_target="tpu_custom_call" | custom-call | flops 201326592 | bytes 2097152 | tf_op jit(solution)/shard_map/pallas_call | solution.py:75
  54.2 4.5 %collective-permute-done.10 = f32[192,256]{0,1:T(8,128)S(1)} collective-permute-done((f32[192,256]{0,1:T(8,128)S(1)}, f32[192,256]{0,1:T(8,128)S(1)}, u32[]{:S(2)}, u32[]{:S(2)}) %collective-permute-start.10) | collective-permute-done | bytes 196640 | tf_op jit(solution)/shard_map/ppermute | solution.py:31
  59.0 4.4 %shard_map.89 = (f32[384,256]{1,0:T(8,128)S(1)}, f32[384,256]{1,0:T(8,128)S(1)}) custom-call(s32[5]{0:T(128)S(1)} %concatenate.120.ids, bf16[384,8192]{1,0:T(8,128)(2,1)} %tokens_ref.9, bf16[384,8192]{1,0:T(8,128)(2,1)} %tokens_ref.11, bf16[4,768,128]{2,1,0:T(8,128)(2,1)S(1)} %pad_maximum_fusion.1.piece_ref, ...), custom_call_target="tpu_custom_call" | custom-call | flops 603979776 | bytes 3932160 | tf_op jit(solution)/shard_map/pallas_call | solution.py:119
  63.4 3.7 %shard_map.86 = (f32[384,128]{1,0:T(8,128)S(1)}, f32[384,128]{1,0:T(8,128)S(1)}) custom-call(s32[4]{0:T(128)S(1)} %pad_add_fusion.2.ids, bf16[384,8192]{1,0:T(8,128)(2,1)} %tokens_ref.9, bf16[4,512,128]{2,1,0:T(8,128)(2,1)S(1)} %pad_maximum_fusion.3.piece_ref, f32[384,128]{1,0:T(8,128)S(1)} %get-tuple-element.19.acc_ref, ...), custom_call_target="tpu_custom_call" | custom-call | flops 201326592 | bytes 2097152 | tf_op jit(solution)/shard_map/pallas_call | solution.py:75
  67.6 3.7 %shard_map.87 = (f32[384,128]{1,0:T(8,128)S(1)}, f32[384,128]{1,0:T(8,128)S(1)}) custom-call(s32[4]{0:T(128)S(1)} %pad_add_fusion.1.ids, bf16[384,8192]{1,0:T(8,128)(2,1)} %tokens_ref.9, bf16[4,512,128]{2,1,0:T(8,128)(2,1)S(1)} %collective-permute-done.5.piece_ref, f32[384,128]{1,0:T(8,128)S(1)} %get-tuple-element.21.acc_ref, ...), custom_call_target="tpu_custom_call" | custom-call | flops 201326592 | bytes 2097152 | tf_op jit(solution)/shard_map/pallas_call | solution.py:75
  75.0 4.4 %shard_map.90 = (f32[384,256]{1,0:T(8,128)S(1)}, f32[384,256]{1,0:T(8,128)S(1)}) custom-call(s32[5]{0:T(128)S(1)} %concatenate.119.ids, bf16[384,8192]{1,0:T(8,128)(2,1)} %tokens_ref.9, bf16[384,8192]{1,0:T(8,128)(2,1)} %tokens_ref.11, bf16[4,768,128]{2,1,0:T(8,128)(2,1)S(1)} %pad_maximum_fusion.piece_ref, f32[384,256]{1,0:T(8,128)S(1)} %get-tuple-element.27.acc_b, ...), custom_call_target="tpu_custom_call" | custom-call | flops 603979776 | bytes 3932160 | tf_op jit(solution)/shard_map/pallas_call | solution.py:119
  80.9 3.7 %shard_map.88 = (f32[384,128]{1,0:T(8,128)S(1)}, f32[384,128]{1,0:T(8,128)S(1)}) custom-call(s32[4]{0:T(128)S(1)} %pad_add_fusion.ids, bf16[384,8192]{1,0:T(8,128)(2,1)} %tokens_ref.9, bf16[4,512,128]{2,1,0:T(8,128)(2,1)S(1)} %collective-permute-done.4.piece_ref, f32[384,128]{1,0:T(8,128)S(1)} %get-tuple-element.23.acc_ref, ...), custom_call_target="tpu_custom_call" | custom-call | flops 201326592 | bytes 2097152 | tf_op jit(solution)/shard_map/pallas_call | solution.py:75
  92.7 4.4 %shard_map.91 = (f32[384,256]{1,0:T(8,128)S(1)}, f32[384,256]{1,0:T(8,128)S(1)}) custom-call(s32[5]{0:T(128)S(1)} %concatenate.117.ids, bf16[384,8192]{1,0:T(8,128)(2,1)} %tokens_ref.9, bf16[384,8192]{1,0:T(8,128)(2,1)} %tokens_ref.11, bf16[4,768,128]{2,1,0:T(8,128)(2,1)S(1)} %collective-permute-done.18.piece_ref, f32[384,256]{1,0:T(8,128)S(1)} %copy-done.2, ...), custom_call_target="tpu_custom_call" | custom-call | flops 603979776 | bytes 3932160 | tf_op jit(solution)/shard_map/pallas_call | solution.py:119
  97.8 4.4 %shard_map.92 = (f32[384,256]{1,0:T(8,128)S(1)}, f32[384,256]{1,0:T(8,128)S(1)}) custom-call(s32[5]{0:T(128)S(1)} %concatenate.106.ids, bf16[384,8192]{1,0:T(8,128)(2,1)} %tokens_ref.9, bf16[384,8192]{1,0:T(8,128)(2,1)} %tokens_ref.11, bf16[4,768,128]{2,1,0:T(8,128)(2,1)S(1)} %collective-permute-done.17.piece_ref, f32[384,256]{1,0:T(8,128)S(1)} %get-tuple-element.31.acc_b, ...), custom_call_target="tpu_custom_call" | custom-call | flops 603979776 | bytes 3932160 | tf_op jit(solution)/shard_map/pallas_call | solution.py:119
  106.5 4.0 %collective-permute-done.19 = bf16[384,256]{0,1:T(8,128)(2,1)S(1)} collective-permute-done((bf16[384,256]{0,1:T(8,128)(2,1)S(1)}, bf16[384,256]{0,1:T(8,128)(2,1)S(1)}, u32[]{:S(2)}, u32[]{:S(2)}) %collective-permute-start.19) | collective-permute-done | bytes 196640 | tf_op jit(solution)/shard_map/ppermute | solution.py:31
  111.0 3.3 %collective-permute-done.20 = bf16[384,256]{0,1:T(8,128)(2,1)S(1)} collective-permute-done((bf16[384,256]{0,1:T(8,128)(2,1)S(1)}, bf16[384,256]{0,1:T(8,128)(2,1)S(1)}, u32[]{:S(2)}, u32[]{:S(2)}) %collective-permute-start.20) | collective-permute-done | bytes 196640 | tf_op jit(solution)/shard_map/ppermute | solution.py:31
  118.9 5.3 %shard_map.94 = bf16[8,128,256]{2,1,0:T(8,128)(2,1)S(1)} custom-call(s32[8]{0:T(128)S(1)} %stack.275.ids, bf16[128,384]{1,0:T(8,128)(2,1)S(1)} %fusion.7.small_ref, bf16[384,8192]{1,0:T(8,128)(2,1)} %tokens_ref.9), custom_call_target="tpu_custom_call" | custom-call | flops 201326592 | bytes 2097152 | tf_op jit(solution)/shard_map/pallas_call | solution.py:150
  126.4 5.3 %shard_map.96 = bf16[8,128,256]{2,1,0:T(8,128)(2,1)S(1)} custom-call(s32[8]{0:T(128)S(1)} %stack.293.ids, bf16[128,384]{1,0:T(8,128)(2,1)S(1)} %fusion.7.small_ref, bf16[384,8192]{1,0:T(8,128)(2,1)} %tokens_ref.9), custom_call_target="tpu_custom_call" | custom-call | flops 201326592 | bytes 2097152 | tf_op jit(solution)/shard_map/pallas_call | solution.py:150
  139.2 5.3 %shard_map.98 = bf16[8,128,256]{2,1,0:T(8,128)(2,1)S(1)} custom-call(s32[8]{0:T(128)S(1)} %stack.311.ids, bf16[128,384]{1,0:T(8,128)(2,1)S(1)} %get-tuple-element.71.small_ref, bf16[384,8192]{1,0:T(8,128)(2,1)} %tokens_ref.11), custom_call_target="tpu_custom_call" | custom-call | flops 201326592 | bytes 2097152 | tf_op jit(solution)/shard_map/pallas_call | solution.py:150
  145.4 5.3 %shard_map.93 = bf16[8,128,256]{2,1,0:T(8,128)(2,1)S(1)} custom-call(s32[8]{0:T(128)S(1)} %stack.266.ids, bf16[128,384]{1,0:T(8,128)(2,1)S(1)} %fusion.7.small_ref, bf16[384,8192]{1,0:T(8,128)(2,1)} %tokens_ref.9), custom_call_target="tpu_custom_call" | custom-call | flops 201326592 | bytes 2097152 | tf_op jit(solution)/shard_map/pallas_call | solution.py:150
  150.7 5.3 %shard_map.95 = bf16[8,128,256]{2,1,0:T(8,128)(2,1)S(1)} custom-call(s32[8]{0:T(128)S(1)} %stack.284.ids, bf16[128,384]{1,0:T(8,128)(2,1)S(1)} %fusion.7.small_ref, bf16[384,8192]{1,0:T(8,128)(2,1)} %tokens_ref.9), custom_call_target="tpu_custom_call" | custom-call | flops 201326592 | bytes 2097152 | tf_op jit(solution)/shard_map/pallas_call | solution.py:150
  156.0 5.3 %shard_map.97 = bf16[8,128,256]{2,1,0:T(8,128)(2,1)S(1)} custom-call(s32[8]{0:T(128)S(1)} %stack.302.ids, bf16[128,384]{1,0:T(8,128)(2,1)S(1)} %get-tuple-element.71.small_ref, bf16[384,8192]{1,0:T(8,128)(2,1)} %tokens_ref.11), custom_call_target="tpu_custom_call" | custom-call | flops 201326592 | bytes 2097152 | tf_op jit(solution)/shard_map/pallas_call | solution.py:150
  165.9 6.3 %collective-permute-done.22 = bf16[4,128,256]{2,1,0:T(8,128)(2,1)S(1)} collective-permute-done((bf16[4,128,256]{2,1,0:T(8,128)(2,1)S(1)}, bf16[4,128,256]{2,1,0:T(8,128)(2,1)S(1)}, u32[]{:S(2)}, u32[]{:S(2)}) %collective-permute-start.22) | collective-permute-done | bytes 262176 | tf_op jit(solution)/shard_map/ppermute | solution.py:31
  175.1 7.4 %collective-permute-done.37 = bf16[4,128,256]{2,1,0:T(8,128)(2,1)S(1)} collective-permute-done((bf16[4,128,256]{2,1,0:T(8,128)(2,1)S(1)}, bf16[4,128,256]{2,1,0:T(8,128)(2,1)S(1)}, u32[]{:S(2)}, u32[]{:S(2)}) %collective-permute-start.37) | collective-permute-done | bytes 262176 | tf_op jit(solution)/shard_map/ppermute | solution.py:31
  188.0 4.3 %collective-permute-done.39 = bf16[128,256]{1,0:T(8,128)(2,1)S(1)} collective-permute-done((bf16[128,256]{1,0:T(8,128)(2,1)S(1)}, bf16[128,256]{1,0:T(8,128)(2,1)S(1)}, u32[]{:S(2)}, u32[]{:S(2)}) %collective-permute-start.39) | collective-permute-done | bytes 65568 | tf_op jit(solution)/shard_map/ppermute | solution.py:31
  (185 shorter events, 91.7 us)
Async XLA Ops:
  3.5 19.7 %collective-permute-start.14 = (bf16[1,768,128]{2,1,0:T(8,128)(2,1)S(1)}, bf16[1,768,128]{2,1,0:T(8,128)(2,1)S(1)}, u32[]{:S(2)}, u32[]{:S(2)}) collective-permute-start(bf16[1,768,128]{2,1,0:T(8,128)(2,1)S(1)} %maximum_select_fusion.3), channel_id=1, source_target_pairs={{0,8},{1,9},{2,10},{3,11},{4,12},{5,13},{6,14},{7,15},{8,0},{9,1},... | collective-permute-start | bytes 589832 | tf_op jit(solution)/shard_map/ppermute | solution.py:31
  8.6 13.7 %collective-permute-start.1 = (bf16[1,512,128]{2,1,0:T(8,128)(2,1)S(1)}, bf16[1,512,128]{2,1,0:T(8,128)(2,1)S(1)}, u32[]{:S(2)}, u32[]{:S(2)}) collective-permute-start(bf16[1,512,128]{2,1,0:T(8,128)(2,1)S(1)} %fusion.12), channel_id=1, source_target_pairs={{0,8},{1,9},{2,10},{3,11},{4,12},{5,13},{6,14},{7,15},{8,0},{9,1},... | collective-permute-start | bytes 393224 | tf_op jit(solution)/shard_map/ppermute | solution.py:31
  9.8 41.7 %collective-permute-start = (bf16[512,128]{1,0:T(8,128)(2,1)S(1)}, bf16[512,128]{1,0:T(8,128)(2,1)S(1)}, u32[]{:S(2)}, u32[]{:S(2)}) collective-permute-start(bf16[512,128]{1,0:T(8,128)(2,1)S(1)} %fusion.11), channel_id=1, source_target_pairs={{0,2},{1,3},{2,0},{3,1},{4,6},{5,7},{6,4},{7,5},{8,10},{9,11},{10,... | collective-permute-start | bytes 393224 | tf_op jit(solution)/shard_map/ppermute | solution.py:31
  23.9 16.1 %collective-permute-start.15 = (bf16[2,768,128]{2,1,0:T(8,128)(2,1)}, bf16[2,768,128]{2,1,0:T(8,128)(2,1)S(1)}, u32[]{:S(2)}, u32[]{:S(2)}) collective-permute-start(bf16[2,768,128]{2,1,0:T(8,128)(2,1)} %pad_maximum_fusion.7), channel_id=1, source_target_pairs={{0,4},{1,5},{2,6},{3,7},{4,0},{5,1},{6,2},{7,3},{8,12},{9,13},{10,... | collective-permute-start | bytes 1179656 | tf_op jit(solution)/shard_map/ppermute | solution.py:31
  32.4 20.7 %collective-permute-start.3 = (bf16[3,512,128]{2,1,0:T(8,128)(2,1)}, bf16[3,512,128]{2,1,0:T(8,128)(2,1)}, u32[]{:S(2)}, u32[]{:S(2)}) collective-permute-start(bf16[3,512,128]{2,1,0:T(8,128)(2,1)} %pad_maximum_fusion.5), channel_id=1, source_target_pairs={{0,2},{1,3},{2,0},{3,1},{4,6},{5,7},{6,4},{7,5},{8,10},{9,11},{10,... | collective-permute-start | bytes 1179656 | tf_op jit(solution)/shard_map/ppermute | solution.py:31
  34.1 9.9 %collective-permute-start.9 = (f32[192,256]{0,1:T(8,128)S(1)}, f32[192,256]{0,1:T(8,128)S(1)}, u32[]{:S(2)}, u32[]{:S(2)}) collective-permute-start(f32[192,256]{0,1:T(8,128)S(1)} %add.269), channel_id=1, source_target_pairs={{0,4},{1,5},{2,6},{3,7},{4,0},{5,1},{6,2},{7,3},{8,12},{9,13},{10,... | collective-permute-start | bytes 589832 | tf_op jit(solution)/shard_map/ppermute | solution.py:31
  34.8 32.2 %collective-permute-start.5 = (bf16[4,512,128]{2,1,0:T(8,128)(2,1)S(1)}, bf16[4,512,128]{2,1,0:T(8,128)(2,1)S(1)}, u32[]{:S(2)}, u32[]{:S(2)}) collective-permute-start(bf16[4,512,128]{2,1,0:T(8,128)(2,1)S(1)} %pad_maximum_fusion.4.piece_ref), channel_id=1, source_target_pairs={{0,1},{1,0},{2,3},{3,2},{4,5},{5,4},{6,7},{7,6},{8,9},{9,8},{10,11... | collective-permute-start | bytes 1572872 | tf_op jit(solution)/shard_map/ppermute | solution.py:31
  41.0 32.8 %collective-permute-start.16 = (bf16[3,768,128]{2,1,0:T(8,128)(2,1)}, bf16[3,768,128]{2,1,0:T(8,128)(2,1)}, u32[]{:S(2)}, u32[]{:S(2)}) collective-permute-start(bf16[3,768,128]{2,1,0:T(8,128)(2,1)} %pad_maximum_fusion.2), channel_id=1, source_target_pairs={{0,2},{1,3},{2,0},{3,1},{4,6},{5,7},{6,4},{7,5},{8,10},{9,11},{10,... | collective-permute-start | bytes 1769480 | tf_op jit(solution)/shard_map/ppermute | solution.py:31
  44.0 14.7 %collective-permute-start.10 = (f32[192,256]{0,1:T(8,128)S(1)}, f32[192,256]{0,1:T(8,128)S(1)}, u32[]{:S(2)}, u32[]{:S(2)}) collective-permute-start(f32[192,256]{0,1:T(8,128)S(1)} %add.270), channel_id=1, source_target_pairs={{0,8},{1,9},{2,10},{3,11},{4,12},{5,13},{6,14},{7,15},{8,0},{9,1},... | collective-permute-start | bytes 589832 | tf_op jit(solution)/shard_map/ppermute | solution.py:31
  51.5 22.3 %collective-permute-start.13 = (bf16[768,128]{1,0:T(8,128)(2,1)}, bf16[768,128]{1,0:T(8,128)(2,1)S(1)}, u32[]{:S(2)}, u32[]{:S(2)}) collective-permute-start(bf16[768,128]{1,0:T(8,128)(2,1)} %maximum_select_fusion.2), channel_id=1, source_target_pairs={{0,2},{1,3},{2,0},{3,1},{4,6},{5,7},{6,4},{7,5},{8,10},{9,11},{10,... | collective-permute-start | bytes 589832 | tf_op jit(solution)/shard_map/ppermute | solution.py:31
  54.1 26.8 %collective-permute-start.4 = (bf16[4,512,128]{2,1,0:T(8,128)(2,1)S(1)}, bf16[4,512,128]{2,1,0:T(8,128)(2,1)S(1)}, u32[]{:S(2)}, u32[]{:S(2)}) collective-permute-start(bf16[4,512,128]{2,1,0:T(8,128)(2,1)S(1)} %pad_maximum_fusion.3.piece_ref), channel_id=1, source_target_pairs={{0,1},{1,0},{2,3},{3,2},{4,5},{5,4},{6,7},{7,6},{8,9},{9,8},{10,11... | collective-permute-start | bytes 1572872 | tf_op jit(solution)/shard_map/ppermute | solution.py:31
  58.8 12.5 %collective-permute-start.11 = (f32[192,256]{0,1:T(8,128)S(1)}, f32[192,256]{0,1:T(8,128)S(1)}, u32[]{:S(2)}, u32[]{:S(2)}) collective-permute-start(f32[192,256]{0,1:T(8,128)S(1)} %add.271), channel_id=1, source_target_pairs={{0,1},{1,0},{2,3},{3,2},{4,5},{5,4},{6,7},{7,6},{8,9},{9,8},{10,11... | collective-permute-start | bytes 589832 | tf_op jit(solution)/shard_map/ppermute | solution.py:31
  67.0 23.7 %collective-permute-start.18 = (bf16[4,768,128]{2,1,0:T(8,128)(2,1)S(1)}, bf16[4,768,128]{2,1,0:T(8,128)(2,1)S(1)}, u32[]{:S(2)}, u32[]{:S(2)}) collective-permute-start(bf16[4,768,128]{2,1,0:T(8,128)(2,1)S(1)} %pad_maximum_fusion.1.piece_ref), channel_id=1, source_target_pairs={{0,1},{1,0},{2,3},{3,2},{4,5},{5,4},{6,7},{7,6},{8,9},{9,8},{10,11... | collective-permute-start | bytes 2359304 | tf_op jit(solution)/shard_map/ppermute | solution.py:31
  72.3 14.8 %collective-permute-start.12 = (f32[384,256]{0,1:T(8,128)}, f32[384,256]{0,1:T(8,128)}, u32[]{:S(2)}, u32[]{:S(2)}) collective-permute-start(f32[384,256]{0,1:T(8,128)} %maximum_select_fusion), channel_id=1, source_target_pairs={{0,16},{16,0},{1,17},{17,1},{2,18},{18,2},{3,19},{19,3},{4,20},{20... | collective-permute-start | bytes 1179656 | tf_op jit(solution)/shard_map/ppermute | solution.py:31
  74.9 22.9 %collective-permute-start.17 = (bf16[4,768,128]{2,1,0:T(8,128)(2,1)S(1)}, bf16[4,768,128]{2,1,0:T(8,128)(2,1)S(1)}, u32[]{:S(2)}, u32[]{:S(2)}) collective-permute-start(bf16[4,768,128]{2,1,0:T(8,128)(2,1)S(1)} %pad_maximum_fusion.piece_ref), channel_id=1, source_target_pairs={{0,1},{1,0},{2,3},{3,2},{4,5},{5,4},{6,7},{7,6},{8,9},{9,8},{10,11... | collective-permute-start | bytes 2359304 | tf_op jit(solution)/shard_map/ppermute | solution.py:31
  86.3 10.8 %collective-permute-start.6 = (bf16[384,128]{0,1:T(8,128)(2,1)S(1)}, bf16[384,128]{0,1:T(8,128)(2,1)}, u32[]{:S(2)}, u32[]{:S(2)}) collective-permute-start(bf16[384,128]{0,1:T(8,128)(2,1)S(1)} %copy.9), channel_id=1, source_target_pairs={{0,16},{16,0},{1,17},{17,1},{2,18},{18,2},{3,19},{19,3},{4,20},{20... | collective-permute-start | bytes 294920 | tf_op jit(solution)/shard_map/ppermute | solution.py:31
  124.2 37.8 %collective-permute-start.21 = (bf16[8,128,256]{2,1,0:T(8,128)(2,1)S(1)}, bf16[8,128,256]{2,1,0:T(8,128)(2,1)}, u32[]{:S(2)}, u32[]{:S(2)}) collective-permute-start(bf16[8,128,256]{2,1,0:T(8,128)(2,1)S(1)} %shard_map.94), channel_id=1, source_target_pairs={{0,1},{1,0},{2,3},{3,2},{4,5},{5,4},{6,7},{7,6},{8,9},{9,8},{10,11... | collective-permute-start | bytes 1572872 | tf_op jit(solution)/shard_map/ppermute | solution.py:31
  131.7 31.8 %collective-permute-start.26 = (bf16[8,128,256]{2,1,0:T(8,128)(2,1)S(1)}, bf16[8,128,256]{2,1,0:T(8,128)(2,1)S(1)}, u32[]{:S(2)}, u32[]{:S(2)}) collective-permute-start(bf16[8,128,256]{2,1,0:T(8,128)(2,1)S(1)} %shard_map.96), channel_id=1, source_target_pairs={{0,1},{1,0},{2,3},{3,2},{4,5},{5,4},{6,7},{7,6},{8,9},{9,8},{10,11... | collective-permute-start | bytes 1572872 | tf_op jit(solution)/shard_map/ppermute | solution.py:31
  136.8 24.6 %collective-permute-start.34 = (f32[64,256]{1,0:T(8,128)S(1)}, f32[64,256]{1,0:T(8,128)S(1)}, u32[]{:S(2)}, u32[]{:S(2)}) collective-permute-start(f32[64,256]{1,0:T(8,128)S(1)} %add.316), channel_id=1, source_target_pairs={{0,8},{1,9},{2,10},{3,11},{4,12},{5,13},{6,14},{7,15},{8,0},{9,1},... | collective-permute-start | bytes 196616 | tf_op jit(solution)/shard_map/ppermute | solution.py:31
  144.5 20.7 %collective-permute-start.36 = (bf16[8,128,256]{2,1,0:T(8,128)(2,1)S(1)}, bf16[8,128,256]{2,1,0:T(8,128)(2,1)S(1)}, u32[]{:S(2)}, u32[]{:S(2)}) collective-permute-start(bf16[8,128,256]{2,1,0:T(8,128)(2,1)S(1)} %shard_map.98), channel_id=1, source_target_pairs={{0,1},{1,0},{2,3},{3,2},{4,5},{5,4},{6,7},{7,6},{8,9},{9,8},{10,11... | collective-permute-start | bytes 1572872 | tf_op jit(solution)/shard_map/ppermute | solution.py:31
  161.4 41.5 %collective-permute-start.35 = (f32[64,256]{1,0:T(8,128)S(1)}, f32[64,256]{1,0:T(8,128)S(1)}, u32[]{:S(2)}, u32[]{:S(2)}) collective-permute-start(f32[64,256]{1,0:T(8,128)S(1)} %add.317), channel_id=1, source_target_pairs={{0,1},{1,0},{2,3},{3,2},{4,5},{5,4},{6,7},{7,6},{8,9},{9,8},{10,11... | collective-permute-start | bytes 196616 | tf_op jit(solution)/shard_map/ppermute | solution.py:31
  163.7 20.8 %collective-permute-start.27 = (bf16[4,128,256]{2,1,0:T(8,128)(2,1)S(1)}, bf16[4,128,256]{2,1,0:T(8,128)(2,1)S(1)}, u32[]{:S(2)}, u32[]{:S(2)}) collective-permute-start(bf16[4,128,256]{2,1,0:T(8,128)(2,1)S(1)} %add_convert_fusion.1), channel_id=1, source_target_pairs={{0,2},{1,3},{2,0},{3,1},{4,6},{5,7},{6,4},{7,5},{8,10},{9,11},{10,... | collective-permute-start | bytes 786440 | tf_op jit(solution)/shard_map/ppermute | solution.py:31
  165.3 17.2 %collective-permute-start.37 = (bf16[4,128,256]{2,1,0:T(8,128)(2,1)S(1)}, bf16[4,128,256]{2,1,0:T(8,128)(2,1)S(1)}, u32[]{:S(2)}, u32[]{:S(2)}) collective-permute-start(bf16[4,128,256]{2,1,0:T(8,128)(2,1)S(1)} %add_convert_fusion), channel_id=1, source_target_pairs={{0,2},{1,3},{2,0},{3,1},{4,6},{5,7},{6,4},{7,5},{8,10},{9,11},{10,... | collective-permute-start | bytes 786440 | tf_op jit(solution)/shard_map/ppermute | solution.py:31
  173.3 21.6 %collective-permute-start.23 = (bf16[128,256]{1,0:T(8,128)(2,1)S(1)}, bf16[128,256]{1,0:T(8,128)(2,1)S(1)}, u32[]{:S(2)}, u32[]{:S(2)}) collective-permute-start(bf16[128,256]{1,0:T(8,128)(2,1)S(1)} %get-tuple-element.59), channel_id=1, source_target_pairs={{0,4},{1,5},{2,6},{3,7},{4,0},{5,1},{6,2},{7,3},{8,12},{9,13},{10,... | collective-permute-start | bytes 196616 | tf_op jit(solution)/shard_map/ppermute | solution.py:31
  (31 other events, 238.2 us)

commit v3 on v2

v3 whole, which is shorter than its diff:
```python
import functools

import functools

import jax
import jax.numpy as jnp
from jax import lax
from jax.experimental import pallas as pl
from jax.experimental.pallas import tpu as pltpu
from jax.sharding import PartitionSpec as P

F32 = jnp.float32
BF16 = jnp.bfloat16
VMEM_BYTES = 20 * 1024 * 1024


def mm(a, b, dims=((1,), (0,))):
    return lax.dot_general(a, b, (dims, ((), ())), preferred_element_type=F32)


def exact(a, b, dims=((1,), (0,))):
    return lax.dot_general(
        a.astype(F32),
        b.astype(F32),
        (dims, ((), ())),
        precision=lax.Precision.HIGH,
        preferred_element_type=F32,
    )


def swap(value, bits, axis="dp"):
    peers = lax.axis_size(axis)
    return lax.ppermute(value, axis, [(i, i ^ bits) for i in range(peers)])


def share_sections(value):
    sections = lax.axis_size("section")
    here = lax.axis_index("section")
    if sections == 2:
        other = swap(value, 1, "section")
        return [jnp.where(here == 0, value, other), jnp.where(here == 0, other, value)]
    around = [(i, (i + 1) % sections) for i in range(sections)]
    held = [value]
    for _ in range(sections - 1):
        held.append(lax.ppermute(held[-1], "section", around))
    stacked = jnp.stack(held)
    order = (here - jnp.arange(sections)) % sections
    return [lax.dynamic_index_in_dim(stacked, order[s], 0, keepdims=False) for s in range(sections)]


def share_sections_of(own, sent):
    here = lax.axis_index("section")
    all_sent = share_sections(sent)
    return [jnp.where(here == s, own, v.astype(F32)) for s, v in enumerate(all_sent)]


def pick(values, index):
    if len(values) == 2:
        return jnp.where(index == 0, values[0], values[1])
    return lax.dynamic_index_in_dim(jnp.stack(values), index, 0, keepdims=False)


def after(value, *others):
    return lax.optimization_barrier((value, *others))[0]


def project_kernel(count, ids, base_ref, cot_ref, gain_ref, *refs):
    pieces, acc_ref, out_ref = refs[:count], refs[count], refs[count + 1]
    tall, rank = pieces[0].shape
    part = tall * 2 // 5
    half = part // 2
    out_ref[...] = acc_ref[...]
    skip = ids[count] * half
    for t, piece in enumerate(pieces):
        start = pl.multiple_of(ids[t] * part, part)
        half_start = pl.multiple_of(start + skip, half)
        block = base_ref[:, pl.ds(start, part)]
        block_f = block.astype(F32)
        normed = (block_f * gain_ref[:, pl.ds(start, part)]).astype(BF16)
        square = block_f * block_f
        lanes = out_ref.shape[1] - 5 * rank
        total = square[:, :lanes]
        for at in range(lanes, part, lanes):
            total = total + square[:, at : at + lanes]
        out_ref[:, :rank] += mm(normed, piece[:part])
        out_ref[:, rank : 2 * rank] += mm(block, piece[part : 2 * part])
        out_ref[:, 2 * rank : 3 * rank] += mm(
            base_ref[:, pl.ds(half_start, half)], piece[2 * part :]
        )
        out_ref[:, 3 * rank : 4 * rank] += mm(
            cot_ref[:, pl.ds(start, part)], piece[part : 2 * part]
        )
        out_ref[:, 4 * rank : 5 * rank] += mm(
            cot_ref[:, pl.ds(half_start, half)], piece[2 * part :]
        )
        out_ref[:, 5 * rank :] += total
    if len(refs) > count + 2:
        refs[count + 2][...] = out_ref[:, : 3 * rank].astype(BF16)
        refs[count + 3][...] = out_ref[:, 3 * rank : 5 * rank].astype(BF16)


def project(ids, base, cotangent, gain, pieces, acc, rounded=False):
    rows = base.shape[0]
    count = len(pieces)
    tall, rank = pieces[0].shape
    in_vmem = pl.BlockSpec(memory_space=pltpu.VMEM)
    shapes = [jax.ShapeDtypeStruct(acc.shape, F32)]
    if rounded:
        shapes += [
            jax.ShapeDtypeStruct((rows, 3 * rank), BF16),
            jax.ShapeDtypeStruct((rows, 2 * rank), BF16),
        ]
    return pl.pallas_call(
        functools.partial(project_kernel, count),
        in_specs=[pl.BlockSpec(memory_space=pltpu.SMEM)] + [in_vmem] * (count + 4),
        out_specs=[in_vmem] * len(shapes),
        out_shape=shapes,
        compiler_params=pltpu.CompilerParams(vmem_limit_bytes=VMEM_BYTES),
        cost_estimate=pl.CostEstimate(
            flops=4 * rows * count * tall * rank,
            bytes_accessed=2 * count * tall * (rows + rank),
            transcendentals=0,
        ),
    )(ids, base, cotangent, gain, *pieces, acc)


def outer_kernel(ids, small_ref, tokens_ref, *outs):
    small = small_ref[...]
    at = 0
    for out in outs:
        count, _, columns = out.shape
        for j in range(count):
            start = pl.multiple_of(ids[at] * columns, columns)
            out[j] = mm(small, tokens_ref[:, pl.ds(start, columns)]).astype(BF16)
            at += 1


def outer_blocks(id_lists, small_t, tokens, columns):
    rank, rows = small_t.shape
    counts = [len(ids) for ids in id_lists]
    in_vmem = pl.BlockSpec(memory_space=pltpu.VMEM)
    return pl.pallas_call(
        outer_kernel,
        in_specs=[pl.BlockSpec(memory_space=pltpu.SMEM), in_vmem, in_vmem],
        out_specs=[in_vmem] * len(counts),
        out_shape=[jax.ShapeDtypeStruct((n, rank, columns), BF16) for n in counts],
        compiler_params=pltpu.CompilerParams(vmem_limit_bytes=VMEM_BYTES),
        cost_estimate=pl.CostEstimate(
            flops=2 * rows * sum(counts) * columns * rank,
            bytes_accessed=2 * sum(counts) * columns * (rows + rank),
            transcendentals=0,
        ),
    )(jnp.stack(sum(id_lists, [])).astype(jnp.int32), small_t, tokens)


def gather_shards(own):
    peers = lax.axis_size("dp")
    held = {0: own}
    bit = peers // 2
    while bit > 2:
        for m in list(held):
            held[m ^ bit] = swap(held[m], bit)
        bit //= 2
    near = sorted(held)
    sent = []
    for m in near:
        value = held[m]
        if len(sent) > 1:
            value = after(value, sent[-2])
        held[m ^ 2] = swap(value, 2)
        sent.append(held[m ^ 2])
    for m in list(held):
        held[m ^ 1] = swap(held[m], 1)
    return near, held


def sum_small(local, wait_for):
    peers = lax.axis_size("dp")
    core = lax.axis_index("dp") % 2
    half = local.shape[0] // 2
    keep = lax.dynamic_slice_in_dim(local, core * half, half, 0)
    give = lax.dynamic_slice_in_dim(local, (1 - core) * half, half, 0)
    keep = after(keep + swap(give, 1), wait_for)
    bit = peers // 2
    while bit > 2:
        keep = keep + swap(keep, bit)
        bit //= 2
    return keep + swap(keep.astype(BF16), 2).astype(F32)


def sum_thin(value):
    peers = lax.axis_size("dp")
    bit = 1
    while bit < peers:
        value = value + swap(value, bit)
        bit *= 2
    return value


def block_marks():
    near = [4 * k for k in range(lax.axis_size("dp") // 4)]
    return near, near + [m ^ 2 for m in near]


def scatter_sum(give, keep):
    near, _ = block_marks()
    half = len(near)
    got = swap(give, 1)
    summed = (keep[half:].astype(F32) + got[half:].astype(F32)).astype(BF16)
    got_x = swap(summed, 2)
    total = keep[:half].astype(F32) + got[:half].astype(F32) + got_x.astype(F32)
    sent = total[1:].astype(BF16)
    result = total[0]
    for k, m in enumerate(near[1:]):
        result = result + swap(sent[k], m).astype(F32)
    return result


def on_device(base, cotangent, gain, weight_in, weight_out, subspace):
    sections = lax.axis_size("section")
    here = lax.axis_index("section")
    spot = lax.axis_index("dp")
    rows, width = base.shape
    part, size = subspace.shape
    rank = weight_in.shape[2]
    last = sections - 1
    is_last = here == last
    flag = is_last.astype(jnp.int32)
    own_in, own_out = weight_in[0], weight_out[0]
    own = jnp.where(
        is_last,
        jnp.concatenate([own_in, own_out, subspace[part // 2 :, rank:]]),
        jnp.concatenate([own_in, subspace[:, :rank], subspace[: part // 2, rank:]]),
    )
    near, shards = gather_shards(own)

    row_gain = lax.dynamic_slice_in_dim(gain, spot * part, part, 1)
    scaled_in = (row_gain.reshape(part, 1) * own_in.astype(F32)).astype(BF16)
    gram_cols = jnp.where(is_last, subspace[:, rank:], subspace[:, :rank])
    local = jnp.concatenate([mm(a, subspace, ((0,), (0,))) for a in (own_out, scaled_in, gram_cols)])
    small = sum_small(local, shards[4])
    halves = share_sections(small)
    core = spot % 2
    mine = jnp.stack(halves)
    other = swap(mine, 1)
    smalls = jnp.where(
        core == 0,
        jnp.concatenate([mine, other], axis=1),
        jnp.concatenate([other, mine], axis=1),
    )

    acc = jnp.zeros((rows, 6 * rank), F32)
    marks = [
        near,
        [m ^ 1 for m in near],
        [m ^ 2 for m in near[:-1]] + [m ^ 3 for m in near[:-1]],
        [near[-1] ^ 2, near[-1] ^ 3],
    ]
    for k, some in enumerate(marks):
        ids = jnp.stack([spot ^ m for m in some] + [flag]).astype(jnp.int32)
        acc, *rounded = project(
            ids, base, cotangent, gain, [shards[m] for m in some], acc, k == len(marks) - 1
        )
    from_b = [p.astype(F32) for p in share_sections_of(acc[:, : 3 * rank], rounded[0])]
    from_c = [p.astype(F32) for p in share_sections_of(acc[:, 3 * rank : 5 * rank], rounded[1])]
    base_p = [p[:, :rank] for p in from_b]
    base_s = jnp.concatenate(
        [from_b[0][:, rank : 2 * rank], from_b[0][:, 2 * rank :] + from_b[last][:, 2 * rank :]], axis=1
    )
    cot_s = jnp.concatenate(
        [from_c[0][:, :rank], from_c[0][:, rank:] + from_c[last][:, rank:]], axis=1
    )
    cot_w = from_c[last][:, :rank]
    gram = jnp.concatenate([smalls[0, 2 * rank :], smalls[last, 2 * rank :]])
    square = jnp.sum(acc[:, 5 * rank :], axis=1, keepdims=True)

    acts, codes, inners, inverses, resid_s = [], [], [], [], []
    for s in range(sections):
        m_s, q_t = smalls[s, :rank], smalls[s, rank : 2 * rank]
        if s == 0:
            total, moved, inner = square, None, base_p[s]
            resid_s.append(base_s)
        else:
            moved = exact(codes[-1], gram)
            total = square + jnp.sum(
                (2.0 * base_s + moved) * codes[-1].astype(F32), axis=-1, keepdims=True
            )
            inner = base_p[s] + exact(codes[-1], q_t, ((1,), (1,)))
            resid_s.append(base_s + moved)
        inverse = lax.rsqrt(jnp.maximum(total, 0.0) / width + 1e-05)
        inner = inner * inverse
        active = inner * jax.nn.sigmoid(inner)
        grown = exact(active, m_s)
        codes.append((grown if s == 0 else moved + grown).astype(BF16))
        acts.append(active.astype(BF16))
        inners.append(inner)
        inverses.append(inverse)

    _, every = block_marks()
    if sections == 2:
        ids = [[(who ^ m) * 2 + flag for m in every] for who in (spot ^ 1, spot)]
        half_out = scatter_sum(*outer_blocks(ids, acts[last].T, cotangent, part // 2))
        whole_out = swap(half_out, 1, "section")
        sum_out = jnp.concatenate([whole_out, half_out], axis=1)
    else:
        ids = [[who ^ m for m in every] for who in (spot ^ 1, spot)]
        sum_out = scatter_sum(*outer_blocks(ids, acts[last].T, cotangent, part))

    scaled, t_in, t_out = [None] * sections, [None] * sections, [None] * sections
    back = None
    for s in range(last, -1, -1):
        m_s, q_t = smalls[s, :rank], smalls[s, rank : 2 * rank]
        if s == last:
            grad_active, grad_y = cot_w, cot_s
            t_out[s] = jnp.zeros((rank, size), F32)
        else:
            grad_active = exact(back, m_s, ((1,), (1,)))
            grad_y = exact(back, gram) if s > 0 else None
            t_out[s] = mm(acts[s], back, ((0,), (0,)))
        inner, inverse = inners[s], inverses[s]
        logistic = jax.nn.sigmoid(inner)
        grad_inner = grad_active * logistic * (1.0 + inner * (1.0 - logistic))
        scaled[s] = (inverse * grad_inner).astype(BF16)
        if s > 0:
            t_in[s] = mm(scaled[s], codes[s - 1], ((0,), (0,)))
            along = jnp.sum(inner * grad_inner, axis=-1, keepdims=True) * (inverse * inverse / width)
            back = (grad_y + exact(scaled[s], q_t) - resid_s[s] * along).astype(BF16)
        else:
            t_in[s] = jnp.zeros((rank, size), F32)
    scaled_t = pick(scaled, here).T
    ids = [[(who ^ m) * 2 + k for m in every] for k in range(2) for who in (spot ^ 1, spot)]
    blocks = outer_blocks(ids, scaled_t, base, part // 2)
    sum_in = jnp.concatenate([scatter_sum(*blocks[:2]), scatter_sum(*blocks[2:])], axis=1)
    lift = lambda thin: exact(thin, subspace, ((1,), (1,)))
    if sections == 2:
        lifted = lift(sum_thin(jnp.where(is_last, t_in[1], t_out[0])))
        lift_in = jnp.where(is_last, lifted, 0.0)
        lift_out = lifted
    else:
        lift_in = lift(sum_thin(pick(t_in, here)))
        lift_out = lift(sum_thin(pick(t_out, here)))
    grad_in = (row_gain * (sum_in + lift_in)).T
    grad_out = jnp.where(is_last, sum_out, lift_out).T
    return pick(codes, here)[None], grad_in[None], grad_out[None]


def solution(mesh):
    placed = (
        P("dp", None),
        P("dp", None),
        P("section", None),
        P("section", "dp", None),
        P("section", "dp", None),
        P("dp", None),
    )
    return jax.shard_map(
        on_device,
        mesh=mesh,
        in_specs=placed,
        out_specs=(P("section", "dp", None), P("section", "dp", None), P("section", "dp", None)),
        check_vma=False,
    )
```

time: 208 us -> 169 us (0.81)
  Pallas kernels: 64.3 us -> 15.1 us
  waiting for transfers between devices: 53.1 us -> 71.8 us
  starting transfers between devices: 46.9 us -> 37.6 us
  local copies, waits for them, and re-layouts: 12.7 us -> 18.3 us
  matrix products: 10.9 us -> 7.16 us
    pallas_call x14 -> x6, Pallas kernels: 64.3 us -> 15.1 us  [the longest x4 11.9 us: project(): pl.pallas_call(functools.partial(project_kernel, count), in_specs=[pl.Blo...]
    ppermute x42 -> x43, waiting for transfers between devices: 53.1 us -> 71.8 us  [swap(): return lax.ppermute(value, axis, [(i, i ^ bits) for i in range(peers)])]
    ppermute x42 -> x43, starting transfers between devices: 46.9 us -> 37.6 us  [swap(): return lax.ppermute(value, axis, [(i, i ^ bits) for i in range(peers)])]
    unnamed x29 -> x53, local copies, waits for them, and re-layouts: 6.7 us -> 15.5 us
    add x2 -> x5, other arithmetic: 0.15 us -> 6.02 us  [the longest x3 3.29 us: sum_thin(): value = value + swap(value, bit)]
    concatenate x9 -> x1, other arithmetic: 4.82 us -> 0.03 us  [on_device(): jnp.concatenate([mm(a, subspace, ((0,), (0,))) for a in (own_out, scaled_...]
    select_n x5 -> x4, other arithmetic: 6.19 us -> 1.61 us  [the longest x1 1.35 us: on_device(): jnp.where(core == 0, jnp.concatenate([mine, other], axis=1), jnp.concaten...]
    another operation x7 -> x6, other arithmetic: 1.56 us -> 5.18 us
  transfers between devices with their start and end apart: 42 -> 43, of which waited for: 15 -> 17; matrix products, arithmetic and copies ran while one was open for 14% -> 13% of each run, Pallas kernels for 29% -> 8%
where the time goes in v3:
time: 169 us; the launch traced here: 168 us
  waiting for transfers between devices  71.8 us (42%)
  starting transfers between devices  37.6 us (22%)
  local copies, waits for them, and re-layouts  18.3 us (11%)
  other arithmetic  17.1 us (10%)
  Pallas kernels  15.1 us (9%)
  matrix products  7.16 us (4%)
    ppermute x43, waiting for transfers between devices, swap(): return lax.ppermute(value, axis, [(i, i ^ bits) for i in range(peers)])  71.8 us
    ppermute x43, starting transfers between devices, swap(): return lax.ppermute(value, axis, [(i, i ^ bits) for i in range(peers)])  37.6 us
    unnamed x53, local copies, waits for them, and re-layouts  15.5 us
    pallas_call x4, Pallas kernels, project(): pl.pallas_call(functools.partial(project_kernel, count), in_specs=[pl.Blo...  11.9 us
    dot_general x7, matrix products, exact(): lax.dot_general(a.astype(F32), b.astype(F32), (dims, ((), ())), precision...  3.82 us
  transfers between devices with their start and end apart: 43, of which 17 were waited for; matrix products, arithmetic and copies ran while one was open for 13% of the time, Pallas kernels for 8%

profile of v3, /device:TPU:0, one launch (start us, length us, event | category | flops | bytes accessed | tf_op | source)
XLA Modules:
  0.0 168.4 jit_solution(3310208908858173058)
XLA Ops:
  5.1 2.7 %collective-permute-start.2 = (bf16[1280,128]{1,0:T(8,128)(2,1)S(1)}, bf16[1280,128]{1,0:T(8,128)(2,1)S(1)}, u32[]{:S(2)}, u32[]{:S(2)}) collective-permute-start(bf16[1280,128]{1,0:T(8,128)(2,1)S(1)} %fusion.11.refs_0_), channel_id=1, source_target_pairs={{0,4},{1,5},{2,6},{3,7},{4,0},{5,1},{6,2},{7,3},{8,12},{9,13},{10,... | collective-permute-start | bytes 983048 | tf_op jit(solution)/shard_map/ppermute | solution.py:33
  8.8 7.3 %collective-permute-done.2.refs_1_ = bf16[1280,128]{1,0:T(8,128)(2,1)S(1)} collective-permute-done((bf16[1280,128]{1,0:T(8,128)(2,1)S(1)}, bf16[1280,128]{1,0:T(8,128)(2,1)S(1)}, u32[]{:S(2)}, u32[]{:S(2)}) %collective-permute-start.2) | collective-permute-done | bytes 327712 | tf_op jit(solution)/shard_map/ppermute | solution.py:33
  16.1 2.8 %collective-permute-start.17 = (f32[192,256]{1,0:T(8,128)S(1)}, f32[192,256]{1,0:T(8,128)S(1)}, u32[]{:S(2)}, u32[]{:S(2)}) collective-permute-start(f32[192,256]{1,0:T(8,128)S(1)} %dynamic-slice_add_fusion), channel_id=1, source_target_pairs={{0,8},{1,9},{2,10},{3,11},{4,12},{5,13},{6,14},{7,15},{8,0},{9,1},... | collective-permute-start | bytes 589832 | tf_op jit(solution)/shard_map/ppermute | solution.py:33
  19.0 17.0 %collective-permute-done.17 = f32[192,256]{1,0:T(8,128)S(1)} collective-permute-done((f32[192,256]{1,0:T(8,128)S(1)}, f32[192,256]{1,0:T(8,128)S(1)}, u32[]{:S(2)}, u32[]{:S(2)}) %collective-permute-start.17) | collective-permute-done | bytes 196640 | tf_op jit(solution)/shard_map/ppermute | solution.py:33
  38.2 4.0 %collective-permute-done.refs_2_ = bf16[1280,128]{1,0:T(8,128)(2,1)} collective-permute-done((bf16[1280,128]{1,0:T(8,128)(2,1)S(1)}, bf16[1280,128]{1,0:T(8,128)(2,1)}, u32[]{:S(2)}, u32[]{:S(2)}) %collective-permute-start) | collective-permute-done | bytes 327712 | tf_op jit(solution)/shard_map/ppermute | solution.py:33
  42.6 3.6 %collective-permute-done.18 = f32[192,256]{1,0:T(8,128)S(1)} collective-permute-done((f32[192,256]{1,0:T(8,128)S(1)}, f32[192,256]{1,0:T(8,128)S(1)}, u32[]{:S(2)}, u32[]{:S(2)}) %collective-permute-start.18) | collective-permute-done | bytes 196640 | tf_op jit(solution)/shard_map/ppermute | solution.py:33
  48.5 4.8 %collective-permute-done.1.refs_3_ = bf16[1280,128]{1,0:T(8,128)(2,1)} collective-permute-done((bf16[1280,128]{1,0:T(8,128)(2,1)}, bf16[1280,128]{1,0:T(8,128)(2,1)}, u32[]{:S(2)}, u32[]{:S(2)}) %collective-permute-start.1) | collective-permute-done | bytes 327712 | tf_op jit(solution)/shard_map/ppermute | solution.py:33
  59.2 2.8 %copy-done = bf16[384,8192]{1,0:T(8,128)(2,1)S(1)} copy-done((bf16[384,8192]{1,0:T(8,128)(2,1)S(1)}, bf16[384,8192]{1,0:T(8,128)(2,1)}, u32[]{:S(2)}) %copy-start) | copy-done | bytes 6291480
  62.0 2.8 %copy-done.1 = bf16[384,8192]{1,0:T(8,128)(2,1)S(1)} copy-done((bf16[384,8192]{1,0:T(8,128)(2,1)S(1)}, bf16[384,8192]{1,0:T(8,128)(2,1)}, u32[]{:S(2)}) %copy-start.1) | copy-done | bytes 6291480
  64.8 3.0 %shard_map.85.refs_4_ = f32[384,768]{1,0:T(8,128)S(1)} custom-call(s32[5]{0:T(128)S(1)} %stack.245.ids, bf16[384,8192]{1,0:T(8,128)(2,1)S(1)} %copy-done, bf16[384,8192]{1,0:T(8,128)(2,1)S(1)} %copy-done.1, f32[1,8192]{1,0:T(1,128)S(1)} %copy-done.4, bf16[1280,128]{1,0:T(8,128)(2,1)S(1)} %fusion.11.refs_0_, ...), custom_call_target="tpu_custom_call" | custom-call | flops 1006632960 | bytes 5242880 | tf_op jit(solution)/shard_map/pallas_call | solution.py:113
  70.3 2.8 %copy-done.2 = bf16[384,8192]{1,0:T(8,128)(2,1)S(1)} copy-done((bf16[384,8192]{1,0:T(8,128)(2,1)S(1)}, bf16[384,8192]{1,0:T(8,128)(2,1)}, u32[]{:S(2)}) %copy-start.2) | copy-done | bytes 6291480
  73.1 3.1 %shard_map.86.refs_6_ = f32[384,768]{1,0:T(8,128)S(1)} custom-call(s32[5]{0:T(128)S(1)} %stack.240.ids, bf16[384,8192]{1,0:T(8,128)(2,1)S(1)} %bitcast.163, bf16[384,8192]{1,0:T(8,128)(2,1)S(1)} %copy-done.2, f32[1,8192]{1,0:T(1,128)S(1)} %copy-done.4, bf16[1280,128]{1,0:T(8,128)(2,1)} %collective-permute-done.11.refs_0_, ...), custom_call_target="tpu_custom_call" | custom-call | flops 1006632960 | bytes 5242880 | tf_op jit(solution)/shard_map/pallas_call | solution.py:113
  78.7 3.7 %shard_map.87.refs_2_ = f32[384,768]{1,0:T(8,128)S(1)} custom-call(s32[7]{0:T(128)S(1)} %stack.235.ids, bf16[384,8192]{1,0:T(8,128)(2,1)S(1)} %bitcast.163, bf16[384,8192]{1,0:T(8,128)(2,1)S(1)} %copy-done.2, f32[1,8192]{1,0:T(1,128)S(1)} %copy-done.4, bf16[1280,128]{1,0:T(8,128)(2,1)S(1)} %collective-permute-done.6.refs_0_, ...), custom_call_target="tpu_custom_call" | custom-call | flops 1509949440 | bytes 7864320 | tf_op jit(solution)/shard_map/pallas_call | solution.py:113
  90.3 3.2 %collective-permute-done.22 = bf16[384,256]{0,1:T(8,128)(2,1)S(1)} collective-permute-done((bf16[384,256]{0,1:T(8,128)(2,1)S(1)}, bf16[384,256]{0,1:T(8,128)(2,1)S(1)}, u32[]{:S(2)}, u32[]{:S(2)}) %collective-permute-start.22) | collective-permute-done | bytes 196640 | tf_op jit(solution)/shard_map/ppermute | solution.py:33
  93.6 5.3 %collective-permute-done.15 = bf16[384,384]{0,1:T(8,128)(2,1)S(1)} collective-permute-done((bf16[384,384]{0,1:T(8,128)(2,1)}, bf16[384,384]{0,1:T(8,128)(2,1)S(1)}, u32[]{:S(2)}, u32[]{:S(2)}) %collective-permute-start.15) | collective-permute-done | bytes 294944 | tf_op jit(solution)/shard_map/ppermute | solution.py:33
  107.7 2.8 %copy-done.3 = bf16[384,8192]{1,0:T(8,128)(2,1)S(1)} copy-done((bf16[384,8192]{1,0:T(8,128)(2,1)S(1)}, bf16[384,8192]{1,0:T(8,128)(2,1)}, u32[]{:S(2)}) %copy-start.3) | copy-done | bytes 6291480
  117.7 2.0 %collective-permute-done.35 = f32[128,256]{1,0:T(8,128)} collective-permute-done((f32[128,256]{1,0:T(8,128)}, f32[128,256]{1,0:T(8,128)}, u32[]{:S(2)}, u32[]{:S(2)}) %collective-permute-start.35) | collective-permute-done | bytes 131104 | tf_op jit(solution)/shard_map/ppermute | solution.py:33
  120.7 2.4 %collective-permute-start.36 = (f32[128,256]{1,0:T(8,128)S(1)}, f32[128,256]{1,0:T(8,128)S(1)}, u32[]{:S(2)}, u32[]{:S(2)}) collective-permute-start(f32[128,256]{1,0:T(8,128)S(1)} %add.308), channel_id=1, source_target_pairs={{0,8},{1,9},{2,10},{3,11},{4,12},{5,13},{6,14},{7,15},{8,0},{9,1},... | collective-permute-start | bytes 393224 | tf_op jit(solution)/shard_map/ppermute | solution.py:33
  129.2 4.2 %collective-permute-done.24 = bf16[4,128,256]{2,1,0:T(8,128)(2,1)S(1)} collective-permute-done((bf16[4,128,256]{2,1,0:T(8,128)(2,1)S(1)}, bf16[4,128,256]{2,1,0:T(8,128)(2,1)S(1)}, u32[]{:S(2)}, u32[]{:S(2)}) %collective-permute-start.24) | collective-permute-done | bytes 262176 | tf_op jit(solution)/shard_map/ppermute | solution.py:33
  136.3 6.5 %collective-permute-done.38 = bf16[4,128,256]{2,1,0:T(8,128)(2,1)S(1)} collective-permute-done((bf16[4,128,256]{2,1,0:T(8,128)(2,1)S(1)}, bf16[4,128,256]{2,1,0:T(8,128)(2,1)S(1)}, u32[]{:S(2)}, u32[]{:S(2)}) %collective-permute-start.38) | collective-permute-done | bytes 262176 | tf_op jit(solution)/shard_map/ppermute | solution.py:33
  145.7 2.7 %collective-permute-start.41 = (bf16[128,256]{1,0:T(8,128)(2,1)S(1)}, bf16[128,256]{1,0:T(8,128)(2,1)S(1)}, u32[]{:S(2)}, u32[]{:S(2)}) collective-permute-start(bf16[128,256]{1,0:T(8,128)(2,1)S(1)} %get-tuple-element.55), channel_id=1, source_target_pairs={{0,12},{1,13},{2,14},{3,15},{4,8},{5,9},{6,10},{7,11},{8,4},{9,5},... | collective-permute-start | bytes 196616 | tf_op jit(solution)/shard_map/ppermute | solution.py:33
  149.5 5.8 %collective-permute-done.40 = bf16[128,256]{1,0:T(8,128)(2,1)S(1)} collective-permute-done((bf16[128,256]{1,0:T(8,128)(2,1)S(1)}, bf16[128,256]{1,0:T(8,128)(2,1)S(1)}, u32[]{:S(2)}, u32[]{:S(2)}) %collective-permute-start.40) | collective-permute-done | bytes 65568 | tf_op jit(solution)/shard_map/ppermute | solution.py:33
  157.4 2.5 %collective-permute-start.31 = (bf16[128,256]{1,0:T(8,128)(2,1)S(1)}, bf16[128,256]{1,0:T(8,128)(2,1)S(1)}, u32[]{:S(2)}, u32[]{:S(2)}) collective-permute-start(bf16[128,256]{1,0:T(8,128)(2,1)S(1)} %get-tuple-element.62), channel_id=1, source_target_pairs={{0,8},{1,9},{2,10},{3,11},{4,12},{5,13},{6,14},{7,15},{8,0},{9,1},... | collective-permute-start | bytes 196616 | tf_op jit(solution)/shard_map/ppermute | solution.py:33
  163.3 2.6 %collective-permute-done.32 = bf16[128,256]{1,0:T(8,128)(2,1)S(1)} collective-permute-done((bf16[128,256]{1,0:T(8,128)(2,1)S(1)}, bf16[128,256]{1,0:T(8,128)(2,1)S(1)}, u32[]{:S(2)}, u32[]{:S(2)}) %collective-permute-start.32) | collective-permute-done | bytes 65568 | tf_op jit(solution)/shard_map/ppermute | solution.py:33
  (183 shorter events, 66.7 us)
Async XLA Ops:
  5.1 11.0 %collective-permute-start.2 = (bf16[1280,128]{1,0:T(8,128)(2,1)S(1)}, bf16[1280,128]{1,0:T(8,128)(2,1)S(1)}, u32[]{:S(2)}, u32[]{:S(2)}) collective-permute-start(bf16[1280,128]{1,0:T(8,128)(2,1)S(1)} %fusion.11.refs_0_), channel_id=1, source_target_pairs={{0,4},{1,5},{2,6},{3,7},{4,0},{5,1},{6,2},{7,3},{8,12},{9,13},{10,... | collective-permute-start | bytes 983048 | tf_op jit(solution)/shard_map/ppermute | solution.py:33
  16.1 19.9 %collective-permute-start.17 = (f32[192,256]{1,0:T(8,128)S(1)}, f32[192,256]{1,0:T(8,128)S(1)}, u32[]{:S(2)}, u32[]{:S(2)}) collective-permute-start(f32[192,256]{1,0:T(8,128)S(1)} %dynamic-slice_add_fusion), channel_id=1, source_target_pairs={{0,8},{1,9},{2,10},{3,11},{4,12},{5,13},{6,14},{7,15},{8,0},{9,1},... | collective-permute-start | bytes 589832 | tf_op jit(solution)/shard_map/ppermute | solution.py:33
  18.8 23.3 %collective-permute-start = (bf16[1280,128]{1,0:T(8,128)(2,1)S(1)}, bf16[1280,128]{1,0:T(8,128)(2,1)}, u32[]{:S(2)}, u32[]{:S(2)}) collective-permute-start(bf16[1280,128]{1,0:T(8,128)(2,1)S(1)} %fusion.11.refs_0_), channel_id=1, source_target_pairs={{0,8},{1,9},{2,10},{3,11},{4,12},{5,13},{6,14},{7,15},{8,0},{9,1},... | collective-permute-start | bytes 983048 | tf_op jit(solution)/shard_map/ppermute | solution.py:33
  36.1 12.3 %collective-permute-start.6 = (bf16[1280,128]{1,0:T(8,128)(2,1)S(1)}, bf16[1280,128]{1,0:T(8,128)(2,1)S(1)}, u32[]{:S(2)}, u32[]{:S(2)}) collective-permute-start(bf16[1280,128]{1,0:T(8,128)(2,1)S(1)} %fusion.11.refs_0_), channel_id=1, source_target_pairs={{0,2},{1,3},{2,0},{3,1},{4,6},{5,7},{6,4},{7,5},{8,10},{9,11},{10,... | collective-permute-start | bytes 983048 | tf_op jit(solution)/shard_map/ppermute | solution.py:33
  37.7 17.0 %collective-permute-start.11 = (bf16[1280,128]{1,0:T(8,128)(2,1)S(1)}, bf16[1280,128]{1,0:T(8,128)(2,1)}, u32[]{:S(2)}, u32[]{:S(2)}) collective-permute-start(bf16[1280,128]{1,0:T(8,128)(2,1)S(1)} %fusion.11.refs_0_), channel_id=1, source_target_pairs={{0,1},{1,0},{2,3},{3,2},{4,5},{5,4},{6,7},{7,6},{8,9},{9,8},{10,11... | collective-permute-start | bytes 983048 | tf_op jit(solution)/shard_map/ppermute | solution.py:33
  37.7 17.0 %collective-permute-start.3 = (bf16[1280,128]{1,0:T(8,128)(2,1)S(1)}, bf16[1280,128]{1,0:T(8,128)(2,1)S(1)}, u32[]{:S(2)}, u32[]{:S(2)}) collective-permute-start(bf16[1280,128]{1,0:T(8,128)(2,1)S(1)} %collective-permute-done.2.refs_1_), channel_id=1, source_target_pairs={{0,2},{1,3},{2,0},{3,1},{4,6},{5,7},{6,4},{7,5},{8,10},{9,11},{10,... | collective-permute-start | bytes 983048 | tf_op jit(solution)/shard_map/ppermute | solution.py:33
  42.2 11.1 %collective-permute-start.1 = (bf16[1280,128]{1,0:T(8,128)(2,1)}, bf16[1280,128]{1,0:T(8,128)(2,1)}, u32[]{:S(2)}, u32[]{:S(2)}) collective-permute-start(bf16[1280,128]{1,0:T(8,128)(2,1)} %collective-permute-done.refs_2_), channel_id=1, source_target_pairs={{0,4},{1,5},{2,6},{3,7},{4,0},{5,1},{6,2},{7,3},{8,12},{9,13},{10,... | collective-permute-start | bytes 983048 | tf_op jit(solution)/shard_map/ppermute | solution.py:33
  53.3 14.7 %collective-permute-start.7 = (bf16[1280,128]{1,0:T(8,128)(2,1)}, bf16[1280,128]{1,0:T(8,128)(2,1)}, u32[]{:S(2)}, u32[]{:S(2)}) collective-permute-start(bf16[1280,128]{1,0:T(8,128)(2,1)} %collective-permute-done.refs_2_), channel_id=1, source_target_pairs={{0,2},{1,3},{2,0},{3,1},{4,6},{5,7},{6,4},{7,5},{8,10},{9,11},{10,... | collective-permute-start | bytes 983048 | tf_op jit(solution)/shard_map/ppermute | solution.py:33
  54.8 13.1 %collective-permute-start.13 = (bf16[1280,128]{1,0:T(8,128)(2,1)}, bf16[1280,128]{1,0:T(8,128)(2,1)}, u32[]{:S(2)}, u32[]{:S(2)}) collective-permute-start(bf16[1280,128]{1,0:T(8,128)(2,1)} %collective-permute-done.refs_2_), channel_id=1, source_target_pairs={{0,1},{1,0},{2,3},{3,2},{4,5},{5,4},{6,7},{7,6},{8,9},{9,8},{10,11... | collective-permute-start | bytes 983048 | tf_op jit(solution)/shard_map/ppermute | solution.py:33
  54.8 15.5 %collective-permute-start.4 = (bf16[1280,128]{1,0:T(8,128)(2,1)}, bf16[1280,128]{1,0:T(8,128)(2,1)}, u32[]{:S(2)}, u32[]{:S(2)}) collective-permute-start(bf16[1280,128]{1,0:T(8,128)(2,1)} %collective-permute-done.1.refs_3_), channel_id=1, source_target_pairs={{0,2},{1,3},{2,0},{3,1},{4,6},{5,7},{6,4},{7,5},{8,10},{9,11},{10,... | collective-permute-start | bytes 983048 | tf_op jit(solution)/shard_map/ppermute | solution.py:33
  55.4 13.0 %collective-permute-start.14 = (bf16[1280,128]{1,0:T(8,128)(2,1)}, bf16[1280,128]{1,0:T(8,128)(2,1)}, u32[]{:S(2)}, u32[]{:S(2)}) collective-permute-start(bf16[1280,128]{1,0:T(8,128)(2,1)} %collective-permute-done.1.refs_3_), channel_id=1, source_target_pairs={{0,1},{1,0},{2,3},{3,2},{4,5},{5,4},{6,7},{7,6},{8,9},{9,8},{10,11... | collective-permute-start | bytes 983048 | tf_op jit(solution)/shard_map/ppermute | solution.py:33
  57.2 19.0 %collective-permute-start.20 = (f32[192,256]{1,0:T(8,128)}, f32[192,256]{1,0:T(8,128)}, u32[]{:S(2)}, u32[]{:S(2)}) collective-permute-start(f32[192,256]{1,0:T(8,128)} %convert_add_fusion.3), channel_id=1, source_target_pairs={{0,16},{16,0},{1,17},{17,1},{2,18},{18,2},{3,19},{19,3},{4,20},{20... | collective-permute-start | bytes 589832 | tf_op jit(solution)/shard_map/ppermute | solution.py:33
  67.9 10.8 %collective-permute-start.8 = (bf16[1280,128]{1,0:T(8,128)(2,1)S(1)}, bf16[1280,128]{1,0:T(8,128)(2,1)S(1)}, u32[]{:S(2)}, u32[]{:S(2)}) collective-permute-start(bf16[1280,128]{1,0:T(8,128)(2,1)S(1)} %collective-permute-done.6.refs_0_), channel_id=1, source_target_pairs={{0,1},{1,0},{2,3},{3,2},{4,5},{5,4},{6,7},{7,6},{8,9},{9,8},{10,11... | collective-permute-start | bytes 983048 | tf_op jit(solution)/shard_map/ppermute | solution.py:33
  68.0 10.6 %collective-permute-start.9 = (bf16[1280,128]{1,0:T(8,128)(2,1)S(1)}, bf16[1280,128]{1,0:T(8,128)(2,1)S(1)}, u32[]{:S(2)}, u32[]{:S(2)}) collective-permute-start(bf16[1280,128]{1,0:T(8,128)(2,1)S(1)} %collective-permute-done.3.refs_1_), channel_id=1, source_target_pairs={{0,1},{1,0},{2,3},{3,2},{4,5},{5,4},{6,7},{7,6},{8,9},{9,8},{10,11... | collective-permute-start | bytes 983048 | tf_op jit(solution)/shard_map/ppermute | solution.py:33
  70.3 12.1 %collective-permute-start.5 = (bf16[1280,128]{1,0:T(8,128)(2,1)}, bf16[1280,128]{1,0:T(8,128)(2,1)S(1)}, u32[]{:S(2)}, u32[]{:S(2)}) collective-permute-start(bf16[1280,128]{1,0:T(8,128)(2,1)} %collective-permute-done.4.refs_0_), channel_id=1, source_target_pairs={{0,1},{1,0},{2,3},{3,2},{4,5},{5,4},{6,7},{7,6},{8,9},{9,8},{10,11... | collective-permute-start | bytes 983048 | tf_op jit(solution)/shard_map/ppermute | solution.py:33
  78.2 10.6 %collective-permute-start.21 = (f32[2,192,256]{2,1,0:T(8,128)}, f32[2,192,256]{2,1,0:T(8,128)}, u32[]{:S(2)}, u32[]{:S(2)}) collective-permute-start(f32[2,192,256]{2,1,0:T(8,128)} %pad_maximum_fusion.1), channel_id=1, source_target_pairs={{0,1},{1,0},{2,3},{3,2},{4,5},{5,4},{6,7},{7,6},{8,9},{9,8},{10,11... | collective-permute-start | bytes 1179656 | tf_op jit(solution)/shard_map/ppermute | solution.py:33
  88.2 10.7 %collective-permute-start.15 = (bf16[384,384]{0,1:T(8,128)(2,1)}, bf16[384,384]{0,1:T(8,128)(2,1)S(1)}, u32[]{:S(2)}, u32[]{:S(2)}) collective-permute-start(bf16[384,384]{0,1:T(8,128)(2,1)} %copy.11), channel_id=1, source_target_pairs={{0,16},{16,0},{1,17},{17,1},{2,18},{18,2},{3,19},{19,3},{4,20},{20... | collective-permute-start | bytes 884744 | tf_op jit(solution)/shard_map/ppermute | solution.py:33
  103.3 19.8 %collective-permute-start.23 = (bf16[8,128,256]{2,1,0:T(8,128)(2,1)S(1)}, bf16[8,128,256]{2,1,0:T(8,128)(2,1)}, u32[]{:S(2)}, u32[]{:S(2)}) collective-permute-start(bf16[8,128,256]{2,1,0:T(8,128)(2,1)S(1)} %get-tuple-element.22), channel_id=1, source_target_pairs={{0,1},{1,0},{2,3},{3,2},{4,5},{5,4},{6,7},{7,6},{8,9},{9,8},{10,11... | collective-permute-start | bytes 1572872 | tf_op jit(solution)/shard_map/ppermute | solution.py:33
  107.6 17.4 %collective-permute-start.28 = (bf16[8,128,256]{2,1,0:T(8,128)(2,1)S(1)}, bf16[8,128,256]{2,1,0:T(8,128)(2,1)}, u32[]{:S(2)}, u32[]{:S(2)}) collective-permute-start(bf16[8,128,256]{2,1,0:T(8,128)(2,1)S(1)} %get-tuple-element.24), channel_id=1, source_target_pairs={{0,1},{1,0},{2,3},{3,2},{4,5},{5,4},{6,7},{7,6},{8,9},{9,8},{10,11... | collective-permute-start | bytes 1572872 | tf_op jit(solution)/shard_map/ppermute | solution.py:33
  111.8 15.5 %collective-permute-start.37 = (bf16[8,128,256]{2,1,0:T(8,128)(2,1)S(1)}, bf16[8,128,256]{2,1,0:T(8,128)(2,1)}, u32[]{:S(2)}, u32[]{:S(2)}) collective-permute-start(bf16[8,128,256]{2,1,0:T(8,128)(2,1)S(1)} %get-tuple-element.26), channel_id=1, source_target_pairs={{0,1},{1,0},{2,3},{3,2},{4,5},{5,4},{6,7},{7,6},{8,9},{9,8},{10,11... | collective-permute-start | bytes 1572872 | tf_op jit(solution)/shard_map/ppermute | solution.py:33
  120.7 45.3 %collective-permute-start.36 = (f32[128,256]{1,0:T(8,128)S(1)}, f32[128,256]{1,0:T(8,128)S(1)}, u32[]{:S(2)}, u32[]{:S(2)}) collective-permute-start(f32[128,256]{1,0:T(8,128)S(1)} %add.308), channel_id=1, source_target_pairs={{0,8},{1,9},{2,10},{3,11},{4,12},{5,13},{6,14},{7,15},{8,0},{9,1},... | collective-permute-start | bytes 393224 | tf_op jit(solution)/shard_map/ppermute | solution.py:33
  126.0 19.7 %collective-permute-start.29 = (bf16[4,128,256]{2,1,0:T(8,128)(2,1)S(1)}, bf16[4,128,256]{2,1,0:T(8,128)(2,1)S(1)}, u32[]{:S(2)}, u32[]{:S(2)}) collective-permute-start(bf16[4,128,256]{2,1,0:T(8,128)(2,1)S(1)} %add_convert_fusion.1), channel_id=1, source_target_pairs={{0,2},{1,3},{2,0},{3,1},{4,6},{5,7},{6,4},{7,5},{8,10},{9,11},{10,... | collective-permute-start | bytes 786440 | tf_op jit(solution)/shard_map/ppermute | solution.py:33
  128.3 14.5 %collective-permute-start.38 = (bf16[4,128,256]{2,1,0:T(8,128)(2,1)S(1)}, bf16[4,128,256]{2,1,0:T(8,128)(2,1)S(1)}, u32[]{:S(2)}, u32[]{:S(2)}) collective-permute-start(bf16[4,128,256]{2,1,0:T(8,128)(2,1)S(1)} %add_convert_fusion), channel_id=1, source_target_pairs={{0,2},{1,3},{2,0},{3,1},{4,6},{5,7},{6,4},{7,5},{8,10},{9,11},{10,... | collective-permute-start | bytes 786440 | tf_op jit(solution)/shard_map/ppermute | solution.py:33
  134.5 22.9 %collective-permute-start.25 = (bf16[128,256]{1,0:T(8,128)(2,1)S(1)}, bf16[128,256]{1,0:T(8,128)(2,1)S(1)}, u32[]{:S(2)}, u32[]{:S(2)}) collective-permute-start(bf16[128,256]{1,0:T(8,128)(2,1)S(1)} %get-tuple-element.57), channel_id=1, source_target_pairs={{0,4},{1,5},{2,6},{3,7},{4,0},{5,1},{6,2},{7,3},{8,12},{9,13},{10,... | collective-permute-start | bytes 196616 | tf_op jit(solution)/shard_map/ppermute | solution.py:33
  (45 other events, 331.5 us)

commit v4 on v3

--- a/solution.py
+++ b/solution.py
@@ -64,55 +64,55 @@
     return lax.optimization_barrier((value, *others))[0]
 
 
-def project_kernel(count, ids, base_ref, cot_ref, gain_ref, *refs):
+def rest_kernel(count, ids, base_ref, cot_ref, *refs):
     pieces, acc_ref, out_ref = refs[:count], refs[count], refs[count + 1]
     tall, rank = pieces[0].shape
-    part = tall * 2 // 5
+    part = tall * 2 // 3
     half = part // 2
     out_ref[...] = acc_ref[...]
     skip = ids[count] * half
     for t, piece in enumerate(pieces):
         start = pl.multiple_of(ids[t] * part, part)
         half_start = pl.multiple_of(start + skip, half)
-        block = base_ref[:, pl.ds(start, part)]
-        block_f = block.astype(F32)
-        normed = (block_f * gain_ref[:, pl.ds(start, part)]).astype(BF16)
-        square = block_f * block_f
-        lanes = out_ref.shape[1] - 5 * rank
+        for at, tokens in ((0, base_ref), (2 * rank, cot_ref)):
+            out_ref[:, at : at + rank] += mm(tokens[:, pl.ds(start, part)], piece[:part])
+            out_ref[:, at + rank : at + 2 * rank] += mm(
+                tokens[:, pl.ds(half_start, half)], piece[part:]
+            )
+    if len(refs) > count + 2:
+        refs[count + 2][...] = out_ref[...].astype(BF16)
+
+
+def in_kernel(count, ids, base_ref, gain_ref, *refs):
+    pieces, acc_ref, out_ref = refs[:count], refs[count], refs[count + 1]
+    part, rank = pieces[0].shape
+    out_ref[...] = acc_ref[...]
+    lanes = out_ref.shape[1] - rank
+    for t, piece in enumerate(pieces):
+        start = pl.multiple_of(ids[t] * part, part)
+        block = base_ref[:, pl.ds(start, part)].astype(F32)
+        normed = (block * gain_ref[:, pl.ds(start, part)]).astype(BF16)
+        square = block * block
         total = square[:, :lanes]
         for at in range(lanes, part, lanes):
             total = total + square[:, at : at + lanes]
-        out_ref[:, :rank] += mm(normed, piece[:part])
-        out_ref[:, rank : 2 * rank] += mm(block, piece[part : 2 * part])
-        out_ref[:, 2 * rank : 3 * rank] += mm(
-            base_ref[:, pl.ds(half_start, half)], piece[2 * part :]
-        )
-        out_ref[:, 3 * rank : 4 * rank] += mm(
-            cot_ref[:, pl.ds(start, part)], piece[part : 2 * part]
-        )
-        out_ref[:, 4 * rank : 5 * rank] += mm(
-            cot_ref[:, pl.ds(half_start, half)], piece[2 * part :]
-        )
-        out_ref[:, 5 * rank :] += total
+        out_ref[:, :rank] += mm(normed, piece[...])
+        out_ref[:, rank:] += total
     if len(refs) > count + 2:
-        refs[count + 2][...] = out_ref[:, : 3 * rank].astype(BF16)
-        refs[count + 3][...] = out_ref[:, 3 * rank : 5 * rank].astype(BF16)
-
-
-def project(ids, base, cotangent, gain, pieces, acc, rounded=False):
-    rows = base.shape[0]
+        refs[count + 2][...] = out_ref[:, :rank].astype(BF16)
+
+
+def project(kernel, ids, tokens, pieces, acc, rounded_width):
+    rows = acc.shape[0]
     count = len(pieces)
     tall, rank = pieces[0].shape
     in_vmem = pl.BlockSpec(memory_space=pltpu.VMEM)
     shapes = [jax.ShapeDtypeStruct(acc.shape, F32)]
-    if rounded:
-        shapes += [
-            jax.ShapeDtypeStruct((rows, 3 * rank), BF16),
-            jax.ShapeDtypeStruct((rows, 2 * rank), BF16),
-        ]
+    if rounded_width:
+        shapes.append(jax.ShapeDtypeStruct((rows, rounded_width), BF16))
     return pl.pallas_call(
-        functools.partial(project_kernel, count),
-        in_specs=[pl.BlockSpec(memory_space=pltpu.SMEM)] + [in_vmem] * (count + 4),
+        functools.partial(kernel, count),
+        in_specs=[pl.BlockSpec(memory_space=pltpu.SMEM)] + [in_vmem] * (count + 1 + len(tokens)),
         out_specs=[in_vmem] * len(shapes),
         out_shape=shapes,
         compiler_params=pltpu.CompilerParams(vmem_limit_bytes=VMEM_BYTES),
@@ -121,7 +121,7 @@
             bytes_accessed=2 * count * tall * (rows + rank),
             transcendentals=0,
         ),
-    )(ids, base, cotangent, gain, *pieces, acc)
+    )(ids, *tokens, *pieces, acc)
 
 
 def outer_kernel(ids, small_ref, tokens_ref, *outs):
@@ -155,23 +155,21 @@
 
 def gather_shards(own):
     peers = lax.axis_size("dp")
+    order = sorted(range(4, peers, 4), key=lambda m: (m.bit_count(), m))
     held = {0: own}
-    bit = peers // 2
-    while bit > 2:
-        for m in list(held):
-            held[m ^ bit] = swap(held[m], bit)
-        bit //= 2
-    near = sorted(held)
-    sent = []
-    for m in near:
-        value = held[m]
-        if len(sent) > 1:
-            value = after(value, sent[-2])
-        held[m ^ 2] = swap(value, 2)
-        sent.append(held[m ^ 2])
+    for m in order:
+        if m.bit_count() == 1:
+            held[m] = swap(own, m)
+    held[2] = swap(own, 2)
+    for k, m in enumerate(order):
+        low = m & -m
+        before = held[(order[k - 1] if k else 0) ^ 2]
+        if m != low:
+            held[m] = swap(after(held[m ^ low], held[order[k - 2] ^ 2]), low)
+        held[m ^ 2] = swap(after(held[m], before), 2)
     for m in list(held):
         held[m ^ 1] = swap(held[m], 1)
-    return near, held
+    return [0] + order, held
 
 
 def sum_small(local, wait_for):
@@ -188,12 +186,14 @@
     return keep + swap(keep.astype(BF16), 2).astype(F32)
 
 
-def sum_thin(value):
+def sum_thin(value, waits):
     peers = lax.axis_size("dp")
-    bit = 1
+    bit, step = 1, 0
     while bit < peers:
+        if step:
+            value = after(value, waits[min(step, len(waits)) - 1])
         value = value + swap(value, bit)
-        bit *= 2
+        bit, step = bit * 2, step + 1
     return value
 
 
@@ -213,7 +213,7 @@
     result = total[0]
     for k, m in enumerate(near[1:]):
         result = result + swap(sent[k], m).astype(F32)
-    return result
+    return result, got, got_x
 
 
 def on_device(base, cotangent, gain, weight_in, weight_out, subspace):
@@ -227,52 +227,62 @@
     is_last = here == last
     flag = is_last.astype(jnp.int32)
     own_in, own_out = weight_in[0], weight_out[0]
-    own = jnp.where(
+    own_rest = jnp.where(
         is_last,
-        jnp.concatenate([own_in, own_out, subspace[part // 2 :, rank:]]),
-        jnp.concatenate([own_in, subspace[:, :rank], subspace[: part // 2, rank:]]),
-    )
-    near, shards = gather_shards(own)
+        jnp.concatenate([own_out, subspace[part // 2 :, rank:]]),
+        jnp.concatenate([subspace[:, :rank], subspace[: part // 2, rank:]]),
+    )
+    near, rest = gather_shards(own_rest)
+    _, ins = gather_shards(own_in)
 
     row_gain = lax.dynamic_slice_in_dim(gain, spot * part, part, 1)
-    scaled_in = (row_gain.reshape(part, 1) * own_in.astype(F32)).astype(BF16)
     gram_cols = jnp.where(is_last, subspace[:, rank:], subspace[:, :rank])
-    local = jnp.concatenate([mm(a, subspace, ((0,), (0,))) for a in (own_out, scaled_in, gram_cols)])
-    small = sum_small(local, shards[4])
-    halves = share_sections(small)
-    core = spot % 2
-    mine = jnp.stack(halves)
+    late_in, late_out, late_gram, late_space, _ = lax.optimization_barrier(
+        (own_in, own_out, gram_cols, subspace, ins[4])
+    )
+    scaled_in = (row_gain.reshape(part, 1) * late_in.astype(F32)).astype(BF16)
+    local = jnp.concatenate(
+        [mm(a, late_space, ((0,), (0,))) for a in (late_out, scaled_in, late_gram)]
+    )
+    small = sum_small(local, rest[4])
+    mine = jnp.stack(share_sections(small))
     other = swap(mine, 1)
     smalls = jnp.where(
-        core == 0,
+        spot % 2 == 0,
         jnp.concatenate([mine, other], axis=1),
         jnp.concatenate([other, mine], axis=1),
     )
 
-    acc = jnp.zeros((rows, 6 * rank), F32)
     marks = [
         near,
         [m ^ 1 for m in near],
         [m ^ 2 for m in near[:-1]] + [m ^ 3 for m in near[:-1]],
         [near[-1] ^ 2, near[-1] ^ 3],
     ]
+    acc_rest = jnp.zeros((rows, 4 * rank), F32)
+    acc_in = jnp.zeros((rows, 2 * rank), F32)
     for k, some in enumerate(marks):
         ids = jnp.stack([spot ^ m for m in some] + [flag]).astype(jnp.int32)
-        acc, *rounded = project(
-            ids, base, cotangent, gain, [shards[m] for m in some], acc, k == len(marks) - 1
+        final = k == len(marks) - 1
+        acc_rest, *sent_rest = project(
+            rest_kernel, ids, (base, cotangent), [rest[m] for m in some], acc_rest, final * 4 * rank
         )
-    from_b = [p.astype(F32) for p in share_sections_of(acc[:, : 3 * rank], rounded[0])]
-    from_c = [p.astype(F32) for p in share_sections_of(acc[:, 3 * rank : 5 * rank], rounded[1])]
-    base_p = [p[:, :rank] for p in from_b]
-    base_s = jnp.concatenate(
-        [from_b[0][:, rank : 2 * rank], from_b[0][:, 2 * rank :] + from_b[last][:, 2 * rank :]], axis=1
-    )
-    cot_s = jnp.concatenate(
-        [from_c[0][:, :rank], from_c[0][:, rank:] + from_c[last][:, rank:]], axis=1
-    )
-    cot_w = from_c[last][:, :rank]
+        acc_in, *sent_in = project(
+            in_kernel, ids, (base, gain), [ins[m] for m in some], acc_in, final * rank
+        )
+    wide = share_sections_of(acc_rest, sent_rest[0])
+    base_p = share_sections_of(acc_in[:, :rank], sent_in[0])
+    split = lambda at: jnp.concatenate(
+        [
+            wide[0][:, at : at + rank],
+            wide[0][:, at + rank : at + 2 * rank] + wide[last][:, at + rank : at + 2 * rank],
+        ],
+        axis=1,
+    )
+    base_s, cot_s = split(0), split(2 * rank)
+    cot_w = wide[last][:, 2 * rank : 3 * rank]
     gram = jnp.concatenate([smalls[0, 2 * rank :], smalls[last, 2 * rank :]])
-    square = jnp.sum(acc[:, 5 * rank :], axis=1, keepdims=True)
+    square = jnp.sum(acc_in[:, rank:], axis=1, keepdims=True)
 
     acts, codes, inners, inverses, resid_s = [], [], [], [], []
     for s in range(sections):
@@ -299,12 +309,12 @@
     _, every = block_marks()
     if sections == 2:
         ids = [[(who ^ m) * 2 + flag for m in every] for who in (spot ^ 1, spot)]
-        half_out = scatter_sum(*outer_blocks(ids, acts[last].T, cotangent, part // 2))
+        half_out, got_first, got_x = scatter_sum(*outer_blocks(ids, acts[last].T, cotangent, part // 2))
         whole_out = swap(half_out, 1, "section")
         sum_out = jnp.concatenate([whole_out, half_out], axis=1)
     else:
         ids = [[who ^ m for m in every] for who in (spot ^ 1, spot)]
-        sum_out = scatter_sum(*outer_blocks(ids, acts[last].T, cotangent, part))
+        sum_out, got_first, got_x = scatter_sum(*outer_blocks(ids, acts[last].T, cotangent, part))
 
     scaled, t_in, t_out = [None] * sections, [None] * sections, [None] * sections
     back = None
@@ -327,18 +337,20 @@
             back = (grad_y + exact(scaled[s], q_t) - resid_s[s] * along).astype(BF16)
         else:
             t_in[s] = jnp.zeros((rank, size), F32)
-    scaled_t = pick(scaled, here).T
+    scaled_t = after(pick(scaled, here).T, got_first)
     ids = [[(who ^ m) * 2 + k for m in every] for k in range(2) for who in (spot ^ 1, spot)]
     blocks = outer_blocks(ids, scaled_t, base, part // 2)
-    sum_in = jnp.concatenate([scatter_sum(*blocks[:2]), scatter_sum(*blocks[2:])], axis=1)
+    lower, upper = scatter_sum(*blocks[:2]), scatter_sum(*blocks[2:])
+    sum_in = jnp.concatenate([lower[0], upper[0]], axis=1)
+    waits = [got_x, lower[2], upper[2]]
     lift = lambda thin: exact(thin, subspace, ((1,), (1,)))
     if sections == 2:
-        lifted = lift(sum_thin(jnp.where(is_last, t_in[1], t_out[0])))
+        lifted = lift(sum_thin(jnp.where(is_last, t_in[1], t_out[0]), waits))
         lift_in = jnp.where(is_last, lifted, 0.0)
         lift_out = lifted
     else:
-        lift_in = lift(sum_thin(pick(t_in, here)))
-        lift_out = lift(sum_thin(pick(t_out, here)))
+        lift_in = lift(sum_thin(pick(t_in, here), waits))
+        lift_out = lift(sum_thin(pick(t_out, here), waits))
     grad_in = (row_gain * (sum_in + lift_in)).T
     grad_out = jnp.where(is_last, sum_out, lift_out).T
     return pick(codes, here)[None], grad_in[None], grad_out[None]

time: 169 us -> 159 us (0.941)
  waiting for transfers between devices: 71.8 us -> 43.6 us
  starting transfers between devices: 37.6 us -> 54.5 us
  other arithmetic: 17.1 us -> 13.2 us
  matrix products: 7.16 us -> 11 us
  Pallas kernels: 15.1 us -> 17.7 us
    ppermute x43 -> x58, waiting for transfers between devices: 71.8 us -> 43.6 us  [swap(): return lax.ppermute(value, axis, [(i, i ^ bits) for i in range(peers)])]
    ppermute x43 -> x58, starting transfers between devices: 37.6 us -> 54.5 us  [swap(): return lax.ppermute(value, axis, [(i, i ^ bits) for i in range(peers)])]
    unnamed x53 -> x69, local copies, waits for them, and re-layouts: 15.5 us -> 10.6 us
    pallas_call x4 -> x8, Pallas kernels: 11.9 us -> 14.6 us  [project(): pl.pallas_call(functools.partial(kernel, count), in_specs=[pl.BlockSpec(m...]
    dot_general x5, matrix products: 3.34 us -> 5.76 us  [mm(): return lax.dot_general(a, b, (dims, ((), ())), preferred_element_type=F32)]
    add x3, other arithmetic: 3.29 us -> 1.02 us  [sum_thin(): value = value + swap(value, bit)]
    convert_element_type x3, other arithmetic: 3.04 us -> 1.15 us  [scatter_sum(): summed = (keep[half:].astype(F32) + got[half:].astype(F32)).astype(BF16)]
    pallas_call x3 -> x4, local copies, waits for them, and re-layouts: 1.42 us -> 3.14 us  [project(): pl.pallas_call(functools.partial(kernel, count), in_specs=[pl.BlockSpec(m...]
  transfers between devices with their start and end apart: 43 -> 58, of which waited for: 17 -> 12; matrix products, arithmetic and copies ran while one was open for 13% -> 17% of each run, Pallas kernels for 8% -> 10%
where the time goes in v4:
time: 159 us; the launch traced here: 158 us
  starting transfers between devices  54.5 us (34%)
  waiting for transfers between devices  43.6 us (27%)
  Pallas kernels  17.7 us (11%)
  local copies, waits for them, and re-layouts  16.7 us (11%)
  other arithmetic  13.2 us (8%)
  matrix products  11 us (7%)
    ppermute x58, starting transfers between devices, swap(): return lax.ppermute(value, axis, [(i, i ^ bits) for i in range(peers)])  54.5 us
    ppermute x58, waiting for transfers between devices, swap(): return lax.ppermute(value, axis, [(i, i ^ bits) for i in range(peers)])  43.6 us
    pallas_call x8, Pallas kernels, project(): pl.pallas_call(functools.partial(kernel, count), in_specs=[pl.BlockSpec(m...  14.6 us
    unnamed x69, local copies, waits for them, and re-layouts  10.6 us
    dot_general x5, matrix products, mm(): return lax.dot_general(a, b, (dims, ((), ())), preferred_element_type=F32)  5.76 us
    dot_general x7, matrix products, exact(): lax.dot_general(a.astype(F32), b.astype(F32), (dims, ((), ())), precision...  5.25 us
  transfers between devices with their start and end apart: 58, of which 12 were waited for; matrix products, arithmetic and copies ran while one was open for 17% of the time, Pallas kernels for 10%

profile of v4, /device:TPU:0, one launch (start us, length us, event | category | flops | bytes accessed | tf_op | source)
XLA Modules:
  0.0 158.1 jit_solution(1851642913261915634)
XLA Ops:
  0.6 3.1 %collective-permute-start.1 = (bf16[512,128]{1,0:T(8,128)(2,1)}, bf16[512,128]{1,0:T(8,128)(2,1)}, u32[]{:S(2)}, u32[]{:S(2)}) collective-permute-start(bf16[512,128]{1,0:T(8,128)(2,1)} %bitcast.166), channel_id=1, source_target_pairs={{0,4},{1,5},{2,6},{3,7},{4,0},{5,1},{6,2},{7,3},{8,12},{9,13},{10,... | collective-permute-start | bytes 393224 | tf_op jit(solution)/shard_map/ppermute | solution.py:33
  14.2 3.0 %collective-permute-start = (bf16[512,128]{1,0:T(8,128)(2,1)}, bf16[512,128]{1,0:T(8,128)(2,1)}, u32[]{:S(2)}, u32[]{:S(2)}) collective-permute-start(bf16[512,128]{1,0:T(8,128)(2,1)} %bitcast.169), channel_id=1, source_target_pairs={{0,8},{1,9},{2,10},{3,11},{4,12},{5,13},{6,14},{7,15},{8,0},{9,1},... | collective-permute-start | bytes 393224 | tf_op jit(solution)/shard_map/ppermute | solution.py:33
  19.1 9.7 %collective-permute-done.refs_2_ = bf16[512,128]{1,0:T(8,128)(2,1)} collective-permute-done((bf16[512,128]{1,0:T(8,128)(2,1)}, bf16[512,128]{1,0:T(8,128)(2,1)}, u32[]{:S(2)}, u32[]{:S(2)}) %collective-permute-start) | collective-permute-done | bytes 131104 | tf_op jit(solution)/shard_map/ppermute | solution.py:33
  33.8 3.4 %collective-permute-start.18 = (f32[192,256]{1,0:T(8,128)}, f32[192,256]{1,0:T(8,128)}, u32[]{:S(2)}, u32[]{:S(2)}) collective-permute-start(f32[192,256]{1,0:T(8,128)} %dynamic-slice_add_fusion), channel_id=1, source_target_pairs={{0,8},{1,9},{2,10},{3,11},{4,12},{5,13},{6,14},{7,15},{8,0},{9,1},... | collective-permute-start | bytes 589832 | tf_op jit(solution)/shard_map/ppermute | solution.py:33
  43.1 2.9 %collective-permute-done.18 = f32[192,256]{1,0:T(8,128)} collective-permute-done((f32[192,256]{1,0:T(8,128)}, f32[192,256]{1,0:T(8,128)}, u32[]{:S(2)}, u32[]{:S(2)}) %collective-permute-start.18) | collective-permute-done | bytes 196640 | tf_op jit(solution)/shard_map/ppermute | solution.py:33
  47.1 2.8 %copy-done = bf16[384,8192]{1,0:T(8,128)(2,1)S(1)} copy-done((bf16[384,8192]{1,0:T(8,128)(2,1)S(1)}, bf16[384,8192]{1,0:T(8,128)(2,1)}, u32[]{:S(2)}) %copy-start) | copy-done | bytes 6291480
  51.6 1.8 %shard_map.85.refs_4_ = f32[384,256]{1,0:T(8,128)S(1)} custom-call(s32[5]{0:T(128)S(1)} %stack.245.ids, bf16[384,8192]{1,0:T(8,128)(2,1)S(1)} %copy-done, f32[1,8192]{1,0:T(1,128)S(1)} %copy-done.1, bf16[512,128]{1,0:T(8,128)(2,1)S(1)} %bitcast.171, bf16[512,128]{1,0:T(8,128)(2,1)} %collective-permute-done.1.refs_1_, ...), custom_call_target="tpu_custom_call" | custom-call | flops 402653184 | bytes 2097152 | tf_op jit(solution)/shard_map/pallas_call | solution.py:113
  57.6 2.0 %shard_map.87.refs_2_ = f32[384,256]{1,0:T(8,128)S(1)} custom-call(s32[7]{0:T(128)S(1)} %stack.235.ids, bf16[384,8192]{1,0:T(8,128)(2,1)S(1)} %bitcast.159, f32[1,8192]{1,0:T(1,128)S(1)} %copy-done.1, bf16[512,128]{1,0:T(8,128)(2,1)S(1)} %copy-done.9, bf16[512,128]{1,0:T(8,128)(2,1)S(1)} %copy-done.11, bf16[512,128]{1,0:T(8,128)(2,1)} %collective-permute-done.5.refs_2_, ...), custom_call_target="tpu_custom_call" | custom-call | flops 603979776 | bytes 3145728 | tf_op jit(solution)/shard_map/pallas_call | solution.py:113
  59.7 1.9 %shard_map.89.refs_4_ = f32[384,512]{1,0:T(8,128)S(1)} custom-call(s32[5]{0:T(128)S(1)} %stack.245.ids, bf16[384,8192]{1,0:T(8,128)(2,1)S(1)} %bitcast.159, bf16[384,8192]{1,0:T(8,128)(2,1)S(1)} %bitcast.163, bf16[768,128]{1,0:T(8,128)(2,1)S(1)} %maximum_select_fusion.2.refs_0_, bf16[768,128]{1,0:T(8,128)(2,1)S(1)} %collective-permute-done.17.refs_1_, ...), custom_call_target="tpu_custom_call" | custom-call | flops 603979776 | bytes 3145728 | tf_op jit(solution)/shard_map/pallas_call | solution.py:113
  66.1 5.0 %collective-permute-done.28.refs_0_ = bf16[768,128]{1,0:T(8,128)(2,1)S(1)} collective-permute-done((bf16[768,128]{1,0:T(8,128)(2,1)S(1)}, bf16[768,128]{1,0:T(8,128)(2,1)S(1)}, u32[]{:S(2)}, u32[]{:S(2)}) %collective-permute-start.28) | collective-permute-done | bytes 196640 | tf_op jit(solution)/shard_map/ppermute | solution.py:33
  72.5 1.9 %shard_map.90.refs_6_ = f32[384,512]{1,0:T(8,128)S(1)} custom-call(s32[5]{0:T(128)S(1)} %stack.240.ids, bf16[384,8192]{1,0:T(8,128)(2,1)S(1)} %bitcast.159, bf16[384,8192]{1,0:T(8,128)(2,1)S(1)} %bitcast.163, bf16[768,128]{1,0:T(8,128)(2,1)S(1)} %collective-permute-done.33.refs_0_, bf16[768,128]{1,0:T(8,128)(2,1)S(1)} %collective-permute-done.34.refs_1_, ...), custom_call_target="tpu_custom_call" | custom-call | flops 603979776 | bytes 3145728 | tf_op jit(solution)/shard_map/pallas_call | solution.py:113
  74.5 2.5 %shard_map.91.refs_2_ = f32[384,512]{1,0:T(8,128)S(1)} custom-call(s32[7]{0:T(128)S(1)} %stack.235.ids, bf16[384,8192]{1,0:T(8,128)(2,1)S(1)} %bitcast.159, bf16[384,8192]{1,0:T(8,128)(2,1)S(1)} %bitcast.163, bf16[768,128]{1,0:T(8,128)(2,1)S(1)} %collective-permute-done.24.refs_0_, bf16[768,128]{1,0:T(8,128)(2,1)S(1)} %collective-permute-done.25.refs_1_, ...), custom_call_target="tpu_custom_call" | custom-call | flops 905969664 | bytes 4718592 | tf_op jit(solution)/shard_map/pallas_call | solution.py:113
  88.0 6.7 %collective-permute-done.37 = bf16[384,512]{0,1:T(8,128)(2,1)} collective-permute-done((bf16[384,512]{0,1:T(8,128)(2,1)S(1)}, bf16[384,512]{0,1:T(8,128)(2,1)}, u32[]{:S(2)}, u32[]{:S(2)}) %collective-permute-start.37) | collective-permute-done | bytes 393248 | tf_op jit(solution)/shard_map/ppermute | solution.py:33
  101.4 1.8 %convolution_select_fusion = f32[128,256]{1,0:T(8,128)} fusion(f32[128,256]{1,0:T(8,128)S(1)} %fusion.50, bf16[384,256]{0,1:T(8,128)(2,1)S(1)} %fusion.2, pred[]{:T(512)S(6)} %eq.10, f32[384,256]{0,1:T(8,128)S(1)} %copy-done.23, f32[384]{0:T(512)S(1)} %add_rsqrt_fusion.1, pred[]{:T(512)S(6)} %eq.9, bf16[384,128]{0,1:T(8,128)(2,1)} %copy.11, ...), kind=kOutput, calls=%fused_computation.12 | convolution fusion | flops 25640960 | bytes 854018 | tf_op jit(solution)/shard_map/dot_general | solution.py:18
  105.7 1.8 %shard_map.94 = (bf16[8,128,256]{2,1,0:T(8,128)(2,1)S(1)}, bf16[8,128,256]{2,1,0:T(8,128)(2,1)S(1)}, bf16[8,128,256]{2,1,0:T(8,128)(2,1)S(1)}, bf16[8,128,256]{2,1,0:T(8,128)(2,1)S(1)}) custom-call(s32[32]{0:T(128)S(1)} %stack.281.ids, bf16[128,384]{1,0:T(8,128)(2,1)S(1)} %fusion.9.small_ref, bf16[384,8192]{1,0:T(8,128)(2,1)S(1)} %bitcast.161), custom_call_target="tpu_custom_call" | custom-call | flops 805306368 | bytes 8388608 | tf_op jit(solution)/shard_map/pallas_call | solution.py:142
  110.4 1.8 %collective-permute-done.50 = bf16[4,128,256]{2,1,0:T(8,128)(2,1)} collective-permute-done((bf16[4,128,256]{2,1,0:T(8,128)(2,1)S(1)}, bf16[4,128,256]{2,1,0:T(8,128)(2,1)}, u32[]{:S(2)}, u32[]{:S(2)}) %collective-permute-start.50) | collective-permute-done | bytes 262176 | tf_op jit(solution)/shard_map/ppermute | solution.py:33
  113.3 3.1 %collective-permute-start.56 = (bf16[128,256]{1,0:T(8,128)(2,1)S(1)}, bf16[128,256]{1,0:T(8,128)(2,1)S(1)}, u32[]{:S(2)}, u32[]{:S(2)}) collective-permute-start(bf16[128,256]{1,0:T(8,128)(2,1)S(1)} %get-tuple-element.79), channel_id=1, source_target_pairs={{0,12},{1,13},{2,14},{3,15},{4,8},{5,9},{6,10},{7,11},{8,4},{9,5},... | collective-permute-start | bytes 196616 | tf_op jit(solution)/shard_map/ppermute | solution.py:33
  124.9 3.0 %collective-permute-done.45 = bf16[4,128,256]{2,1,0:T(8,128)(2,1)S(1)} collective-permute-done((bf16[4,128,256]{2,1,0:T(8,128)(2,1)S(1)}, bf16[4,128,256]{2,1,0:T(8,128)(2,1)S(1)}, u32[]{:S(2)}, u32[]{:S(2)}) %collective-permute-start.45) | collective-permute-done | bytes 262176 | tf_op jit(solution)/shard_map/ppermute | solution.py:33
  129.0 4.0 %collective-permute-start.48 = (bf16[128,256]{1,0:T(8,128)(2,1)S(1)}, bf16[128,256]{1,0:T(8,128)(2,1)S(1)}, u32[]{:S(2)}, u32[]{:S(2)}) collective-permute-start(bf16[128,256]{1,0:T(8,128)(2,1)S(1)} %get-tuple-element.85), channel_id=1, source_target_pairs={{0,12},{1,13},{2,14},{3,15},{4,8},{5,9},{6,10},{7,11},{8,4},{9,5},... | collective-permute-start | bytes 196616 | tf_op jit(solution)/shard_map/ppermute | solution.py:33
  134.6 3.0 %collective-permute-start.43 = (bf16[128,256]{1,0:T(8,128)(2,1)S(1)}, bf16[128,256]{1,0:T(8,128)(2,1)S(1)}, u32[]{:S(2)}, u32[]{:S(2)}) collective-permute-start(bf16[128,256]{1,0:T(8,128)(2,1)S(1)} %get-tuple-element.82), channel_id=1, source_target_pairs={{0,12},{1,13},{2,14},{3,15},{4,8},{5,9},{6,10},{7,11},{8,4},{9,5},... | collective-permute-start | bytes 196616 | tf_op jit(solution)/shard_map/ppermute | solution.py:33
  137.6 4.1 %collective-permute-start.42 = (bf16[128,256]{1,0:T(8,128)(2,1)S(1)}, bf16[128,256]{1,0:T(8,128)(2,1)S(1)}, u32[]{:S(2)}, u32[]{:S(2)}) collective-permute-start(bf16[128,256]{1,0:T(8,128)(2,1)S(1)} %get-tuple-element.83), channel_id=1, source_target_pairs={{0,8},{1,9},{2,10},{3,11},{4,12},{5,13},{6,14},{7,15},{8,0},{9,1},... | collective-permute-start | bytes 196616 | tf_op jit(solution)/shard_map/ppermute | solution.py:33
  141.7 2.0 %collective-permute-start.52 = (f32[128,256]{1,0:T(8,128)S(1)}, f32[128,256]{1,0:T(8,128)S(1)}, u32[]{:S(2)}, u32[]{:S(2)}) collective-permute-start(f32[128,256]{1,0:T(8,128)S(1)} %add.324), channel_id=1, source_target_pairs={{0,4},{1,5},{2,6},{3,7},{4,0},{5,1},{6,2},{7,3},{8,12},{9,13},{10,... | collective-permute-start | bytes 393224 | tf_op jit(solution)/shard_map/ppermute | solution.py:33
  143.7 5.0 %collective-permute-done.52 = f32[128,256]{1,0:T(8,128)S(1)} collective-permute-done((f32[128,256]{1,0:T(8,128)S(1)}, f32[128,256]{1,0:T(8,128)S(1)}, u32[]{:S(2)}, u32[]{:S(2)}) %collective-permute-start.52) | collective-permute-done | bytes 131104 | tf_op jit(solution)/shard_map/ppermute | solution.py:33
  150.1 6.0 %collective-permute-done.53 = f32[128,256]{1,0:T(8,128)S(1)} collective-permute-done((f32[128,256]{1,0:T(8,128)S(1)}, f32[128,256]{1,0:T(8,128)S(1)}, u32[]{:S(2)}, u32[]{:S(2)}) %collective-permute-start.53) | collective-permute-done | bytes 131104 | tf_op jit(solution)/shard_map/ppermute | solution.py:33
  (235 shorter events, 74.3 us)
Async XLA Ops:
  3.7 13.4 %collective-permute-start.2 = (bf16[512,128]{1,0:T(8,128)(2,1)}, bf16[512,128]{1,0:T(8,128)(2,1)S(1)}, u32[]{:S(2)}, u32[]{:S(2)}) collective-permute-start(bf16[512,128]{1,0:T(8,128)(2,1)} %bitcast.167), channel_id=1, source_target_pairs={{0,2},{1,3},{2,0},{3,1},{4,6},{5,7},{6,4},{7,5},{8,10},{9,11},{10,... | collective-permute-start | bytes 393224 | tf_op jit(solution)/shard_map/ppermute | solution.py:33
  8.2 10.5 %collective-permute-start.17 = (bf16[768,128]{1,0:T(8,128)(2,1)S(1)}, bf16[768,128]{1,0:T(8,128)(2,1)S(1)}, u32[]{:S(2)}, u32[]{:S(2)}) collective-permute-start(bf16[768,128]{1,0:T(8,128)(2,1)S(1)} %maximum_select_fusion.2.refs_0_), channel_id=1, source_target_pairs={{0,4},{1,5},{2,6},{3,7},{4,0},{5,1},{6,2},{7,3},{8,12},{9,13},{10,... | collective-permute-start | bytes 589832 | tf_op jit(solution)/shard_map/ppermute | solution.py:33
  8.7 10.0 %collective-permute-start.24 = (bf16[768,128]{1,0:T(8,128)(2,1)S(1)}, bf16[768,128]{1,0:T(8,128)(2,1)S(1)}, u32[]{:S(2)}, u32[]{:S(2)}) collective-permute-start(bf16[768,128]{1,0:T(8,128)(2,1)S(1)} %maximum_select_fusion.2.refs_0_), channel_id=1, source_target_pairs={{0,2},{1,3},{2,0},{3,1},{4,6},{5,7},{6,4},{7,5},{8,10},{9,11},{10,... | collective-permute-start | bytes 589832 | tf_op jit(solution)/shard_map/ppermute | solution.py:33
  14.2 16.7 %collective-permute-start.16 = (f32[192,256]{1,0:T(8,128)}, f32[192,256]{1,0:T(8,128)}, u32[]{:S(2)}, u32[]{:S(2)}) collective-permute-start(f32[192,256]{1,0:T(8,128)} %constant_dynamic-slice_fusion), channel_id=1, source_target_pairs={{0,1},{1,0},{2,3},{3,2},{4,5},{5,4},{6,7},{7,6},{8,9},{9,8},{10,11... | collective-permute-start | bytes 589832 | tf_op jit(solution)/shard_map/ppermute | solution.py:33
  14.2 14.6 %collective-permute-start = (bf16[512,128]{1,0:T(8,128)(2,1)}, bf16[512,128]{1,0:T(8,128)(2,1)}, u32[]{:S(2)}, u32[]{:S(2)}) collective-permute-start(bf16[512,128]{1,0:T(8,128)(2,1)} %bitcast.169), channel_id=1, source_target_pairs={{0,8},{1,9},{2,10},{3,11},{4,12},{5,13},{6,14},{7,15},{8,0},{9,1},... | collective-permute-start | bytes 393224 | tf_op jit(solution)/shard_map/ppermute | solution.py:33
  17.2 13.4 %collective-permute-start.3 = (bf16[512,128]{1,0:T(8,128)(2,1)}, bf16[512,128]{1,0:T(8,128)(2,1)S(1)}, u32[]{:S(2)}, u32[]{:S(2)}) collective-permute-start(bf16[512,128]{1,0:T(8,128)(2,1)} %collective-permute-done.1.refs_1_), channel_id=1, source_target_pairs={{0,2},{1,3},{2,0},{3,1},{4,6},{5,7},{6,4},{7,5},{8,10},{9,11},{10,... | collective-permute-start | bytes 393224 | tf_op jit(solution)/shard_map/ppermute | solution.py:33
  18.7 14.5 %collective-permute-start.11 = (bf16[512,128]{1,0:T(8,128)(2,1)}, bf16[512,128]{1,0:T(8,128)(2,1)S(1)}, u32[]{:S(2)}, u32[]{:S(2)}) collective-permute-start(bf16[512,128]{1,0:T(8,128)(2,1)} %bitcast.170), channel_id=1, source_target_pairs={{0,1},{1,0},{2,3},{3,2},{4,5},{5,4},{6,7},{7,6},{8,9},{9,8},{10,11... | collective-permute-start | bytes 393224 | tf_op jit(solution)/shard_map/ppermute | solution.py:33
  18.7 19.6 %collective-permute-start.23 = (bf16[768,128]{1,0:T(8,128)(2,1)S(1)}, bf16[768,128]{1,0:T(8,128)(2,1)S(1)}, u32[]{:S(2)}, u32[]{:S(2)}) collective-permute-start(bf16[768,128]{1,0:T(8,128)(2,1)S(1)} %maximum_select_fusion.2.refs_0_), channel_id=1, source_target_pairs={{0,8},{1,9},{2,10},{3,11},{4,12},{5,13},{6,14},{7,15},{8,0},{9,1},... | collective-permute-start | bytes 589832 | tf_op jit(solution)/shard_map/ppermute | solution.py:33
  28.8 10.0 %collective-permute-start.25 = (bf16[768,128]{1,0:T(8,128)(2,1)S(1)}, bf16[768,128]{1,0:T(8,128)(2,1)S(1)}, u32[]{:S(2)}, u32[]{:S(2)}) collective-permute-start(bf16[768,128]{1,0:T(8,128)(2,1)S(1)} %collective-permute-done.17.refs_1_), channel_id=1, source_target_pairs={{0,2},{1,3},{2,0},{3,1},{4,6},{5,7},{6,4},{7,5},{8,10},{9,11},{10,... | collective-permute-start | bytes 589832 | tf_op jit(solution)/shard_map/ppermute | solution.py:33
  33.8 12.2 %collective-permute-start.18 = (f32[192,256]{1,0:T(8,128)}, f32[192,256]{1,0:T(8,128)}, u32[]{:S(2)}, u32[]{:S(2)}) collective-permute-start(f32[192,256]{1,0:T(8,128)} %dynamic-slice_add_fusion), channel_id=1, source_target_pairs={{0,8},{1,9},{2,10},{3,11},{4,12},{5,13},{6,14},{7,15},{8,0},{9,1},... | collective-permute-start | bytes 589832 | tf_op jit(solution)/shard_map/ppermute | solution.py:33
  40.8 16.6 %collective-permute-start.26 = (bf16[768,128]{1,0:T(8,128)(2,1)S(1)}, bf16[768,128]{1,0:T(8,128)(2,1)S(1)}, u32[]{:S(2)}, u32[]{:S(2)}) collective-permute-start(bf16[768,128]{1,0:T(8,128)(2,1)S(1)} %collective-permute-done.23.refs_2_), channel_id=1, source_target_pairs={{0,4},{1,5},{2,6},{3,7},{4,0},{5,1},{6,2},{7,3},{8,12},{9,13},{10,... | collective-permute-start | bytes 589832 | tf_op jit(solution)/shard_map/ppermute | solution.py:33
  42.5 15.0 %collective-permute-start.27 = (bf16[768,128]{1,0:T(8,128)(2,1)S(1)}, bf16[768,128]{1,0:T(8,128)(2,1)S(1)}, u32[]{:S(2)}, u32[]{:S(2)}) collective-permute-start(bf16[768,128]{1,0:T(8,128)(2,1)S(1)} %collective-permute-done.23.refs_2_), channel_id=1, source_target_pairs={{0,2},{1,3},{2,0},{3,1},{4,6},{5,7},{6,4},{7,5},{8,10},{9,11},{10,... | collective-permute-start | bytes 589832 | tf_op jit(solution)/shard_map/ppermute | solution.py:33
  43.1 13.8 %collective-permute-start.9 = (bf16[512,128]{1,0:T(8,128)(2,1)}, bf16[512,128]{1,0:T(8,128)(2,1)}, u32[]{:S(2)}, u32[]{:S(2)}) collective-permute-start(bf16[512,128]{1,0:T(8,128)(2,1)} %copy-done.10), channel_id=1, source_target_pairs={{0,1},{1,0},{2,3},{3,2},{4,5},{5,4},{6,7},{7,6},{8,9},{9,8},{10,11... | collective-permute-start | bytes 393224 | tf_op jit(solution)/shard_map/ppermute | solution.py:33
  46.0 11.0 %collective-permute-start.10 = (bf16[512,128]{1,0:T(8,128)(2,1)}, bf16[512,128]{1,0:T(8,128)(2,1)}, u32[]{:S(2)}, u32[]{:S(2)}) collective-permute-start(bf16[512,128]{1,0:T(8,128)(2,1)} %collective-permute-done.5.refs_2_), channel_id=1, source_target_pairs={{0,1},{1,0},{2,3},{3,2},{4,5},{5,4},{6,7},{7,6},{8,9},{9,8},{10,11... | collective-permute-start | bytes 393224 | tf_op jit(solution)/shard_map/ppermute | solution.py:33
  61.6 12.8 %collective-permute-start.30 = (bf16[768,128]{1,0:T(8,128)(2,1)S(1)}, bf16[768,128]{1,0:T(8,128)(2,1)S(1)}, u32[]{:S(2)}, u32[]{:S(2)}) collective-permute-start(bf16[768,128]{1,0:T(8,128)(2,1)S(1)} %collective-permute-done.24.refs_0_), channel_id=1, source_target_pairs={{0,1},{1,0},{2,3},{3,2},{4,5},{5,4},{6,7},{7,6},{8,9},{9,8},{10,11... | collective-permute-start | bytes 589832 | tf_op jit(solution)/shard_map/ppermute | solution.py:33
  63.6 10.8 %collective-permute-start.31 = (bf16[768,128]{1,0:T(8,128)(2,1)S(1)}, bf16[768,128]{1,0:T(8,128)(2,1)S(1)}, u32[]{:S(2)}, u32[]{:S(2)}) collective-permute-start(bf16[768,128]{1,0:T(8,128)(2,1)S(1)} %collective-permute-done.25.refs_1_), channel_id=1, source_target_pairs={{0,1},{1,0},{2,3},{3,2},{4,5},{5,4},{6,7},{7,6},{8,9},{9,8},{10,11... | collective-permute-start | bytes 589832 | tf_op jit(solution)/shard_map/ppermute | solution.py:33
  82.6 12.1 %collective-permute-start.37 = (bf16[384,512]{0,1:T(8,128)(2,1)S(1)}, bf16[384,512]{0,1:T(8,128)(2,1)}, u32[]{:S(2)}, u32[]{:S(2)}) collective-permute-start(bf16[384,512]{0,1:T(8,128)(2,1)S(1)} %copy.14), channel_id=1, source_target_pairs={{0,16},{16,0},{1,17},{17,1},{2,18},{18,2},{3,19},{19,3},{4,20},{20... | collective-permute-start | bytes 1179656 | tf_op jit(solution)/shard_map/ppermute | solution.py:33
  84.8 11.4 %collective-permute-start.15 = (bf16[384,128]{0,1:T(8,128)(2,1)}, bf16[384,128]{0,1:T(8,128)(2,1)}, u32[]{:S(2)}, u32[]{:S(2)}) collective-permute-start(bf16[384,128]{0,1:T(8,128)(2,1)} %copy.11), channel_id=1, source_target_pairs={{0,16},{16,0},{1,17},{17,1},{2,18},{18,2},{3,19},{19,3},{4,20},{20... | collective-permute-start | bytes 294920 | tf_op jit(solution)/shard_map/ppermute | solution.py:33
  107.6 10.3 %collective-permute-start.44 = (bf16[8,128,256]{2,1,0:T(8,128)(2,1)S(1)}, bf16[8,128,256]{2,1,0:T(8,128)(2,1)}, u32[]{:S(2)}, u32[]{:S(2)}) collective-permute-start(bf16[8,128,256]{2,1,0:T(8,128)(2,1)S(1)} %get-tuple-element.48), channel_id=1, source_target_pairs={{0,1},{1,0},{2,3},{3,2},{4,5},{5,4},{6,7},{7,6},{8,9},{9,8},{10,11... | collective-permute-start | bytes 1572872 | tf_op jit(solution)/shard_map/ppermute | solution.py:33
  109.8 14.4 %collective-permute-start.39 = (bf16[8,128,256]{2,1,0:T(8,128)(2,1)S(1)}, bf16[8,128,256]{2,1,0:T(8,128)(2,1)S(1)}, u32[]{:S(2)}, u32[]{:S(2)}) collective-permute-start(bf16[8,128,256]{2,1,0:T(8,128)(2,1)S(1)} %get-tuple-element.46), channel_id=1, source_target_pairs={{0,1},{1,0},{2,3},{3,2},{4,5},{5,4},{6,7},{7,6},{8,9},{9,8},{10,11... | collective-permute-start | bytes 1572872 | tf_op jit(solution)/shard_map/ppermute | solution.py:33
  122.8 27.4 %collective-permute-start.57 = (f32[128,256]{1,0:T(8,128)S(1)}, f32[128,256]{1,0:T(8,128)S(1)}, u32[]{:S(2)}, u32[]{:S(2)}) collective-permute-start(f32[128,256]{1,0:T(8,128)S(1)} %fusion.23), channel_id=1, source_target_pairs={{0,16},{16,0},{1,17},{17,1},{2,18},{18,2},{3,19},{19,3},{4,20},{20... | collective-permute-start | bytes 393224 | tf_op jit(solution)/shard_map/ppermute | solution.py:33
  124.3 10.1 %collective-permute-start.40 = (bf16[4,128,256]{2,1,0:T(8,128)(2,1)S(1)}, bf16[4,128,256]{2,1,0:T(8,128)(2,1)S(1)}, u32[]{:S(2)}, u32[]{:S(2)}) collective-permute-start(bf16[4,128,256]{2,1,0:T(8,128)(2,1)S(1)} %add_convert_fusion.2), channel_id=1, source_target_pairs={{0,2},{1,3},{2,0},{3,1},{4,6},{5,7},{6,4},{7,5},{8,10},{9,11},{10,... | collective-permute-start | bytes 786440 | tf_op jit(solution)/shard_map/ppermute | solution.py:33
  134.6 15.5 %collective-permute-start.43 = (bf16[128,256]{1,0:T(8,128)(2,1)S(1)}, bf16[128,256]{1,0:T(8,128)(2,1)S(1)}, u32[]{:S(2)}, u32[]{:S(2)}) collective-permute-start(bf16[128,256]{1,0:T(8,128)(2,1)S(1)} %get-tuple-element.82), channel_id=1, source_target_pairs={{0,12},{1,13},{2,14},{3,15},{4,8},{5,9},{6,10},{7,11},{8,4},{9,5},... | collective-permute-start | bytes 196616 | tf_op jit(solution)/shard_map/ppermute | solution.py:33
  137.6 12.5 %collective-permute-start.42 = (bf16[128,256]{1,0:T(8,128)(2,1)S(1)}, bf16[128,256]{1,0:T(8,128)(2,1)S(1)}, u32[]{:S(2)}, u32[]{:S(2)}) collective-permute-start(bf16[128,256]{1,0:T(8,128)(2,1)S(1)} %get-tuple-element.83), channel_id=1, source_target_pairs={{0,8},{1,9},{2,10},{3,11},{4,12},{5,13},{6,14},{7,15},{8,0},{9,1},... | collective-permute-start | bytes 196616 | tf_op jit(solution)/shard_map/ppermute | solution.py:33
  (67 other events, 485.4 us)

commit v5 on v1

v5 whole, which is shorter than its diff:
```python
import functools

import jax
import jax.numpy as jnp
from jax import lax
from jax.experimental import pallas as pl
from jax.experimental.pallas import tpu as pltpu
from jax.sharding import PartitionSpec as P

F32 = jnp.float32
BF16 = jnp.bfloat16
VMEM_BYTES = 12 * 1024 * 1024
IN_VMEM = pl.BlockSpec(memory_space=pltpu.VMEM)
IN_SMEM = pl.BlockSpec(memory_space=pltpu.SMEM)
CONTRACT = ((1,), (0,))
ROWS = ((0,), (0,))
COLUMNS = ((1,), (1,))


def mm(a, b, dims=CONTRACT):
    return lax.dot_general(a, b, (dims, ((), ())), preferred_element_type=F32)


def parts_of(a):
    if a.dtype == BF16:
        return [a]
    high = a.astype(BF16)
    return [high, (a - high.astype(F32)).astype(BF16)]


def exact(a, b, dims=CONTRACT):
    left, right = parts_of(a), parts_of(b)
    total = mm(left[0], right[0], dims)
    for i, x in enumerate(left):
        for j, y in enumerate(right):
            if i + j == 1:
                total = total + mm(x, y, dims)
    return total


def call(kernel, scalars, arrays, shapes, flops, vmem_bytes=VMEM_BYTES):
    size = lambda shape, dtype: jnp.dtype(dtype).itemsize * functools.reduce(lambda x, y: x * y, shape, 1)
    moved = sum(size(a.shape, a.dtype) for a in arrays) + sum(size(*s) for s in shapes)
    return pl.pallas_call(
        kernel,
        in_specs=[IN_SMEM] + [IN_VMEM] * len(arrays),
        out_specs=[IN_VMEM] * len(shapes),
        out_shape=[jax.ShapeDtypeStruct(*s) for s in shapes],
        compiler_params=pltpu.CompilerParams(vmem_limit_bytes=vmem_bytes),
        cost_estimate=pl.CostEstimate(flops=flops, bytes_accessed=moved, transcendentals=0),
    )(jnp.stack(scalars).astype(jnp.int32), *arrays)


def swap(value, bits, axis="dp"):
    peers = lax.axis_size(axis)
    return lax.ppermute(value, axis, [(i, i ^ bits) for i in range(peers)])


def after(value, *others):
    return lax.optimization_barrier((value, *others))[0]


def from_sections(value):
    sections = lax.axis_size("section")
    here = lax.axis_index("section")
    if sections == 2:
        return [swap(value, 1, "section")]
    around = [(i, (i + 1) % sections) for i in range(sections)]
    held = [value]
    for _ in range(sections - 1):
        held.append(lax.ppermute(held[-1], "section", around))
    stacked = jnp.stack(held)
    order = (here - jnp.arange(sections)) % sections
    return [lax.dynamic_index_in_dim(stacked, order[s], 0, keepdims=False) for s in range(sections)]


def own_kernel(scalars, in_ref, out_ref, space_ref, own_ref):
    is_last = scalars[0] == 1
    part, rank = in_ref.shape
    half = part // 2
    own_ref[:part] = in_ref[...]
    own_ref[part : 2 * part] = jnp.where(is_last, out_ref[...], space_ref[:, :rank])
    own_ref[2 * part :] = jnp.where(is_last, space_ref[half:, rank:], space_ref[:half, rank:])


def small_kernel(scalars, in_ref, out_ref, space_ref, gain_ref, keep_ref, give_ref, all_ref):
    is_last, core = scalars[0] == 1, scalars[1]
    part, rank = in_ref.shape
    space = space_ref[...]
    start = pl.multiple_of(scalars[2] * part, part)
    scaled_t = in_ref[...].astype(F32).T * gain_ref[:, pl.ds(start, part)]
    all_ref[:rank] = mm(out_ref[...], space, ROWS)
    all_ref[rank : 2 * rank] = mm(scaled_t.astype(BF16), space)
    columns = jnp.where(is_last, space_ref[:, rank:], space_ref[:, :rank])
    all_ref[2 * rank :] = mm(columns, space, ROWS)
    half = keep_ref.shape[0]
    first, second = all_ref[:half], all_ref[half:]
    keep_ref[...] = jnp.where(core == 0, first, second)
    give_ref[...] = jnp.where(core == 0, second, first)


def project_kernel(shape, stack, with_base, with_cot, count, scalars, *refs):
    tall, rank = shape
    part = tall * 2 // 5
    half = part // 2
    skip = scalars[count] * half
    refs = list(refs)
    take = lambda n: [refs.pop(0) for _ in range(n)]
    base_ref, gain_ref = take(2) if with_base else (None, None)
    cot_ref = take(1)[0] if with_cot else None
    shards = []
    while len(shards) < count:
        ref = refs.pop(0)
        shards += [ref] if len(ref.shape) == 2 else [ref.at[i] for i in range(ref.shape[0])]
    acc_b = take(1)[0] if with_base else None
    acc_c = take(1)[0] if with_cot else None
    out_b = take(1)[0] if with_base else None
    out_c = take(1)[0] if with_cot else None
    if with_base:
        out_b[...] = acc_b[...]
    if with_cot:
        out_c[...] = acc_c[...]
    for t, shard in enumerate(shards):
        start = pl.multiple_of(scalars[t] * part, part)
        half_start = pl.multiple_of(start + skip, half)
        if with_base:
            block = base_ref[:, pl.ds(start, part)]
            block_f = block.astype(F32)
            normed = (block_f * gain_ref[:, pl.ds(start, part)]).astype(BF16)
            square = block_f * block_f
            total = square[:, :rank]
            for at in range(rank, part, rank):
                total = total + square[:, at : at + rank]
            out_b[:, :rank] += mm(normed, shard[:part])
            out_b[:, rank : 2 * rank] += mm(block, shard[part : 2 * part])
            out_b[:, 2 * rank : 3 * rank] += mm(
                base_ref[:, pl.ds(half_start, half)], shard[2 * part :]
            )
            out_b[:, 3 * rank :] += total
        if with_cot:
            out_c[:, :rank] += mm(cot_ref[:, pl.ds(start, part)], shard[part : 2 * part])
            out_c[:, rank:] += mm(cot_ref[:, pl.ds(half_start, half)], shard[2 * part :])
        if stack:
            refs[0][t] = shard[...]
    if not stack and refs:
        if with_base:
            refs.pop(0)[...] = out_b[:, : 3 * rank].astype(BF16)
        if with_cot:
            refs.pop(0)[...] = out_c[...].astype(BF16)


def project(ids, flag, shards, base=None, cot=None, stack=False, final=False):
    tall, rank = shards[0].shape[-2:]
    count = len(ids)
    tokens, accs, shapes, rounded = [], [], [], []
    if base:
        rows = base[0].shape[0]
        tokens += base[:2]
        accs.append(base[2])
        shapes.append(((rows, 4 * rank), F32))
        rounded.append(((rows, 3 * rank), BF16))
    if cot:
        rows = cot[0].shape[0]
        tokens += cot[:1]
        accs.append(cot[1])
        shapes.append(((rows, 2 * rank), F32))
        rounded.append(((rows, 2 * rank), BF16))
    if stack:
        shapes.append(((count, tall, rank), BF16))
    if final:
        shapes += rounded
    kernel = functools.partial(project_kernel, (tall, rank), stack, bool(base), bool(cot), count)
    flops = 2 * rows * count * tall * rank * len(accs)
    return call(kernel, [*ids, flag], [*tokens, *shards, *accs], shapes, flops)


def outer_into(scalars, at, small, tokens_ref, outs):
    for out in outs:
        count, _, columns = out.shape
        for j in range(count):
            start = pl.multiple_of(scalars[at] * columns, columns)
            out[j] = mm(small, tokens_ref[:, pl.ds(start, columns)]).astype(BF16)
            at += 1


def small_parts(sections, here, core, keeps, others, s):
    value = lambda refs: (
        jnp.where(here == s, refs[0][...], refs[1][...]) if sections == 2 else refs[1 + s][...]
    )
    mine, theirs = value(keeps), value(others)
    whole = jnp.concatenate(
        [jnp.where(core == 0, mine, theirs), jnp.where(core == 0, theirs, mine)]
    )
    rank = whole.shape[0] // 3
    return whole[:rank], whole[rank : 2 * rank], whole[2 * rank :]


def forward_chain(sections, width, here, core, own_b, sent_b, keeps, others):
    rank = own_b.shape[1] // 4
    last = sections - 1
    sent = lambda s: sent_b[0 if sections == 2 else s][...].astype(F32)
    based = lambda s, at: jnp.where(
        here == s, own_b[:, at : at + rank], sent(s)[:, at : at + rank]
    )
    base_s = jnp.concatenate(
        [based(0, rank), based(0, 2 * rank) + based(last, 2 * rank)], axis=1
    )
    square = jnp.sum(own_b[:, 3 * rank :], axis=1, keepdims=True)
    smalls = [small_parts(sections, here, core, keeps, others, s) for s in range(sections)]
    gram = jnp.concatenate([smalls[0][2], smalls[last][2]])
    state = []
    code = None
    for s in range(sections):
        m_s, q_t, _ = smalls[s]
        inner, total, resid_s, moved = based(s, 0), square, base_s, None
        if s:
            moved = exact(code, gram)
            total = square + jnp.sum(
                (2.0 * base_s + moved) * code.astype(F32), axis=1, keepdims=True
            )
            inner = inner + exact(code, q_t, COLUMNS)
            resid_s = base_s + moved
        inverse = lax.rsqrt(jnp.maximum(total, 0.0) * (1.0 / width) + 1e-05)
        inner = inner * inverse
        logistic = 1.0 / (1.0 + jnp.exp(-inner))
        active = inner * logistic
        before = code
        state.append((m_s, q_t, inner, logistic, inverse, active, resid_s, before))
        if s == last:
            yield state, gram, before, moved
            code = (moved + exact(active, m_s)).astype(BF16)
            yield code
            return
        grown = exact(active, m_s)
        code = (grown if s == 0 else moved + grown).astype(BF16)


def forward_kernel(sections, width, scalars, own_b, *refs):
    here, core = scalars[0], scalars[1]
    n = 1 if sections == 2 else sections
    sent_b, refs = refs[:n], refs[n:]
    keeps, refs = refs[: n + 1], refs[n + 1 :]
    others, refs = refs[: n + 1], refs[n + 1 :]
    tokens_ref, outs = refs[0], refs[1:]
    state = next(forward_chain(sections, width, here, core, own_b, sent_b, keeps, others))[0]
    outer_into(scalars, 2, state[-1][5].T.astype(BF16), tokens_ref, outs)


def backward_kernel(sections, width, scalars, own_b, own_c, *refs):
    here, core = scalars[0], scalars[1]
    n = 1 if sections == 2 else sections
    sent_b, refs = refs[:n], refs[n:]
    sent_c, refs = refs[:n], refs[n:]
    keeps, refs = refs[: n + 1], refs[n + 1 :]
    others, refs = refs[: n + 1], refs[n + 1 :]
    tokens_ref, codes_ref, refs = refs[0], refs[1], refs[2:]
    thin_count = 1 if sections == 2 else 2
    thin_refs, outs = refs[:thin_count], refs[thin_count:]
    rank = own_c.shape[1] // 2
    last = sections - 1
    chain = forward_chain(sections, width, here, core, own_b, sent_b, keeps, others)
    state, gram, _, _ = next(chain)
    final_code = next(chain)
    sent = lambda s: sent_c[0 if sections == 2 else s][...].astype(F32)
    cot = lambda s, at: jnp.where(
        here == s, own_c[:, at : at + rank], sent(s)[:, at : at + rank]
    )
    grad_active = cot(last, 0)
    grad_y = jnp.concatenate([cot(0, 0), cot(0, rank) + cot(last, rank)], axis=1)
    mine = None
    mine_code = final_code
    thin_in = thin_out = None
    choose = lambda s, value, other: value if other is None else jnp.where(here == s, value, other)
    for s in range(last, -1, -1):
        m_s, q_t, inner, logistic, inverse, active, resid_s, before = state[s]
        if s < last:
            grad_active = exact(back, m_s, COLUMNS)
            grad_y = exact(back, gram) if s else None
            thin_out = choose(s, mm(active.T.astype(BF16), back), thin_out)
        grad_inner = grad_active * logistic * (1.0 + inner * (1.0 - logistic))
        scaled = inverse * grad_inner
        scaled_t = scaled.T.astype(BF16)
        scaled = scaled.astype(BF16)
        mine = choose(s, scaled_t, mine)
        if s:
            mine_code = jnp.where(here == s - 1, before, mine_code)
            thin_in = choose(s, mm(scaled_t, before), thin_in)
            along = jnp.sum(inner * grad_inner, axis=1, keepdims=True)
            along = along * (inverse * inverse * (1.0 / width))
            back = (grad_y + exact(scaled, q_t) - resid_s * along).astype(BF16)
    codes_ref[...] = mine_code
    if sections == 2:
        thin_refs[0][...] = jnp.where(here == last, thin_in, thin_out)
    else:
        thin_refs[0][...] = jnp.where(here == 0, 0.0, thin_in)
        thin_refs[1][...] = thin_out
    outer_into(scalars, 2, mine, tokens_ref, outs)


def end_kernel(sections, scalars, space_ref, gain_ref, *refs):
    is_last = scalars[0] == 1
    part = space_ref.shape[0]
    grad_in, grad_out = refs[-2:]
    refs = list(refs[:-2])
    pair = lambda: refs.pop(0)[...].astype(F32) + refs.pop(0)[...].astype(F32)
    thin_in = pair()
    thin_out = thin_in if sections == 2 else pair()
    space = space_ref[...]
    lift_in = exact(thin_in, space, COLUMNS)
    lift_out = lift_in if sections == 2 else exact(thin_out, space, COLUMNS)
    if sections == 2:
        lift_in = jnp.where(is_last, lift_in, 0.0)
        half_first, half_second = refs.pop(0)[...], refs.pop(0)[...]
        sum_out = jnp.concatenate([half_first, half_second], axis=1)
    else:
        sum_out = refs.pop(0)[...]
    sum_in = jnp.concatenate([pair(), pair()], axis=1)
    start = pl.multiple_of(scalars[1] * part, part)
    total = gain_ref[:, pl.ds(start, part)] * (sum_in + lift_in)
    grad_in[...] = total.T
    grad_out[...] = jnp.where(is_last, sum_out, lift_out).T


def gather_shards(own):
    peers = lax.axis_size("dp")
    order = sorted(range(4, peers, 4), key=lambda m: (m.bit_count(), m))
    held = {0: own}
    for m in order:
        if m.bit_count() == 1:
            held[m] = swap(own, m)
    held[2] = swap(own, 2)
    for k, m in enumerate(order):
        low = m & -m
        before = held[(order[k - 1] if k else 0) ^ 2]
        if m != low:
            held[m] = swap(after(held[m ^ low], held[order[k - 2] ^ 2]), low)
        held[m ^ 2] = swap(after(held[m], before), 2)
    return [0] + order, held


def sum_small(keep, give, far):
    peers = lax.axis_size("dp")
    keep = keep + swap(give, 1)
    bit = 4
    while bit < peers // 2:
        keep = keep + swap(keep, bit)
        bit *= 2
    keep = keep + swap(keep.astype(BF16), 2).astype(F32)
    keep = after(keep, far)
    return keep + swap(keep, peers // 2)


def sum_thin(value, waits):
    peers = lax.axis_size("dp")
    bit, step = 1, 0
    while bit < peers:
        if step:
            value = after(value + got, waits[min(step, len(waits)) - 1])
        got = swap(value, bit)
        bit, step = bit * 2, step + 1
    return value, got


def block_marks():
    near = list(range(0, lax.axis_size("dp"), 4))
    return near + [m ^ 2 for m in near]


def scatter_sum(give, keep):
    half = give.shape[0] // 2
    got = swap(give, 1)
    summed = (keep[half:].astype(F32) + got[half:].astype(F32)).astype(BF16)
    got_x = swap(summed, 2)
    total = keep[:half].astype(F32) + got[:half].astype(F32) + got_x.astype(F32)
    bit = 4
    while True:
        left = total.reshape((total.shape[0] // 2, 2) + total.shape[1:])
        arrived = swap(left[:, 1].astype(BF16), bit)
        if left.shape[0] == 1:
            return (left[0, 0], arrived[0]), got, got_x
        total = left[:, 0] + arrived.astype(F32)
        bit *= 2


def on_device(base, cotangent, gain, weight_in, weight_out, subspace):
    sections = lax.axis_size("section")
    here = lax.axis_index("section")
    spot = lax.axis_index("dp")
    core = spot % 2
    rows, width = base.shape
    part, size = subspace.shape
    rank = weight_in.shape[2]
    last = sections - 1
    flag = (here == last).astype(jnp.int32)
    own_in, own_out = weight_in[0], weight_out[0]
    own = call(own_kernel, [flag], [own_in, own_out, subspace], [((part * 5 // 2, rank), BF16)], 0)[0]
    near, shards = gather_shards(own)

    late_in, late_out, late_space, _ = lax.optimization_barrier(
        (own_in, own_out, subspace, shards[4])
    )
    tall = (3 * rank, size)
    keep, give, _ = call(
        small_kernel,
        [flag, core, spot],
        [late_in, late_out, late_space, gain],
        [((tall[0] // 2, size), F32)] * 2 + [(tall, F32)],
        2 * part * tall[0] * size,
    )
    small = sum_small(keep, give, shards[near[-1]])
    small_other = swap(small, 1)
    keeps = [small, *from_sections(small)]
    others = [small_other, *from_sections(small_other)]

    acc_b = jnp.zeros((rows, 4 * rank), F32)
    acc_c = jnp.zeros((rows, 2 * rank), F32)
    ids = lambda marks: [spot ^ m for m in marks]
    early = near[:-1]
    steps = [(near, [shards[m] for m in near]), ([m ^ 2 for m in early], [shards[m ^ 2] for m in early])]
    for marks, some in steps:
        acc_b, acc_c, stacked = project(
            ids(marks), flag, some, (base, gain, acc_b), (cotangent, acc_c), stack=True
        )
        acc_b, acc_c = project(
            ids([m ^ 1 for m in marks]),
            flag,
            [swap(stacked, 1)],
            (base, gain, acc_b),
            (cotangent, acc_c),
        )
    end = near[-1] ^ 2
    pair = [shards[end], swap(shards[end], 1)]
    acc_b, send_b = project(ids([end, end ^ 1]), flag, pair, base=(base, gain, acc_b), final=True)
    acc_c, send_c = project(ids([end, end ^ 1]), flag, pair, cot=(cotangent, acc_c), final=True)
    sent_b, sent_c = from_sections(send_b), from_sections(send_c)
    sent_b = [after(v, send_c) for v in sent_b]

    every = block_marks()
    half = part // 2
    if sections == 2:
        columns, block_ids = half, lambda who: [(who ^ m) * 2 + flag for m in every]
    else:
        columns, block_ids = part, lambda who: [who ^ m for m in every]
    blocks = lambda n: ((len(every), rank, n), BF16)
    chain_flops = 2 * rows * size * rank * 20 * sections
    block_flops = 2 * rows * width * rank
    chain_bytes = VMEM_BYTES if sections == 2 else 4 * VMEM_BYTES
    give_out, keep_out = call(
        functools.partial(forward_kernel, sections, width),
        [here, core, *block_ids(spot ^ 1), *block_ids(spot)],
        [acc_b, *sent_b, *keeps, *others, cotangent],
        [blocks(columns)] * 2,
        chain_flops + block_flops,
        chain_bytes,
    )
    sum_out, got_out, got_out_x = scatter_sum(give_out, keep_out)
    sum_out = sum_out[0] + sum_out[1].astype(F32)
    ends_out = [sum_out]
    if sections == 2:
        ends_out = [swap(sum_out, 1, "section"), sum_out]

    sent_c = [after(v, got_out) for v in sent_c]
    halves = [
        (who ^ m) * 2 + k for k in range(2) for who in (spot ^ 1, spot) for m in every
    ]
    thin_count = 1 if sections == 2 else 2
    codes, *rest = call(
        functools.partial(backward_kernel, sections, width),
        [here, core, *halves],
        [acc_b, acc_c, *sent_b, *sent_c, *keeps, *others, base],
        [((rows, size), BF16)] + [((rank, size), F32)] * thin_count + [blocks(half)] * 4,
        2 * chain_flops + block_flops,
        chain_bytes,
    )
    thins, halves = rest[:thin_count], rest[thin_count:]
    lower, got_lower, got_lower_x = scatter_sum(*halves[:2])
    upper, got_upper, got_upper_x = scatter_sum(*halves[2:])
    waits = [got_lower, got_out_x, got_lower_x]
    terms = [term for thin in thins for term in sum_thin(thin, waits)]
    grad_in, grad_out = call(
        functools.partial(end_kernel, sections),
        [flag, spot],
        [subspace, gain, *terms, *ends_out, *lower, *upper],
        [((part, rank), F32)] * 2,
        4 * part * size * rank,
    )
    return codes[None], grad_in[None], grad_out[None]


def solution(mesh):
    placed = (
        P("dp", None),
        P("dp", None),
        P("section", None),
        P("section", "dp", None),
        P("section", "dp", None),
        P("dp", None),
    )
    return jax.shard_map(
        on_device,
        mesh=mesh,
        in_specs=placed,
        out_specs=(P("section", "dp", None), P("section", "dp", None), P("section", "dp", None)),
        check_vma=False,
    )
```

time: 219 us -> 180 us (0.82)
  waiting for transfers between devices: 150 us -> 76 us
  local copies, waits for them, and re-layouts: 8.9 us -> 34.5 us
  Pallas kernels: 0 us -> 24.9 us
  starting transfers between devices: 13.1 us -> 36.7 us
  matrix products: 19.1 us -> 0 us
  between operations: 18.3 us -> 0.97 us
  other arithmetic: 9.2 us -> 5.63 us
    all_gather x1 -> x0, waiting for transfers between devices: 44.4 us -> none  [on_device(): wide = lax.all_gather(mine, 'dp', axis=0, tiled=True)]
    reduce_scatter x1 -> x0, waiting for transfers between devices: 39.8 us -> none  [on_device(): lax.psum_scatter(jnp.concatenate([grad_in, grad_out], axis=1), 'dp', scat...]
    unnamed x21 -> x60, local copies, waits for them, and re-layouts: 7.05 us -> 33.9 us
    pallas_call x0 -> x11, Pallas kernels: none -> 24.9 us  [call(): pl.pallas_call(kernel, in_specs=[IN_SMEM] + [IN_VMEM] * len(arrays), out_...]
    ppermute x10 -> x36, starting transfers between devices: 13 us -> 36.7 us  [swap(): return lax.ppermute(value, axis, [(i, i ^ bits) for i in range(peers)])]
    dot_general x14 -> x0, matrix products: 19.1 us -> none  [the longest x8 17.1 us: mm(): return lax.dot_general(a, b, (dims, ((), ())), preferred_element_type=F32)]
    ppermute x10 -> x36, waiting for transfers between devices: 65.4 us -> 76 us  [swap(): return lax.ppermute(value, axis, [(i, i ^ bits) for i in range(peers)])]
    reduce_sum x1 -> x0, other arithmetic: 4.1 us -> none  [on_device(): squares = jnp.sum(base_f * base_f, axis=-1, keepdims=True)]
  transfers between devices with their start and end apart: 12 -> 36, of which waited for: 10 -> 21; matrix products, arithmetic and copies ran while one was open for 10% -> 3% of each run, Pallas kernels for 0% -> 10%
where the time goes in v5:
time: 180 us; the launch traced here: 179 us
  waiting for transfers between devices  76 us (42%)
  starting transfers between devices  36.7 us (20%)
  local copies, waits for them, and re-layouts  34.5 us (19%)
  Pallas kernels  24.9 us (14%)
  other arithmetic  5.63 us (3%)
    ppermute x36, waiting for transfers between devices, swap(): return lax.ppermute(value, axis, [(i, i ^ bits) for i in range(peers)])  76 us
    ppermute x36, starting transfers between devices, swap(): return lax.ppermute(value, axis, [(i, i ^ bits) for i in range(peers)])  36.7 us
    unnamed x60, local copies, waits for them, and re-layouts  33.9 us
    pallas_call x11, Pallas kernels, call(): pl.pallas_call(kernel, in_specs=[IN_SMEM] + [IN_VMEM] * len(arrays), out_...  24.9 us
  transfers between devices with their start and end apart: 36, of which 21 were waited for; matrix products, arithmetic and copies ran while one was open for 3% of the time, Pallas kernels for 10%

profile of v5, /device:TPU:0, one launch (start us, length us, event | category | flops | bytes accessed | tf_op | source)
XLA Modules:
  0.0 178.7 jit_solution(380808369655381686)
XLA Ops:
  3.5 3.1 %collective-permute-start.1 = (bf16[1280,128]{1,0:T(8,128)(2,1)S(1)}, bf16[1280,128]{1,0:T(8,128)(2,1)S(1)}, u32[]{:S(2)}, u32[]{:S(2)}) collective-permute-start(bf16[1280,128]{1,0:T(8,128)(2,1)S(1)} %shard_map.85.refs_3_), channel_id=1, source_target_pairs={{0,4},{1,5},{2,6},{3,7},{4,0},{5,1},{6,2},{7,3},{8,12},{9,13},{10,... | collective-permute-start | bytes 983048 | tf_op jit(solution)/shard_map/ppermute | solution.py:56
  10.6 9.3 %collective-permute-done.1.refs_4_ = bf16[1280,128]{1,0:T(8,128)(2,1)S(1)} collective-permute-done((bf16[1280,128]{1,0:T(8,128)(2,1)S(1)}, bf16[1280,128]{1,0:T(8,128)(2,1)S(1)}, u32[]{:S(2)}, u32[]{:S(2)}) %collective-permute-start.1) | collective-permute-done | bytes 327712 | tf_op jit(solution)/shard_map/ppermute | solution.py:56
  24.9 5.2 %collective-permute-done.3.refs_4_ = bf16[1280,128]{1,0:T(8,128)(2,1)S(1)} collective-permute-done((bf16[1280,128]{1,0:T(8,128)(2,1)S(1)}, bf16[1280,128]{1,0:T(8,128)(2,1)S(1)}, u32[]{:S(2)}, u32[]{:S(2)}) %collective-permute-start.3) | collective-permute-done | bytes 327712 | tf_op jit(solution)/shard_map/ppermute | solution.py:56
  31.0 7.8 %collective-permute-done.4.refs_6_ = bf16[1280,128]{1,0:T(8,128)(2,1)S(1)} collective-permute-done((bf16[1280,128]{1,0:T(8,128)(2,1)S(1)}, bf16[1280,128]{1,0:T(8,128)(2,1)S(1)}, u32[]{:S(2)}, u32[]{:S(2)}) %collective-permute-start.4) | collective-permute-done | bytes 327712 | tf_op jit(solution)/shard_map/ppermute | solution.py:56
  41.7 2.8 %copy-done.4 = bf16[384,8192]{1,0:T(8,128)(2,1)S(1)} copy-done((bf16[384,8192]{1,0:T(8,128)(2,1)S(1)}, bf16[384,8192]{1,0:T(8,128)(2,1)}, u32[]{:S(2)}) %copy-start.4) | copy-done | bytes 6291480
  45.3 3.5 %shard_map.86 = (f32[384,512]{1,0:T(8,128)S(1)}, f32[384,256]{1,0:T(8,128)S(1)}, bf16[4,1280,128]{2,1,0:T(8,128)(2,1)}) custom-call(s32[5]{0:T(128)S(1)} %stack.300.scalars, bf16[384,8192]{1,0:T(8,128)(2,1)S(1)} %copy-done.4, f32[1,8192]{1,0:T(1,128)S(1)} %copy-done.10, bf16[384,8192]{1,0:T(8,128)(2,1)S(1)} %copy-done, ...), custom_call_target="tpu_custom_call" | custom-call | flops 1006632960 | bytes 17596416 | tf_op jit(solution)/shard_map/pallas_call | solution.py:44
  55.7 2.8 %copy-done.1 = bf16[384,8192]{1,0:T(8,128)(2,1)S(1)} copy-done((bf16[384,8192]{1,0:T(8,128)(2,1)S(1)}, bf16[384,8192]{1,0:T(8,128)(2,1)}, u32[]{:S(2)}) %copy-start.1) | copy-done | bytes 6291480
  58.5 2.8 %copy-done.5 = bf16[384,8192]{1,0:T(8,128)(2,1)S(1)} copy-done((bf16[384,8192]{1,0:T(8,128)(2,1)S(1)}, bf16[384,8192]{1,0:T(8,128)(2,1)}, u32[]{:S(2)}) %copy-start.5) | copy-done | bytes 6291480
  63.7 3.4 %shard_map.88 = (f32[384,512]{1,0:T(8,128)S(1)}, f32[384,256]{1,0:T(8,128)S(1)}, bf16[3,1280,128]{2,1,0:T(8,128)(2,1)}) custom-call(s32[4]{0:T(128)S(1)} %add_add_fusion.1.scalars, bf16[384,8192]{1,0:T(8,128)(2,1)S(1)} %copy-done.5, f32[1,8192]{1,0:T(1,128)S(1)} %copy-done.11, bf16[384,8192]{1,0:T(8,128)(2,1)S(1)} %copy-done.1, ...), custom_call_target="tpu_custom_call" | custom-call | flops 754974720 | bytes 16941056 | tf_op jit(solution)/shard_map/pallas_call | solution.py:44
  69.2 3.6 %collective-permute-done.14 = bf16[192,256]{1,0:T(8,128)(2,1)S(1)} collective-permute-done((bf16[192,256]{1,0:T(8,128)(2,1)S(1)}, bf16[192,256]{1,0:T(8,128)(2,1)S(1)}, u32[]{:S(2)}, u32[]{:S(2)}) %collective-permute-start.14) | collective-permute-done | bytes 98336 | tf_op jit(solution)/shard_map/ppermute | solution.py:56
  76.2 3.2 %collective-permute-done.6.refs_2_.refs_1_ = bf16[1280,128]{1,0:T(8,128)(2,1)S(1)} collective-permute-done((bf16[1280,128]{1,0:T(8,128)(2,1)S(1)}, bf16[1280,128]{1,0:T(8,128)(2,1)S(1)}, u32[]{:S(2)}, u32[]{:S(2)}) %collective-permute-start.6) | collective-permute-done | bytes 327712 | tf_op jit(solution)/shard_map/ppermute | solution.py:56
  79.5 5.7 %collective-permute-done.15 = f32[192,256]{1,0:T(8,128)} collective-permute-done((f32[192,256]{1,0:T(8,128)}, f32[192,256]{1,0:T(8,128)}, u32[]{:S(2)}, u32[]{:S(2)}) %collective-permute-start.15) | collective-permute-done | bytes 196640 | tf_op jit(solution)/shard_map/ppermute | solution.py:56
  86.4 2.8 %copy-done.2 = bf16[384,8192]{1,0:T(8,128)(2,1)S(1)} copy-done((bf16[384,8192]{1,0:T(8,128)(2,1)S(1)}, bf16[384,8192]{1,0:T(8,128)(2,1)}, u32[]{:S(2)}) %copy-start.2) | copy-done | bytes 6291480
  89.2 2.8 %copy-done.6 = bf16[384,8192]{1,0:T(8,128)(2,1)S(1)} copy-done((bf16[384,8192]{1,0:T(8,128)(2,1)S(1)}, bf16[384,8192]{1,0:T(8,128)(2,1)}, u32[]{:S(2)}) %copy-start.6) | copy-done | bytes 6291480
  100.7 2.8 %copy-done.3 = bf16[384,8192]{1,0:T(8,128)(2,1)S(1)} copy-done((bf16[384,8192]{1,0:T(8,128)(2,1)S(1)}, bf16[384,8192]{1,0:T(8,128)(2,1)}, u32[]{:S(2)}) %copy-start.3) | copy-done | bytes 6291480
  107.0 4.2 %collective-permute-done.16.refs_2_.refs_3_ = f32[192,256]{1,0:T(8,128)S(1)} collective-permute-done((f32[192,256]{1,0:T(8,128)S(1)}, f32[192,256]{1,0:T(8,128)S(1)}, u32[]{:S(2)}, u32[]{:S(2)}) %collective-permute-start.16) | collective-permute-done | bytes 196640 | tf_op jit(solution)/shard_map/ppermute | solution.py:56
  111.8 3.1 %collective-permute-done.18.refs_4_.refs_5_ = f32[192,256]{1,0:T(8,128)S(1)} collective-permute-done((f32[192,256]{1,0:T(8,128)S(1)}, f32[192,256]{1,0:T(8,128)S(1)}, u32[]{:S(2)}, u32[]{:S(2)}) %collective-permute-start.18) | collective-permute-done | bytes 196640 | tf_op jit(solution)/shard_map/ppermute | solution.py:56
  121.5 5.8 %collective-permute-done.11.refs_1_ = bf16[384,256]{1,0:T(8,128)(2,1)} collective-permute-done((bf16[384,256]{1,0:T(8,128)(2,1)}, bf16[384,256]{1,0:T(8,128)(2,1)}, u32[]{:S(2)}, u32[]{:S(2)}) %collective-permute-start.11) | collective-permute-done | bytes 196640 | tf_op jit(solution)/shard_map/ppermute | solution.py:56
  129.0 2.8 %copy-done.7 = bf16[384,8192]{1,0:T(8,128)(2,1)S(1)} copy-done((bf16[384,8192]{1,0:T(8,128)(2,1)S(1)}, bf16[384,8192]{1,0:T(8,128)(2,1)}, u32[]{:S(2)}) %copy-start.7) | copy-done | bytes 6291480
  132.8 4.2 %shard_map.94 = (bf16[384,256]{1,0:T(8,128)(2,1)}, f32[128,256]{1,0:T(8,128)S(1)}, bf16[8,128,256]{2,1,0:T(8,128)(2,1)S(1)}, bf16[8,128,256]{2,1,0:T(8,128)(2,1)...) custom-call(s32[34]{0:T(128)S(1)} %stack.278.scalars, f32[384,512]{1,0:T(8,128)S(1)} %get-tuple-element.53.own_b, ...), custom_call_target="tpu_custom_call" | custom-call | flops 2818572288 | bytes 11173888 | tf_op jit(solution)/shard_map/pallas_call | solution.py:44
  138.8 5.2 %collective-permute-done.27 = bf16[2,128,256]{2,1,0:T(8,128)(2,1)S(1)} collective-permute-done((bf16[2,128,256]{2,1,0:T(8,128)(2,1)S(1)}, bf16[2,128,256]{2,1,0:T(8,128)(2,1)S(1)}, u32[]{:S(2)}, u32[]{:S(2)}) %collective-permute-start.27) | collective-permute-done | bytes 131104 | tf_op jit(solution)/shard_map/ppermute | solution.py:56
  146.9 3.2 %collective-permute-done.28 = bf16[1,128,256]{2,1,0:T(8,128)(2,1)S(1)} collective-permute-done((bf16[1,128,256]{2,1,0:T(8,128)(2,1)S(1)}, bf16[1,128,256]{2,1,0:T(8,128)(2,1)S(1)}, u32[]{:S(2)}, u32[]{:S(2)}) %collective-permute-start.28) | collective-permute-done | bytes 65568 | tf_op jit(solution)/shard_map/ppermute | solution.py:56
  153.9 4.3 %collective-permute-done.22 = f32[128,256]{1,0:T(8,128)S(1)} collective-permute-done((f32[128,256]{1,0:T(8,128)S(1)}, f32[128,256]{1,0:T(8,128)S(1)}, u32[]{:S(2)}, u32[]{:S(2)}) %collective-permute-start.22) | collective-permute-done | bytes 131104 | tf_op jit(solution)/shard_map/ppermute | solution.py:56
  170.9 3.6 %collective-permute-done.26.refs_1_ = f32[128,256]{1,0:T(8,128)S(1)} collective-permute-done((f32[128,256]{1,0:T(8,128)S(1)}, f32[128,256]{1,0:T(8,128)S(1)}, u32[]{:S(2)}, u32[]{:S(2)}) %collective-permute-start.26) | collective-permute-done | bytes 131104 | tf_op jit(solution)/shard_map/ppermute | solution.py:56
  (155 shorter events, 79.8 us)
Async XLA Ops:
  3.5 16.5 %collective-permute-start.1 = (bf16[1280,128]{1,0:T(8,128)(2,1)S(1)}, bf16[1280,128]{1,0:T(8,128)(2,1)S(1)}, u32[]{:S(2)}, u32[]{:S(2)}) collective-permute-start(bf16[1280,128]{1,0:T(8,128)(2,1)S(1)} %shard_map.85.refs_3_), channel_id=1, source_target_pairs={{0,4},{1,5},{2,6},{3,7},{4,0},{5,1},{6,2},{7,3},{8,12},{9,13},{10,... | collective-permute-start | bytes 983048 | tf_op jit(solution)/shard_map/ppermute | solution.py:56
  6.6 13.4 %collective-permute-start.2 = (bf16[1280,128]{1,0:T(8,128)(2,1)S(1)}, bf16[1280,128]{1,0:T(8,128)(2,1)S(1)}, u32[]{:S(2)}, u32[]{:S(2)}) collective-permute-start(bf16[1280,128]{1,0:T(8,128)(2,1)S(1)} %shard_map.85.refs_3_), channel_id=1, source_target_pairs={{0,2},{1,3},{2,0},{3,1},{4,6},{5,7},{6,4},{7,5},{8,10},{9,11},{10,... | collective-permute-start | bytes 983048 | tf_op jit(solution)/shard_map/ppermute | solution.py:56
  8.0 16.9 %collective-permute-start = (bf16[1280,128]{1,0:T(8,128)(2,1)S(1)}, bf16[1280,128]{1,0:T(8,128)(2,1)S(1)}, u32[]{:S(2)}, u32[]{:S(2)}) collective-permute-start(bf16[1280,128]{1,0:T(8,128)(2,1)S(1)} %shard_map.85.refs_3_), channel_id=1, source_target_pairs={{0,8},{1,9},{2,10},{3,11},{4,12},{5,13},{6,14},{7,15},{8,0},{9,1},... | collective-permute-start | bytes 983048 | tf_op jit(solution)/shard_map/ppermute | solution.py:56
  20.7 9.4 %collective-permute-start.3 = (bf16[1280,128]{1,0:T(8,128)(2,1)S(1)}, bf16[1280,128]{1,0:T(8,128)(2,1)S(1)}, u32[]{:S(2)}, u32[]{:S(2)}) collective-permute-start(bf16[1280,128]{1,0:T(8,128)(2,1)S(1)} %collective-permute-done.1.refs_4_), channel_id=1, source_target_pairs={{0,2},{1,3},{2,0},{3,1},{4,6},{5,7},{6,4},{7,5},{8,10},{9,11},{10,... | collective-permute-start | bytes 983048 | tf_op jit(solution)/shard_map/ppermute | solution.py:56
  30.9 7.9 %collective-permute-start.4 = (bf16[1280,128]{1,0:T(8,128)(2,1)S(1)}, bf16[1280,128]{1,0:T(8,128)(2,1)S(1)}, u32[]{:S(2)}, u32[]{:S(2)}) collective-permute-start(bf16[1280,128]{1,0:T(8,128)(2,1)S(1)} %collective-permute-done.refs_5_), channel_id=1, source_target_pairs={{0,4},{1,5},{2,6},{3,7},{4,0},{5,1},{6,2},{7,3},{8,12},{9,13},{10,... | collective-permute-start | bytes 983048 | tf_op jit(solution)/shard_map/ppermute | solution.py:56
  48.8 14.9 %collective-permute-start.5 = (bf16[1280,128]{1,0:T(8,128)(2,1)}, bf16[1280,128]{1,0:T(8,128)(2,1)}, u32[]{:S(2)}, u32[]{:S(2)}) collective-permute-start(bf16[1280,128]{1,0:T(8,128)(2,1)} %copy-done.20), channel_id=1, source_target_pairs={{0,2},{1,3},{2,0},{3,1},{4,6},{5,7},{6,4},{7,5},{8,10},{9,11},{10,... | collective-permute-start | bytes 983048 | tf_op jit(solution)/shard_map/ppermute | solution.py:56
  55.3 11.8 %collective-permute-start.13 = (f32[192,256]{1,0:T(8,128)S(1)}, f32[192,256]{1,0:T(8,128)S(1)}, u32[]{:S(2)}, u32[]{:S(2)}) collective-permute-start(f32[192,256]{1,0:T(8,128)S(1)} %add.193), channel_id=1, source_target_pairs={{0,4},{1,5},{2,6},{3,7},{4,0},{5,1},{6,2},{7,3},{8,12},{9,13},{10,... | collective-permute-start | bytes 589832 | tf_op jit(solution)/shard_map/ppermute | solution.py:56
  67.1 19.3 %collective-permute-start.9 = (bf16[3,1280,128]{2,1,0:T(8,128)(2,1)}, bf16[3,1280,128]{2,1,0:T(8,128)(2,1)S(1)}, u32[]{:S(2)}, u32[]{:S(2)}) collective-permute-start(bf16[3,1280,128]{2,1,0:T(8,128)(2,1)} %get-tuple-element.49), channel_id=1, source_target_pairs={{0,1},{1,0},{2,3},{3,2},{4,5},{5,4},{6,7},{7,6},{8,9},{9,8},{10,11... | collective-permute-start | bytes 2949128 | tf_op jit(solution)/shard_map/ppermute | solution.py:56
  67.8 11.6 %collective-permute-start.6 = (bf16[1280,128]{1,0:T(8,128)(2,1)S(1)}, bf16[1280,128]{1,0:T(8,128)(2,1)S(1)}, u32[]{:S(2)}, u32[]{:S(2)}) collective-permute-start(bf16[1280,128]{1,0:T(8,128)(2,1)S(1)} %collective-permute-done.4.refs_6_), channel_id=1, source_target_pairs={{0,2},{1,3},{2,0},{3,1},{4,6},{5,7},{6,4},{7,5},{8,10},{9,11},{10,... | collective-permute-start | bytes 983048 | tf_op jit(solution)/shard_map/ppermute | solution.py:56
  73.5 11.7 %collective-permute-start.15 = (f32[192,256]{1,0:T(8,128)}, f32[192,256]{1,0:T(8,128)}, u32[]{:S(2)}, u32[]{:S(2)}) collective-permute-start(f32[192,256]{1,0:T(8,128)} %convert_add_fusion.3), channel_id=1, source_target_pairs={{0,8},{1,9},{2,10},{3,11},{4,12},{5,13},{6,14},{7,15},{8,0},{9,1},... | collective-permute-start | bytes 589832 | tf_op jit(solution)/shard_map/ppermute | solution.py:56
  79.4 15.5 %collective-permute-start.7 = (bf16[1280,128]{1,0:T(8,128)(2,1)S(1)}, bf16[1280,128]{1,0:T(8,128)(2,1)S(1)}, u32[]{:S(2)}, u32[]{:S(2)}) collective-permute-start(bf16[1280,128]{1,0:T(8,128)(2,1)S(1)} %collective-permute-done.6.refs_2_.refs_1_), channel_id=1, source_target_pairs={{0,1},{1,0},{2,3},{3,2},{4,5},{5,4},{6,7},{7,6},{8,9},{9,8},{10,11... | collective-permute-start | bytes 983048 | tf_op jit(solution)/shard_map/ppermute | solution.py:56
  86.2 12.7 %collective-permute-start.17 = (f32[192,256]{1,0:T(8,128)S(1)}, f32[192,256]{1,0:T(8,128)S(1)}, u32[]{:S(2)}, u32[]{:S(2)}) collective-permute-start(f32[192,256]{1,0:T(8,128)S(1)} %add.196.refs_1_.refs_2_), channel_id=1, source_target_pairs={{0,1},{1,0},{2,3},{3,2},{4,5},{5,4},{6,7},{7,6},{8,9},{9,8},{10,11... | collective-permute-start | bytes 589832 | tf_op jit(solution)/shard_map/ppermute | solution.py:56
  96.9 10.0 %collective-permute-start.10 = (bf16[384,384]{1,0:T(8,128)(2,1)}, bf16[384,384]{1,0:T(8,128)(2,1)S(1)}, u32[]{:S(2)}, u32[]{:S(2)}) collective-permute-start(bf16[384,384]{1,0:T(8,128)(2,1)} %get-tuple-element.56), channel_id=1, source_target_pairs={{0,16},{16,0},{1,17},{17,1},{2,18},{18,2},{3,19},{19,3},{4,20},{20... | collective-permute-start | bytes 884744 | tf_op jit(solution)/shard_map/ppermute | solution.py:56
  98.5 12.6 %collective-permute-start.16 = (f32[192,256]{1,0:T(8,128)S(1)}, f32[192,256]{1,0:T(8,128)S(1)}, u32[]{:S(2)}, u32[]{:S(2)}) collective-permute-start(f32[192,256]{1,0:T(8,128)S(1)} %add.196.refs_1_.refs_2_), channel_id=1, source_target_pairs={{0,16},{16,0},{1,17},{17,1},{2,18},{18,2},{3,19},{19,3},{4,20},{20... | collective-permute-start | bytes 589832 | tf_op jit(solution)/shard_map/ppermute | solution.py:56
  99.0 16.0 %collective-permute-start.18 = (f32[192,256]{1,0:T(8,128)S(1)}, f32[192,256]{1,0:T(8,128)S(1)}, u32[]{:S(2)}, u32[]{:S(2)}) collective-permute-start(f32[192,256]{1,0:T(8,128)S(1)} %collective-permute-done.17.refs_3_.refs_4_), channel_id=1, source_target_pairs={{0,16},{16,0},{1,17},{17,1},{2,18},{18,2},{3,19},{19,3},{4,20},{20... | collective-permute-start | bytes 589832 | tf_op jit(solution)/shard_map/ppermute | solution.py:56
  119.7 7.7 %collective-permute-start.19 = (bf16[8,128,256]{2,1,0:T(8,128)(2,1)S(1)}, bf16[8,128,256]{2,1,0:T(8,128)(2,1)}, u32[]{:S(2)}, u32[]{:S(2)}) collective-permute-start(bf16[8,128,256]{2,1,0:T(8,128)(2,1)S(1)} %get-tuple-element.65), channel_id=1, source_target_pairs={{0,1},{1,0},{2,3},{3,2},{4,5},{5,4},{6,7},{7,6},{8,9},{9,8},{10,11... | collective-permute-start | bytes 1572872 | tf_op jit(solution)/shard_map/ppermute | solution.py:56
  128.4 8.6 %collective-permute-start.23 = (bf16[4,128,256]{2,1,0:T(8,128)(2,1)S(1)}, bf16[4,128,256]{2,1,0:T(8,128)(2,1)S(1)}, u32[]{:S(2)}, u32[]{:S(2)}) collective-permute-start(bf16[4,128,256]{2,1,0:T(8,128)(2,1)S(1)} %add_convert_fusion.2), channel_id=1, source_target_pairs={{0,2},{1,3},{2,0},{3,1},{4,6},{5,7},{6,4},{7,5},{8,10},{9,11},{10,... | collective-permute-start | bytes 786440 | tf_op jit(solution)/shard_map/ppermute | solution.py:56
  138.8 13.0 %collective-permute-start.21 = (bf16[8,128,256]{2,1,0:T(8,128)(2,1)S(1)}, bf16[8,128,256]{2,1,0:T(8,128)(2,1)S(1)}, u32[]{:S(2)}, u32[]{:S(2)}) collective-permute-start(bf16[8,128,256]{2,1,0:T(8,128)(2,1)S(1)} %get-tuple-element.69), channel_id=1, source_target_pairs={{0,1},{1,0},{2,3},{3,2},{4,5},{5,4},{6,7},{7,6},{8,9},{9,8},{10,11... | collective-permute-start | bytes 1572872 | tf_op jit(solution)/shard_map/ppermute | solution.py:56
  145.4 13.9 %collective-permute-start.33 = (bf16[4,128,256]{2,1,0:T(8,128)(2,1)S(1)}, bf16[4,128,256]{2,1,0:T(8,128)(2,1)S(1)}, u32[]{:S(2)}, u32[]{:S(2)}) collective-permute-start(bf16[4,128,256]{2,1,0:T(8,128)(2,1)S(1)} %add_convert_fusion), channel_id=1, source_target_pairs={{0,2},{1,3},{2,0},{3,1},{4,6},{5,7},{6,4},{7,5},{8,10},{9,11},{10,... | collective-permute-start | bytes 786440 | tf_op jit(solution)/shard_map/ppermute | solution.py:56
  150.1 20.8 %collective-permute-start.29 = (f32[128,256]{1,0:T(8,128)S(1)}, f32[128,256]{1,0:T(8,128)S(1)}, u32[]{:S(2)}, u32[]{:S(2)}) collective-permute-start(f32[128,256]{1,0:T(8,128)S(1)} %fusion.9.refs_3_), channel_id=1, source_target_pairs={{0,16},{16,0},{1,17},{17,1},{2,18},{18,2},{3,19},{19,3},{4,20},{20... | collective-permute-start | bytes 393224 | tf_op jit(solution)/shard_map/ppermute | solution.py:56
  153.3 8.9 %collective-permute-start.25 = (bf16[4,128,256]{2,1,0:T(8,128)(2,1)S(1)}, bf16[4,128,256]{2,1,0:T(8,128)(2,1)S(1)}, u32[]{:S(2)}, u32[]{:S(2)}) collective-permute-start(bf16[4,128,256]{2,1,0:T(8,128)(2,1)S(1)} %add_convert_fusion.1), channel_id=1, source_target_pairs={{0,2},{1,3},{2,0},{3,1},{4,6},{5,7},{6,4},{7,5},{8,10},{9,11},{10,... | collective-permute-start | bytes 786440 | tf_op jit(solution)/shard_map/ppermute | solution.py:56
  162.4 8.0 %collective-permute-start.30 = (bf16[2,128,256]{2,1,0:T(8,128)(2,1)S(1)}, bf16[2,128,256]{2,1,0:T(8,128)(2,1)S(1)}, u32[]{:S(2)}, u32[]{:S(2)}) collective-permute-start(bf16[2,128,256]{2,1,0:T(8,128)(2,1)S(1)} %fusion.7), channel_id=1, source_target_pairs={{0,4},{1,5},{2,6},{3,7},{4,0},{5,1},{6,2},{7,3},{8,12},{9,13},{10,... | collective-permute-start | bytes 393224 | tf_op jit(solution)/shard_map/ppermute | solution.py:56
  163.5 11.1 %collective-permute-start.26 = (f32[128,256]{1,0:T(8,128)S(1)}, f32[128,256]{1,0:T(8,128)S(1)}, u32[]{:S(2)}, u32[]{:S(2)}) collective-permute-start(f32[128,256]{1,0:T(8,128)S(1)} %add.200.refs_0_), channel_id=1, source_target_pairs={{0,8},{1,9},{2,10},{3,11},{4,12},{5,13},{6,14},{7,15},{8,0},{9,1},... | collective-permute-start | bytes 393224 | tf_op jit(solution)/shard_map/ppermute | solution.py:56
  167.1 9.1 %collective-permute-start.35 = (bf16[1,128,256]{2,1,0:T(8,128)(2,1)S(1)}, bf16[1,128,256]{2,1,0:T(8,128)(2,1)S(1)}, u32[]{:S(2)}, u32[]{:S(2)}) collective-permute-start(bf16[1,128,256]{2,1,0:T(8,128)(2,1)S(1)} %fusion.12), channel_id=1, source_target_pairs={{0,8},{1,9},{2,10},{3,11},{4,12},{5,13},{6,14},{7,15},{8,0},{9,1},... | collective-permute-start | bytes 196616 | tf_op jit(solution)/shard_map/ppermute | solution.py:56
  (42 other events, 163.8 us)

commit v6 on v5

v6 whole, which is shorter than its diff:
```python
import functools

import jax
import jax.numpy as jnp
from jax import lax
from jax.experimental import pallas as pl
from jax.experimental.pallas import tpu as pltpu
from jax.sharding import PartitionSpec as P

F32 = jnp.float32
BF16 = jnp.bfloat16
VMEM_BYTES = 50 * 1024 * 1024
IN_VMEM = pl.BlockSpec(memory_space=pltpu.VMEM)
IN_SMEM = pl.BlockSpec(memory_space=pltpu.SMEM)
IN_HBM = pl.BlockSpec(memory_space=pltpu.HBM)
CONTRACT = ((1,), (0,))
ROWS = ((0,), (0,))
COLUMNS = ((1,), (1,))


def mm(a, b, dims=CONTRACT):
    return lax.dot_general(a, b, (dims, ((), ())), preferred_element_type=F32)


def parts_of(a):
    if a.dtype == BF16:
        return [a]
    high = a.astype(BF16)
    return [high, (a - high.astype(F32)).astype(BF16)]


def exact(a, b, dims=CONTRACT):
    left, right = parts_of(a), parts_of(b)
    total = mm(left[0], right[0], dims)
    for i, x in enumerate(left):
        for j, y in enumerate(right):
            if i + j == 1:
                total = total + mm(x, y, dims)
    return total


def call(kernel, scalars, far, arrays, shapes, scratch=(), vmem_bytes=VMEM_BYTES):
    return pl.pallas_call(
        kernel,
        in_specs=[IN_SMEM] + [IN_HBM] * len(far) + [IN_VMEM] * len(arrays),
        out_specs=[IN_VMEM] * len(shapes),
        out_shape=[jax.ShapeDtypeStruct(*s) for s in shapes],
        scratch_shapes=list(scratch),
        compiler_params=pltpu.CompilerParams(vmem_limit_bytes=vmem_bytes),
        cost_estimate=pl.CostEstimate(flops=0, bytes_accessed=0, transcendentals=0),
    )(jnp.stack(scalars).astype(jnp.int32), *far, *arrays)


def fetch(pairs, sems, first=0):
    copies = [pltpu.make_async_copy(a, b, sems.at[first + i]) for i, (a, b) in enumerate(pairs)]
    for copy in copies:
        copy.start()
    return copies


def swap(value, bits, axis="dp"):
    peers = lax.axis_size(axis)
    return lax.ppermute(value, axis, [(i, i ^ bits) for i in range(peers)])


def after(value, *others):
    return lax.optimization_barrier((value, *others))[0]


def from_sections(value):
    sections = lax.axis_size("section")
    here = lax.axis_index("section")
    if sections == 2:
        return [swap(value, 1, "section")]
    around = [(i, (i + 1) % sections) for i in range(sections)]
    held = [value]
    for _ in range(sections - 1):
        held.append(lax.ppermute(held[-1], "section", around))
    stacked = jnp.stack(held)
    order = (here - jnp.arange(sections)) % sections
    return [lax.dynamic_index_in_dim(stacked, order[s], 0, keepdims=False) for s in range(sections)]


def own_kernel(scalars, in_far, out_ref, space_ref, gain_far, own_ref, in_ref, gain_ref, sems):
    part, rank = in_ref.shape
    half = part // 2
    start = pl.multiple_of(scalars[1] * part, part)
    first = fetch([(in_far, in_ref), (gain_far.at[:, pl.ds(start, part)], gain_ref)], sems)
    places = own_ref.at[part : 2 * part], own_ref.at[2 * part :]

    def copy_both(sources):
        for copy in fetch(list(zip(sources, places)), sems, 2):
            copy.wait()

    @pl.when(scalars[0] == 1)
    def _():
        copy_both((out_ref, space_ref.at[half:, rank:]))

    @pl.when(scalars[0] == 0)
    def _():
        copy_both((space_ref.at[:, :rank], space_ref.at[:half, rank:]))

    for copy in first:
        copy.wait()
    column = jnp.broadcast_to(gain_ref[...], (rank, part)).T
    own_ref[:part] = (in_ref[...].astype(F32) * column).astype(BF16)


def small_kernel(scalars, out_far, space_far, own_ref, keep_ref, give_ref, *scratch):
    out_ref, space_ref, all_ref, sems = scratch
    is_last, core = scalars[0] == 1, scalars[1]
    part, rank = out_ref.shape
    for copy in fetch([(space_far, space_ref), (out_far, out_ref)], sems):
        copy.wait()
    space = space_ref[...]
    all_ref[:rank] = mm(out_ref[...], space, ROWS)
    all_ref[rank : 2 * rank] = mm(own_ref[:part], space, ROWS)
    columns = jnp.where(is_last, space_ref[:, rank:], space_ref[:, :rank])
    all_ref[2 * rank :] = mm(columns, space, ROWS)
    half = keep_ref.shape[0]
    first, second = all_ref[:half], all_ref[half:]
    keep_ref[...] = jnp.where(core == 0, first, second)
    give_ref[...] = jnp.where(core == 0, second, first)


def project_kernel(stacked, final, count, scalars, base_far, cot_far, *refs):
    refs = list(refs)
    base_ref, cot_ref, sems = refs[-3:]
    shards, refs = [], refs[:-3]
    while len(shards) < count:
        ref = refs.pop(0)
        shards += [ref] if len(ref.shape) == 2 else [ref.at[i] for i in range(ref.shape[0])]
    acc, out = refs.pop(0), refs.pop(0)
    rank = out.shape[1] // 6
    part = base_ref.shape[2]
    half = part // 2
    starts = [pl.multiple_of(scalars[t] * part, part) for t in range(count)]
    block = lambda ref, t: ref.at[:, pl.ds(starts[t], part)]
    copies = []
    for t in range(count):
        pairs = [(block(base_far, t), base_ref.at[t]), (block(cot_far, t), cot_ref.at[t])]
        copies.append(fetch(pairs, sems, 2 * t))
    skip = pl.multiple_of(scalars[count] * half, half)
    out[...] = acc[...]
    for t, shard in enumerate(shards):
        if stacked:
            refs[0][t] = shard[...]
        copies[t][0].wait()
        tokens = base_ref[t]
        tokens_f = tokens.astype(F32)
        square = tokens_f * tokens_f
        total = square[:, :rank]
        for at in range(rank, part, rank):
            total = total + square[:, at : at + rank]
        wide = jnp.concatenate([shard[:part], shard[part : 2 * part]], axis=1)
        out[:, : 2 * rank] += mm(tokens, wide)
        out[:, 2 * rank : 3 * rank] += mm(base_ref[t, :, pl.ds(skip, half)], shard[2 * part :])
        out[:, 5 * rank :] += total
        copies[t][1].wait()
        out[:, 3 * rank : 4 * rank] += mm(cot_ref[t], shard[part : 2 * part])
        out[:, 4 * rank : 5 * rank] += mm(cot_ref[t, :, pl.ds(skip, half)], shard[2 * part :])
    if final:
        refs[0][...] = out[:, : 5 * rank].astype(BF16)


def project(ids, flag, shards, tokens, acc, stacked=False, final=False):
    base, cotangent = tokens
    tall, rank = shards[0].shape[-2:]
    rows, part, count = base.shape[0], tall * 2 // 5, len(ids)
    shapes = [(acc.shape, F32)]
    if stacked:
        shapes.append(((count, tall, rank), BF16))
    if final:
        shapes.append(((rows, 5 * rank), BF16))
    blocks = pltpu.VMEM((count, rows, part), BF16)
    return call(
        functools.partial(project_kernel, stacked, final, count),
        [*ids, flag],
        [base, cotangent],
        [*shards, acc],
        shapes,
        [blocks, blocks, pltpu.SemaphoreType.DMA((2 * count,))],
    )


def outer_into(small, copies, blocks_ref, outs):
    at = 0
    for out in outs:
        for j in range(out.shape[0]):
            copies[at].wait()
            out[j] = mm(small, blocks_ref[at]).astype(BF16)
            at += 1


def small_parts(sections, here, core, keeps, others, s):
    value = lambda refs: (
        jnp.where(here == s, refs[0][...], refs[1][...].astype(F32))
        if sections == 2
        else refs[1 + s][...].astype(F32)
    )
    mine, theirs = value(keeps), value(others)
    whole = jnp.concatenate(
        [jnp.where(core == 0, mine, theirs), jnp.where(core == 0, theirs, mine)]
    )
    rank = whole.shape[0] // 3
    return whole[:rank], whole[rank : 2 * rank], whole[2 * rank :]


def chain_kernel(sections, width, scalars, base_far, cot_far, own, *refs):
    here, core = scalars[0], scalars[1]
    n = 1 if sections == 2 else sections
    thin_count = 1 if sections == 2 else 2
    refs = list(refs)
    take = lambda count: [refs.pop(0) for _ in range(count)]
    sent, keeps, others = take(n), take(n + 1), take(n + 1)
    codes_ref, thin_refs = take(1)[0], take(thin_count)
    outs_c, outs_b = take(2), take(4)
    cot_ref, base_ref, sems = refs
    at, copies = 2, []
    for far, blocks_ref in ((cot_far, cot_ref), (base_far, base_ref)):
        count, _, columns = blocks_ref.shape
        pairs = []
        for j in range(count):
            start = pl.multiple_of(scalars[at + j] * columns, columns)
            pairs.append((far.at[:, pl.ds(start, columns)], blocks_ref.at[j]))
        copies.append(fetch(pairs, sems, at - 2))
        at += count

    rank = own.shape[1] // 6
    last = sections - 1
    values = [
        jnp.where(
            here == s, own[:, : 5 * rank], sent[0 if sections == 2 else s][...].astype(F32)
        )
        for s in range(sections)
    ]
    column = lambda s, k: values[s][:, k * rank : (k + 1) * rank]
    spread = lambda k: jnp.concatenate(
        [column(0, k), column(0, k + 1) + column(last, k + 1)], axis=1
    )
    base_s = spread(1)
    square = jnp.sum(own[:, 5 * rank :], axis=1, keepdims=True)
    smalls = [small_parts(sections, here, core, keeps, others, s) for s in range(sections)]
    gram = jnp.concatenate([smalls[0][2], smalls[last][2]])
    choose = lambda s, value, other: value if other is None else jnp.where(here == s, value, other)
    state = []
    code = mine_code = None
    for s in range(sections):
        m_s, q_t, _ = smalls[s]
        inner, total, resid_s, before = column(s, 0), square, base_s, code
        if s:
            moved = exact(code, gram)
            total = square + jnp.sum(
                (2.0 * base_s + moved) * code.astype(F32), axis=1, keepdims=True
            )
            inner = inner + exact(code, q_t, COLUMNS)
            resid_s = base_s + moved
        inverse = lax.rsqrt(jnp.maximum(total, 0.0) * (1.0 / width) + 1e-05)
        inner = inner * inverse
        logistic = 1.0 / (1.0 + jnp.exp(-inner))
        active = inner * logistic
        grown = exact(active, m_s)
        code = (moved + grown if s else grown).astype(BF16)
        mine_code = choose(s, code, mine_code)
        state.append((m_s, q_t, inner, logistic, inverse, active, resid_s, before))
    codes_ref[...] = mine_code
    active_t = state[last][5].T.astype(BF16)
    outer_into(active_t, copies[0], cot_ref, outs_c)

    grad_active, grad_y = column(last, 3), spread(3)
    mine = thin_in = thin_out = None
    for s in range(last, -1, -1):
        m_s, q_t, inner, logistic, inverse, active, resid_s, before = state[s]
        if s < last:
            grad_active = exact(back, m_s, COLUMNS)
            grad_y = exact(back, gram) if s else None
            thin_out = choose(s, mm(active.T.astype(BF16), back), thin_out)
        grad_inner = grad_active * logistic * (1.0 + inner * (1.0 - logistic))
        scaled = inverse * grad_inner
        scaled_t = scaled.T.astype(BF16)
        scaled = scaled.astype(BF16)
        mine = choose(s, scaled_t, mine)
        if s:
            thin_in = choose(s, mm(scaled_t, before), thin_in)
            along = jnp.sum(inner * grad_inner, axis=1, keepdims=True)
            along = along * (inverse * inverse * (1.0 / width))
            back = (grad_y + exact(scaled, q_t) - resid_s * along).astype(BF16)
    if sections == 2:
        thin_refs[0][...] = jnp.where(here == last, thin_in, thin_out)
    else:
        thin_refs[0][...] = jnp.where(here == 0, 0.0, thin_in)
        thin_refs[1][...] = thin_out
    outer_into(mine, copies[1], base_ref, outs_b)


def end_kernel(sections, scalars, gain_ref, space_ref, *refs):
    is_last = scalars[0] == 1
    part = space_ref.shape[0]
    grad_in, grad_out = refs[-2:]
    refs = list(refs[:-2])
    pair = lambda: refs.pop(0)[...].astype(F32) + refs.pop(0)[...].astype(F32)
    thin_in = pair()
    thin_out = thin_in if sections == 2 else pair()
    space = space_ref[...]
    lift_in = exact(thin_in, space, COLUMNS)
    lift_out = lift_in if sections == 2 else exact(thin_out, space, COLUMNS)
    if sections == 2:
        lift_in = jnp.where(is_last, lift_in, 0.0)
        half_first, half_second = refs.pop(0)[...], refs.pop(0)[...]
        sum_out = jnp.concatenate([half_first, half_second], axis=1)
    else:
        sum_out = refs.pop(0)[...]
    sum_in = jnp.concatenate([pair(), pair()], axis=1)
    start = pl.multiple_of(scalars[1] * part, part)
    total = gain_ref[:, pl.ds(start, part)] * (sum_in + lift_in)
    grad_in[...] = total.T
    grad_out[...] = jnp.where(is_last, sum_out, lift_out).T


def sum_thin(value, waits):
    peers = lax.axis_size("dp")
    bit, step = 1, 0
    while bit < peers:
        if step:
            value = after(value + got, waits[min(step, len(waits)) - 1])
        got = swap(value, bit)
        bit, step = bit * 2, step + 1
    return value, got


def scatter_sum(got, keep, waits=()):
    half = got.shape[0] // 2
    summed = (keep[half:].astype(F32) + got[half:].astype(F32)).astype(BF16)
    got_x = swap(summed, 2)
    total = keep[:half].astype(F32) + got[:half].astype(F32) + got_x.astype(F32)
    bit = 4
    while True:
        left = total.reshape((total.shape[0] // 2, 2) + total.shape[1:])
        give = left[:, 1].astype(BF16)
        if waits:
            give = after(give, *waits[0])
            waits = waits[1:]
        arrived = swap(give, bit)
        if left.shape[0] == 1:
            return (left[0, 0], arrived[0]), got_x
        total = left[:, 0] + arrived.astype(F32)
        bit *= 2


def on_device(base, cotangent, gain, weight_in, weight_out, subspace):
    sections = lax.axis_size("section")
    here = lax.axis_index("section")
    spot = lax.axis_index("dp")
    core = spot % 2
    rows, width = base.shape
    part, size = subspace.shape
    rank = weight_in.shape[2]
    last = sections - 1
    flag = (here == last).astype(jnp.int32)
    own_in, own_out = weight_in[0], weight_out[0]
    own = call(
        own_kernel,
        [flag, spot],
        [own_in, own_out, subspace, gain],
        [],
        [((part * 5 // 2, rank), BF16)],
        [pltpu.VMEM((part, rank), BF16), pltpu.VMEM((1, part), F32), pltpu.SemaphoreType.DMA((4,))],
        62 * 1024 * 1024,
    )[0]

    peers = lax.axis_size("dp")
    order = sorted(range(4, peers, 4), key=lambda m: (m.bit_count(), m))
    shards = {0: own}
    for m in order:
        if m.bit_count() == 1:
            shards[m] = swap(own, m)
    shards[2] = swap(own, 2)

    tall = (3 * rank, size)
    keep, give = call(
        small_kernel,
        [flag, core],
        [own_out, subspace],
        [after(own, shards[peers // 2])],
        [((tall[0] // 2, size), F32)] * 2,
        [
            pltpu.VMEM((part, rank), BF16),
            pltpu.VMEM((part, size), BF16),
            pltpu.VMEM(tall, F32),
            pltpu.SemaphoreType.DMA((2,)),
        ],
        60 * 1024 * 1024,
    )
    small = keep + swap(give, 1)
    bit = 4
    while bit < peers // 2:
        small = small + swap(small, bit)
        bit *= 2

    tokens = (base, cotangent)
    acc = jnp.zeros((rows, 6 * rank), F32)

    def both_cores(marks, acc):
        ids = [spot ^ m for m in marks]
        acc, stacked = project(ids, flag, [shards[m] for m in marks], tokens, acc, stacked=True)
        ids = [spot ^ m ^ 1 for m in marks]
        return acc, lambda acc: project(ids, flag, [swap(stacked, 1)], tokens, acc)[0]

    ends = order[-1] ^ 2
    first_marks = [0, order[0], 2]
    for k, m in enumerate(order):
        low = m & -m
        if m != low:
            shards[m] = swap(after(shards[m ^ low], shards[order[k - 2] ^ 2]), low)
        before = shards[order[k - 1] ^ 2] if k else shards[2]
        shards[m ^ 2] = swap(after(shards[m], before, *([small] if m ^ 2 == ends else [])), 2)
    near_sum = small
    small = after(small, shards[peers // 2])
    small = small + swap(small, peers // 2)
    small = small + swap(small.astype(BF16), 2).astype(F32)
    small_other = swap(small, 1)
    keeps = [small, *from_sections(small.astype(BF16))]
    others = [small_other, *from_sections(small_other.astype(BF16))]

    acc = after(acc, shards[order[-1]], shards[order[-2] ^ 2], near_sum)
    acc, other_core = both_cores(first_marks, acc)
    acc = other_core(acc)
    rest_marks = [m for m in order + [m ^ 2 for m in order] if m not in (*first_marks, ends)]
    acc, other_core = both_cores(rest_marks, acc)
    acc = other_core(acc)
    acc, send = project(
        [spot ^ ends, spot ^ ends ^ 1],
        flag,
        [shards[ends], swap(shards[ends], 1)],
        tokens,
        acc,
        final=True,
    )
    sent = from_sections(send)

    near = list(range(0, peers, 4))
    every = near + [m ^ 2 for m in near]
    half = part // 2
    if sections == 2:
        columns, block_id = half, lambda i: i * 2 + flag
    else:
        columns, block_id = part, lambda i: i
    both = (spot ^ 1, spot)
    out_ids = [block_id(who ^ m) for who in both for m in every]
    in_ids = [(who ^ m) * 2 + k for k in range(2) for who in both for m in every]
    blocks = lambda n: ((len(every), rank, n), BF16)
    thin_count = 1 if sections == 2 else 2
    codes, *rest = call(
        functools.partial(chain_kernel, sections, width),
        [here, core, *out_ids, *in_ids],
        [base, cotangent],
        [acc, *sent, *keeps, *others],
        [((rows, size), BF16)]
        + [((rank, size), F32)] * thin_count
        + [blocks(columns)] * 2
        + [blocks(half)] * 4,
        [
            pltpu.VMEM((len(out_ids), rows, columns), BF16),
            pltpu.VMEM((len(in_ids), rows, half), BF16),
            pltpu.SemaphoreType.DMA((len(out_ids) + len(in_ids),)),
        ],
        (50 if sections == 2 else 58) * 1024 * 1024,
    )
    thins, chunks = rest[:thin_count], rest[thin_count:]
    got = [swap(give, 1) for give in chunks[::2]]
    lower, lower_x = scatter_sum(got[1], chunks[3])
    upper, upper_x = scatter_sum(got[2], chunks[5])
    sum_out, _ = scatter_sum(got[0], chunks[1], [got[1:], [lower_x], [upper_x]])
    sum_out = sum_out[0] + sum_out[1].astype(F32)
    ends_out = [sum_out]
    if sections == 2:
        ends_out = [swap(sum_out, 1, "section"), sum_out]
    waits = [got[2], lower_x, upper_x]
    terms = [term for thin in thins for term in sum_thin(thin, waits)]
    grad_in, grad_out = call(
        functools.partial(end_kernel, sections),
        [flag, spot],
        [],
        [gain, subspace, *terms, *ends_out, *lower, *upper],
        [((part, rank), F32)] * 2,
    )
    return codes[None], grad_in[None], grad_out[None]


def solution(mesh):
    placed = (
        P("dp", None),
        P("dp", None),
        P("section", None),
        P("section", "dp", None),
        P("section", "dp", None),
        P("dp", None),
    )
    return jax.shard_map(
        on_device,
        mesh=mesh,
        in_specs=placed,
        out_specs=(P("section", "dp", None), P("section", "dp", None), P("section", "dp", None)),
        check_vma=False,
    )
```

time: 180 us -> 167 us (0.928)
  local copies, waits for them, and re-layouts: 34.5 us -> 2.65 us
  Pallas kernels: 24.9 us -> 41.9 us
  waiting for transfers between devices: 76 us -> 79.3 us
    unnamed x60 -> x16, local copies, waits for them, and re-layouts: 33.9 us -> 1.09 us
    pallas_call x11 -> x9, Pallas kernels: 24.9 us -> 41.9 us  [call(): pl.pallas_call(kernel, in_specs=[IN_SMEM] + [IN_HBM] * len(far) + [IN_VME...]
    ppermute x36 -> x35, waiting for transfers between devices: 76 us -> 79.3 us  [swap(): return lax.ppermute(value, axis, [(i, i ^ bits) for i in range(peers)])]
    ppermute x36 -> x35, starting transfers between devices: 36.7 us -> 35.6 us  [swap(): return lax.ppermute(value, axis, [(i, i ^ bits) for i in range(peers)])]
  transfers between devices with their start and end apart: 36 -> 35, of which waited for: 21 -> 17; matrix products, arithmetic and copies ran while one was open for 3% -> 3% of each run, Pallas kernels for 10% -> 6%
where the time goes in v6:
time: 167 us; the launch traced here: 166 us
  waiting for transfers between devices  79.3 us (47%)
  Pallas kernels  41.9 us (25%)
  starting transfers between devices  35.6 us (21%)
  other arithmetic  5.7 us (3%)
  local copies, waits for them, and re-layouts  2.65 us (2%)
    ppermute x35, waiting for transfers between devices, swap(): return lax.ppermute(value, axis, [(i, i ^ bits) for i in range(peers)])  79.3 us
    pallas_call x9, Pallas kernels, call(): pl.pallas_call(kernel, in_specs=[IN_SMEM] + [IN_HBM] * len(far) + [IN_VME...  41.9 us
    ppermute x35, starting transfers between devices, swap(): return lax.ppermute(value, axis, [(i, i ^ bits) for i in range(peers)])  35.6 us
  transfers between devices with their start and end apart: 35, of which 17 were waited for; matrix products, arithmetic and copies ran while one was open for 3% of the time, Pallas kernels for 6%

profile of v6, /device:TPU:0, one launch (start us, length us, event | category | flops | bytes accessed | tf_op | source)
XLA Modules:
  0.0 166.3 jit_solution(8187209709715899120)
XLA Ops:
  1.2 2.6 %shard_map.85.own_ref.refs_0_ = bf16[1280,128]{1,0:T(8,128)(2,1)} custom-call(s32[2]{0:T(128)} %pad_add_fusion.1.scalars, bf16[512,128]{1,0:T(8,128)(2,1)} %bitcast.134, bf16[512,128]{1,0:T(8,128)(2,1)} %bitcast.132, bf16[512,256]{1,0:T(8,128)(2,1)} %space_ref.3, f32[1,8192]{1,0:T(1,128)} %gain_ref.1), custom_call_target="tpu_custom_call" | custom-call | tf_op jit(solution)/shard_map/pallas_call | solution.py:43
  3.8 3.1 %collective-permute-start.1 = (bf16[1280,128]{1,0:T(8,128)(2,1)}, bf16[1280,128]{1,0:T(8,128)(2,1)S(1)}, u32[]{:S(2)}, u32[]{:S(2)}) collective-permute-start(bf16[1280,128]{1,0:T(8,128)(2,1)} %shard_map.85.own_ref.refs_0_), channel_id=1, source_target_pairs={{0,4},{1,5},{2,6},{3,7},{4,0},{5,1},{6,2},{7,3},{8,12},{9,13},{10,... | collective-permute-start | bytes 983048 | tf_op jit(solution)/shard_map/ppermute | solution.py:63
  8.4 2.6 %collective-permute-start = (bf16[1280,128]{1,0:T(8,128)(2,1)}, bf16[1280,128]{1,0:T(8,128)(2,1)S(1)}, u32[]{:S(2)}, u32[]{:S(2)}) collective-permute-start(bf16[1280,128]{1,0:T(8,128)(2,1)} %shard_map.85.own_ref.refs_0_), channel_id=1, source_target_pairs={{0,8},{1,9},{2,10},{3,11},{4,12},{5,13},{6,14},{7,15},{8,0},{9,1},... | collective-permute-start | bytes 983048 | tf_op jit(solution)/shard_map/ppermute | solution.py:63
  11.0 9.5 %collective-permute-done.1.refs_1_ = bf16[1280,128]{1,0:T(8,128)(2,1)S(1)} collective-permute-done((bf16[1280,128]{1,0:T(8,128)(2,1)}, bf16[1280,128]{1,0:T(8,128)(2,1)S(1)}, u32[]{:S(2)}, u32[]{:S(2)}) %collective-permute-start.1) | collective-permute-done | bytes 327712 | tf_op jit(solution)/shard_map/ppermute | solution.py:63
  20.5 2.6 %collective-permute-start.3 = (bf16[1280,128]{1,0:T(8,128)(2,1)S(1)}, bf16[1280,128]{1,0:T(8,128)(2,1)S(1)}, u32[]{:S(2)}, u32[]{:S(2)}) collective-permute-start(bf16[1280,128]{1,0:T(8,128)(2,1)S(1)} %collective-permute-done.1.refs_1_), channel_id=1, source_target_pairs={{0,2},{1,3},{2,0},{3,1},{4,6},{5,7},{6,4},{7,5},{8,10},{9,11},{10,... | collective-permute-start | bytes 983048 | tf_op jit(solution)/shard_map/ppermute | solution.py:63
  25.5 3.0 %shard_map.86 = (f32[192,256]{1,0:T(8,128)}, f32[192,256]{1,0:T(8,128)}) custom-call(s32[2]{0:T(128)} %pad_add_fusion.2.scalars, bf16[512,128]{1,0:T(8,128)(2,1)} %bitcast.133, bf16[512,256]{1,0:T(8,128)(2,1)} %space_ref.3, bf16[1280,128]{1,0:T(8,128)(2,1)} %shard_map.85.own_ref.refs_0_), custom_call_target="tpu_custom_call" | custom-call | tf_op jit(solution)/shard_map/pallas_call | solution.py:43
  32.7 2.1 %collective-permute-start.7 = (f32[192,256]{1,0:T(8,128)S(1)}, f32[192,256]{1,0:T(8,128)S(1)}, u32[]{:S(2)}, u32[]{:S(2)}) collective-permute-start(f32[192,256]{1,0:T(8,128)S(1)} %add.193), channel_id=1, source_target_pairs={{0,4},{1,5},{2,6},{3,7},{4,0},{5,1},{6,2},{7,3},{8,12},{9,13},{10,... | collective-permute-start | bytes 589832 | tf_op jit(solution)/shard_map/ppermute | solution.py:63
  34.8 8.1 %collective-permute-done.7 = f32[192,256]{1,0:T(8,128)S(1)} collective-permute-done((f32[192,256]{1,0:T(8,128)S(1)}, f32[192,256]{1,0:T(8,128)S(1)}, u32[]{:S(2)}, u32[]{:S(2)}) %collective-permute-start.7) | collective-permute-done | bytes 196640 | tf_op jit(solution)/shard_map/ppermute | solution.py:63
  44.8 4.7 %shard_map.87 = (f32[384,768]{1,0:T(8,128)S(1)}, bf16[3,1280,128]{2,1,0:T(8,128)(2,1)}) custom-call(s32[4]{0:T(128)S(1)} %add_add_fusion.1.scalars, bf16[384,8192]{1,0:T(8,128)(2,1)} %base_far.11, bf16[384,8192]{1,0:T(8,128)(2,1)} %cot_far.11, bf16[1280,128]{1,0:T(8,128)(2,1)S(1)} %copy-done, bf16[1280,128]{1,0:T(8,128)(2,1)S(1)} %collective-permute-done.1.refs_1_, ...), custom_call_target="tpu_custom_call" | custom-call | tf_op jit(solution)/shard_map/pallas_call | solution.py:43
  49.8 2.6 %collective-permute-done.10.refs_0_ = bf16[3,1280,128]{2,1,0:T(8,128)(2,1)S(1)} collective-permute-done((bf16[3,1280,128]{2,1,0:T(8,128)(2,1)}, bf16[3,1280,128]{2,1,0:T(8,128)(2,1)S(1)}, u32[]{:S(2)}, u32[]{:S(2)}) %collective-permute-start.10) | collective-permute-done | bytes 983072 | tf_op jit(solution)/shard_map/ppermute | solution.py:63
  52.3 3.3 %shard_map.88.refs_4_ = f32[384,768]{1,0:T(8,128)S(1)} custom-call(s32[4]{0:T(128)S(1)} %add_add_fusion.scalars, bf16[384,8192]{1,0:T(8,128)(2,1)} %base_far.11, bf16[384,8192]{1,0:T(8,128)(2,1)} %cot_far.11, bf16[3,1280,128]{2,1,0:T(8,128)(2,1)S(1)} %collective-permute-done.10.refs_0_, f32[384,768]{1,0:T(8,128)S(1)} %get-tuple-element.40.refs_1_), custom_call_target="tpu_custom_call" | custom-call | tf_op jit(solution)/shard_map/pallas_call | solution.py:43
  55.7 4.6 %shard_map.89 = (f32[384,768]{1,0:T(8,128)S(1)}, bf16[4,1280,128]{2,1,0:T(8,128)(2,1)}) custom-call(s32[5]{0:T(128)S(1)} %stack.303.scalars, bf16[384,8192]{1,0:T(8,128)(2,1)} %base_far.11, bf16[384,8192]{1,0:T(8,128)(2,1)} %cot_far.11, bf16[1280,128]{1,0:T(8,128)(2,1)S(1)} %collective-permute-done.refs_0_, ...), custom_call_target="tpu_custom_call" | custom-call | tf_op jit(solution)/shard_map/pallas_call | solution.py:43
  62.6 8.0 %collective-permute-done.8.refs_0_ = bf16[1280,128]{1,0:T(8,128)(2,1)S(1)} collective-permute-done((bf16[1280,128]{1,0:T(8,128)(2,1)S(1)}, bf16[1280,128]{1,0:T(8,128)(2,1)S(1)}, u32[]{:S(2)}, u32[]{:S(2)}) %collective-permute-start.8) | collective-permute-done | bytes 327712 | tf_op jit(solution)/shard_map/ppermute | solution.py:63
  70.5 2.7 %collective-permute-done.13 = f32[192,256]{1,0:T(8,128)S(1)} collective-permute-done((f32[192,256]{1,0:T(8,128)}, f32[192,256]{1,0:T(8,128)S(1)}, u32[]{:S(2)}, u32[]{:S(2)}) %collective-permute-start.13) | collective-permute-done | bytes 196640 | tf_op jit(solution)/shard_map/ppermute | solution.py:63
  75.7 3.8 %shard_map.90.refs_2_ = f32[384,768]{1,0:T(8,128)S(1)} custom-call(s32[5]{0:T(128)S(1)} %stack.298.scalars, bf16[384,8192]{1,0:T(8,128)(2,1)} %base_far.11, bf16[384,8192]{1,0:T(8,128)(2,1)} %cot_far.11, bf16[4,1280,128]{2,1,0:T(8,128)(2,1)S(1)} %collective-permute-done.11.refs_0_, f32[384,768]{1,0:T(8,128)S(1)} %get-tuple-element.42.refs_1_), custom_call_target="tpu_custom_call" | custom-call | tf_op jit(solution)/shard_map/pallas_call | solution.py:43
  79.5 2.8 %shard_map.91 = (f32[384,768]{1,0:T(8,128)S(1)}, bf16[384,640]{1,0:T(8,128)(2,1)S(1)}) custom-call(s32[3]{0:T(128)S(1)} %pad_add_fusion.scalars, bf16[384,8192]{1,0:T(8,128)(2,1)} %base_far.11, bf16[384,8192]{1,0:T(8,128)(2,1)} %cot_far.11, bf16[1280,128]{1,0:T(8,128)(2,1)S(1)} %collective-permute-done.8.refs_0_, ...), custom_call_target="tpu_custom_call" | custom-call | tf_op jit(solution)/shard_map/pallas_call | solution.py:43
  87.4 12.0 %collective-permute-done.15.refs_2_ = bf16[192,256]{1,0:T(8,128)(2,1)S(1)} collective-permute-done((bf16[192,256]{1,0:T(8,128)(2,1)S(1)}, bf16[192,256]{1,0:T(8,128)(2,1)S(1)}, u32[]{:S(2)}, u32[]{:S(2)}) %collective-permute-start.15) | collective-permute-done | bytes 98336 | tf_op jit(solution)/shard_map/ppermute | solution.py:63
  100.5 15.3 %shard_map.92 = (bf16[384,256]{1,0:T(8,128)(2,1)}, f32[128,256]{1,0:T(8,128)S(1)}, bf16[8,128,256]{2,1,0:T(8,128)(2,1)S(1)}, bf16[8,128,256]{2,1,0:T(8,128)(2,1)...) custom-call(s32[50]{0:T(128)S(1)} %stack.286.scalars, ...), custom_call_target="tpu_custom_call" | custom-call | tf_op jit(solution)/shard_map/pallas_call | solution.py:43
  124.2 13.2 %collective-permute-done.20 = f32[128,256]{1,0:T(8,128)S(1)} collective-permute-done((f32[128,256]{1,0:T(8,128)S(1)}, f32[128,256]{1,0:T(8,128)S(1)}, u32[]{:S(2)}, u32[]{:S(2)}) %collective-permute-start.20) | collective-permute-done | bytes 131104 | tf_op jit(solution)/shard_map/ppermute | solution.py:63
  139.9 2.4 %collective-permute-done.27 = bf16[4,128,256]{2,1,0:T(8,128)(2,1)S(1)} collective-permute-done((bf16[4,128,256]{2,1,0:T(8,128)(2,1)S(1)}, bf16[4,128,256]{2,1,0:T(8,128)(2,1)S(1)}, u32[]{:S(2)}, u32[]{:S(2)}) %collective-permute-start.27) | collective-permute-done | bytes 262176 | tf_op jit(solution)/shard_map/ppermute | solution.py:63
  145.5 4.7 %collective-permute-done.28 = bf16[2,128,256]{2,1,0:T(8,128)(2,1)S(1)} collective-permute-done((bf16[2,128,256]{2,1,0:T(8,128)(2,1)S(1)}, bf16[2,128,256]{2,1,0:T(8,128)(2,1)S(1)}, u32[]{:S(2)}, u32[]{:S(2)}) %collective-permute-start.28) | collective-permute-done | bytes 131104 | tf_op jit(solution)/shard_map/ppermute | solution.py:63
  150.4 3.0 %collective-permute-start.32 = (bf16[1,128,256]{2,1,0:T(8,128)(2,1)S(1)}, bf16[1,128,256]{2,1,0:T(8,128)(2,1)S(1)}, u32[]{:S(2)}, u32[]{:S(2)}) collective-permute-start(bf16[1,128,256]{2,1,0:T(8,128)(2,1)S(1)} %fusion.11), channel_id=1, source_target_pairs={{0,8},{1,9},{2,10},{3,11},{4,12},{5,13},{6,14},{7,15},{8,0},{9,1},... | collective-permute-start | bytes 196616 | tf_op jit(solution)/shard_map/ppermute | solution.py:63
  153.5 5.9 %collective-permute-done.29 = bf16[1,128,256]{2,1,0:T(8,128)(2,1)S(1)} collective-permute-done((bf16[1,128,256]{2,1,0:T(8,128)(2,1)S(1)}, bf16[1,128,256]{2,1,0:T(8,128)(2,1)S(1)}, u32[]{:S(2)}, u32[]{:S(2)}) %collective-permute-start.29) | collective-permute-done | bytes 65568 | tf_op jit(solution)/shard_map/ppermute | solution.py:63
  162.4 2.1 %collective-permute-done.30.refs_2_ = f32[128,256]{1,0:T(8,128)S(1)} collective-permute-done((f32[128,256]{1,0:T(8,128)S(1)}, f32[128,256]{1,0:T(8,128)S(1)}, u32[]{:S(2)}, u32[]{:S(2)}) %collective-permute-start.30) | collective-permute-done | bytes 131104 | tf_op jit(solution)/shard_map/ppermute | solution.py:63
  (106 shorter events, 40.6 us)
Async XLA Ops:
  3.8 16.7 %collective-permute-start.1 = (bf16[1280,128]{1,0:T(8,128)(2,1)}, bf16[1280,128]{1,0:T(8,128)(2,1)S(1)}, u32[]{:S(2)}, u32[]{:S(2)}) collective-permute-start(bf16[1280,128]{1,0:T(8,128)(2,1)} %shard_map.85.own_ref.refs_0_), channel_id=1, source_target_pairs={{0,4},{1,5},{2,6},{3,7},{4,0},{5,1},{6,2},{7,3},{8,12},{9,13},{10,... | collective-permute-start | bytes 983048 | tf_op jit(solution)/shard_map/ppermute | solution.py:63
  6.9 13.6 %collective-permute-start.2 = (bf16[1280,128]{1,0:T(8,128)(2,1)}, bf16[1280,128]{1,0:T(8,128)(2,1)S(1)}, u32[]{:S(2)}, u32[]{:S(2)}) collective-permute-start(bf16[1280,128]{1,0:T(8,128)(2,1)} %shard_map.85.own_ref.refs_0_), channel_id=1, source_target_pairs={{0,2},{1,3},{2,0},{3,1},{4,6},{5,7},{6,4},{7,5},{8,10},{9,11},{10,... | collective-permute-start | bytes 983048 | tf_op jit(solution)/shard_map/ppermute | solution.py:63
  8.4 17.1 %collective-permute-start = (bf16[1280,128]{1,0:T(8,128)(2,1)}, bf16[1280,128]{1,0:T(8,128)(2,1)S(1)}, u32[]{:S(2)}, u32[]{:S(2)}) collective-permute-start(bf16[1280,128]{1,0:T(8,128)(2,1)} %shard_map.85.own_ref.refs_0_), channel_id=1, source_target_pairs={{0,8},{1,9},{2,10},{3,11},{4,12},{5,13},{6,14},{7,15},{8,0},{9,1},... | collective-permute-start | bytes 983048 | tf_op jit(solution)/shard_map/ppermute | solution.py:63
  20.5 9.4 %collective-permute-start.3 = (bf16[1280,128]{1,0:T(8,128)(2,1)S(1)}, bf16[1280,128]{1,0:T(8,128)(2,1)S(1)}, u32[]{:S(2)}, u32[]{:S(2)}) collective-permute-start(bf16[1280,128]{1,0:T(8,128)(2,1)S(1)} %collective-permute-done.1.refs_1_), channel_id=1, source_target_pairs={{0,2},{1,3},{2,0},{3,1},{4,6},{5,7},{6,4},{7,5},{8,10},{9,11},{10,... | collective-permute-start | bytes 983048 | tf_op jit(solution)/shard_map/ppermute | solution.py:63
  29.9 13.7 %collective-permute-start.4 = (bf16[1280,128]{1,0:T(8,128)(2,1)S(1)}, bf16[1280,128]{1,0:T(8,128)(2,1)S(1)}, u32[]{:S(2)}, u32[]{:S(2)}) collective-permute-start(bf16[1280,128]{1,0:T(8,128)(2,1)S(1)} %collective-permute-done.refs_0_), channel_id=1, source_target_pairs={{0,4},{1,5},{2,6},{3,7},{4,0},{5,1},{6,2},{7,3},{8,12},{9,13},{10,... | collective-permute-start | bytes 983048 | tf_op jit(solution)/shard_map/ppermute | solution.py:63
  29.9 13.7 %collective-permute-start.5 = (bf16[1280,128]{1,0:T(8,128)(2,1)S(1)}, bf16[1280,128]{1,0:T(8,128)(2,1)S(1)}, u32[]{:S(2)}, u32[]{:S(2)}) collective-permute-start(bf16[1280,128]{1,0:T(8,128)(2,1)S(1)} %collective-permute-done.refs_0_), channel_id=1, source_target_pairs={{0,2},{1,3},{2,0},{3,1},{4,6},{5,7},{6,4},{7,5},{8,10},{9,11},{10,... | collective-permute-start | bytes 983048 | tf_op jit(solution)/shard_map/ppermute | solution.py:63
  32.7 10.2 %collective-permute-start.7 = (f32[192,256]{1,0:T(8,128)S(1)}, f32[192,256]{1,0:T(8,128)S(1)}, u32[]{:S(2)}, u32[]{:S(2)}) collective-permute-start(f32[192,256]{1,0:T(8,128)S(1)} %add.193), channel_id=1, source_target_pairs={{0,4},{1,5},{2,6},{3,7},{4,0},{5,1},{6,2},{7,3},{8,12},{9,13},{10,... | collective-permute-start | bytes 589832 | tf_op jit(solution)/shard_map/ppermute | solution.py:63
  60.3 15.4 %collective-permute-start.11 = (bf16[4,1280,128]{2,1,0:T(8,128)(2,1)}, bf16[4,1280,128]{2,1,0:T(8,128)(2,1)S(1)}, u32[]{:S(2)}, u32[]{:S(2)}) collective-permute-start(bf16[4,1280,128]{2,1,0:T(8,128)(2,1)} %get-tuple-element.41), channel_id=1, source_target_pairs={{0,1},{1,0},{2,3},{3,2},{4,5},{5,4},{6,7},{7,6},{8,9},{9,8},{10,11... | collective-permute-start | bytes 3932168 | tf_op jit(solution)/shard_map/ppermute | solution.py:63
  60.5 10.0 %collective-permute-start.8 = (bf16[1280,128]{1,0:T(8,128)(2,1)S(1)}, bf16[1280,128]{1,0:T(8,128)(2,1)S(1)}, u32[]{:S(2)}, u32[]{:S(2)}) collective-permute-start(bf16[1280,128]{1,0:T(8,128)(2,1)S(1)} %collective-permute-done.4.refs_1_), channel_id=1, source_target_pairs={{0,2},{1,3},{2,0},{3,1},{4,6},{5,7},{6,4},{7,5},{8,10},{9,11},{10,... | collective-permute-start | bytes 983048 | tf_op jit(solution)/shard_map/ppermute | solution.py:63
  61.2 12.1 %collective-permute-start.13 = (f32[192,256]{1,0:T(8,128)}, f32[192,256]{1,0:T(8,128)S(1)}, u32[]{:S(2)}, u32[]{:S(2)}) collective-permute-start(f32[192,256]{1,0:T(8,128)} %add.194), channel_id=1, source_target_pairs={{0,8},{1,9},{2,10},{3,11},{4,12},{5,13},{6,14},{7,15},{8,0},{9,1},... | collective-permute-start | bytes 589832 | tf_op jit(solution)/shard_map/ppermute | solution.py:63
  70.5 9.0 %collective-permute-start.9 = (bf16[1280,128]{1,0:T(8,128)(2,1)S(1)}, bf16[1280,128]{1,0:T(8,128)(2,1)S(1)}, u32[]{:S(2)}, u32[]{:S(2)}) collective-permute-start(bf16[1280,128]{1,0:T(8,128)(2,1)S(1)} %collective-permute-done.8.refs_0_), channel_id=1, source_target_pairs={{0,1},{1,0},{2,3},{3,2},{4,5},{5,4},{6,7},{7,6},{8,9},{9,8},{10,11... | collective-permute-start | bytes 983048 | tf_op jit(solution)/shard_map/ppermute | solution.py:63
  74.2 10.8 %collective-permute-start.14 = (bf16[192,256]{1,0:T(8,128)(2,1)S(1)}, bf16[192,256]{1,0:T(8,128)(2,1)S(1)}, u32[]{:S(2)}, u32[]{:S(2)}) collective-permute-start(bf16[192,256]{1,0:T(8,128)(2,1)S(1)} %get-tuple-element.63), channel_id=1, source_target_pairs={{0,2},{1,3},{2,0},{3,1},{4,6},{5,7},{6,4},{7,5},{8,10},{9,11},{10,... | collective-permute-start | bytes 294920 | tf_op jit(solution)/shard_map/ppermute | solution.py:63
  83.4 17.1 %collective-permute-start.12 = (bf16[384,640]{1,0:T(8,128)(2,1)S(1)}, bf16[384,640]{1,0:T(8,128)(2,1)S(1)}, u32[]{:S(2)}, u32[]{:S(2)}) collective-permute-start(bf16[384,640]{1,0:T(8,128)(2,1)S(1)} %get-tuple-element.44), channel_id=1, source_target_pairs={{0,16},{16,0},{1,17},{17,1},{2,18},{18,2},{3,19},{19,3},{4,20},{20... | collective-permute-start | bytes 1474568 | tf_op jit(solution)/shard_map/ppermute | solution.py:63
  85.1 14.3 %collective-permute-start.15 = (bf16[192,256]{1,0:T(8,128)(2,1)S(1)}, bf16[192,256]{1,0:T(8,128)(2,1)S(1)}, u32[]{:S(2)}, u32[]{:S(2)}) collective-permute-start(bf16[192,256]{1,0:T(8,128)(2,1)S(1)} %get-tuple-element.61), channel_id=1, source_target_pairs={{0,16},{16,0},{1,17},{17,1},{2,18},{18,2},{3,19},{19,3},{4,20},{20... | collective-permute-start | bytes 294920 | tf_op jit(solution)/shard_map/ppermute | solution.py:63
  86.5 14.0 %collective-permute-start.17 = (bf16[192,256]{1,0:T(8,128)(2,1)S(1)}, bf16[192,256]{1,0:T(8,128)(2,1)S(1)}, u32[]{:S(2)}, u32[]{:S(2)}) collective-permute-start(bf16[192,256]{1,0:T(8,128)(2,1)S(1)} %convert_element_type.136), channel_id=1, source_target_pairs={{0,16},{16,0},{1,17},{17,1},{2,18},{18,2},{3,19},{19,3},{4,20},{20... | collective-permute-start | bytes 294920 | tf_op jit(solution)/shard_map/ppermute | solution.py:63
  119.8 17.7 %collective-permute-start.24 = (bf16[4,128,256]{2,1,0:T(8,128)(2,1)S(1)}, bf16[4,128,256]{2,1,0:T(8,128)(2,1)S(1)}, u32[]{:S(2)}, u32[]{:S(2)}) collective-permute-start(bf16[4,128,256]{2,1,0:T(8,128)(2,1)S(1)} %add_convert_fusion.1), channel_id=1, source_target_pairs={{0,2},{1,3},{2,0},{3,1},{4,6},{5,7},{6,4},{7,5},{8,10},{9,11},{10,... | collective-permute-start | bytes 786440 | tf_op jit(solution)/shard_map/ppermute | solution.py:63
  120.6 17.1 %collective-permute-start.22 = (bf16[4,128,256]{2,1,0:T(8,128)(2,1)S(1)}, bf16[4,128,256]{2,1,0:T(8,128)(2,1)S(1)}, u32[]{:S(2)}, u32[]{:S(2)}) collective-permute-start(bf16[4,128,256]{2,1,0:T(8,128)(2,1)S(1)} %add_convert_fusion.2), channel_id=1, source_target_pairs={{0,2},{1,3},{2,0},{3,1},{4,6},{5,7},{6,4},{7,5},{8,10},{9,11},{10,... | collective-permute-start | bytes 786440 | tf_op jit(solution)/shard_map/ppermute | solution.py:63
  122.0 15.4 %collective-permute-start.20 = (f32[128,256]{1,0:T(8,128)S(1)}, f32[128,256]{1,0:T(8,128)S(1)}, u32[]{:S(2)}, u32[]{:S(2)}) collective-permute-start(f32[128,256]{1,0:T(8,128)S(1)} %add.197), channel_id=1, source_target_pairs={{0,2},{1,3},{2,0},{3,1},{4,6},{5,7},{6,4},{7,5},{8,10},{9,11},{10,... | collective-permute-start | bytes 393224 | tf_op jit(solution)/shard_map/ppermute | solution.py:63
  122.7 19.5 %collective-permute-start.27 = (bf16[4,128,256]{2,1,0:T(8,128)(2,1)S(1)}, bf16[4,128,256]{2,1,0:T(8,128)(2,1)S(1)}, u32[]{:S(2)}, u32[]{:S(2)}) collective-permute-start(bf16[4,128,256]{2,1,0:T(8,128)(2,1)S(1)} %add_convert_fusion), channel_id=1, source_target_pairs={{0,2},{1,3},{2,0},{3,1},{4,6},{5,7},{6,4},{7,5},{8,10},{9,11},{10,... | collective-permute-start | bytes 786440 | tf_op jit(solution)/shard_map/ppermute | solution.py:63
  137.8 12.6 %collective-permute-start.31 = (bf16[2,128,256]{2,1,0:T(8,128)(2,1)S(1)}, bf16[2,128,256]{2,1,0:T(8,128)(2,1)S(1)}, u32[]{:S(2)}, u32[]{:S(2)}) collective-permute-start(bf16[2,128,256]{2,1,0:T(8,128)(2,1)S(1)} %fusion.7), channel_id=1, source_target_pairs={{0,4},{1,5},{2,6},{3,7},{4,0},{5,1},{6,2},{7,3},{8,12},{9,13},{10,... | collective-permute-start | bytes 393224 | tf_op jit(solution)/shard_map/ppermute | solution.py:63
  142.4 11.0 %collective-permute-start.23 = (f32[128,256]{1,0:T(8,128)S(1)}, f32[128,256]{1,0:T(8,128)S(1)}, u32[]{:S(2)}, u32[]{:S(2)}) collective-permute-start(f32[128,256]{1,0:T(8,128)S(1)} %add.198), channel_id=1, source_target_pairs={{0,4},{1,5},{2,6},{3,7},{4,0},{5,1},{6,2},{7,3},{8,12},{9,13},{10,... | collective-permute-start | bytes 393224 | tf_op jit(solution)/shard_map/ppermute | solution.py:63
  144.5 16.6 %collective-permute-start.34 = (bf16[1,128,256]{2,1,0:T(8,128)(2,1)S(1)}, bf16[1,128,256]{2,1,0:T(8,128)(2,1)S(1)}, u32[]{:S(2)}, u32[]{:S(2)}) collective-permute-start(bf16[1,128,256]{2,1,0:T(8,128)(2,1)S(1)} %fusion.12), channel_id=1, source_target_pairs={{0,8},{1,9},{2,10},{3,11},{4,12},{5,13},{6,14},{7,15},{8,0},{9,1},... | collective-permute-start | bytes 196616 | tf_op jit(solution)/shard_map/ppermute | solution.py:63
  150.3 9.2 %collective-permute-start.29 = (bf16[1,128,256]{2,1,0:T(8,128)(2,1)S(1)}, bf16[1,128,256]{2,1,0:T(8,128)(2,1)S(1)}, u32[]{:S(2)}, u32[]{:S(2)}) collective-permute-start(bf16[1,128,256]{2,1,0:T(8,128)(2,1)S(1)} %fusion.10), channel_id=1, source_target_pairs={{0,8},{1,9},{2,10},{3,11},{4,12},{5,13},{6,14},{7,15},{8,0},{9,1},... | collective-permute-start | bytes 196616 | tf_op jit(solution)/shard_map/ppermute | solution.py:63
  150.4 10.7 %collective-permute-start.32 = (bf16[1,128,256]{2,1,0:T(8,128)(2,1)S(1)}, bf16[1,128,256]{2,1,0:T(8,128)(2,1)S(1)}, u32[]{:S(2)}, u32[]{:S(2)}) collective-permute-start(bf16[1,128,256]{2,1,0:T(8,128)(2,1)S(1)} %fusion.11), channel_id=1, source_target_pairs={{0,8},{1,9},{2,10},{3,11},{4,12},{5,13},{6,14},{7,15},{8,0},{9,1},... | collective-permute-start | bytes 196616 | tf_op jit(solution)/shard_map/ppermute | solution.py:63
  (19 other events, 136.2 us)

commit v7 on v6

--- a/solution.py
+++ b/solution.py
@@ -9,7 +9,7 @@
 
 F32 = jnp.float32
 BF16 = jnp.bfloat16
-VMEM_BYTES = 50 * 1024 * 1024
+VMEM_BYTES = 16 * 1024 * 1024
 IN_VMEM = pl.BlockSpec(memory_space=pltpu.VMEM)
 IN_SMEM = pl.BlockSpec(memory_space=pltpu.SMEM)
 IN_HBM = pl.BlockSpec(memory_space=pltpu.HBM)
@@ -39,7 +39,7 @@
     return total
 
 
-def call(kernel, scalars, far, arrays, shapes, scratch=(), vmem_bytes=VMEM_BYTES):
+def call(kernel, scalars, far, arrays, shapes, scratch=(), vmem_bytes=VMEM_BYTES, flops=0):
     return pl.pallas_call(
         kernel,
         in_specs=[IN_SMEM] + [IN_HBM] * len(far) + [IN_VMEM] * len(arrays),
@@ -47,7 +47,7 @@
         out_shape=[jax.ShapeDtypeStruct(*s) for s in shapes],
         scratch_shapes=list(scratch),
         compiler_params=pltpu.CompilerParams(vmem_limit_bytes=vmem_bytes),
-        cost_estimate=pl.CostEstimate(flops=0, bytes_accessed=0, transcendentals=0),
+        cost_estimate=pl.CostEstimate(flops=flops, bytes_accessed=0, transcendentals=0),
     )(jnp.stack(scalars).astype(jnp.int32), *far, *arrays)
 
 
@@ -123,30 +123,19 @@
     give_ref[...] = jnp.where(core == 0, second, first)
 
 
-def project_kernel(stacked, final, count, scalars, base_far, cot_far, *refs):
-    refs = list(refs)
-    base_ref, cot_ref, sems = refs[-3:]
-    shards, refs = [], refs[:-3]
-    while len(shards) < count:
-        ref = refs.pop(0)
-        shards += [ref] if len(ref.shape) == 2 else [ref.at[i] for i in range(ref.shape[0])]
-    acc, out = refs.pop(0), refs.pop(0)
+def project_kernel(first, final, count, scalars, base_ref, cot_ref, *refs):
+    shards, refs = refs[:count], list(refs[count:])
+    acc = None if first else refs.pop(0)
+    out = refs.pop(0)
     rank = out.shape[1] // 6
-    part = base_ref.shape[2]
+    part = shards[0].shape[0] * 2 // 5
     half = part // 2
-    starts = [pl.multiple_of(scalars[t] * part, part) for t in range(count)]
-    block = lambda ref, t: ref.at[:, pl.ds(starts[t], part)]
-    copies = []
-    for t in range(count):
-        pairs = [(block(base_far, t), base_ref.at[t]), (block(cot_far, t), cot_ref.at[t])]
-        copies.append(fetch(pairs, sems, 2 * t))
-    skip = pl.multiple_of(scalars[count] * half, half)
-    out[...] = acc[...]
+    skip = scalars[count] * half
+    out[...] = jnp.zeros_like(out) if first else acc[...]
     for t, shard in enumerate(shards):
-        if stacked:
-            refs[0][t] = shard[...]
-        copies[t][0].wait()
-        tokens = base_ref[t]
+        start = pl.multiple_of(scalars[t] * part, part)
+        half_start = pl.multiple_of(start + skip, half)
+        tokens = base_ref[:, pl.ds(start, part)]
         tokens_f = tokens.astype(F32)
         square = tokens_f * tokens_f
         total = square[:, :rank]
@@ -154,41 +143,36 @@
             total = total + square[:, at : at + rank]
         wide = jnp.concatenate([shard[:part], shard[part : 2 * part]], axis=1)
         out[:, : 2 * rank] += mm(tokens, wide)
-        out[:, 2 * rank : 3 * rank] += mm(base_ref[t, :, pl.ds(skip, half)], shard[2 * part :])
+        out[:, 2 * rank : 3 * rank] += mm(base_ref[:, pl.ds(half_start, half)], shard[2 * part :])
+        out[:, 3 * rank : 4 * rank] += mm(cot_ref[:, pl.ds(start, part)], shard[part : 2 * part])
+        out[:, 4 * rank : 5 * rank] += mm(cot_ref[:, pl.ds(half_start, half)], shard[2 * part :])
         out[:, 5 * rank :] += total
-        copies[t][1].wait()
-        out[:, 3 * rank : 4 * rank] += mm(cot_ref[t], shard[part : 2 * part])
-        out[:, 4 * rank : 5 * rank] += mm(cot_ref[t, :, pl.ds(skip, half)], shard[2 * part :])
     if final:
         refs[0][...] = out[:, : 5 * rank].astype(BF16)
 
 
-def project(ids, flag, shards, tokens, acc, stacked=False, final=False):
-    base, cotangent = tokens
-    tall, rank = shards[0].shape[-2:]
-    rows, part, count = base.shape[0], tall * 2 // 5, len(ids)
-    shapes = [(acc.shape, F32)]
-    if stacked:
-        shapes.append(((count, tall, rank), BF16))
+def project(ids, flag, shards, tokens, acc=None, final=False):
+    tall, rank = shards[0].shape
+    rows, count = tokens[0].shape[0], len(ids)
+    shapes = [((rows, 6 * rank), F32)]
     if final:
         shapes.append(((rows, 5 * rank), BF16))
-    blocks = pltpu.VMEM((count, rows, part), BF16)
     return call(
-        functools.partial(project_kernel, stacked, final, count),
+        functools.partial(project_kernel, acc is None, final, count),
         [*ids, flag],
-        [base, cotangent],
-        [*shards, acc],
+        [],
+        [*tokens, *shards] + ([] if acc is None else [acc]),
         shapes,
-        [blocks, blocks, pltpu.SemaphoreType.DMA((2 * count,))],
-    )
-
-
-def outer_into(small, copies, blocks_ref, outs):
-    at = 0
+        flops=4 * rows * tall * rank * count,
+    )
+
+
+def outer_into(scalars, at, small, tokens_ref, outs):
     for out in outs:
-        for j in range(out.shape[0]):
-            copies[at].wait()
-            out[j] = mm(small, blocks_ref[at]).astype(BF16)
+        count, _, columns = out.shape
+        for j in range(count):
+            start = pl.multiple_of(scalars[at] * columns, columns)
+            out[j] = mm(small, tokens_ref[:, pl.ds(start, columns)]).astype(BF16)
             at += 1
 
 
@@ -206,7 +190,7 @@
     return whole[:rank], whole[rank : 2 * rank], whole[2 * rank :]
 
 
-def chain_kernel(sections, width, scalars, base_far, cot_far, own, *refs):
+def chain_kernel(sections, width, scalars, base_ref, cot_ref, own, *refs):
     here, core = scalars[0], scalars[1]
     n = 1 if sections == 2 else sections
     thin_count = 1 if sections == 2 else 2
@@ -215,17 +199,6 @@
     sent, keeps, others = take(n), take(n + 1), take(n + 1)
     codes_ref, thin_refs = take(1)[0], take(thin_count)
     outs_c, outs_b = take(2), take(4)
-    cot_ref, base_ref, sems = refs
-    at, copies = 2, []
-    for far, blocks_ref in ((cot_far, cot_ref), (base_far, base_ref)):
-        count, _, columns = blocks_ref.shape
-        pairs = []
-        for j in range(count):
-            start = pl.multiple_of(scalars[at + j] * columns, columns)
-            pairs.append((far.at[:, pl.ds(start, columns)], blocks_ref.at[j]))
-        copies.append(fetch(pairs, sems, at - 2))
-        at += count
-
     rank = own.shape[1] // 6
     last = sections - 1
     values = [
@@ -265,7 +238,7 @@
         state.append((m_s, q_t, inner, logistic, inverse, active, resid_s, before))
     codes_ref[...] = mine_code
     active_t = state[last][5].T.astype(BF16)
-    outer_into(active_t, copies[0], cot_ref, outs_c)
+    outer_into(scalars, 2, active_t, cot_ref, outs_c)
 
     grad_active, grad_y = column(last, 3), spread(3)
     mine = thin_in = thin_out = None
@@ -290,7 +263,7 @@
     else:
         thin_refs[0][...] = jnp.where(here == 0, 0.0, thin_in)
         thin_refs[1][...] = thin_out
-    outer_into(mine, copies[1], base_ref, outs_b)
+    outer_into(scalars, 2 + 2 * outs_c[0].shape[0], mine, base_ref, outs_b)
 
 
 def end_kernel(sections, scalars, gain_ref, space_ref, *refs):
@@ -322,7 +295,8 @@
     bit, step = 1, 0
     while bit < peers:
         if step:
-            value = after(value + got, waits[min(step, len(waits)) - 1])
+            wait = waits[min(step, len(waits)) - 1]
+            value = value + got if wait is None else after(value + got, wait)
         got = swap(value, bit)
         bit, step = bit * 2, step + 1
     return value, got
@@ -398,23 +372,13 @@
         bit *= 2
 
     tokens = (base, cotangent)
-    acc = jnp.zeros((rows, 6 * rank), F32)
-
-    def both_cores(marks, acc):
-        ids = [spot ^ m for m in marks]
-        acc, stacked = project(ids, flag, [shards[m] for m in marks], tokens, acc, stacked=True)
-        ids = [spot ^ m ^ 1 for m in marks]
-        return acc, lambda acc: project(ids, flag, [swap(stacked, 1)], tokens, acc)[0]
-
     ends = order[-1] ^ 2
-    first_marks = [0, order[0], 2]
     for k, m in enumerate(order):
         low = m & -m
         if m != low:
             shards[m] = swap(after(shards[m ^ low], shards[order[k - 2] ^ 2]), low)
         before = shards[order[k - 1] ^ 2] if k else shards[2]
         shards[m ^ 2] = swap(after(shards[m], before, *([small] if m ^ 2 == ends else [])), 2)
-    near_sum = small
     small = after(small, shards[peers // 2])
     small = small + swap(small, peers // 2)
     small = small + swap(small.astype(BF16), 2).astype(F32)
@@ -422,20 +386,13 @@
     keeps = [small, *from_sections(small.astype(BF16))]
     others = [small_other, *from_sections(small_other.astype(BF16))]
 
-    acc = after(acc, shards[order[-1]], shards[order[-2] ^ 2], near_sum)
-    acc, other_core = both_cores(first_marks, acc)
-    acc = other_core(acc)
-    rest_marks = [m for m in order + [m ^ 2 for m in order] if m not in (*first_marks, ends)]
-    acc, other_core = both_cores(rest_marks, acc)
-    acc = other_core(acc)
-    acc, send = project(
-        [spot ^ ends, spot ^ ends ^ 1],
-        flag,
-        [shards[ends], swap(shards[ends], 1)],
-        tokens,
-        acc,
-        final=True,
-    )
+    marks = [m for m in range(0, peers, 2) if m != ends]
+    for m in marks:
+        shards[m ^ 1] = swap(shards[m], 1)
+    marks += [m ^ 1 for m in marks]
+    acc = project([spot ^ m for m in marks], flag, [shards[m] for m in marks], tokens)[0]
+    pair = [shards[ends], swap(shards[ends], 1)]
+    acc, send = project([spot ^ ends, spot ^ ends ^ 1], flag, pair, tokens, acc, final=True)
     sent = from_sections(send)
 
     near = list(range(0, peers, 4))
@@ -453,18 +410,13 @@
     codes, *rest = call(
         functools.partial(chain_kernel, sections, width),
         [here, core, *out_ids, *in_ids],
-        [base, cotangent],
-        [acc, *sent, *keeps, *others],
+        [],
+        [base, cotangent, acc, *sent, *keeps, *others],
         [((rows, size), BF16)]
         + [((rank, size), F32)] * thin_count
         + [blocks(columns)] * 2
         + [blocks(half)] * 4,
-        [
-            pltpu.VMEM((len(out_ids), rows, columns), BF16),
-            pltpu.VMEM((len(in_ids), rows, half), BF16),
-            pltpu.SemaphoreType.DMA((len(out_ids) + len(in_ids),)),
-        ],
-        (50 if sections == 2 else 58) * 1024 * 1024,
+        vmem_bytes=(VMEM_BYTES if sections == 2 else 32 * 1024 * 1024),
     )
     thins, chunks = rest[:thin_count], rest[thin_count:]
     got = [swap(give, 1) for give in chunks[::2]]
@@ -475,7 +427,7 @@
     ends_out = [sum_out]
     if sections == 2:
         ends_out = [swap(sum_out, 1, "section"), sum_out]
-    waits = [got[2], lower_x, upper_x]
+    waits = [None, got[2], lower_x]
     terms = [term for thin in thins for term in sum_thin(thin, waits)]
     grad_in, grad_out = call(
         functools.partial(end_kernel, sections),

time: 167 us -> 146 us (0.87)
  Pallas kernels: 41.9 us -> 18 us
  local copies, waits for them, and re-layouts: 2.65 us -> 12.4 us
  other arithmetic: 5.7 us -> 2.98 us
  starting transfers between devices: 35.6 us -> 33.7 us
  waiting for transfers between devices: 79.3 us -> 77.5 us
    pallas_call x9 -> x6, Pallas kernels: 41.9 us -> 18 us  [call(): pl.pallas_call(kernel, in_specs=[IN_SMEM] + [IN_HBM] * len(far) + [IN_VME...]
    unnamed x16 -> x20, local copies, waits for them, and re-layouts: 1.09 us -> 12.1 us
    ppermute x35 -> x40, starting transfers between devices: 35.6 us -> 33.7 us  [swap(): return lax.ppermute(value, axis, [(i, i ^ bits) for i in range(peers)])]
    ppermute x35 -> x40, waiting for transfers between devices: 79.3 us -> 77.5 us  [swap(): return lax.ppermute(value, axis, [(i, i ^ bits) for i in range(peers)])]
  transfers between devices with their start and end apart: 35 -> 40, of which waited for: 17 -> 22; matrix products, arithmetic and copies ran while one was open for 3% -> 2% of each run, Pallas kernels for 6% -> 6%
where the time goes in v7:
time: 146 us
  waiting for transfers between devices  77.5 us (53%)
  starting transfers between devices  33.7 us (23%)
  Pallas kernels  18 us (12%)
  local copies, waits for them, and re-layouts  12.4 us (8%)
  other arithmetic  2.98 us (2%)
    ppermute x40, waiting for transfers between devices, swap(): return lax.ppermute(value, axis, [(i, i ^ bits) for i in range(peers)])  77.5 us
    ppermute x40, starting transfers between devices, swap(): return lax.ppermute(value, axis, [(i, i ^ bits) for i in range(peers)])  33.7 us
    pallas_call x6, Pallas kernels, call(): pl.pallas_call(kernel, in_specs=[IN_SMEM] + [IN_HBM] * len(far) + [IN_VME...  18 us
    unnamed x20, local copies, waits for them, and re-layouts  12.1 us
  transfers between devices with their start and end apart: 40, of which 22 were waited for; matrix products, arithmetic and copies ran while one was open for 2% of the time, Pallas kernels for 6%

profile of v7, /device:TPU:0, one launch (start us, length us, event | category | flops | bytes accessed | tf_op | source)
XLA Modules:
  0.0 145.6 jit_solution(166838635889999996)
XLA Ops:
  1.2 2.5 %shard_map.85.own_ref.refs_0_ = bf16[1280,128]{1,0:T(8,128)(2,1)} custom-call(s32[2]{0:T(128)} %pad_add_fusion.1.scalars, bf16[512,128]{1,0:T(8,128)(2,1)} %bitcast.134, bf16[512,128]{1,0:T(8,128)(2,1)} %bitcast.132, bf16[512,256]{1,0:T(8,128)(2,1)} %space_ref.3, f32[1,8192]{1,0:T(1,128)} %gain_ref.1), custom_call_target="tpu_custom_call" | custom-call | tf_op jit(solution)/shard_map/pallas_call | solution.py:43
  3.8 3.0 %collective-permute-start.2 = (bf16[1280,128]{1,0:T(8,128)(2,1)}, bf16[1280,128]{1,0:T(8,128)(2,1)S(1)}, u32[]{:S(2)}, u32[]{:S(2)}) collective-permute-start(bf16[1280,128]{1,0:T(8,128)(2,1)} %shard_map.85.own_ref.refs_0_), channel_id=1, source_target_pairs={{0,2},{1,3},{2,0},{3,1},{4,6},{5,7},{6,4},{7,5},{8,10},{9,11},{10,... | collective-permute-start | bytes 983048 | tf_op jit(solution)/shard_map/ppermute | solution.py:63
  8.3 2.6 %collective-permute-start = (bf16[1280,128]{1,0:T(8,128)(2,1)}, bf16[1280,128]{1,0:T(8,128)(2,1)S(1)}, u32[]{:S(2)}, u32[]{:S(2)}) collective-permute-start(bf16[1280,128]{1,0:T(8,128)(2,1)} %shard_map.85.own_ref.refs_0_), channel_id=1, source_target_pairs={{0,8},{1,9},{2,10},{3,11},{4,12},{5,13},{6,14},{7,15},{8,0},{9,1},... | collective-permute-start | bytes 983048 | tf_op jit(solution)/shard_map/ppermute | solution.py:63
  10.9 3.8 %collective-permute-done.2.refs_1_ = bf16[1280,128]{1,0:T(8,128)(2,1)S(1)} collective-permute-done((bf16[1280,128]{1,0:T(8,128)(2,1)}, bf16[1280,128]{1,0:T(8,128)(2,1)S(1)}, u32[]{:S(2)}, u32[]{:S(2)}) %collective-permute-start.2) | collective-permute-done | bytes 327712 | tf_op jit(solution)/shard_map/ppermute | solution.py:63
  14.7 8.4 %collective-permute-done.1.refs_2_ = bf16[1280,128]{1,0:T(8,128)(2,1)S(1)} collective-permute-done((bf16[1280,128]{1,0:T(8,128)(2,1)}, bf16[1280,128]{1,0:T(8,128)(2,1)S(1)}, u32[]{:S(2)}, u32[]{:S(2)}) %collective-permute-start.1) | collective-permute-done | bytes 327712 | tf_op jit(solution)/shard_map/ppermute | solution.py:63
  25.4 3.0 %shard_map.86 = (f32[192,256]{1,0:T(8,128)}, f32[192,256]{1,0:T(8,128)}) custom-call(s32[2]{0:T(128)} %pad_add_fusion.2.scalars, bf16[512,128]{1,0:T(8,128)(2,1)} %bitcast.133, bf16[512,256]{1,0:T(8,128)(2,1)} %space_ref.3, bf16[1280,128]{1,0:T(8,128)(2,1)} %shard_map.85.own_ref.refs_0_), custom_call_target="tpu_custom_call" | custom-call | tf_op jit(solution)/shard_map/pallas_call | solution.py:43
  34.3 4.7 %collective-permute-done.7 = f32[192,256]{1,0:T(8,128)S(1)} collective-permute-done((f32[192,256]{1,0:T(8,128)S(1)}, f32[192,256]{1,0:T(8,128)S(1)}, u32[]{:S(2)}, u32[]{:S(2)}) %collective-permute-start.7) | collective-permute-done | bytes 196640 | tf_op jit(solution)/shard_map/ppermute | solution.py:63
  41.1 2.6 %collective-permute-start.18 = (f32[192,256]{1,0:T(8,128)S(1)}, f32[192,256]{1,0:T(8,128)S(1)}, u32[]{:S(2)}, u32[]{:S(2)}) collective-permute-start(f32[192,256]{1,0:T(8,128)S(1)} %add.194), channel_id=1, source_target_pairs={{0,8},{1,9},{2,10},{3,11},{4,12},{5,13},{6,14},{7,15},{8,0},{9,1},... | collective-permute-start | bytes 589832 | tf_op jit(solution)/shard_map/ppermute | solution.py:63
  43.8 3.7 %collective-permute-done.4.refs_6_ = bf16[1280,128]{1,0:T(8,128)(2,1)S(1)} collective-permute-done((bf16[1280,128]{1,0:T(8,128)(2,1)S(1)}, bf16[1280,128]{1,0:T(8,128)(2,1)S(1)}, u32[]{:S(2)}, u32[]{:S(2)}) %collective-permute-start.4) | collective-permute-done | bytes 327712 | tf_op jit(solution)/shard_map/ppermute | solution.py:63
  48.6 3.5 %collective-permute-done.18 = f32[192,256]{1,0:T(8,128)S(1)} collective-permute-done((f32[192,256]{1,0:T(8,128)S(1)}, f32[192,256]{1,0:T(8,128)S(1)}, u32[]{:S(2)}, u32[]{:S(2)}) %collective-permute-start.18) | collective-permute-done | bytes 196640 | tf_op jit(solution)/shard_map/ppermute | solution.py:63
  52.8 5.8 %collective-permute-done.8.refs_0_ = bf16[1280,128]{1,0:T(8,128)(2,1)S(1)} collective-permute-done((bf16[1280,128]{1,0:T(8,128)(2,1)S(1)}, bf16[1280,128]{1,0:T(8,128)(2,1)S(1)}, u32[]{:S(2)}, u32[]{:S(2)}) %collective-permute-start.8) | collective-permute-done | bytes 327712 | tf_op jit(solution)/shard_map/ppermute | solution.py:63
  58.7 2.8 %copy-done = bf16[384,8192]{1,0:T(8,128)(2,1)S(1)} copy-done((bf16[384,8192]{1,0:T(8,128)(2,1)S(1)}, bf16[384,8192]{1,0:T(8,128)(2,1)}, u32[]{:S(2)}) %copy-start) | copy-done | bytes 6291480
  61.4 2.8 %copy-done.3 = bf16[384,8192]{1,0:T(8,128)(2,1)S(1)} copy-done((bf16[384,8192]{1,0:T(8,128)(2,1)S(1)}, bf16[384,8192]{1,0:T(8,128)(2,1)}, u32[]{:S(2)}) %copy-start.3) | copy-done | bytes 6291480
  65.2 5.0 %shard_map.87.refs_2_ = f32[384,768]{1,0:T(8,128)S(1)} custom-call(s32[15]{0:T(128)S(1)} %stack.295.scalars, bf16[384,8192]{1,0:T(8,128)(2,1)S(1)} %copy-done, bf16[384,8192]{1,0:T(8,128)(2,1)S(1)} %copy-done.3, bf16[1280,128]{1,0:T(8,128)(2,1)S(1)} %copy-done.6, bf16[1280,128]{1,0:T(8,128)(2,1)S(1)} %collective-permute-done.2.refs_1_, ...), custom_call_target="tpu_custom_call" | custom-call | flops 3523215360 | tf_op jit(solution)/shard_map/pallas_call | solution.py:43
  75.9 11.8 %collective-permute-done.20.refs_2_ = bf16[192,256]{1,0:T(8,128)(2,1)S(1)} collective-permute-done((bf16[192,256]{1,0:T(8,128)(2,1)S(1)}, bf16[192,256]{1,0:T(8,128)(2,1)S(1)}, u32[]{:S(2)}, u32[]{:S(2)}) %collective-permute-start.20) | collective-permute-done | bytes 98336 | tf_op jit(solution)/shard_map/ppermute | solution.py:63
  89.5 2.8 %copy-done.2 = bf16[384,8192]{1,0:T(8,128)(2,1)S(1)} copy-done((bf16[384,8192]{1,0:T(8,128)(2,1)S(1)}, bf16[384,8192]{1,0:T(8,128)(2,1)}, u32[]{:S(2)}) %copy-start.2) | copy-done | bytes 6291480
  92.3 2.8 %copy-done.5 = bf16[384,8192]{1,0:T(8,128)(2,1)S(1)} copy-done((bf16[384,8192]{1,0:T(8,128)(2,1)S(1)}, bf16[384,8192]{1,0:T(8,128)(2,1)}, u32[]{:S(2)}) %copy-start.5) | copy-done | bytes 6291480
  95.1 4.3 %shard_map.89 = (bf16[384,256]{1,0:T(8,128)(2,1)}, f32[128,256]{1,0:T(8,128)S(1)}, bf16[8,128,256]{2,1,0:T(8,128)(2,1)S(1)}, bf16[8,128,256]{2,1,0:T(8,128)(2,1)...) custom-call(s32[50]{0:T(128)S(1)} %stack.274.scalars, ...), custom_call_target="tpu_custom_call" | custom-call | tf_op jit(solution)/shard_map/pallas_call | solution.py:43
  102.9 5.0 %collective-permute-done.24 = f32[128,256]{1,0:T(8,128)S(1)} collective-permute-done((f32[128,256]{1,0:T(8,128)S(1)}, f32[128,256]{1,0:T(8,128)S(1)}, u32[]{:S(2)}, u32[]{:S(2)}) %collective-permute-start.24) | collective-permute-done | bytes 131104 | tf_op jit(solution)/shard_map/ppermute | solution.py:63
  112.9 4.4 %collective-permute-done.37 = bf16[4,128,256]{2,1,0:T(8,128)(2,1)S(1)} collective-permute-done((bf16[4,128,256]{2,1,0:T(8,128)(2,1)S(1)}, bf16[4,128,256]{2,1,0:T(8,128)(2,1)S(1)}, u32[]{:S(2)}, u32[]{:S(2)}) %collective-permute-start.37) | collective-permute-done | bytes 262176 | tf_op jit(solution)/shard_map/ppermute | solution.py:63
  119.6 3.4 %collective-permute-done.28 = bf16[4,128,256]{2,1,0:T(8,128)(2,1)S(1)} collective-permute-done((bf16[4,128,256]{2,1,0:T(8,128)(2,1)S(1)}, bf16[4,128,256]{2,1,0:T(8,128)(2,1)S(1)}, u32[]{:S(2)}, u32[]{:S(2)}) %collective-permute-start.28) | collective-permute-done | bytes 262176 | tf_op jit(solution)/shard_map/ppermute | solution.py:63
  129.3 3.5 %collective-permute-done.32 = bf16[2,128,256]{2,1,0:T(8,128)(2,1)S(1)} collective-permute-done((bf16[2,128,256]{2,1,0:T(8,128)(2,1)S(1)}, bf16[2,128,256]{2,1,0:T(8,128)(2,1)S(1)}, u32[]{:S(2)}, u32[]{:S(2)}) %collective-permute-start.32) | collective-permute-done | bytes 131104 | tf_op jit(solution)/shard_map/ppermute | solution.py:63
  136.0 2.8 %collective-permute-done.33 = bf16[1,128,256]{2,1,0:T(8,128)(2,1)S(1)} collective-permute-done((bf16[1,128,256]{2,1,0:T(8,128)(2,1)S(1)}, bf16[1,128,256]{2,1,0:T(8,128)(2,1)S(1)}, u32[]{:S(2)}, u32[]{:S(2)}) %collective-permute-start.33) | collective-permute-done | bytes 65568 | tf_op jit(solution)/shard_map/ppermute | solution.py:63
  141.2 2.7 %collective-permute-done.34.refs_2_ = f32[128,256]{1,0:T(8,128)S(1)} collective-permute-done((f32[128,256]{1,0:T(8,128)S(1)}, f32[128,256]{1,0:T(8,128)S(1)}, u32[]{:S(2)}, u32[]{:S(2)}) %collective-permute-start.34) | collective-permute-done | bytes 131104 | tf_op jit(solution)/shard_map/ppermute | solution.py:63
  (113 shorter events, 47.1 us)
Async XLA Ops:
  3.8 10.9 %collective-permute-start.2 = (bf16[1280,128]{1,0:T(8,128)(2,1)}, bf16[1280,128]{1,0:T(8,128)(2,1)S(1)}, u32[]{:S(2)}, u32[]{:S(2)}) collective-permute-start(bf16[1280,128]{1,0:T(8,128)(2,1)} %shard_map.85.own_ref.refs_0_), channel_id=1, source_target_pairs={{0,2},{1,3},{2,0},{3,1},{4,6},{5,7},{6,4},{7,5},{8,10},{9,11},{10,... | collective-permute-start | bytes 983048 | tf_op jit(solution)/shard_map/ppermute | solution.py:63
  6.8 16.3 %collective-permute-start.1 = (bf16[1280,128]{1,0:T(8,128)(2,1)}, bf16[1280,128]{1,0:T(8,128)(2,1)S(1)}, u32[]{:S(2)}, u32[]{:S(2)}) collective-permute-start(bf16[1280,128]{1,0:T(8,128)(2,1)} %shard_map.85.own_ref.refs_0_), channel_id=1, source_target_pairs={{0,4},{1,5},{2,6},{3,7},{4,0},{5,1},{6,2},{7,3},{8,12},{9,13},{10,... | collective-permute-start | bytes 983048 | tf_op jit(solution)/shard_map/ppermute | solution.py:63
  8.3 17.1 %collective-permute-start = (bf16[1280,128]{1,0:T(8,128)(2,1)}, bf16[1280,128]{1,0:T(8,128)(2,1)S(1)}, u32[]{:S(2)}, u32[]{:S(2)}) collective-permute-start(bf16[1280,128]{1,0:T(8,128)(2,1)} %shard_map.85.own_ref.refs_0_), channel_id=1, source_target_pairs={{0,8},{1,9},{2,10},{3,11},{4,12},{5,13},{6,14},{7,15},{8,0},{9,1},... | collective-permute-start | bytes 983048 | tf_op jit(solution)/shard_map/ppermute | solution.py:63
  31.7 9.5 %collective-permute-start.5 = (bf16[1280,128]{1,0:T(8,128)(2,1)S(1)}, bf16[1280,128]{1,0:T(8,128)(2,1)S(1)}, u32[]{:S(2)}, u32[]{:S(2)}) collective-permute-start(bf16[1280,128]{1,0:T(8,128)(2,1)S(1)} %collective-permute-done.refs_4_), channel_id=1, source_target_pairs={{0,2},{1,3},{2,0},{3,1},{4,6},{5,7},{6,4},{7,5},{8,10},{9,11},{10,... | collective-permute-start | bytes 983048 | tf_op jit(solution)/shard_map/ppermute | solution.py:63
  32.2 15.3 %collective-permute-start.4 = (bf16[1280,128]{1,0:T(8,128)(2,1)S(1)}, bf16[1280,128]{1,0:T(8,128)(2,1)S(1)}, u32[]{:S(2)}, u32[]{:S(2)}) collective-permute-start(bf16[1280,128]{1,0:T(8,128)(2,1)S(1)} %collective-permute-done.refs_4_), channel_id=1, source_target_pairs={{0,4},{1,5},{2,6},{3,7},{4,0},{5,1},{6,2},{7,3},{8,12},{9,13},{10,... | collective-permute-start | bytes 983048 | tf_op jit(solution)/shard_map/ppermute | solution.py:63
  33.8 13.8 %collective-permute-start.10 = (bf16[1280,128]{1,0:T(8,128)(2,1)}, bf16[1280,128]{1,0:T(8,128)(2,1)S(1)}, u32[]{:S(2)}, u32[]{:S(2)}) collective-permute-start(bf16[1280,128]{1,0:T(8,128)(2,1)} %shard_map.85.own_ref.refs_0_), channel_id=1, source_target_pairs={{0,1},{1,0},{2,3},{3,2},{4,5},{5,4},{6,7},{7,6},{8,9},{9,8},{10,11... | collective-permute-start | bytes 983048 | tf_op jit(solution)/shard_map/ppermute | solution.py:63
  33.8 14.3 %collective-permute-start.11 = (bf16[1280,128]{1,0:T(8,128)(2,1)S(1)}, bf16[1280,128]{1,0:T(8,128)(2,1)S(1)}, u32[]{:S(2)}, u32[]{:S(2)}) collective-permute-start(bf16[1280,128]{1,0:T(8,128)(2,1)S(1)} %collective-permute-done.2.refs_1_), channel_id=1, source_target_pairs={{0,1},{1,0},{2,3},{3,2},{4,5},{5,4},{6,7},{7,6},{8,9},{9,8},{10,11... | collective-permute-start | bytes 983048 | tf_op jit(solution)/shard_map/ppermute | solution.py:63
  39.0 9.6 %collective-permute-start.12 = (bf16[1280,128]{1,0:T(8,128)(2,1)S(1)}, bf16[1280,128]{1,0:T(8,128)(2,1)S(1)}, u32[]{:S(2)}, u32[]{:S(2)}) collective-permute-start(bf16[1280,128]{1,0:T(8,128)(2,1)S(1)} %collective-permute-done.1.refs_2_), channel_id=1, source_target_pairs={{0,1},{1,0},{2,3},{3,2},{4,5},{5,4},{6,7},{7,6},{8,9},{9,8},{10,11... | collective-permute-start | bytes 983048 | tf_op jit(solution)/shard_map/ppermute | solution.py:63
  41.1 11.0 %collective-permute-start.18 = (f32[192,256]{1,0:T(8,128)S(1)}, f32[192,256]{1,0:T(8,128)S(1)}, u32[]{:S(2)}, u32[]{:S(2)}) collective-permute-start(f32[192,256]{1,0:T(8,128)S(1)} %add.194), channel_id=1, source_target_pairs={{0,8},{1,9},{2,10},{3,11},{4,12},{5,13},{6,14},{7,15},{8,0},{9,1},... | collective-permute-start | bytes 589832 | tf_op jit(solution)/shard_map/ppermute | solution.py:63
  47.5 11.1 %collective-permute-start.13 = (bf16[1280,128]{1,0:T(8,128)(2,1)S(1)}, bf16[1280,128]{1,0:T(8,128)(2,1)S(1)}, u32[]{:S(2)}, u32[]{:S(2)}) collective-permute-start(bf16[1280,128]{1,0:T(8,128)(2,1)S(1)} %collective-permute-done.3.refs_3_), channel_id=1, source_target_pairs={{0,1},{1,0},{2,3},{3,2},{4,5},{5,4},{6,7},{7,6},{8,9},{9,8},{10,11... | collective-permute-start | bytes 983048 | tf_op jit(solution)/shard_map/ppermute | solution.py:63
  48.1 10.6 %collective-permute-start.8 = (bf16[1280,128]{1,0:T(8,128)(2,1)S(1)}, bf16[1280,128]{1,0:T(8,128)(2,1)S(1)}, u32[]{:S(2)}, u32[]{:S(2)}) collective-permute-start(bf16[1280,128]{1,0:T(8,128)(2,1)S(1)} %collective-permute-done.4.refs_6_), channel_id=1, source_target_pairs={{0,2},{1,3},{2,0},{3,1},{4,6},{5,7},{6,4},{7,5},{8,10},{9,11},{10,... | collective-permute-start | bytes 983048 | tf_op jit(solution)/shard_map/ppermute | solution.py:63
  48.6 10.0 %collective-permute-start.15 = (bf16[1280,128]{1,0:T(8,128)(2,1)S(1)}, bf16[1280,128]{1,0:T(8,128)(2,1)S(1)}, u32[]{:S(2)}, u32[]{:S(2)}) collective-permute-start(bf16[1280,128]{1,0:T(8,128)(2,1)S(1)} %collective-permute-done.5.refs_5_), channel_id=1, source_target_pairs={{0,1},{1,0},{2,3},{3,2},{4,5},{5,4},{6,7},{7,6},{8,9},{9,8},{10,11... | collective-permute-start | bytes 983048 | tf_op jit(solution)/shard_map/ppermute | solution.py:63
  52.2 21.2 %collective-permute-start.19 = (bf16[192,256]{1,0:T(8,128)(2,1)S(1)}, bf16[192,256]{1,0:T(8,128)(2,1)S(1)}, u32[]{:S(2)}, u32[]{:S(2)}) collective-permute-start(bf16[192,256]{1,0:T(8,128)(2,1)S(1)} %get-tuple-element.51), channel_id=1, source_target_pairs={{0,2},{1,3},{2,0},{3,1},{4,6},{5,7},{6,4},{7,5},{8,10},{9,11},{10,... | collective-permute-start | bytes 294920 | tf_op jit(solution)/shard_map/ppermute | solution.py:63
  58.6 11.6 %collective-permute-start.9 = (bf16[1280,128]{1,0:T(8,128)(2,1)S(1)}, bf16[1280,128]{1,0:T(8,128)(2,1)S(1)}, u32[]{:S(2)}, u32[]{:S(2)}) collective-permute-start(bf16[1280,128]{1,0:T(8,128)(2,1)S(1)} %collective-permute-done.8.refs_0_), channel_id=1, source_target_pairs={{0,1},{1,0},{2,3},{3,2},{4,5},{5,4},{6,7},{7,6},{8,9},{9,8},{10,11... | collective-permute-start | bytes 983048 | tf_op jit(solution)/shard_map/ppermute | solution.py:63
  71.6 17.9 %collective-permute-start.17 = (bf16[384,640]{1,0:T(8,128)(2,1)S(1)}, bf16[384,640]{1,0:T(8,128)(2,1)S(1)}, u32[]{:S(2)}, u32[]{:S(2)}) collective-permute-start(bf16[384,640]{1,0:T(8,128)(2,1)S(1)} %get-tuple-element.33), channel_id=1, source_target_pairs={{0,16},{16,0},{1,17},{17,1},{2,18},{18,2},{3,19},{19,3},{4,20},{20... | collective-permute-start | bytes 1474568 | tf_op jit(solution)/shard_map/ppermute | solution.py:63
  73.7 14.1 %collective-permute-start.20 = (bf16[192,256]{1,0:T(8,128)(2,1)S(1)}, bf16[192,256]{1,0:T(8,128)(2,1)S(1)}, u32[]{:S(2)}, u32[]{:S(2)}) collective-permute-start(bf16[192,256]{1,0:T(8,128)(2,1)S(1)} %get-tuple-element.49), channel_id=1, source_target_pairs={{0,16},{16,0},{1,17},{17,1},{2,18},{18,2},{3,19},{19,3},{4,20},{20... | collective-permute-start | bytes 294920 | tf_op jit(solution)/shard_map/ppermute | solution.py:63
  74.9 14.6 %collective-permute-start.22 = (bf16[192,256]{1,0:T(8,128)(2,1)S(1)}, bf16[192,256]{1,0:T(8,128)(2,1)S(1)}, u32[]{:S(2)}, u32[]{:S(2)}) collective-permute-start(bf16[192,256]{1,0:T(8,128)(2,1)S(1)} %convert_element_type.136), channel_id=1, source_target_pairs={{0,16},{16,0},{1,17},{17,1},{2,18},{18,2},{3,19},{19,3},{4,20},{20... | collective-permute-start | bytes 294920 | tf_op jit(solution)/shard_map/ppermute | solution.py:63
  108.0 9.3 %collective-permute-start.37 = (bf16[4,128,256]{2,1,0:T(8,128)(2,1)S(1)}, bf16[4,128,256]{2,1,0:T(8,128)(2,1)S(1)}, u32[]{:S(2)}, u32[]{:S(2)}) collective-permute-start(bf16[4,128,256]{2,1,0:T(8,128)(2,1)S(1)} %add_convert_fusion), channel_id=1, source_target_pairs={{0,2},{1,3},{2,0},{3,1},{4,6},{5,7},{6,4},{7,5},{8,10},{9,11},{10,... | collective-permute-start | bytes 786440 | tf_op jit(solution)/shard_map/ppermute | solution.py:63
  108.7 14.3 %collective-permute-start.28 = (bf16[4,128,256]{2,1,0:T(8,128)(2,1)S(1)}, bf16[4,128,256]{2,1,0:T(8,128)(2,1)S(1)}, u32[]{:S(2)}, u32[]{:S(2)}) collective-permute-start(bf16[4,128,256]{2,1,0:T(8,128)(2,1)S(1)} %add_convert_fusion.2), channel_id=1, source_target_pairs={{0,2},{1,3},{2,0},{3,1},{4,6},{5,7},{6,4},{7,5},{8,10},{9,11},{10,... | collective-permute-start | bytes 786440 | tf_op jit(solution)/shard_map/ppermute | solution.py:63
  110.3 16.5 %collective-permute-start.31 = (bf16[4,128,256]{2,1,0:T(8,128)(2,1)S(1)}, bf16[4,128,256]{2,1,0:T(8,128)(2,1)S(1)}, u32[]{:S(2)}, u32[]{:S(2)}) collective-permute-start(bf16[4,128,256]{2,1,0:T(8,128)(2,1)S(1)} %add_convert_fusion.1), channel_id=1, source_target_pairs={{0,2},{1,3},{2,0},{3,1},{4,6},{5,7},{6,4},{7,5},{8,10},{9,11},{10,... | collective-permute-start | bytes 786440 | tf_op jit(solution)/shard_map/ppermute | solution.py:63
  117.5 11.3 %collective-permute-start.38 = (bf16[2,128,256]{2,1,0:T(8,128)(2,1)S(1)}, bf16[2,128,256]{2,1,0:T(8,128)(2,1)S(1)}, u32[]{:S(2)}, u32[]{:S(2)}) collective-permute-start(bf16[2,128,256]{2,1,0:T(8,128)(2,1)S(1)} %fusion.8), channel_id=1, source_target_pairs={{0,4},{1,5},{2,6},{3,7},{4,0},{5,1},{6,2},{7,3},{8,12},{9,13},{10,... | collective-permute-start | bytes 393224 | tf_op jit(solution)/shard_map/ppermute | solution.py:63
  123.1 12.2 %collective-permute-start.35 = (bf16[2,128,256]{2,1,0:T(8,128)(2,1)S(1)}, bf16[2,128,256]{2,1,0:T(8,128)(2,1)S(1)}, u32[]{:S(2)}, u32[]{:S(2)}) collective-permute-start(bf16[2,128,256]{2,1,0:T(8,128)(2,1)S(1)} %fusion.7), channel_id=1, source_target_pairs={{0,4},{1,5},{2,6},{3,7},{4,0},{5,1},{6,2},{7,3},{8,12},{9,13},{10,... | collective-permute-start | bytes 393224 | tf_op jit(solution)/shard_map/ppermute | solution.py:63
  125.2 15.4 %collective-permute-start.29 = (f32[128,256]{1,0:T(8,128)S(1)}, f32[128,256]{1,0:T(8,128)S(1)}, u32[]{:S(2)}, u32[]{:S(2)}) collective-permute-start(f32[128,256]{1,0:T(8,128)S(1)} %add.199.refs_0_), channel_id=1, source_target_pairs={{0,8},{1,9},{2,10},{3,11},{4,12},{5,13},{6,14},{7,15},{8,0},{9,1},... | collective-permute-start | bytes 393224 | tf_op jit(solution)/shard_map/ppermute | solution.py:63
  128.8 11.8 %collective-permute-start.39 = (bf16[1,128,256]{2,1,0:T(8,128)(2,1)S(1)}, bf16[1,128,256]{2,1,0:T(8,128)(2,1)S(1)}, u32[]{:S(2)}, u32[]{:S(2)}) collective-permute-start(bf16[1,128,256]{2,1,0:T(8,128)(2,1)S(1)} %fusion.12), channel_id=1, source_target_pairs={{0,8},{1,9},{2,10},{3,11},{4,12},{5,13},{6,14},{7,15},{8,0},{9,1},... | collective-permute-start | bytes 196616 | tf_op jit(solution)/shard_map/ppermute | solution.py:63
  (26 other events, 247.0 us)

commit v8 on v7

--- a/solution.py
+++ b/solution.py
@@ -190,7 +190,7 @@
     return whole[:rank], whole[rank : 2 * rank], whole[2 * rank :]
 
 
-def chain_kernel(sections, width, scalars, base_ref, cot_ref, own, *refs):
+def chain_kernel(sections, width, scalars, base_far, cot_far, own, *refs):
     here, core = scalars[0], scalars[1]
     n = 1 if sections == 2 else sections
     thin_count = 1 if sections == 2 else 2
@@ -199,6 +199,12 @@
     sent, keeps, others = take(n), take(n + 1), take(n + 1)
     codes_ref, thin_refs = take(1)[0], take(thin_count)
     outs_c, outs_b = take(2), take(4)
+    base_ref, cot_ref, sems = refs
+    count = sems.shape[0] // 2
+    step = base_ref.shape[0] // count
+    slices = [slice(k * step, (k + 1) * step) for k in range(count)]
+    cot_copies = fetch([(cot_far.at[k], cot_ref.at[k]) for k in slices], sems)
+    base_copies = fetch([(base_far.at[k], base_ref.at[k]) for k in slices], sems, count)
     rank = own.shape[1] // 6
     last = sections - 1
     values = [
@@ -238,6 +244,8 @@
         state.append((m_s, q_t, inner, logistic, inverse, active, resid_s, before))
     codes_ref[...] = mine_code
     active_t = state[last][5].T.astype(BF16)
+    for copy in cot_copies:
+        copy.wait()
     outer_into(scalars, 2, active_t, cot_ref, outs_c)
 
     grad_active, grad_y = column(last, 3), spread(3)
@@ -263,6 +271,8 @@
     else:
         thin_refs[0][...] = jnp.where(here == 0, 0.0, thin_in)
         thin_refs[1][...] = thin_out
+    for copy in base_copies:
+        copy.wait()
     outer_into(scalars, 2 + 2 * outs_c[0].shape[0], mine, base_ref, outs_b)
 
 
@@ -316,7 +326,7 @@
             waits = waits[1:]
         arrived = swap(give, bit)
         if left.shape[0] == 1:
-            return (left[0, 0], arrived[0]), got_x
+            return (left[0, 0], arrived[0]), got_x, total
         total = left[:, 0] + arrived.astype(F32)
         bit *= 2
 
@@ -345,17 +355,18 @@
     peers = lax.axis_size("dp")
     order = sorted(range(4, peers, 4), key=lambda m: (m.bit_count(), m))
     shards = {0: own}
-    for m in order:
+    shards[2] = swap(own, 2)
+    for k, m in enumerate(order):
         if m.bit_count() == 1:
-            shards[m] = swap(own, m)
-    shards[2] = swap(own, 2)
-
+            shards[m] = swap(after(own, shards[order[k - 1]]) if k else own, m)
+
+    shards[order[0] ^ 2] = swap(after(shards[order[0]], shards[2]), 2)
     tall = (3 * rank, size)
     keep, give = call(
         small_kernel,
         [flag, core],
         [own_out, subspace],
-        [after(own, shards[peers // 2])],
+        [after(own, shards[order[0] ^ 2])],
         [((tall[0] // 2, size), F32)] * 2,
         [
             pltpu.VMEM((part, rank), BF16),
@@ -366,6 +377,7 @@
         60 * 1024 * 1024,
     )
     small = keep + swap(give, 1)
+    small = small + swap(small.astype(BF16), 2).astype(F32)
     bit = 4
     while bit < peers // 2:
         small = small + swap(small, bit)
@@ -377,11 +389,11 @@
         low = m & -m
         if m != low:
             shards[m] = swap(after(shards[m ^ low], shards[order[k - 2] ^ 2]), low)
-        before = shards[order[k - 1] ^ 2] if k else shards[2]
-        shards[m ^ 2] = swap(after(shards[m], before, *([small] if m ^ 2 == ends else [])), 2)
+        if k:
+            ties = [small] if m ^ 2 == ends else []
+            shards[m ^ 2] = swap(after(shards[m], shards[order[k - 1] ^ 2], *ties), 2)
     small = after(small, shards[peers // 2])
     small = small + swap(small, peers // 2)
-    small = small + swap(small.astype(BF16), 2).astype(F32)
     small_other = swap(small, 1)
     keeps = [small, *from_sections(small.astype(BF16))]
     others = [small_other, *from_sections(small_other.astype(BF16))]
@@ -391,7 +403,7 @@
         shards[m ^ 1] = swap(shards[m], 1)
     marks += [m ^ 1 for m in marks]
     acc = project([spot ^ m for m in marks], flag, [shards[m] for m in marks], tokens)[0]
-    pair = [shards[ends], swap(shards[ends], 1)]
+    pair = [shards[ends], swap(after(shards[ends], acc), 1)]
     acc, send = project([spot ^ ends, spot ^ ends ^ 1], flag, pair, tokens, acc, final=True)
     sent = from_sections(send)
 
@@ -410,24 +422,29 @@
     codes, *rest = call(
         functools.partial(chain_kernel, sections, width),
         [here, core, *out_ids, *in_ids],
-        [],
-        [base, cotangent, acc, *sent, *keeps, *others],
+        [base, cotangent],
+        [acc, *sent, *keeps, *others],
         [((rows, size), BF16)]
         + [((rank, size), F32)] * thin_count
         + [blocks(columns)] * 2
         + [blocks(half)] * 4,
-        vmem_bytes=(VMEM_BYTES if sections == 2 else 32 * 1024 * 1024),
+        [
+            pltpu.VMEM(base.shape, BF16),
+            pltpu.VMEM(base.shape, BF16),
+            pltpu.SemaphoreType.DMA((8,)),
+        ],
+        50 * 1024 * 1024,
     )
     thins, chunks = rest[:thin_count], rest[thin_count:]
     got = [swap(give, 1) for give in chunks[::2]]
-    lower, lower_x = scatter_sum(got[1], chunks[3])
-    upper, upper_x = scatter_sum(got[2], chunks[5])
-    sum_out, _ = scatter_sum(got[0], chunks[1], [got[1:], [lower_x], [upper_x]])
+    sum_out, out_x, out_near = scatter_sum(got[0], chunks[1])
+    lower, lower_x, _ = scatter_sum(got[1], chunks[3], [[out_x]])
+    upper, _, _ = scatter_sum(got[2], chunks[5], [[out_near]])
     sum_out = sum_out[0] + sum_out[1].astype(F32)
     ends_out = [sum_out]
     if sections == 2:
         ends_out = [swap(sum_out, 1, "section"), sum_out]
-    waits = [None, got[2], lower_x]
+    waits = [got[2], out_x, lower_x]
     terms = [term for thin in thins for term in sum_thin(thin, waits)]
     grad_in, grad_out = call(
         functools.partial(end_kernel, sections),

time: 146 us -> 166 us (1.14)
  starting transfers between devices: 33.7 us -> 41.3 us
  local copies, waits for them, and re-layouts: 12.4 us -> 18.6 us
  Pallas kernels: 18 us -> 23 us
  other arithmetic: 2.98 us -> 6.57 us
  waiting for transfers between devices: 77.5 us -> 74.8 us
    ppermute x40, starting transfers between devices: 33.7 us -> 41.3 us  [swap(): return lax.ppermute(value, axis, [(i, i ^ bits) for i in range(peers)])]
    unnamed x20 -> x34, local copies, waits for them, and re-layouts: 12.1 us -> 18.2 us
    pallas_call x6, Pallas kernels: 18 us -> 23 us  [call(): pl.pallas_call(kernel, in_specs=[IN_SMEM] + [IN_HBM] * len(far) + [IN_VME...]
    ppermute x40, waiting for transfers between devices: 77.5 us -> 74.8 us  [swap(): return lax.ppermute(value, axis, [(i, i ^ bits) for i in range(peers)])]
  transfers between devices with their start and end apart: 40 -> 40, of which waited for: 22 -> 17; matrix products, arithmetic and copies ran while one was open for 2% -> 4% of each run, Pallas kernels for 6% -> 4%
where the time goes in v8:
time: 166 us; the launch traced here: 165 us
  waiting for transfers between devices  74.8 us (45%)
  starting transfers between devices  41.3 us (25%)
  Pallas kernels  23 us (14%)
  local copies, waits for them, and re-layouts  18.6 us (11%)
  other arithmetic  6.57 us (4%)
    ppermute x40, waiting for transfers between devices, swap(): return lax.ppermute(value, axis, [(i, i ^ bits) for i in range(peers)])  74.8 us
    ppermute x40, starting transfers between devices, swap(): return lax.ppermute(value, axis, [(i, i ^ bits) for i in range(peers)])  41.3 us
    pallas_call x6, Pallas kernels, call(): pl.pallas_call(kernel, in_specs=[IN_SMEM] + [IN_HBM] * len(far) + [IN_VME...  23 us
    unnamed x34, local copies, waits for them, and re-layouts  18.2 us
  transfers between devices with their start and end apart: 40, of which 17 were waited for; matrix products, arithmetic and copies ran while one was open for 4% of the time, Pallas kernels for 4%

profile of v8, /device:TPU:0, one launch (start us, length us, event | category | flops | bytes accessed | tf_op | source)
XLA Modules:
  0.0 165.1 jit_solution(4346593186281712666)
XLA Ops:
  1.3 2.6 %shard_map.85.own_ref.refs_0_ = bf16[1280,128]{1,0:T(8,128)(2,1)} custom-call(s32[2]{0:T(128)} %pad_add_fusion.1.scalars, bf16[512,128]{1,0:T(8,128)(2,1)} %bitcast.133, bf16[512,128]{1,0:T(8,128)(2,1)} %bitcast.131, bf16[512,256]{1,0:T(8,128)(2,1)} %space_ref.3, f32[1,8192]{1,0:T(1,128)} %gain_ref.1), custom_call_target="tpu_custom_call" | custom-call | tf_op jit(solution)/shard_map/pallas_call | solution.py:43
  3.9 3.0 %collective-permute-start.2 = (bf16[1280,128]{1,0:T(8,128)(2,1)}, bf16[1280,128]{1,0:T(8,128)(2,1)S(1)}, u32[]{:S(2)}, u32[]{:S(2)}) collective-permute-start(bf16[1280,128]{1,0:T(8,128)(2,1)} %shard_map.85.own_ref.refs_0_), channel_id=1, source_target_pairs={{0,2},{1,3},{2,0},{3,1},{4,6},{5,7},{6,4},{7,5},{8,10},{9,11},{10,... | collective-permute-start | bytes 983048 | tf_op jit(solution)/shard_map/ppermute | solution.py:63
  8.5 6.3 %collective-permute-done.2.refs_1_ = bf16[1280,128]{1,0:T(8,128)(2,1)S(1)} collective-permute-done((bf16[1280,128]{1,0:T(8,128)(2,1)}, bf16[1280,128]{1,0:T(8,128)(2,1)S(1)}, u32[]{:S(2)}, u32[]{:S(2)}) %collective-permute-start.2) | collective-permute-done | bytes 327712 | tf_op jit(solution)/shard_map/ppermute | solution.py:63
  17.2 7.3 %collective-permute-done.3.refs_3_ = bf16[1280,128]{1,0:T(8,128)(2,1)S(1)} collective-permute-done((bf16[1280,128]{1,0:T(8,128)(2,1)S(1)}, bf16[1280,128]{1,0:T(8,128)(2,1)S(1)}, u32[]{:S(2)}, u32[]{:S(2)}) %collective-permute-start.3) | collective-permute-done | bytes 327712 | tf_op jit(solution)/shard_map/ppermute | solution.py:63
  24.5 3.0 %shard_map.86 = (f32[192,256]{1,0:T(8,128)}, f32[192,256]{1,0:T(8,128)}) custom-call(s32[2]{0:T(128)} %pad_add_fusion.2.scalars, bf16[512,128]{1,0:T(8,128)(2,1)} %bitcast.132, bf16[512,256]{1,0:T(8,128)(2,1)} %space_ref.3, bf16[1280,128]{1,0:T(8,128)(2,1)} %shard_map.85.own_ref.refs_0_), custom_call_target="tpu_custom_call" | custom-call | tf_op jit(solution)/shard_map/pallas_call | solution.py:43
  27.6 2.7 %collective-permute-start.1 = (bf16[1280,128]{1,0:T(8,128)(2,1)}, bf16[1280,128]{1,0:T(8,128)(2,1)S(1)}, u32[]{:S(2)}, u32[]{:S(2)}) collective-permute-start(bf16[1280,128]{1,0:T(8,128)(2,1)} %shard_map.85.own_ref.refs_0_), channel_id=1, source_target_pairs={{0,8},{1,9},{2,10},{3,11},{4,12},{5,13},{6,14},{7,15},{8,0},{9,1},... | collective-permute-start | bytes 983048 | tf_op jit(solution)/shard_map/ppermute | solution.py:63
  32.4 13.5 %collective-permute-done.1.refs_4_ = bf16[1280,128]{1,0:T(8,128)(2,1)S(1)} collective-permute-done((bf16[1280,128]{1,0:T(8,128)(2,1)}, bf16[1280,128]{1,0:T(8,128)(2,1)S(1)}, u32[]{:S(2)}, u32[]{:S(2)}) %collective-permute-start.1) | collective-permute-done | bytes 327712 | tf_op jit(solution)/shard_map/ppermute | solution.py:63
  49.3 5.9 %collective-permute-done.5.refs_5_ = bf16[1280,128]{1,0:T(8,128)(2,1)S(1)} collective-permute-done((bf16[1280,128]{1,0:T(8,128)(2,1)S(1)}, bf16[1280,128]{1,0:T(8,128)(2,1)S(1)}, u32[]{:S(2)}, u32[]{:S(2)}) %collective-permute-start.5) | collective-permute-done | bytes 327712 | tf_op jit(solution)/shard_map/ppermute | solution.py:63
  55.2 2.1 %collective-permute-done.4.refs_6_ = bf16[1280,128]{1,0:T(8,128)(2,1)S(1)} collective-permute-done((bf16[1280,128]{1,0:T(8,128)(2,1)S(1)}, bf16[1280,128]{1,0:T(8,128)(2,1)S(1)}, u32[]{:S(2)}, u32[]{:S(2)}) %collective-permute-start.4) | collective-permute-done | bytes 327712 | tf_op jit(solution)/shard_map/ppermute | solution.py:63
  57.3 2.6 %collective-permute-done.8 = f32[192,256]{1,0:T(8,128)S(1)} collective-permute-done((f32[192,256]{1,0:T(8,128)S(1)}, f32[192,256]{1,0:T(8,128)S(1)}, u32[]{:S(2)}, u32[]{:S(2)}) %collective-permute-start.8) | collective-permute-done | bytes 196640 | tf_op jit(solution)/shard_map/ppermute | solution.py:63
  65.0 2.8 %copy-done = bf16[384,8192]{1,0:T(8,128)(2,1)S(1)} copy-done((bf16[384,8192]{1,0:T(8,128)(2,1)S(1)}, bf16[384,8192]{1,0:T(8,128)(2,1)}, u32[]{:S(2)}) %copy-start) | copy-done | bytes 6291480
  67.8 2.8 %copy-done.2 = bf16[384,8192]{1,0:T(8,128)(2,1)S(1)} copy-done((bf16[384,8192]{1,0:T(8,128)(2,1)S(1)}, bf16[384,8192]{1,0:T(8,128)(2,1)}, u32[]{:S(2)}) %copy-start.2) | copy-done | bytes 6291480
  74.5 5.6 %shard_map.87.refs_2_ = f32[384,768]{1,0:T(8,128)S(1)} custom-call(s32[15]{0:T(128)S(1)} %stack.295.scalars, bf16[384,8192]{1,0:T(8,128)(2,1)S(1)} %copy-done, bf16[384,8192]{1,0:T(8,128)(2,1)S(1)} %copy-done.2, bf16[1280,128]{1,0:T(8,128)(2,1)S(1)} %copy-done.4, bf16[1280,128]{1,0:T(8,128)(2,1)S(1)} %collective-permute-done.2.refs_1_, ...), custom_call_target="tpu_custom_call" | custom-call | flops 3523215360 | tf_op jit(solution)/shard_map/pallas_call | solution.py:43
  80.4 2.7 %collective-permute-start.19 = (f32[192,256]{1,0:T(8,128)}, f32[192,256]{1,0:T(8,128)}, u32[]{:S(2)}, u32[]{:S(2)}) collective-permute-start(f32[192,256]{1,0:T(8,128)} %add.195), channel_id=1, source_target_pairs={{0,8},{1,9},{2,10},{3,11},{4,12},{5,13},{6,14},{7,15},{8,0},{9,1},... | collective-permute-start | bytes 589832 | tf_op jit(solution)/shard_map/ppermute | solution.py:63
  83.2 2.8 %copy-done.1 = bf16[384,8192]{1,0:T(8,128)(2,1)S(1)} copy-done((bf16[384,8192]{1,0:T(8,128)(2,1)S(1)}, bf16[384,8192]{1,0:T(8,128)(2,1)}, u32[]{:S(2)}) %copy-start.1) | copy-done | bytes 6291480
  86.0 2.8 %copy-done.3 = bf16[384,8192]{1,0:T(8,128)(2,1)S(1)} copy-done((bf16[384,8192]{1,0:T(8,128)(2,1)S(1)}, bf16[384,8192]{1,0:T(8,128)(2,1)}, u32[]{:S(2)}) %copy-start.3) | copy-done | bytes 6291480
  97.5 10.3 %collective-permute-done.20.refs_2_ = bf16[192,256]{1,0:T(8,128)(2,1)S(1)} collective-permute-done((bf16[192,256]{1,0:T(8,128)(2,1)S(1)}, bf16[192,256]{1,0:T(8,128)(2,1)S(1)}, u32[]{:S(2)}, u32[]{:S(2)}) %collective-permute-start.20) | collective-permute-done | bytes 98336 | tf_op jit(solution)/shard_map/ppermute | solution.py:63
  109.0 8.1 %shard_map.89 = (bf16[384,256]{1,0:T(8,128)(2,1)}, f32[128,256]{1,0:T(8,128)S(1)}, bf16[8,128,256]{2,1,0:T(8,128)(2,1)S(1)}, bf16[8,128,256]{2,1,0:T(8,128)(2,1)...) custom-call(s32[50]{0:T(128)S(1)} %stack.274.scalars, ...), custom_call_target="tpu_custom_call" | custom-call | tf_op jit(solution)/shard_map/pallas_call | solution.py:43
  126.6 5.6 %collective-permute-done.27 = bf16[4,128,256]{2,1,0:T(8,128)(2,1)S(1)} collective-permute-done((bf16[4,128,256]{2,1,0:T(8,128)(2,1)S(1)}, bf16[4,128,256]{2,1,0:T(8,128)(2,1)S(1)}, u32[]{:S(2)}, u32[]{:S(2)}) %collective-permute-start.27) | collective-permute-done | bytes 262176 | tf_op jit(solution)/shard_map/ppermute | solution.py:63
  134.4 8.2 %collective-permute-done.30 = bf16[4,128,256]{2,1,0:T(8,128)(2,1)S(1)} collective-permute-done((bf16[4,128,256]{2,1,0:T(8,128)(2,1)S(1)}, bf16[4,128,256]{2,1,0:T(8,128)(2,1)S(1)}, u32[]{:S(2)}, u32[]{:S(2)}) %collective-permute-start.30) | collective-permute-done | bytes 262176 | tf_op jit(solution)/shard_map/ppermute | solution.py:63
  148.0 2.4 %collective-permute-start.38 = (bf16[2,128,256]{2,1,0:T(8,128)(2,1)S(1)}, bf16[2,128,256]{2,1,0:T(8,128)(2,1)S(1)}, u32[]{:S(2)}, u32[]{:S(2)}) collective-permute-start(bf16[2,128,256]{2,1,0:T(8,128)(2,1)S(1)} %fusion.7), channel_id=1, source_target_pairs={{0,4},{1,5},{2,6},{3,7},{4,0},{5,1},{6,2},{7,3},{8,12},{9,13},{10,... | collective-permute-start | bytes 393224 | tf_op jit(solution)/shard_map/ppermute | solution.py:63
  150.4 1.9 %collective-permute-start.36 = (bf16[1,128,256]{2,1,0:T(8,128)(2,1)S(1)}, bf16[1,128,256]{2,1,0:T(8,128)(2,1)S(1)}, u32[]{:S(2)}, u32[]{:S(2)}) collective-permute-start(bf16[1,128,256]{2,1,0:T(8,128)(2,1)S(1)} %fusion.10), channel_id=1, source_target_pairs={{0,8},{1,9},{2,10},{3,11},{4,12},{5,13},{6,14},{7,15},{8,0},{9,1},... | collective-permute-start | bytes 196616 | tf_op jit(solution)/shard_map/ppermute | solution.py:63
  157.1 2.7 %collective-permute-done.36 = bf16[1,128,256]{2,1,0:T(8,128)(2,1)S(1)} collective-permute-done((bf16[1,128,256]{2,1,0:T(8,128)(2,1)S(1)}, bf16[1,128,256]{2,1,0:T(8,128)(2,1)S(1)}, u32[]{:S(2)}, u32[]{:S(2)}) %collective-permute-start.36) | collective-permute-done | bytes 65568 | tf_op jit(solution)/shard_map/ppermute | solution.py:63
  159.8 2.9 %collective-permute-done.31.refs_1_ = f32[128,256]{1,0:T(8,128)S(1)} collective-permute-done((f32[128,256]{1,0:T(8,128)S(1)}, f32[128,256]{1,0:T(8,128)S(1)}, u32[]{:S(2)}, u32[]{:S(2)}) %collective-permute-start.31) | collective-permute-done | bytes 131104 | tf_op jit(solution)/shard_map/ppermute | solution.py:63
  (127 shorter events, 53.7 us)
Async XLA Ops:
  3.9 10.9 %collective-permute-start.2 = (bf16[1280,128]{1,0:T(8,128)(2,1)}, bf16[1280,128]{1,0:T(8,128)(2,1)S(1)}, u32[]{:S(2)}, u32[]{:S(2)}) collective-permute-start(bf16[1280,128]{1,0:T(8,128)(2,1)} %shard_map.85.own_ref.refs_0_), channel_id=1, source_target_pairs={{0,2},{1,3},{2,0},{3,1},{4,6},{5,7},{6,4},{7,5},{8,10},{9,11},{10,... | collective-permute-start | bytes 983048 | tf_op jit(solution)/shard_map/ppermute | solution.py:63
  6.9 9.4 %collective-permute-start = (bf16[1280,128]{1,0:T(8,128)(2,1)}, bf16[1280,128]{1,0:T(8,128)(2,1)S(1)}, u32[]{:S(2)}, u32[]{:S(2)}) collective-permute-start(bf16[1280,128]{1,0:T(8,128)(2,1)} %shard_map.85.own_ref.refs_0_), channel_id=1, source_target_pairs={{0,4},{1,5},{2,6},{3,7},{4,0},{5,1},{6,2},{7,3},{8,12},{9,13},{10,... | collective-permute-start | bytes 983048 | tf_op jit(solution)/shard_map/ppermute | solution.py:63
  27.6 18.3 %collective-permute-start.1 = (bf16[1280,128]{1,0:T(8,128)(2,1)}, bf16[1280,128]{1,0:T(8,128)(2,1)S(1)}, u32[]{:S(2)}, u32[]{:S(2)}) collective-permute-start(bf16[1280,128]{1,0:T(8,128)(2,1)} %shard_map.85.own_ref.refs_0_), channel_id=1, source_target_pairs={{0,8},{1,9},{2,10},{3,11},{4,12},{5,13},{6,14},{7,15},{8,0},{9,1},... | collective-permute-start | bytes 983048 | tf_op jit(solution)/shard_map/ppermute | solution.py:63
  31.3 16.0 %collective-permute-start.7 = (bf16[192,256]{1,0:T(8,128)(2,1)S(1)}, bf16[192,256]{1,0:T(8,128)(2,1)S(1)}, u32[]{:S(2)}, u32[]{:S(2)}) collective-permute-start(bf16[192,256]{1,0:T(8,128)(2,1)S(1)} %get-tuple-element.57), channel_id=1, source_target_pairs={{0,2},{1,3},{2,0},{3,1},{4,6},{5,7},{6,4},{7,5},{8,10},{9,11},{10,... | collective-permute-start | bytes 294920 | tf_op jit(solution)/shard_map/ppermute | solution.py:63
  31.9 16.8 %collective-permute-start.10 = (bf16[1280,128]{1,0:T(8,128)(2,1)}, bf16[1280,128]{1,0:T(8,128)(2,1)S(1)}, u32[]{:S(2)}, u32[]{:S(2)}) collective-permute-start(bf16[1280,128]{1,0:T(8,128)(2,1)} %shard_map.85.own_ref.refs_0_), channel_id=1, source_target_pairs={{0,1},{1,0},{2,3},{3,2},{4,5},{5,4},{6,7},{7,6},{8,9},{9,8},{10,11... | collective-permute-start | bytes 983048 | tf_op jit(solution)/shard_map/ppermute | solution.py:63
  31.9 16.8 %collective-permute-start.11 = (bf16[1280,128]{1,0:T(8,128)(2,1)S(1)}, bf16[1280,128]{1,0:T(8,128)(2,1)S(1)}, u32[]{:S(2)}, u32[]{:S(2)}) collective-permute-start(bf16[1280,128]{1,0:T(8,128)(2,1)S(1)} %collective-permute-done.2.refs_1_), channel_id=1, source_target_pairs={{0,1},{1,0},{2,3},{3,2},{4,5},{5,4},{6,7},{7,6},{8,9},{9,8},{10,11... | collective-permute-start | bytes 983048 | tf_op jit(solution)/shard_map/ppermute | solution.py:63
  45.9 9.3 %collective-permute-start.5 = (bf16[1280,128]{1,0:T(8,128)(2,1)S(1)}, bf16[1280,128]{1,0:T(8,128)(2,1)S(1)}, u32[]{:S(2)}, u32[]{:S(2)}) collective-permute-start(bf16[1280,128]{1,0:T(8,128)(2,1)S(1)} %collective-permute-done.1.refs_4_), channel_id=1, source_target_pairs={{0,2},{1,3},{2,0},{3,1},{4,6},{5,7},{6,4},{7,5},{8,10},{9,11},{10,... | collective-permute-start | bytes 983048 | tf_op jit(solution)/shard_map/ppermute | solution.py:63
  46.6 10.6 %collective-permute-start.4 = (bf16[1280,128]{1,0:T(8,128)(2,1)S(1)}, bf16[1280,128]{1,0:T(8,128)(2,1)S(1)}, u32[]{:S(2)}, u32[]{:S(2)}) collective-permute-start(bf16[1280,128]{1,0:T(8,128)(2,1)S(1)} %collective-permute-done.1.refs_4_), channel_id=1, source_target_pairs={{0,4},{1,5},{2,6},{3,7},{4,0},{5,1},{6,2},{7,3},{8,12},{9,13},{10,... | collective-permute-start | bytes 983048 | tf_op jit(solution)/shard_map/ppermute | solution.py:63
  47.3 12.5 %collective-permute-start.8 = (f32[192,256]{1,0:T(8,128)S(1)}, f32[192,256]{1,0:T(8,128)S(1)}, u32[]{:S(2)}, u32[]{:S(2)}) collective-permute-start(f32[192,256]{1,0:T(8,128)S(1)} %convert_add_fusion.3), channel_id=1, source_target_pairs={{0,4},{1,5},{2,6},{3,7},{4,0},{5,1},{6,2},{7,3},{8,12},{9,13},{10,... | collective-permute-start | bytes 589832 | tf_op jit(solution)/shard_map/ppermute | solution.py:63
  48.7 13.5 %collective-permute-start.12 = (bf16[1280,128]{1,0:T(8,128)(2,1)S(1)}, bf16[1280,128]{1,0:T(8,128)(2,1)S(1)}, u32[]{:S(2)}, u32[]{:S(2)}) collective-permute-start(bf16[1280,128]{1,0:T(8,128)(2,1)S(1)} %collective-permute-done.refs_2_), channel_id=1, source_target_pairs={{0,1},{1,0},{2,3},{3,2},{4,5},{5,4},{6,7},{7,6},{8,9},{9,8},{10,11... | collective-permute-start | bytes 983048 | tf_op jit(solution)/shard_map/ppermute | solution.py:63
  48.8 15.5 %collective-permute-start.14 = (bf16[1280,128]{1,0:T(8,128)(2,1)S(1)}, bf16[1280,128]{1,0:T(8,128)(2,1)S(1)}, u32[]{:S(2)}, u32[]{:S(2)}) collective-permute-start(bf16[1280,128]{1,0:T(8,128)(2,1)S(1)} %collective-permute-done.1.refs_4_), channel_id=1, source_target_pairs={{0,1},{1,0},{2,3},{3,2},{4,5},{5,4},{6,7},{7,6},{8,9},{9,8},{10,11... | collective-permute-start | bytes 983048 | tf_op jit(solution)/shard_map/ppermute | solution.py:63
  55.2 9.8 %collective-permute-start.13 = (bf16[1280,128]{1,0:T(8,128)(2,1)S(1)}, bf16[1280,128]{1,0:T(8,128)(2,1)}, u32[]{:S(2)}, u32[]{:S(2)}) collective-permute-start(bf16[1280,128]{1,0:T(8,128)(2,1)S(1)} %collective-permute-done.3.refs_3_), channel_id=1, source_target_pairs={{0,1},{1,0},{2,3},{3,2},{4,5},{5,4},{6,7},{7,6},{8,9},{9,8},{10,11... | collective-permute-start | bytes 983048 | tf_op jit(solution)/shard_map/ppermute | solution.py:63
  63.0 17.2 %collective-permute-start.9 = (bf16[1280,128]{1,0:T(8,128)(2,1)S(1)}, bf16[1280,128]{1,0:T(8,128)(2,1)}, u32[]{:S(2)}, u32[]{:S(2)}) collective-permute-start(bf16[1280,128]{1,0:T(8,128)(2,1)S(1)} %collective-permute-done.4.refs_6_), channel_id=1, source_target_pairs={{0,2},{1,3},{2,0},{3,1},{4,6},{5,7},{6,4},{7,5},{8,10},{9,11},{10,... | collective-permute-start | bytes 983048 | tf_op jit(solution)/shard_map/ppermute | solution.py:63
  80.4 13.0 %collective-permute-start.19 = (f32[192,256]{1,0:T(8,128)}, f32[192,256]{1,0:T(8,128)}, u32[]{:S(2)}, u32[]{:S(2)}) collective-permute-start(f32[192,256]{1,0:T(8,128)} %add.195), channel_id=1, source_target_pairs={{0,8},{1,9},{2,10},{3,11},{4,12},{5,13},{6,14},{7,15},{8,0},{9,1},... | collective-permute-start | bytes 589832 | tf_op jit(solution)/shard_map/ppermute | solution.py:63
  91.7 17.3 %collective-permute-start.18 = (bf16[384,640]{1,0:T(8,128)(2,1)S(1)}, bf16[384,640]{1,0:T(8,128)(2,1)S(1)}, u32[]{:S(2)}, u32[]{:S(2)}) collective-permute-start(bf16[384,640]{1,0:T(8,128)(2,1)S(1)} %get-tuple-element.38), channel_id=1, source_target_pairs={{0,16},{16,0},{1,17},{17,1},{2,18},{18,2},{3,19},{19,3},{4,20},{20... | collective-permute-start | bytes 1474568 | tf_op jit(solution)/shard_map/ppermute | solution.py:63
  94.5 13.3 %collective-permute-start.20 = (bf16[192,256]{1,0:T(8,128)(2,1)S(1)}, bf16[192,256]{1,0:T(8,128)(2,1)S(1)}, u32[]{:S(2)}, u32[]{:S(2)}) collective-permute-start(bf16[192,256]{1,0:T(8,128)(2,1)S(1)} %get-tuple-element.55), channel_id=1, source_target_pairs={{0,16},{16,0},{1,17},{17,1},{2,18},{18,2},{3,19},{19,3},{4,20},{20... | collective-permute-start | bytes 294920 | tf_op jit(solution)/shard_map/ppermute | solution.py:63
  96.0 13.0 %collective-permute-start.22 = (bf16[192,256]{1,0:T(8,128)(2,1)S(1)}, bf16[192,256]{1,0:T(8,128)(2,1)S(1)}, u32[]{:S(2)}, u32[]{:S(2)}) collective-permute-start(bf16[192,256]{1,0:T(8,128)(2,1)S(1)} %convert_element_type.136), channel_id=1, source_target_pairs={{0,16},{16,0},{1,17},{17,1},{2,18},{18,2},{3,19},{19,3},{4,20},{20... | collective-permute-start | bytes 294920 | tf_op jit(solution)/shard_map/ppermute | solution.py:63
  120.9 11.3 %collective-permute-start.27 = (bf16[4,128,256]{2,1,0:T(8,128)(2,1)S(1)}, bf16[4,128,256]{2,1,0:T(8,128)(2,1)S(1)}, u32[]{:S(2)}, u32[]{:S(2)}) collective-permute-start(bf16[4,128,256]{2,1,0:T(8,128)(2,1)S(1)} %add_convert_fusion.2), channel_id=1, source_target_pairs={{0,2},{1,3},{2,0},{3,1},{4,6},{5,7},{6,4},{7,5},{8,10},{9,11},{10,... | collective-permute-start | bytes 786440 | tf_op jit(solution)/shard_map/ppermute | solution.py:63
  123.4 21.1 %collective-permute-start.37 = (bf16[4,128,256]{2,1,0:T(8,128)(2,1)S(1)}, bf16[4,128,256]{2,1,0:T(8,128)(2,1)S(1)}, u32[]{:S(2)}, u32[]{:S(2)}) collective-permute-start(bf16[4,128,256]{2,1,0:T(8,128)(2,1)S(1)} %add_convert_fusion), channel_id=1, source_target_pairs={{0,2},{1,3},{2,0},{3,1},{4,6},{5,7},{6,4},{7,5},{8,10},{9,11},{10,... | collective-permute-start | bytes 786440 | tf_op jit(solution)/shard_map/ppermute | solution.py:63
  124.2 18.5 %collective-permute-start.30 = (bf16[4,128,256]{2,1,0:T(8,128)(2,1)S(1)}, bf16[4,128,256]{2,1,0:T(8,128)(2,1)S(1)}, u32[]{:S(2)}, u32[]{:S(2)}) collective-permute-start(bf16[4,128,256]{2,1,0:T(8,128)(2,1)S(1)} %add_convert_fusion.1), channel_id=1, source_target_pairs={{0,2},{1,3},{2,0},{3,1},{4,6},{5,7},{6,4},{7,5},{8,10},{9,11},{10,... | collective-permute-start | bytes 786440 | tf_op jit(solution)/shard_map/ppermute | solution.py:63
  132.3 12.4 %collective-permute-start.32 = (bf16[2,128,256]{2,1,0:T(8,128)(2,1)S(1)}, bf16[2,128,256]{2,1,0:T(8,128)(2,1)S(1)}, u32[]{:S(2)}, u32[]{:S(2)}) collective-permute-start(bf16[2,128,256]{2,1,0:T(8,128)(2,1)S(1)} %fusion.5), channel_id=1, source_target_pairs={{0,4},{1,5},{2,6},{3,7},{4,0},{5,1},{6,2},{7,3},{8,12},{9,13},{10,... | collective-permute-start | bytes 393224 | tf_op jit(solution)/shard_map/ppermute | solution.py:63
  134.1 16.2 %collective-permute-start.28 = (f32[128,256]{1,0:T(8,128)S(1)}, f32[128,256]{1,0:T(8,128)S(1)}, u32[]{:S(2)}, u32[]{:S(2)}) collective-permute-start(f32[128,256]{1,0:T(8,128)S(1)} %add.198), channel_id=1, source_target_pairs={{0,4},{1,5},{2,6},{3,7},{4,0},{5,1},{6,2},{7,3},{8,12},{9,13},{10,... | collective-permute-start | bytes 393224 | tf_op jit(solution)/shard_map/ppermute | solution.py:63
  150.4 9.4 %collective-permute-start.36 = (bf16[1,128,256]{2,1,0:T(8,128)(2,1)S(1)}, bf16[1,128,256]{2,1,0:T(8,128)(2,1)S(1)}, u32[]{:S(2)}, u32[]{:S(2)}) collective-permute-start(bf16[1,128,256]{2,1,0:T(8,128)(2,1)S(1)} %fusion.10), channel_id=1, source_target_pairs={{0,8},{1,9},{2,10},{3,11},{4,12},{5,13},{6,14},{7,15},{8,0},{9,1},... | collective-permute-start | bytes 196616 | tf_op jit(solution)/shard_map/ppermute | solution.py:63
  152.3 10.4 %collective-permute-start.31 = (f32[128,256]{1,0:T(8,128)S(1)}, f32[128,256]{1,0:T(8,128)S(1)}, u32[]{:S(2)}, u32[]{:S(2)}) collective-permute-start(f32[128,256]{1,0:T(8,128)S(1)} %add.200.refs_0_), channel_id=1, source_target_pairs={{0,8},{1,9},{2,10},{3,11},{4,12},{5,13},{6,14},{7,15},{8,0},{9,1},... | collective-permute-start | bytes 393224 | tf_op jit(solution)/shard_map/ppermute | solution.py:63
  (33 other events, 281.6 us)

commit v9 on v7

--- a/solution.py
+++ b/solution.py
@@ -198,7 +198,7 @@
     take = lambda count: [refs.pop(0) for _ in range(count)]
     sent, keeps, others = take(n), take(n + 1), take(n + 1)
     codes_ref, thin_refs = take(1)[0], take(thin_count)
-    outs_c, outs_b = take(2), take(4)
+    outs_c, outs_b = take(2), take(2)
     rank = own.shape[1] // 6
     last = sections - 1
     values = [
@@ -283,7 +283,7 @@
         sum_out = jnp.concatenate([half_first, half_second], axis=1)
     else:
         sum_out = refs.pop(0)[...]
-    sum_in = jnp.concatenate([pair(), pair()], axis=1)
+    sum_in = pair()
     start = pl.multiple_of(scalars[1] * part, part)
     total = gain_ref[:, pl.ds(start, part)] * (sum_in + lift_in)
     grad_in[...] = total.T
@@ -345,17 +345,18 @@
     peers = lax.axis_size("dp")
     order = sorted(range(4, peers, 4), key=lambda m: (m.bit_count(), m))
     shards = {0: own}
-    for m in order:
+    shards[2] = swap(own, 2)
+    for k, m in enumerate(order):
         if m.bit_count() == 1:
-            shards[m] = swap(own, m)
-    shards[2] = swap(own, 2)
-
+            shards[m] = swap(after(own, shards[order[k - 1]]) if k else own, m)
+
+    shards[order[0] ^ 2] = swap(after(shards[order[0]], shards[2]), 2)
     tall = (3 * rank, size)
     keep, give = call(
         small_kernel,
         [flag, core],
         [own_out, subspace],
-        [after(own, shards[peers // 2])],
+        [after(own, shards[order[0] ^ 2])],
         [((tall[0] // 2, size), F32)] * 2,
         [
             pltpu.VMEM((part, rank), BF16),
@@ -377,8 +378,9 @@
         low = m & -m
         if m != low:
             shards[m] = swap(after(shards[m ^ low], shards[order[k - 2] ^ 2]), low)
-        before = shards[order[k - 1] ^ 2] if k else shards[2]
-        shards[m ^ 2] = swap(after(shards[m], before, *([small] if m ^ 2 == ends else [])), 2)
+        if k:
+            ties = [small] if m ^ 2 == ends else []
+            shards[m ^ 2] = swap(after(shards[m], shards[order[k - 1] ^ 2], *ties), 2)
     small = after(small, shards[peers // 2])
     small = small + swap(small, peers // 2)
     small = small + swap(small.astype(BF16), 2).astype(F32)
@@ -391,7 +393,7 @@
         shards[m ^ 1] = swap(shards[m], 1)
     marks += [m ^ 1 for m in marks]
     acc = project([spot ^ m for m in marks], flag, [shards[m] for m in marks], tokens)[0]
-    pair = [shards[ends], swap(shards[ends], 1)]
+    pair = [shards[ends], swap(after(shards[ends], acc), 1)]
     acc, send = project([spot ^ ends, spot ^ ends ^ 1], flag, pair, tokens, acc, final=True)
     sent = from_sections(send)
 
@@ -404,7 +406,7 @@
         columns, block_id = part, lambda i: i
     both = (spot ^ 1, spot)
     out_ids = [block_id(who ^ m) for who in both for m in every]
-    in_ids = [(who ^ m) * 2 + k for k in range(2) for who in both for m in every]
+    in_ids = [who ^ m for who in both for m in every]
     blocks = lambda n: ((len(every), rank, n), BF16)
     thin_count = 1 if sections == 2 else 2
     codes, *rest = call(
@@ -415,25 +417,24 @@
         [((rows, size), BF16)]
         + [((rank, size), F32)] * thin_count
         + [blocks(columns)] * 2
-        + [blocks(half)] * 4,
+        + [blocks(part)] * 2,
         vmem_bytes=(VMEM_BYTES if sections == 2 else 32 * 1024 * 1024),
     )
     thins, chunks = rest[:thin_count], rest[thin_count:]
     got = [swap(give, 1) for give in chunks[::2]]
-    lower, lower_x = scatter_sum(got[1], chunks[3])
-    upper, upper_x = scatter_sum(got[2], chunks[5])
-    sum_out, _ = scatter_sum(got[0], chunks[1], [got[1:], [lower_x], [upper_x]])
+    sum_out, out_x = scatter_sum(got[0], chunks[1])
+    sum_in, in_x = scatter_sum(got[1], chunks[3])
     sum_out = sum_out[0] + sum_out[1].astype(F32)
     ends_out = [sum_out]
     if sections == 2:
         ends_out = [swap(sum_out, 1, "section"), sum_out]
-    waits = [None, got[2], lower_x]
+    waits = [got[1], out_x, in_x]
     terms = [term for thin in thins for term in sum_thin(thin, waits)]
     grad_in, grad_out = call(
         functools.partial(end_kernel, sections),
         [flag, spot],
         [],
-        [gain, subspace, *terms, *ends_out, *lower, *upper],
+        [gain, subspace, *terms, *ends_out, *sum_in],
         [((part, rank), F32)] * 2,
     )
     return codes[None], grad_in[None], grad_out[None]

time: 146 us -> 143 us (0.979)
  waiting for transfers between devices: 77.5 us -> 70.5 us
  starting transfers between devices: 33.7 us -> 35.8 us
    ppermute x40 -> x36, waiting for transfers between devices: 77.5 us -> 70.5 us  [swap(): return lax.ppermute(value, axis, [(i, i ^ bits) for i in range(peers)])]
    ppermute x40 -> x36, starting transfers between devices: 33.7 us -> 35.8 us  [swap(): return lax.ppermute(value, axis, [(i, i ^ bits) for i in range(peers)])]
    unnamed x20 -> x22, local copies, waits for them, and re-layouts: 12.1 us -> 12.8 us
  transfers between devices with their start and end apart: 40 -> 36, of which waited for: 22 -> 18; matrix products, arithmetic and copies ran while one was open for 2% -> 3% of each run, Pallas kernels for 6% -> 7%
where the time goes in v9:
time: 143 us
  waiting for transfers between devices  70.5 us (49%)
  starting transfers between devices  35.8 us (25%)
  Pallas kernels  18.9 us (13%)
  local copies, waits for them, and re-layouts  13.1 us (9%)
  other arithmetic  3.91 us (3%)
    ppermute x36, waiting for transfers between devices, swap(): return lax.ppermute(value, axis, [(i, i ^ bits) for i in range(peers)])  70.5 us
    ppermute x36, starting transfers between devices, swap(): return lax.ppermute(value, axis, [(i, i ^ bits) for i in range(peers)])  35.8 us
    pallas_call x6, Pallas kernels, call(): pl.pallas_call(kernel, in_specs=[IN_SMEM] + [IN_HBM] * len(far) + [IN_VME...  18.9 us
    unnamed x22, local copies, waits for them, and re-layouts  12.8 us
  transfers between devices with their start and end apart: 36, of which 18 were waited for; matrix products, arithmetic and copies ran while one was open for 3% of the time, Pallas kernels for 7%

profile of v9, /device:TPU:0, one launch (start us, length us, event | category | flops | bytes accessed | tf_op | source)
XLA Modules:
  0.0 143.1 jit_solution(12945495259359298881)
XLA Ops:
  1.2 2.5 %shard_map.85.own_ref.refs_0_ = bf16[1280,128]{1,0:T(8,128)(2,1)} custom-call(s32[2]{0:T(128)} %pad_add_fusion.1.scalars, bf16[512,128]{1,0:T(8,128)(2,1)} %bitcast.90, bf16[512,128]{1,0:T(8,128)(2,1)} %bitcast.88, bf16[512,256]{1,0:T(8,128)(2,1)} %space_ref.3, f32[1,8192]{1,0:T(1,128)} %gain_ref.1), custom_call_target="tpu_custom_call" | custom-call | tf_op jit(solution)/shard_map/pallas_call | solution.py:43
  3.8 3.0 %collective-permute-start.2 = (bf16[1280,128]{1,0:T(8,128)(2,1)}, bf16[1280,128]{1,0:T(8,128)(2,1)S(1)}, u32[]{:S(2)}, u32[]{:S(2)}) collective-permute-start(bf16[1280,128]{1,0:T(8,128)(2,1)} %shard_map.85.own_ref.refs_0_), channel_id=1, source_target_pairs={{0,2},{1,3},{2,0},{3,1},{4,6},{5,7},{6,4},{7,5},{8,10},{9,11},{10,... | collective-permute-start | bytes 983048 | tf_op jit(solution)/shard_map/ppermute | solution.py:63
  8.4 6.3 %collective-permute-done.2.refs_1_ = bf16[1280,128]{1,0:T(8,128)(2,1)S(1)} collective-permute-done((bf16[1280,128]{1,0:T(8,128)(2,1)}, bf16[1280,128]{1,0:T(8,128)(2,1)S(1)}, u32[]{:S(2)}, u32[]{:S(2)}) %collective-permute-start.2) | collective-permute-done | bytes 327712 | tf_op jit(solution)/shard_map/ppermute | solution.py:63
  16.6 2.7 %collective-permute-start.1 = (bf16[1280,128]{1,0:T(8,128)(2,1)}, bf16[1280,128]{1,0:T(8,128)(2,1)S(1)}, u32[]{:S(2)}, u32[]{:S(2)}) collective-permute-start(bf16[1280,128]{1,0:T(8,128)(2,1)} %shard_map.85.own_ref.refs_0_), channel_id=1, source_target_pairs={{0,8},{1,9},{2,10},{3,11},{4,12},{5,13},{6,14},{7,15},{8,0},{9,1},... | collective-permute-start | bytes 983048 | tf_op jit(solution)/shard_map/ppermute | solution.py:63
  19.9 4.5 %collective-permute-done.3.refs_3_ = bf16[1280,128]{1,0:T(8,128)(2,1)S(1)} collective-permute-done((bf16[1280,128]{1,0:T(8,128)(2,1)S(1)}, bf16[1280,128]{1,0:T(8,128)(2,1)S(1)}, u32[]{:S(2)}, u32[]{:S(2)}) %collective-permute-start.3) | collective-permute-done | bytes 327712 | tf_op jit(solution)/shard_map/ppermute | solution.py:63
  24.4 3.0 %shard_map.86 = (f32[192,256]{1,0:T(8,128)}, f32[192,256]{1,0:T(8,128)}) custom-call(s32[2]{0:T(128)} %pad_add_fusion.2.scalars, bf16[512,128]{1,0:T(8,128)(2,1)} %bitcast.89, bf16[512,256]{1,0:T(8,128)(2,1)} %space_ref.3, bf16[1280,128]{1,0:T(8,128)(2,1)} %shard_map.85.own_ref.refs_0_), custom_call_target="tpu_custom_call" | custom-call | tf_op jit(solution)/shard_map/pallas_call | solution.py:43
  28.1 4.9 %collective-permute-done.1.refs_4_ = bf16[1280,128]{1,0:T(8,128)(2,1)S(1)} collective-permute-done((bf16[1280,128]{1,0:T(8,128)(2,1)}, bf16[1280,128]{1,0:T(8,128)(2,1)S(1)}, u32[]{:S(2)}, u32[]{:S(2)}) %collective-permute-start.1) | collective-permute-done | bytes 327712 | tf_op jit(solution)/shard_map/ppermute | solution.py:63
  37.9 3.8 %collective-permute-done.5.refs_5_ = bf16[1280,128]{1,0:T(8,128)(2,1)S(1)} collective-permute-done((bf16[1280,128]{1,0:T(8,128)(2,1)S(1)}, bf16[1280,128]{1,0:T(8,128)(2,1)S(1)}, u32[]{:S(2)}, u32[]{:S(2)}) %collective-permute-start.5) | collective-permute-done | bytes 327712 | tf_op jit(solution)/shard_map/ppermute | solution.py:63
  41.7 3.1 %collective-permute-done.4.refs_6_ = bf16[1280,128]{1,0:T(8,128)(2,1)S(1)} collective-permute-done((bf16[1280,128]{1,0:T(8,128)(2,1)S(1)}, bf16[1280,128]{1,0:T(8,128)(2,1)S(1)}, u32[]{:S(2)}, u32[]{:S(2)}) %collective-permute-start.4) | collective-permute-done | bytes 327712 | tf_op jit(solution)/shard_map/ppermute | solution.py:63
  44.8 2.1 %collective-permute-done.7 = f32[192,256]{1,0:T(8,128)S(1)} collective-permute-done((f32[192,256]{1,0:T(8,128)S(1)}, f32[192,256]{1,0:T(8,128)S(1)}, u32[]{:S(2)}, u32[]{:S(2)}) %collective-permute-start.7) | collective-permute-done | bytes 196640 | tf_op jit(solution)/shard_map/ppermute | solution.py:63
  48.7 3.3 %collective-permute-start.18 = (f32[192,256]{1,0:T(8,128)S(1)}, f32[192,256]{1,0:T(8,128)S(1)}, u32[]{:S(2)}, u32[]{:S(2)}) collective-permute-start(f32[192,256]{1,0:T(8,128)S(1)} %add.118), channel_id=1, source_target_pairs={{0,8},{1,9},{2,10},{3,11},{4,12},{5,13},{6,14},{7,15},{8,0},{9,1},... | collective-permute-start | bytes 589832 | tf_op jit(solution)/shard_map/ppermute | solution.py:63
  52.6 2.8 %copy-done = bf16[384,8192]{1,0:T(8,128)(2,1)S(1)} copy-done((bf16[384,8192]{1,0:T(8,128)(2,1)S(1)}, bf16[384,8192]{1,0:T(8,128)(2,1)}, u32[]{:S(2)}) %copy-start) | copy-done | bytes 6291480
  55.4 2.8 %copy-done.3 = bf16[384,8192]{1,0:T(8,128)(2,1)S(1)} copy-done((bf16[384,8192]{1,0:T(8,128)(2,1)S(1)}, bf16[384,8192]{1,0:T(8,128)(2,1)}, u32[]{:S(2)}) %copy-start.3) | copy-done | bytes 6291480
  59.2 5.8 %shard_map.87.refs_2_ = f32[384,768]{1,0:T(8,128)S(1)} custom-call(s32[15]{0:T(128)S(1)} %stack.204.scalars, bf16[384,8192]{1,0:T(8,128)(2,1)S(1)} %copy-done, bf16[384,8192]{1,0:T(8,128)(2,1)S(1)} %copy-done.3, bf16[1280,128]{1,0:T(8,128)(2,1)S(1)} %copy-done.6, bf16[1280,128]{1,0:T(8,128)(2,1)S(1)} %collective-permute-done.2.refs_1_, ...), custom_call_target="tpu_custom_call" | custom-call | flops 3523215360 | tf_op jit(solution)/shard_map/pallas_call | solution.py:43
  73.8 10.4 %collective-permute-done.20.refs_2_ = bf16[192,256]{1,0:T(8,128)(2,1)S(1)} collective-permute-done((bf16[192,256]{1,0:T(8,128)(2,1)S(1)}, bf16[192,256]{1,0:T(8,128)(2,1)S(1)}, u32[]{:S(2)}, u32[]{:S(2)}) %collective-permute-start.20) | collective-permute-done | bytes 98336 | tf_op jit(solution)/shard_map/ppermute | solution.py:63
  85.6 2.8 %copy-done.2 = bf16[384,8192]{1,0:T(8,128)(2,1)S(1)} copy-done((bf16[384,8192]{1,0:T(8,128)(2,1)S(1)}, bf16[384,8192]{1,0:T(8,128)(2,1)}, u32[]{:S(2)}) %copy-start.2) | copy-done | bytes 6291480
  88.4 2.8 %copy-done.5 = bf16[384,8192]{1,0:T(8,128)(2,1)S(1)} copy-done((bf16[384,8192]{1,0:T(8,128)(2,1)S(1)}, bf16[384,8192]{1,0:T(8,128)(2,1)}, u32[]{:S(2)}) %copy-start.5) | copy-done | bytes 6291480
  91.2 4.4 %shard_map.89 = (bf16[384,256]{1,0:T(8,128)(2,1)}, f32[128,256]{1,0:T(8,128)S(1)}, bf16[8,128,256]{2,1,0:T(8,128)(2,1)S(1)}, bf16[8,128,256]{2,1,0:T(8,128)(2,1)...) custom-call(s32[34]{0:T(128)S(1)} %stack.192.scalars, bf16[384,8192]{1,0:T(8,128)(2,1)S(1)} %copy-done.2, ...), custom_call_target="tpu_custom_call" | custom-call | tf_op jit(solution)/shard_map/pallas_call | solution.py:43
  99.0 7.0 %collective-permute-done.27 = bf16[4,128,256]{2,1,0:T(8,128)(2,1)S(1)} collective-permute-done((bf16[4,128,256]{2,1,0:T(8,128)(2,1)S(1)}, bf16[4,128,256]{2,1,0:T(8,128)(2,1)S(1)}, u32[]{:S(2)}, u32[]{:S(2)}) %collective-permute-start.27) | collective-permute-done | bytes 262176 | tf_op jit(solution)/shard_map/ppermute | solution.py:63
  106.1 1.8 %collective-permute-start.31 = (bf16[2,128,256]{2,1,0:T(8,128)(2,1)S(1)}, bf16[2,128,256]{2,1,0:T(8,128)(2,1)S(1)}, u32[]{:S(2)}, u32[]{:S(2)}) collective-permute-start(bf16[2,128,256]{2,1,0:T(8,128)(2,1)S(1)} %fusion.6), channel_id=1, source_target_pairs={{0,4},{1,5},{2,6},{3,7},{4,0},{5,1},{6,2},{7,3},{8,12},{9,13},{10,... | collective-permute-start | bytes 393224 | tf_op jit(solution)/shard_map/ppermute | solution.py:63
  112.8 9.6 %collective-permute-done.29 = bf16[4,128,512]{2,1,0:T(8,128)(2,1)S(1)} collective-permute-done((bf16[4,128,512]{2,1,0:T(8,128)(2,1)S(1)}, bf16[4,128,512]{2,1,0:T(8,128)(2,1)S(1)}, u32[]{:S(2)}, u32[]{:S(2)}) %collective-permute-start.29) | collective-permute-done | bytes 524320 | tf_op jit(solution)/shard_map/ppermute | solution.py:63
  126.6 4.5 %collective-permute-done.28 = f32[128,256]{1,0:T(8,128)S(1)} collective-permute-done((f32[128,256]{1,0:T(8,128)S(1)}, f32[128,256]{1,0:T(8,128)S(1)}, u32[]{:S(2)}, u32[]{:S(2)}) %collective-permute-start.28) | collective-permute-done | bytes 131104 | tf_op jit(solution)/shard_map/ppermute | solution.py:63
  131.4 2.9 %collective-permute-start.35 = (bf16[1,128,512]{2,1,0:T(8,128)(2,1)S(1)}, bf16[1,128,512]{2,1,0:T(8,128)(2,1)S(1)}, u32[]{:S(2)}, u32[]{:S(2)}) collective-permute-start(bf16[1,128,512]{2,1,0:T(8,128)(2,1)S(1)} %fusion.5), channel_id=1, source_target_pairs={{0,8},{1,9},{2,10},{3,11},{4,12},{5,13},{6,14},{7,15},{8,0},{9,1},... | collective-permute-start | bytes 393224 | tf_op jit(solution)/shard_map/ppermute | solution.py:63
  134.3 5.5 %collective-permute-done.30.refs_1_ = f32[128,256]{1,0:T(8,128)S(1)} collective-permute-done((f32[128,256]{1,0:T(8,128)S(1)}, f32[128,256]{1,0:T(8,128)S(1)}, u32[]{:S(2)}, u32[]{:S(2)}) %collective-permute-start.30) | collective-permute-done | bytes 131104 | tf_op jit(solution)/shard_map/ppermute | solution.py:63
  (101 shorter events, 39.7 us)
Async XLA Ops:
  3.8 10.9 %collective-permute-start.2 = (bf16[1280,128]{1,0:T(8,128)(2,1)}, bf16[1280,128]{1,0:T(8,128)(2,1)S(1)}, u32[]{:S(2)}, u32[]{:S(2)}) collective-permute-start(bf16[1280,128]{1,0:T(8,128)(2,1)} %shard_map.85.own_ref.refs_0_), channel_id=1, source_target_pairs={{0,2},{1,3},{2,0},{3,1},{4,6},{5,7},{6,4},{7,5},{8,10},{9,11},{10,... | collective-permute-start | bytes 983048 | tf_op jit(solution)/shard_map/ppermute | solution.py:63
  6.8 9.4 %collective-permute-start = (bf16[1280,128]{1,0:T(8,128)(2,1)}, bf16[1280,128]{1,0:T(8,128)(2,1)S(1)}, u32[]{:S(2)}, u32[]{:S(2)}) collective-permute-start(bf16[1280,128]{1,0:T(8,128)(2,1)} %shard_map.85.own_ref.refs_0_), channel_id=1, source_target_pairs={{0,4},{1,5},{2,6},{3,7},{4,0},{5,1},{6,2},{7,3},{8,12},{9,13},{10,... | collective-permute-start | bytes 983048 | tf_op jit(solution)/shard_map/ppermute | solution.py:63
  16.6 16.4 %collective-permute-start.1 = (bf16[1280,128]{1,0:T(8,128)(2,1)}, bf16[1280,128]{1,0:T(8,128)(2,1)S(1)}, u32[]{:S(2)}, u32[]{:S(2)}) collective-permute-start(bf16[1280,128]{1,0:T(8,128)(2,1)} %shard_map.85.own_ref.refs_0_), channel_id=1, source_target_pairs={{0,8},{1,9},{2,10},{3,11},{4,12},{5,13},{6,14},{7,15},{8,0},{9,1},... | collective-permute-start | bytes 983048 | tf_op jit(solution)/shard_map/ppermute | solution.py:63
  27.6 9.8 %collective-permute-start.9 = (bf16[1280,128]{1,0:T(8,128)(2,1)}, bf16[1280,128]{1,0:T(8,128)(2,1)S(1)}, u32[]{:S(2)}, u32[]{:S(2)}) collective-permute-start(bf16[1280,128]{1,0:T(8,128)(2,1)} %shard_map.85.own_ref.refs_0_), channel_id=1, source_target_pairs={{0,1},{1,0},{2,3},{3,2},{4,5},{5,4},{6,7},{7,6},{8,9},{9,8},{10,11... | collective-permute-start | bytes 983048 | tf_op jit(solution)/shard_map/ppermute | solution.py:63
  28.1 9.3 %collective-permute-start.10 = (bf16[1280,128]{1,0:T(8,128)(2,1)S(1)}, bf16[1280,128]{1,0:T(8,128)(2,1)S(1)}, u32[]{:S(2)}, u32[]{:S(2)}) collective-permute-start(bf16[1280,128]{1,0:T(8,128)(2,1)S(1)} %collective-permute-done.2.refs_1_), channel_id=1, source_target_pairs={{0,1},{1,0},{2,3},{3,2},{4,5},{5,4},{6,7},{7,6},{8,9},{9,8},{10,11... | collective-permute-start | bytes 983048 | tf_op jit(solution)/shard_map/ppermute | solution.py:63
  33.0 8.7 %collective-permute-start.5 = (bf16[1280,128]{1,0:T(8,128)(2,1)S(1)}, bf16[1280,128]{1,0:T(8,128)(2,1)S(1)}, u32[]{:S(2)}, u32[]{:S(2)}) collective-permute-start(bf16[1280,128]{1,0:T(8,128)(2,1)S(1)} %collective-permute-done.1.refs_4_), channel_id=1, source_target_pairs={{0,2},{1,3},{2,0},{3,1},{4,6},{5,7},{6,4},{7,5},{8,10},{9,11},{10,... | collective-permute-start | bytes 983048 | tf_op jit(solution)/shard_map/ppermute | solution.py:63
  34.3 10.5 %collective-permute-start.4 = (bf16[1280,128]{1,0:T(8,128)(2,1)S(1)}, bf16[1280,128]{1,0:T(8,128)(2,1)S(1)}, u32[]{:S(2)}, u32[]{:S(2)}) collective-permute-start(bf16[1280,128]{1,0:T(8,128)(2,1)S(1)} %collective-permute-done.1.refs_4_), channel_id=1, source_target_pairs={{0,4},{1,5},{2,6},{3,7},{4,0},{5,1},{6,2},{7,3},{8,12},{9,13},{10,... | collective-permute-start | bytes 983048 | tf_op jit(solution)/shard_map/ppermute | solution.py:63
  36.0 10.9 %collective-permute-start.7 = (f32[192,256]{1,0:T(8,128)S(1)}, f32[192,256]{1,0:T(8,128)S(1)}, u32[]{:S(2)}, u32[]{:S(2)}) collective-permute-start(f32[192,256]{1,0:T(8,128)S(1)} %add.117), channel_id=1, source_target_pairs={{0,4},{1,5},{2,6},{3,7},{4,0},{5,1},{6,2},{7,3},{8,12},{9,13},{10,... | collective-permute-start | bytes 589832 | tf_op jit(solution)/shard_map/ppermute | solution.py:63
  37.4 11.3 %collective-permute-start.11 = (bf16[1280,128]{1,0:T(8,128)(2,1)S(1)}, bf16[1280,128]{1,0:T(8,128)(2,1)S(1)}, u32[]{:S(2)}, u32[]{:S(2)}) collective-permute-start(bf16[1280,128]{1,0:T(8,128)(2,1)S(1)} %collective-permute-done.refs_2_), channel_id=1, source_target_pairs={{0,1},{1,0},{2,3},{3,2},{4,5},{5,4},{6,7},{7,6},{8,9},{9,8},{10,11... | collective-permute-start | bytes 983048 | tf_op jit(solution)/shard_map/ppermute | solution.py:63
  37.4 14.6 %collective-permute-start.13 = (bf16[1280,128]{1,0:T(8,128)(2,1)S(1)}, bf16[1280,128]{1,0:T(8,128)(2,1)S(1)}, u32[]{:S(2)}, u32[]{:S(2)}) collective-permute-start(bf16[1280,128]{1,0:T(8,128)(2,1)S(1)} %collective-permute-done.1.refs_4_), channel_id=1, source_target_pairs={{0,1},{1,0},{2,3},{3,2},{4,5},{5,4},{6,7},{7,6},{8,9},{9,8},{10,11... | collective-permute-start | bytes 983048 | tf_op jit(solution)/shard_map/ppermute | solution.py:63
  41.7 10.9 %collective-permute-start.12 = (bf16[1280,128]{1,0:T(8,128)(2,1)S(1)}, bf16[1280,128]{1,0:T(8,128)(2,1)}, u32[]{:S(2)}, u32[]{:S(2)}) collective-permute-start(bf16[1280,128]{1,0:T(8,128)(2,1)S(1)} %collective-permute-done.3.refs_3_), channel_id=1, source_target_pairs={{0,1},{1,0},{2,3},{3,2},{4,5},{5,4},{6,7},{7,6},{8,9},{9,8},{10,11... | collective-permute-start | bytes 983048 | tf_op jit(solution)/shard_map/ppermute | solution.py:63
  48.7 16.4 %collective-permute-start.18 = (f32[192,256]{1,0:T(8,128)S(1)}, f32[192,256]{1,0:T(8,128)S(1)}, u32[]{:S(2)}, u32[]{:S(2)}) collective-permute-start(f32[192,256]{1,0:T(8,128)S(1)} %add.118), channel_id=1, source_target_pairs={{0,8},{1,9},{2,10},{3,11},{4,12},{5,13},{6,14},{7,15},{8,0},{9,1},... | collective-permute-start | bytes 589832 | tf_op jit(solution)/shard_map/ppermute | solution.py:63
  52.0 13.0 %collective-permute-start.8 = (bf16[1280,128]{1,0:T(8,128)(2,1)S(1)}, bf16[1280,128]{1,0:T(8,128)(2,1)S(1)}, u32[]{:S(2)}, u32[]{:S(2)}) collective-permute-start(bf16[1280,128]{1,0:T(8,128)(2,1)S(1)} %collective-permute-done.4.refs_6_), channel_id=1, source_target_pairs={{0,2},{1,3},{2,0},{3,1},{4,6},{5,7},{6,4},{7,5},{8,10},{9,11},{10,... | collective-permute-start | bytes 983048 | tf_op jit(solution)/shard_map/ppermute | solution.py:63
  68.0 17.6 %collective-permute-start.17 = (bf16[384,640]{1,0:T(8,128)(2,1)S(1)}, bf16[384,640]{1,0:T(8,128)(2,1)S(1)}, u32[]{:S(2)}, u32[]{:S(2)}) collective-permute-start(bf16[384,640]{1,0:T(8,128)(2,1)S(1)} %get-tuple-element.34), channel_id=1, source_target_pairs={{0,16},{16,0},{1,17},{17,1},{2,18},{18,2},{3,19},{19,3},{4,20},{20... | collective-permute-start | bytes 1474568 | tf_op jit(solution)/shard_map/ppermute | solution.py:63
  70.5 13.8 %collective-permute-start.20 = (bf16[192,256]{1,0:T(8,128)(2,1)S(1)}, bf16[192,256]{1,0:T(8,128)(2,1)S(1)}, u32[]{:S(2)}, u32[]{:S(2)}) collective-permute-start(bf16[192,256]{1,0:T(8,128)(2,1)S(1)} %get-tuple-element.47), channel_id=1, source_target_pairs={{0,16},{16,0},{1,17},{17,1},{2,18},{18,2},{3,19},{19,3},{4,20},{20... | collective-permute-start | bytes 294920 | tf_op jit(solution)/shard_map/ppermute | solution.py:63
  72.3 13.4 %collective-permute-start.22 = (bf16[192,256]{1,0:T(8,128)(2,1)S(1)}, bf16[192,256]{1,0:T(8,128)(2,1)S(1)}, u32[]{:S(2)}, u32[]{:S(2)}) collective-permute-start(bf16[192,256]{1,0:T(8,128)(2,1)S(1)} %convert_element_type.99), channel_id=1, source_target_pairs={{0,16},{16,0},{1,17},{17,1},{2,18},{18,2},{3,19},{19,3},{4,20},{20... | collective-permute-start | bytes 294920 | tf_op jit(solution)/shard_map/ppermute | solution.py:63
  95.6 12.3 %collective-permute-start.24 = (bf16[8,128,512]{2,1,0:T(8,128)(2,1)S(1)}, bf16[8,128,512]{2,1,0:T(8,128)(2,1)S(1)}, u32[]{:S(2)}, u32[]{:S(2)}) collective-permute-start(bf16[8,128,512]{2,1,0:T(8,128)(2,1)S(1)} %get-tuple-element.38), channel_id=1, source_target_pairs={{0,1},{1,0},{2,3},{3,2},{4,5},{5,4},{6,7},{7,6},{8,9},{9,8},{10,11... | collective-permute-start | bytes 3145736 | tf_op jit(solution)/shard_map/ppermute | solution.py:63
  99.0 10.5 %collective-permute-start.23 = (f32[128,256]{1,0:T(8,128)S(1)}, f32[128,256]{1,0:T(8,128)S(1)}, u32[]{:S(2)}, u32[]{:S(2)}) collective-permute-start(f32[128,256]{1,0:T(8,128)S(1)} %get-tuple-element.37), channel_id=1, source_target_pairs={{0,1},{1,0},{2,3},{3,2},{4,5},{5,4},{6,7},{7,6},{8,9},{9,8},{10,11... | collective-permute-start | bytes 393224 | tf_op jit(solution)/shard_map/ppermute | solution.py:63
  108.1 14.3 %collective-permute-start.29 = (bf16[4,128,512]{2,1,0:T(8,128)(2,1)S(1)}, bf16[4,128,512]{2,1,0:T(8,128)(2,1)S(1)}, u32[]{:S(2)}, u32[]{:S(2)}) collective-permute-start(bf16[4,128,512]{2,1,0:T(8,128)(2,1)S(1)} %add_convert_fusion), channel_id=1, source_target_pairs={{0,2},{1,3},{2,0},{3,1},{4,6},{5,7},{6,4},{7,5},{8,10},{9,11},{10,... | collective-permute-start | bytes 1572872 | tf_op jit(solution)/shard_map/ppermute | solution.py:63
  111.2 13.6 %collective-permute-start.32 = (bf16[1,128,256]{2,1,0:T(8,128)(2,1)S(1)}, bf16[1,128,256]{2,1,0:T(8,128)(2,1)S(1)}, u32[]{:S(2)}, u32[]{:S(2)}) collective-permute-start(bf16[1,128,256]{2,1,0:T(8,128)(2,1)S(1)} %fusion.8), channel_id=1, source_target_pairs={{0,8},{1,9},{2,10},{3,11},{4,12},{5,13},{6,14},{7,15},{8,0},{9,1},... | collective-permute-start | bytes 196616 | tf_op jit(solution)/shard_map/ppermute | solution.py:63
  111.4 12.4 %collective-permute-start.25 = (f32[128,256]{1,0:T(8,128)S(1)}, f32[128,256]{1,0:T(8,128)S(1)}, u32[]{:S(2)}, u32[]{:S(2)}) collective-permute-start(f32[128,256]{1,0:T(8,128)S(1)} %add.121), channel_id=1, source_target_pairs={{0,2},{1,3},{2,0},{3,1},{4,6},{5,7},{6,4},{7,5},{8,10},{9,11},{10,... | collective-permute-start | bytes 393224 | tf_op jit(solution)/shard_map/ppermute | solution.py:63
  124.9 9.5 %collective-permute-start.33 = (f32[128,256]{1,0:T(8,128)S(1)}, f32[128,256]{1,0:T(8,128)S(1)}, u32[]{:S(2)}, u32[]{:S(2)}) collective-permute-start(f32[128,256]{1,0:T(8,128)S(1)} %fusion.7.refs_3_), channel_id=1, source_target_pairs={{0,16},{16,0},{1,17},{17,1},{2,18},{18,2},{3,19},{19,3},{4,20},{20... | collective-permute-start | bytes 393224 | tf_op jit(solution)/shard_map/ppermute | solution.py:63
  131.1 8.7 %collective-permute-start.30 = (f32[128,256]{1,0:T(8,128)S(1)}, f32[128,256]{1,0:T(8,128)S(1)}, u32[]{:S(2)}, u32[]{:S(2)}) collective-permute-start(f32[128,256]{1,0:T(8,128)S(1)} %add.124.refs_0_), channel_id=1, source_target_pairs={{0,8},{1,9},{2,10},{3,11},{4,12},{5,13},{6,14},{7,15},{8,0},{9,1},... | collective-permute-start | bytes 393224 | tf_op jit(solution)/shard_map/ppermute | solution.py:63
  131.4 9.9 %collective-permute-start.35 = (bf16[1,128,512]{2,1,0:T(8,128)(2,1)S(1)}, bf16[1,128,512]{2,1,0:T(8,128)(2,1)S(1)}, u32[]{:S(2)}, u32[]{:S(2)}) collective-permute-start(bf16[1,128,512]{2,1,0:T(8,128)(2,1)S(1)} %fusion.5), channel_id=1, source_target_pairs={{0,8},{1,9},{2,10},{3,11},{4,12},{5,13},{6,14},{7,15},{8,0},{9,1},... | collective-permute-start | bytes 393224 | tf_op jit(solution)/shard_map/ppermute | solution.py:63
  (23 other events, 233.6 us)

commit v10 on v9

--- a/solution.py
+++ b/solution.py
@@ -379,8 +379,7 @@
         if m != low:
             shards[m] = swap(after(shards[m ^ low], shards[order[k - 2] ^ 2]), low)
         if k:
-            ties = [small] if m ^ 2 == ends else []
-            shards[m ^ 2] = swap(after(shards[m], shards[order[k - 1] ^ 2], *ties), 2)
+            shards[m ^ 2] = swap(after(shards[m], shards[order[k - 1] ^ 2]), 2)
     small = after(small, shards[peers // 2])
     small = small + swap(small, peers // 2)
     small = small + swap(small.astype(BF16), 2).astype(F32)
@@ -422,13 +421,13 @@
     )
     thins, chunks = rest[:thin_count], rest[thin_count:]
     got = [swap(give, 1) for give in chunks[::2]]
-    sum_out, out_x = scatter_sum(got[0], chunks[1])
     sum_in, in_x = scatter_sum(got[1], chunks[3])
+    sum_out, out_x = scatter_sum(got[0], chunks[1], [[in_x]])
     sum_out = sum_out[0] + sum_out[1].astype(F32)
     ends_out = [sum_out]
     if sections == 2:
         ends_out = [swap(sum_out, 1, "section"), sum_out]
-    waits = [got[1], out_x, in_x]
+    waits = [None, out_x, None]
     terms = [term for thin in thins for term in sum_thin(thin, waits)]
     grad_in, grad_out = call(
         functools.partial(end_kernel, sections),

time: 143 us -> 147 us (1.028)
  starting transfers between devices: 35.8 us -> 39 us
    ppermute x36, starting transfers between devices: 35.8 us -> 39 us  [swap(): return lax.ppermute(value, axis, [(i, i ^ bits) for i in range(peers)])]
  transfers between devices with their start and end apart: 36 -> 36, of which waited for: 18 -> 18; matrix products, arithmetic and copies ran while one was open for 3% -> 2% of each run, Pallas kernels for 7% -> 7%
where the time goes in v10:
time: 147 us
  waiting for transfers between devices  70.9 us (48%)
  starting transfers between devices  39 us (27%)
  Pallas kernels  18.9 us (13%)
  local copies, waits for them, and re-layouts  13.1 us (9%)
  other arithmetic  3.9 us (3%)
    ppermute x36, waiting for transfers between devices, swap(): return lax.ppermute(value, axis, [(i, i ^ bits) for i in range(peers)])  70.9 us
    ppermute x36, starting transfers between devices, swap(): return lax.ppermute(value, axis, [(i, i ^ bits) for i in range(peers)])  39 us
    pallas_call x6, Pallas kernels, call(): pl.pallas_call(kernel, in_specs=[IN_SMEM] + [IN_HBM] * len(far) + [IN_VME...  18.9 us
    unnamed x22, local copies, waits for them, and re-layouts  12.8 us
  transfers between devices with their start and end apart: 36, of which 18 were waited for; matrix products, arithmetic and copies ran while one was open for 2% of the time, Pallas kernels for 7%

profile of v10, /device:TPU:0, one launch (start us, length us, event | category | flops | bytes accessed | tf_op | source)
XLA Modules:
  0.0 146.7 jit_solution(4226185661772976205)
XLA Ops:
  3.8 3.0 %collective-permute-start.2 = (bf16[1280,128]{1,0:T(8,128)(2,1)}, bf16[1280,128]{1,0:T(8,128)(2,1)S(1)}, u32[]{:S(2)}, u32[]{:S(2)}) collective-permute-start(bf16[1280,128]{1,0:T(8,128)(2,1)} %shard_map.85.refs_0_.own_ref), channel_id=1, source_target_pairs={{0,2},{1,3},{2,0},{3,1},{4,6},{5,7},{6,4},{7,5},{8,10},{9,11},{10,... | collective-permute-start | bytes 983048 | tf_op jit(solution)/shard_map/ppermute | solution.py:63
  8.4 6.3 %collective-permute-done.2.refs_1_ = bf16[1280,128]{1,0:T(8,128)(2,1)S(1)} collective-permute-done((bf16[1280,128]{1,0:T(8,128)(2,1)}, bf16[1280,128]{1,0:T(8,128)(2,1)S(1)}, u32[]{:S(2)}, u32[]{:S(2)}) %collective-permute-start.2) | collective-permute-done | bytes 327712 | tf_op jit(solution)/shard_map/ppermute | solution.py:63
  16.6 2.7 %collective-permute-start.1 = (bf16[1280,128]{1,0:T(8,128)(2,1)}, bf16[1280,128]{1,0:T(8,128)(2,1)S(1)}, u32[]{:S(2)}, u32[]{:S(2)}) collective-permute-start(bf16[1280,128]{1,0:T(8,128)(2,1)} %shard_map.85.refs_0_.own_ref), channel_id=1, source_target_pairs={{0,8},{1,9},{2,10},{3,11},{4,12},{5,13},{6,14},{7,15},{8,0},{9,1},... | collective-permute-start | bytes 983048 | tf_op jit(solution)/shard_map/ppermute | solution.py:63
  19.9 4.5 %collective-permute-done.3.refs_3_ = bf16[1280,128]{1,0:T(8,128)(2,1)S(1)} collective-permute-done((bf16[1280,128]{1,0:T(8,128)(2,1)S(1)}, bf16[1280,128]{1,0:T(8,128)(2,1)S(1)}, u32[]{:S(2)}, u32[]{:S(2)}) %collective-permute-start.3) | collective-permute-done | bytes 327712 | tf_op jit(solution)/shard_map/ppermute | solution.py:63
  24.4 3.0 %shard_map.88 = (f32[192,256]{1,0:T(8,128)}, f32[192,256]{1,0:T(8,128)}) custom-call(s32[2]{0:T(128)} %pad_add_fusion.2.scalars, bf16[512,128]{1,0:T(8,128)(2,1)} %bitcast.89, bf16[512,256]{1,0:T(8,128)(2,1)} %space_ref.3, bf16[1280,128]{1,0:T(8,128)(2,1)} %shard_map.85.refs_0_.own_ref), custom_call_target="tpu_custom_call" | custom-call | tf_op jit(solution)/shard_map/pallas_call | solution.py:43
  28.1 4.9 %collective-permute-done.1.refs_4_ = bf16[1280,128]{1,0:T(8,128)(2,1)S(1)} collective-permute-done((bf16[1280,128]{1,0:T(8,128)(2,1)}, bf16[1280,128]{1,0:T(8,128)(2,1)S(1)}, u32[]{:S(2)}, u32[]{:S(2)}) %collective-permute-start.1) | collective-permute-done | bytes 327712 | tf_op jit(solution)/shard_map/ppermute | solution.py:63
  37.9 3.8 %collective-permute-done.5.refs_5_ = bf16[1280,128]{1,0:T(8,128)(2,1)S(1)} collective-permute-done((bf16[1280,128]{1,0:T(8,128)(2,1)S(1)}, bf16[1280,128]{1,0:T(8,128)(2,1)S(1)}, u32[]{:S(2)}, u32[]{:S(2)}) %collective-permute-start.5) | collective-permute-done | bytes 327712 | tf_op jit(solution)/shard_map/ppermute | solution.py:63
  41.7 3.1 %collective-permute-done.4.refs_6_ = bf16[1280,128]{1,0:T(8,128)(2,1)S(1)} collective-permute-done((bf16[1280,128]{1,0:T(8,128)(2,1)S(1)}, bf16[1280,128]{1,0:T(8,128)(2,1)S(1)}, u32[]{:S(2)}, u32[]{:S(2)}) %collective-permute-start.4) | collective-permute-done | bytes 327712 | tf_op jit(solution)/shard_map/ppermute | solution.py:63
  49.4 3.2 %collective-permute-start.18 = (f32[192,256]{1,0:T(8,128)S(1)}, f32[192,256]{1,0:T(8,128)S(1)}, u32[]{:S(2)}, u32[]{:S(2)}) collective-permute-start(f32[192,256]{1,0:T(8,128)S(1)} %add.118), channel_id=1, source_target_pairs={{0,8},{1,9},{2,10},{3,11},{4,12},{5,13},{6,14},{7,15},{8,0},{9,1},... | collective-permute-start | bytes 589832 | tf_op jit(solution)/shard_map/ppermute | solution.py:63
  52.6 2.8 %copy-done = bf16[384,8192]{1,0:T(8,128)(2,1)S(1)} copy-done((bf16[384,8192]{1,0:T(8,128)(2,1)S(1)}, bf16[384,8192]{1,0:T(8,128)(2,1)}, u32[]{:S(2)}) %copy-start) | copy-done | bytes 6291480
  55.4 2.8 %copy-done.3 = bf16[384,8192]{1,0:T(8,128)(2,1)S(1)} copy-done((bf16[384,8192]{1,0:T(8,128)(2,1)S(1)}, bf16[384,8192]{1,0:T(8,128)(2,1)}, u32[]{:S(2)}) %copy-start.3) | copy-done | bytes 6291480
  59.2 5.8 %shard_map.86.refs_2_ = f32[384,768]{1,0:T(8,128)S(1)} custom-call(s32[15]{0:T(128)S(1)} %stack.203.scalars, bf16[384,8192]{1,0:T(8,128)(2,1)S(1)} %copy-done, bf16[384,8192]{1,0:T(8,128)(2,1)S(1)} %copy-done.3, bf16[1280,128]{1,0:T(8,128)(2,1)S(1)} %copy-done.6, bf16[1280,128]{1,0:T(8,128)(2,1)S(1)} %collective-permute-done.2.refs_1_, ...), custom_call_target="tpu_custom_call" | custom-call | flops 3523215360 | tf_op jit(solution)/shard_map/pallas_call | solution.py:43
  73.8 10.4 %collective-permute-done.20.refs_2_ = bf16[192,256]{1,0:T(8,128)(2,1)S(1)} collective-permute-done((bf16[192,256]{1,0:T(8,128)(2,1)S(1)}, bf16[192,256]{1,0:T(8,128)(2,1)S(1)}, u32[]{:S(2)}, u32[]{:S(2)}) %collective-permute-start.20) | collective-permute-done | bytes 98336 | tf_op jit(solution)/shard_map/ppermute | solution.py:63
  85.6 2.8 %copy-done.2 = bf16[384,8192]{1,0:T(8,128)(2,1)S(1)} copy-done((bf16[384,8192]{1,0:T(8,128)(2,1)S(1)}, bf16[384,8192]{1,0:T(8,128)(2,1)}, u32[]{:S(2)}) %copy-start.2) | copy-done | bytes 6291480
  88.4 2.8 %copy-done.5 = bf16[384,8192]{1,0:T(8,128)(2,1)S(1)} copy-done((bf16[384,8192]{1,0:T(8,128)(2,1)S(1)}, bf16[384,8192]{1,0:T(8,128)(2,1)}, u32[]{:S(2)}) %copy-start.5) | copy-done | bytes 6291480
  91.2 4.4 %shard_map.89 = (bf16[384,256]{1,0:T(8,128)(2,1)}, f32[128,256]{1,0:T(8,128)S(1)}, bf16[8,128,256]{2,1,0:T(8,128)(2,1)S(1)}, bf16[8,128,256]{2,1,0:T(8,128)(2,1)...) custom-call(s32[34]{0:T(128)S(1)} %stack.192.scalars, bf16[384,8192]{1,0:T(8,128)(2,1)S(1)} %copy-done.2, ...), custom_call_target="tpu_custom_call" | custom-call | tf_op jit(solution)/shard_map/pallas_call | solution.py:43
  96.2 3.0 %collective-permute-done.23 = f32[128,256]{1,0:T(8,128)S(1)} collective-permute-done((f32[128,256]{1,0:T(8,128)S(1)}, f32[128,256]{1,0:T(8,128)S(1)}, u32[]{:S(2)}, u32[]{:S(2)}) %collective-permute-start.23) | collective-permute-done | bytes 131104 | tf_op jit(solution)/shard_map/ppermute | solution.py:63
  103.0 2.6 %collective-permute-done.24 = f32[128,256]{1,0:T(8,128)S(1)} collective-permute-done((f32[128,256]{1,0:T(8,128)S(1)}, f32[128,256]{1,0:T(8,128)S(1)}, u32[]{:S(2)}, u32[]{:S(2)}) %collective-permute-start.24) | collective-permute-done | bytes 131104 | tf_op jit(solution)/shard_map/ppermute | solution.py:63
  105.7 5.6 %collective-permute-done.26 = bf16[4,128,256]{2,1,0:T(8,128)(2,1)S(1)} collective-permute-done((bf16[4,128,256]{2,1,0:T(8,128)(2,1)S(1)}, bf16[4,128,256]{2,1,0:T(8,128)(2,1)S(1)}, u32[]{:S(2)}, u32[]{:S(2)}) %collective-permute-start.26) | collective-permute-done | bytes 262176 | tf_op jit(solution)/shard_map/ppermute | solution.py:63
  113.1 8.6 %collective-permute-done.30 = bf16[4,128,512]{2,1,0:T(8,128)(2,1)S(1)} collective-permute-done((bf16[4,128,512]{2,1,0:T(8,128)(2,1)S(1)}, bf16[4,128,512]{2,1,0:T(8,128)(2,1)S(1)}, u32[]{:S(2)}, u32[]{:S(2)}) %collective-permute-start.30) | collective-permute-done | bytes 524320 | tf_op jit(solution)/shard_map/ppermute | solution.py:63
  123.6 3.0 %collective-permute-done.31 = bf16[2,128,256]{2,1,0:T(8,128)(2,1)S(1)} collective-permute-done((bf16[2,128,256]{2,1,0:T(8,128)(2,1)S(1)}, bf16[2,128,256]{2,1,0:T(8,128)(2,1)S(1)}, u32[]{:S(2)}, u32[]{:S(2)}) %collective-permute-start.31) | collective-permute-done | bytes 131104 | tf_op jit(solution)/shard_map/ppermute | solution.py:63
  129.3 3.0 %collective-permute-start.28 = (f32[128,256]{1,0:T(8,128)S(1)}, f32[128,256]{1,0:T(8,128)S(1)}, u32[]{:S(2)}, u32[]{:S(2)}) collective-permute-start(f32[128,256]{1,0:T(8,128)S(1)} %add.124.refs_0_), channel_id=1, source_target_pairs={{0,8},{1,9},{2,10},{3,11},{4,12},{5,13},{6,14},{7,15},{8,0},{9,1},... | collective-permute-start | bytes 393224 | tf_op jit(solution)/shard_map/ppermute | solution.py:63
  134.3 3.2 %collective-permute-done.34 = bf16[2,128,512]{2,1,0:T(8,128)(2,1)S(1)} collective-permute-done((bf16[2,128,512]{2,1,0:T(8,128)(2,1)S(1)}, bf16[2,128,512]{2,1,0:T(8,128)(2,1)S(1)}, u32[]{:S(2)}, u32[]{:S(2)}) %collective-permute-start.34) | collective-permute-done | bytes 262176 | tf_op jit(solution)/shard_map/ppermute | solution.py:63
  138.9 6.0 %collective-permute-done.35 = bf16[1,128,512]{2,1,0:T(8,128)(2,1)S(1)} collective-permute-done((bf16[1,128,512]{2,1,0:T(8,128)(2,1)S(1)}, bf16[1,128,512]{2,1,0:T(8,128)(2,1)S(1)}, u32[]{:S(2)}, u32[]{:S(2)}) %collective-permute-start.35) | collective-permute-done | bytes 131104 | tf_op jit(solution)/shard_map/ppermute | solution.py:63
  (101 shorter events, 44.5 us)
Async XLA Ops:
  3.8 10.9 %collective-permute-start.2 = (bf16[1280,128]{1,0:T(8,128)(2,1)}, bf16[1280,128]{1,0:T(8,128)(2,1)S(1)}, u32[]{:S(2)}, u32[]{:S(2)}) collective-permute-start(bf16[1280,128]{1,0:T(8,128)(2,1)} %shard_map.85.refs_0_.own_ref), channel_id=1, source_target_pairs={{0,2},{1,3},{2,0},{3,1},{4,6},{5,7},{6,4},{7,5},{8,10},{9,11},{10,... | collective-permute-start | bytes 983048 | tf_op jit(solution)/shard_map/ppermute | solution.py:63
  6.8 9.4 %collective-permute-start = (bf16[1280,128]{1,0:T(8,128)(2,1)}, bf16[1280,128]{1,0:T(8,128)(2,1)S(1)}, u32[]{:S(2)}, u32[]{:S(2)}) collective-permute-start(bf16[1280,128]{1,0:T(8,128)(2,1)} %shard_map.85.refs_0_.own_ref), channel_id=1, source_target_pairs={{0,4},{1,5},{2,6},{3,7},{4,0},{5,1},{6,2},{7,3},{8,12},{9,13},{10,... | collective-permute-start | bytes 983048 | tf_op jit(solution)/shard_map/ppermute | solution.py:63
  16.2 8.3 %collective-permute-start.3 = (bf16[1280,128]{1,0:T(8,128)(2,1)S(1)}, bf16[1280,128]{1,0:T(8,128)(2,1)S(1)}, u32[]{:S(2)}, u32[]{:S(2)}) collective-permute-start(bf16[1280,128]{1,0:T(8,128)(2,1)S(1)} %collective-permute-done.refs_2_), channel_id=1, source_target_pairs={{0,2},{1,3},{2,0},{3,1},{4,6},{5,7},{6,4},{7,5},{8,10},{9,11},{10,... | collective-permute-start | bytes 983048 | tf_op jit(solution)/shard_map/ppermute | solution.py:63
  16.6 16.4 %collective-permute-start.1 = (bf16[1280,128]{1,0:T(8,128)(2,1)}, bf16[1280,128]{1,0:T(8,128)(2,1)S(1)}, u32[]{:S(2)}, u32[]{:S(2)}) collective-permute-start(bf16[1280,128]{1,0:T(8,128)(2,1)} %shard_map.85.refs_0_.own_ref), channel_id=1, source_target_pairs={{0,8},{1,9},{2,10},{3,11},{4,12},{5,13},{6,14},{7,15},{8,0},{9,1},... | collective-permute-start | bytes 983048 | tf_op jit(solution)/shard_map/ppermute | solution.py:63
  27.5 7.6 %collective-permute-start.16 = (f32[192,256]{1,0:T(8,128)}, f32[192,256]{1,0:T(8,128)S(1)}, u32[]{:S(2)}, u32[]{:S(2)}) collective-permute-start(f32[192,256]{1,0:T(8,128)} %get-tuple-element.33), channel_id=1, source_target_pairs={{0,1},{1,0},{2,3},{3,2},{4,5},{5,4},{6,7},{7,6},{8,9},{9,8},{10,11... | collective-permute-start | bytes 589832 | tf_op jit(solution)/shard_map/ppermute | solution.py:63
  27.6 9.8 %collective-permute-start.7 = (bf16[1280,128]{1,0:T(8,128)(2,1)}, bf16[1280,128]{1,0:T(8,128)(2,1)S(1)}, u32[]{:S(2)}, u32[]{:S(2)}) collective-permute-start(bf16[1280,128]{1,0:T(8,128)(2,1)} %shard_map.85.refs_0_.own_ref), channel_id=1, source_target_pairs={{0,1},{1,0},{2,3},{3,2},{4,5},{5,4},{6,7},{7,6},{8,9},{9,8},{10,11... | collective-permute-start | bytes 983048 | tf_op jit(solution)/shard_map/ppermute | solution.py:63
  28.1 9.3 %collective-permute-start.8 = (bf16[1280,128]{1,0:T(8,128)(2,1)S(1)}, bf16[1280,128]{1,0:T(8,128)(2,1)S(1)}, u32[]{:S(2)}, u32[]{:S(2)}) collective-permute-start(bf16[1280,128]{1,0:T(8,128)(2,1)S(1)} %collective-permute-done.2.refs_1_), channel_id=1, source_target_pairs={{0,1},{1,0},{2,3},{3,2},{4,5},{5,4},{6,7},{7,6},{8,9},{9,8},{10,11... | collective-permute-start | bytes 983048 | tf_op jit(solution)/shard_map/ppermute | solution.py:63
  33.0 8.7 %collective-permute-start.5 = (bf16[1280,128]{1,0:T(8,128)(2,1)S(1)}, bf16[1280,128]{1,0:T(8,128)(2,1)S(1)}, u32[]{:S(2)}, u32[]{:S(2)}) collective-permute-start(bf16[1280,128]{1,0:T(8,128)(2,1)S(1)} %collective-permute-done.1.refs_4_), channel_id=1, source_target_pairs={{0,2},{1,3},{2,0},{3,1},{4,6},{5,7},{6,4},{7,5},{8,10},{9,11},{10,... | collective-permute-start | bytes 983048 | tf_op jit(solution)/shard_map/ppermute | solution.py:63
  34.3 10.5 %collective-permute-start.4 = (bf16[1280,128]{1,0:T(8,128)(2,1)S(1)}, bf16[1280,128]{1,0:T(8,128)(2,1)S(1)}, u32[]{:S(2)}, u32[]{:S(2)}) collective-permute-start(bf16[1280,128]{1,0:T(8,128)(2,1)S(1)} %collective-permute-done.1.refs_4_), channel_id=1, source_target_pairs={{0,4},{1,5},{2,6},{3,7},{4,0},{5,1},{6,2},{7,3},{8,12},{9,13},{10,... | collective-permute-start | bytes 983048 | tf_op jit(solution)/shard_map/ppermute | solution.py:63
  36.0 10.9 %collective-permute-start.17 = (f32[192,256]{1,0:T(8,128)S(1)}, f32[192,256]{1,0:T(8,128)S(1)}, u32[]{:S(2)}, u32[]{:S(2)}) collective-permute-start(f32[192,256]{1,0:T(8,128)S(1)} %add.117), channel_id=1, source_target_pairs={{0,4},{1,5},{2,6},{3,7},{4,0},{5,1},{6,2},{7,3},{8,12},{9,13},{10,... | collective-permute-start | bytes 589832 | tf_op jit(solution)/shard_map/ppermute | solution.py:63
  37.4 11.3 %collective-permute-start.9 = (bf16[1280,128]{1,0:T(8,128)(2,1)S(1)}, bf16[1280,128]{1,0:T(8,128)(2,1)S(1)}, u32[]{:S(2)}, u32[]{:S(2)}) collective-permute-start(bf16[1280,128]{1,0:T(8,128)(2,1)S(1)} %collective-permute-done.refs_2_), channel_id=1, source_target_pairs={{0,1},{1,0},{2,3},{3,2},{4,5},{5,4},{6,7},{7,6},{8,9},{9,8},{10,11... | collective-permute-start | bytes 983048 | tf_op jit(solution)/shard_map/ppermute | solution.py:63
  37.4 12.1 %collective-permute-start.11 = (bf16[1280,128]{1,0:T(8,128)(2,1)S(1)}, bf16[1280,128]{1,0:T(8,128)(2,1)S(1)}, u32[]{:S(2)}, u32[]{:S(2)}) collective-permute-start(bf16[1280,128]{1,0:T(8,128)(2,1)S(1)} %collective-permute-done.1.refs_4_), channel_id=1, source_target_pairs={{0,1},{1,0},{2,3},{3,2},{4,5},{5,4},{6,7},{7,6},{8,9},{9,8},{10,11... | collective-permute-start | bytes 983048 | tf_op jit(solution)/shard_map/ppermute | solution.py:63
  41.7 10.9 %collective-permute-start.10 = (bf16[1280,128]{1,0:T(8,128)(2,1)S(1)}, bf16[1280,128]{1,0:T(8,128)(2,1)}, u32[]{:S(2)}, u32[]{:S(2)}) collective-permute-start(bf16[1280,128]{1,0:T(8,128)(2,1)S(1)} %collective-permute-done.3.refs_3_), channel_id=1, source_target_pairs={{0,1},{1,0},{2,3},{3,2},{4,5},{5,4},{6,7},{7,6},{8,9},{9,8},{10,11... | collective-permute-start | bytes 983048 | tf_op jit(solution)/shard_map/ppermute | solution.py:63
  44.8 7.8 %collective-permute-start.12 = (bf16[1280,128]{1,0:T(8,128)(2,1)S(1)}, bf16[1280,128]{1,0:T(8,128)(2,1)}, u32[]{:S(2)}, u32[]{:S(2)}) collective-permute-start(bf16[1280,128]{1,0:T(8,128)(2,1)S(1)} %collective-permute-done.5.refs_5_), channel_id=1, source_target_pairs={{0,1},{1,0},{2,3},{3,2},{4,5},{5,4},{6,7},{7,6},{8,9},{9,8},{10,11... | collective-permute-start | bytes 983048 | tf_op jit(solution)/shard_map/ppermute | solution.py:63
  48.7 16.3 %collective-permute-start.6 = (bf16[1280,128]{1,0:T(8,128)(2,1)S(1)}, bf16[1280,128]{1,0:T(8,128)(2,1)S(1)}, u32[]{:S(2)}, u32[]{:S(2)}) collective-permute-start(bf16[1280,128]{1,0:T(8,128)(2,1)S(1)} %collective-permute-done.4.refs_6_), channel_id=1, source_target_pairs={{0,2},{1,3},{2,0},{3,1},{4,6},{5,7},{6,4},{7,5},{8,10},{9,11},{10,... | collective-permute-start | bytes 983048 | tf_op jit(solution)/shard_map/ppermute | solution.py:63
  49.4 15.6 %collective-permute-start.18 = (f32[192,256]{1,0:T(8,128)S(1)}, f32[192,256]{1,0:T(8,128)S(1)}, u32[]{:S(2)}, u32[]{:S(2)}) collective-permute-start(f32[192,256]{1,0:T(8,128)S(1)} %add.118), channel_id=1, source_target_pairs={{0,8},{1,9},{2,10},{3,11},{4,12},{5,13},{6,14},{7,15},{8,0},{9,1},... | collective-permute-start | bytes 589832 | tf_op jit(solution)/shard_map/ppermute | solution.py:63
  68.0 17.6 %collective-permute-start.15 = (bf16[384,640]{1,0:T(8,128)(2,1)S(1)}, bf16[384,640]{1,0:T(8,128)(2,1)S(1)}, u32[]{:S(2)}, u32[]{:S(2)}) collective-permute-start(bf16[384,640]{1,0:T(8,128)(2,1)S(1)} %get-tuple-element.30), channel_id=1, source_target_pairs={{0,16},{16,0},{1,17},{17,1},{2,18},{18,2},{3,19},{19,3},{4,20},{20... | collective-permute-start | bytes 1474568 | tf_op jit(solution)/shard_map/ppermute | solution.py:63
  70.5 13.8 %collective-permute-start.20 = (bf16[192,256]{1,0:T(8,128)(2,1)S(1)}, bf16[192,256]{1,0:T(8,128)(2,1)S(1)}, u32[]{:S(2)}, u32[]{:S(2)}) collective-permute-start(bf16[192,256]{1,0:T(8,128)(2,1)S(1)} %get-tuple-element.45), channel_id=1, source_target_pairs={{0,16},{16,0},{1,17},{17,1},{2,18},{18,2},{3,19},{19,3},{4,20},{20... | collective-permute-start | bytes 294920 | tf_op jit(solution)/shard_map/ppermute | solution.py:63
  72.3 13.4 %collective-permute-start.22 = (bf16[192,256]{1,0:T(8,128)(2,1)S(1)}, bf16[192,256]{1,0:T(8,128)(2,1)S(1)}, u32[]{:S(2)}, u32[]{:S(2)}) collective-permute-start(bf16[192,256]{1,0:T(8,128)(2,1)S(1)} %convert_element_type.99), channel_id=1, source_target_pairs={{0,16},{16,0},{1,17},{17,1},{2,18},{18,2},{3,19},{19,3},{4,20},{20... | collective-permute-start | bytes 294920 | tf_op jit(solution)/shard_map/ppermute | solution.py:63
  100.7 10.5 %collective-permute-start.26 = (bf16[4,128,256]{2,1,0:T(8,128)(2,1)S(1)}, bf16[4,128,256]{2,1,0:T(8,128)(2,1)S(1)}, u32[]{:S(2)}, u32[]{:S(2)}) collective-permute-start(bf16[4,128,256]{2,1,0:T(8,128)(2,1)S(1)} %add_convert_fusion.1), channel_id=1, source_target_pairs={{0,2},{1,3},{2,0},{3,1},{4,6},{5,7},{6,4},{7,5},{8,10},{9,11},{10,... | collective-permute-start | bytes 786440 | tf_op jit(solution)/shard_map/ppermute | solution.py:63
  101.6 20.1 %collective-permute-start.30 = (bf16[4,128,512]{2,1,0:T(8,128)(2,1)S(1)}, bf16[4,128,512]{2,1,0:T(8,128)(2,1)S(1)}, u32[]{:S(2)}, u32[]{:S(2)}) collective-permute-start(bf16[4,128,512]{2,1,0:T(8,128)(2,1)S(1)} %add_convert_fusion), channel_id=1, source_target_pairs={{0,2},{1,3},{2,0},{3,1},{4,6},{5,7},{6,4},{7,5},{8,10},{9,11},{10,... | collective-permute-start | bytes 1572872 | tf_op jit(solution)/shard_map/ppermute | solution.py:63
  111.3 18.0 %collective-permute-start.27 = (f32[128,256]{1,0:T(8,128)S(1)}, f32[128,256]{1,0:T(8,128)S(1)}, u32[]{:S(2)}, u32[]{:S(2)}) collective-permute-start(f32[128,256]{1,0:T(8,128)S(1)} %add.122), channel_id=1, source_target_pairs={{0,4},{1,5},{2,6},{3,7},{4,0},{5,1},{6,2},{7,3},{8,12},{9,13},{10,... | collective-permute-start | bytes 393224 | tf_op jit(solution)/shard_map/ppermute | solution.py:63
  126.8 10.6 %collective-permute-start.34 = (bf16[2,128,512]{2,1,0:T(8,128)(2,1)S(1)}, bf16[2,128,512]{2,1,0:T(8,128)(2,1)S(1)}, u32[]{:S(2)}, u32[]{:S(2)}) collective-permute-start(bf16[2,128,512]{2,1,0:T(8,128)(2,1)S(1)} %fusion.2), channel_id=1, source_target_pairs={{0,4},{1,5},{2,6},{3,7},{4,0},{5,1},{6,2},{7,3},{8,12},{9,13},{10,... | collective-permute-start | bytes 786440 | tf_op jit(solution)/shard_map/ppermute | solution.py:63
  129.3 9.6 %collective-permute-start.28 = (f32[128,256]{1,0:T(8,128)S(1)}, f32[128,256]{1,0:T(8,128)S(1)}, u32[]{:S(2)}, u32[]{:S(2)}) collective-permute-start(f32[128,256]{1,0:T(8,128)S(1)} %add.124.refs_0_), channel_id=1, source_target_pairs={{0,8},{1,9},{2,10},{3,11},{4,12},{5,13},{6,14},{7,15},{8,0},{9,1},... | collective-permute-start | bytes 393224 | tf_op jit(solution)/shard_map/ppermute | solution.py:63
  (23 other events, 234.4 us)

commit v11 on v10

--- a/solution.py
+++ b/solution.py
@@ -316,7 +316,7 @@
             waits = waits[1:]
         arrived = swap(give, bit)
         if left.shape[0] == 1:
-            return (left[0, 0], arrived[0]), got_x
+            return (left[0, 0], arrived[0]), got_x, total
         total = left[:, 0] + arrived.astype(F32)
         bit *= 2
 
@@ -421,13 +421,13 @@
     )
     thins, chunks = rest[:thin_count], rest[thin_count:]
     got = [swap(give, 1) for give in chunks[::2]]
-    sum_in, in_x = scatter_sum(got[1], chunks[3])
-    sum_out, out_x = scatter_sum(got[0], chunks[1], [[in_x]])
+    sum_in, in_x, in_near = scatter_sum(got[1], chunks[3])
+    sum_out, out_x, _ = scatter_sum(got[0], chunks[1], [[in_x], [in_near]])
     sum_out = sum_out[0] + sum_out[1].astype(F32)
     ends_out = [sum_out]
     if sections == 2:
         ends_out = [swap(sum_out, 1, "section"), sum_out]
-    waits = [None, out_x, None]
+    waits = [got[1], out_x, None]
     terms = [term for thin in thins for term in sum_thin(thin, waits)]
     grad_in, grad_out = call(
         functools.partial(end_kernel, sections),

time: 147 us -> 153 us (1.041)
  waiting for transfers between devices: 70.9 us -> 80 us
  starting transfers between devices: 39 us -> 36.3 us
    ppermute x36, waiting for transfers between devices: 70.9 us -> 80 us  [swap(): return lax.ppermute(value, axis, [(i, i ^ bits) for i in range(peers)])]
    ppermute x36, starting transfers between devices: 39 us -> 36.3 us  [swap(): return lax.ppermute(value, axis, [(i, i ^ bits) for i in range(peers)])]
  transfers between devices with their start and end apart: 36 -> 36, of which waited for: 18 -> 19; matrix products, arithmetic and copies ran while one was open for 2% -> 2% of each run, Pallas kernels for 7% -> 7%
where the time goes in v11:
time: 153 us
  waiting for transfers between devices  80 us (52%)
  starting transfers between devices  36.3 us (24%)
  Pallas kernels  18.9 us (12%)
  local copies, waits for them, and re-layouts  13.1 us (9%)
  other arithmetic  3.92 us (3%)
    ppermute x36, waiting for transfers between devices, swap(): return lax.ppermute(value, axis, [(i, i ^ bits) for i in range(peers)])  80 us
    ppermute x36, starting transfers between devices, swap(): return lax.ppermute(value, axis, [(i, i ^ bits) for i in range(peers)])  36.3 us
    pallas_call x6, Pallas kernels, call(): pl.pallas_call(kernel, in_specs=[IN_SMEM] + [IN_HBM] * len(far) + [IN_VME...  18.9 us
    unnamed x22, local copies, waits for them, and re-layouts  12.8 us
  transfers between devices with their start and end apart: 36, of which 19 were waited for; matrix products, arithmetic and copies ran while one was open for 2% of the time, Pallas kernels for 7%

profile of v11, /device:TPU:0, one launch (start us, length us, event | category | flops | bytes accessed | tf_op | source)
XLA Modules:
  0.0 153.1 jit_solution(10744407368611121194)
XLA Ops:
  3.8 3.0 %collective-permute-start.2 = (bf16[1280,128]{1,0:T(8,128)(2,1)}, bf16[1280,128]{1,0:T(8,128)(2,1)S(1)}, u32[]{:S(2)}, u32[]{:S(2)}) collective-permute-start(bf16[1280,128]{1,0:T(8,128)(2,1)} %shard_map.85.refs_0_.own_ref), channel_id=1, source_target_pairs={{0,2},{1,3},{2,0},{3,1},{4,6},{5,7},{6,4},{7,5},{8,10},{9,11},{10,... | collective-permute-start | bytes 983048 | tf_op jit(solution)/shard_map/ppermute | solution.py:63
  8.4 6.3 %collective-permute-done.2.refs_1_ = bf16[1280,128]{1,0:T(8,128)(2,1)S(1)} collective-permute-done((bf16[1280,128]{1,0:T(8,128)(2,1)}, bf16[1280,128]{1,0:T(8,128)(2,1)S(1)}, u32[]{:S(2)}, u32[]{:S(2)}) %collective-permute-start.2) | collective-permute-done | bytes 327712 | tf_op jit(solution)/shard_map/ppermute | solution.py:63
  16.6 2.7 %collective-permute-start.1 = (bf16[1280,128]{1,0:T(8,128)(2,1)}, bf16[1280,128]{1,0:T(8,128)(2,1)S(1)}, u32[]{:S(2)}, u32[]{:S(2)}) collective-permute-start(bf16[1280,128]{1,0:T(8,128)(2,1)} %shard_map.85.refs_0_.own_ref), channel_id=1, source_target_pairs={{0,8},{1,9},{2,10},{3,11},{4,12},{5,13},{6,14},{7,15},{8,0},{9,1},... | collective-permute-start | bytes 983048 | tf_op jit(solution)/shard_map/ppermute | solution.py:63
  19.9 4.5 %collective-permute-done.3.refs_3_ = bf16[1280,128]{1,0:T(8,128)(2,1)S(1)} collective-permute-done((bf16[1280,128]{1,0:T(8,128)(2,1)S(1)}, bf16[1280,128]{1,0:T(8,128)(2,1)S(1)}, u32[]{:S(2)}, u32[]{:S(2)}) %collective-permute-start.3) | collective-permute-done | bytes 327712 | tf_op jit(solution)/shard_map/ppermute | solution.py:63
  24.4 3.0 %shard_map.88 = (f32[192,256]{1,0:T(8,128)}, f32[192,256]{1,0:T(8,128)}) custom-call(s32[2]{0:T(128)} %pad_add_fusion.2.scalars, bf16[512,128]{1,0:T(8,128)(2,1)} %bitcast.88, bf16[512,256]{1,0:T(8,128)(2,1)} %space_ref.3, bf16[1280,128]{1,0:T(8,128)(2,1)} %shard_map.85.refs_0_.own_ref), custom_call_target="tpu_custom_call" | custom-call | tf_op jit(solution)/shard_map/pallas_call | solution.py:43
  28.1 4.9 %collective-permute-done.1.refs_4_ = bf16[1280,128]{1,0:T(8,128)(2,1)S(1)} collective-permute-done((bf16[1280,128]{1,0:T(8,128)(2,1)}, bf16[1280,128]{1,0:T(8,128)(2,1)S(1)}, u32[]{:S(2)}, u32[]{:S(2)}) %collective-permute-start.1) | collective-permute-done | bytes 327712 | tf_op jit(solution)/shard_map/ppermute | solution.py:63
  37.9 3.8 %collective-permute-done.5.refs_5_ = bf16[1280,128]{1,0:T(8,128)(2,1)S(1)} collective-permute-done((bf16[1280,128]{1,0:T(8,128)(2,1)S(1)}, bf16[1280,128]{1,0:T(8,128)(2,1)S(1)}, u32[]{:S(2)}, u32[]{:S(2)}) %collective-permute-start.5) | collective-permute-done | bytes 327712 | tf_op jit(solution)/shard_map/ppermute | solution.py:63
  41.7 3.1 %collective-permute-done.4.refs_6_ = bf16[1280,128]{1,0:T(8,128)(2,1)S(1)} collective-permute-done((bf16[1280,128]{1,0:T(8,128)(2,1)S(1)}, bf16[1280,128]{1,0:T(8,128)(2,1)S(1)}, u32[]{:S(2)}, u32[]{:S(2)}) %collective-permute-start.4) | collective-permute-done | bytes 327712 | tf_op jit(solution)/shard_map/ppermute | solution.py:63
  49.4 3.2 %collective-permute-start.18 = (f32[192,256]{1,0:T(8,128)S(1)}, f32[192,256]{1,0:T(8,128)S(1)}, u32[]{:S(2)}, u32[]{:S(2)}) collective-permute-start(f32[192,256]{1,0:T(8,128)S(1)} %add.118), channel_id=1, source_target_pairs={{0,8},{1,9},{2,10},{3,11},{4,12},{5,13},{6,14},{7,15},{8,0},{9,1},... | collective-permute-start | bytes 589832 | tf_op jit(solution)/shard_map/ppermute | solution.py:63
  52.6 2.8 %copy-done = bf16[384,8192]{1,0:T(8,128)(2,1)S(1)} copy-done((bf16[384,8192]{1,0:T(8,128)(2,1)S(1)}, bf16[384,8192]{1,0:T(8,128)(2,1)}, u32[]{:S(2)}) %copy-start) | copy-done | bytes 6291480
  55.4 2.8 %copy-done.3 = bf16[384,8192]{1,0:T(8,128)(2,1)S(1)} copy-done((bf16[384,8192]{1,0:T(8,128)(2,1)S(1)}, bf16[384,8192]{1,0:T(8,128)(2,1)}, u32[]{:S(2)}) %copy-start.3) | copy-done | bytes 6291480
  59.2 5.8 %shard_map.86.refs_2_ = f32[384,768]{1,0:T(8,128)S(1)} custom-call(s32[15]{0:T(128)S(1)} %stack.203.scalars, bf16[384,8192]{1,0:T(8,128)(2,1)S(1)} %copy-done, bf16[384,8192]{1,0:T(8,128)(2,1)S(1)} %copy-done.3, bf16[1280,128]{1,0:T(8,128)(2,1)S(1)} %copy-done.6, bf16[1280,128]{1,0:T(8,128)(2,1)S(1)} %collective-permute-done.2.refs_1_, ...), custom_call_target="tpu_custom_call" | custom-call | flops 3523215360 | tf_op jit(solution)/shard_map/pallas_call | solution.py:43
  73.8 10.4 %collective-permute-done.20.refs_2_ = bf16[192,256]{1,0:T(8,128)(2,1)S(1)} collective-permute-done((bf16[192,256]{1,0:T(8,128)(2,1)S(1)}, bf16[192,256]{1,0:T(8,128)(2,1)S(1)}, u32[]{:S(2)}, u32[]{:S(2)}) %collective-permute-start.20) | collective-permute-done | bytes 98336 | tf_op jit(solution)/shard_map/ppermute | solution.py:63
  85.6 2.8 %copy-done.2 = bf16[384,8192]{1,0:T(8,128)(2,1)S(1)} copy-done((bf16[384,8192]{1,0:T(8,128)(2,1)S(1)}, bf16[384,8192]{1,0:T(8,128)(2,1)}, u32[]{:S(2)}) %copy-start.2) | copy-done | bytes 6291480
  88.4 2.8 %copy-done.5 = bf16[384,8192]{1,0:T(8,128)(2,1)S(1)} copy-done((bf16[384,8192]{1,0:T(8,128)(2,1)S(1)}, bf16[384,8192]{1,0:T(8,128)(2,1)}, u32[]{:S(2)}) %copy-start.5) | copy-done | bytes 6291480
  91.2 4.4 %shard_map.89 = (bf16[384,256]{1,0:T(8,128)(2,1)}, f32[128,256]{1,0:T(8,128)S(1)}, bf16[8,128,256]{2,1,0:T(8,128)(2,1)S(1)}, bf16[8,128,256]{2,1,0:T(8,128)(2,1)...) custom-call(s32[34]{0:T(128)S(1)} %stack.192.scalars, bf16[384,8192]{1,0:T(8,128)(2,1)S(1)} %copy-done.2, ...), custom_call_target="tpu_custom_call" | custom-call | tf_op jit(solution)/shard_map/pallas_call | solution.py:43
  96.2 2.8 %collective-permute-done.26 = bf16[8,128,256]{2,1,0:T(8,128)(2,1)S(1)} collective-permute-done((bf16[8,128,256]{2,1,0:T(8,128)(2,1)S(1)}, bf16[8,128,256]{2,1,0:T(8,128)(2,1)S(1)}, u32[]{:S(2)}, u32[]{:S(2)}) %collective-permute-start.26) | collective-permute-done | bytes 524320 | tf_op jit(solution)/shard_map/ppermute | solution.py:63
  102.8 5.5 %collective-permute-done.27 = bf16[4,128,256]{2,1,0:T(8,128)(2,1)S(1)} collective-permute-done((bf16[4,128,256]{2,1,0:T(8,128)(2,1)S(1)}, bf16[4,128,256]{2,1,0:T(8,128)(2,1)S(1)}, u32[]{:S(2)}, u32[]{:S(2)}) %collective-permute-start.27) | collective-permute-done | bytes 262176 | tf_op jit(solution)/shard_map/ppermute | solution.py:63
  108.4 13.1 %collective-permute-done.25 = f32[128,256]{1,0:T(8,128)S(1)} collective-permute-done((f32[128,256]{1,0:T(8,128)S(1)}, f32[128,256]{1,0:T(8,128)S(1)}, u32[]{:S(2)}, u32[]{:S(2)}) %collective-permute-start.25) | collective-permute-done | bytes 131104 | tf_op jit(solution)/shard_map/ppermute | solution.py:63
  123.4 3.2 %collective-permute-done.28 = f32[128,256]{1,0:T(8,128)S(1)} collective-permute-done((f32[128,256]{1,0:T(8,128)S(1)}, f32[128,256]{1,0:T(8,128)S(1)}, u32[]{:S(2)}, u32[]{:S(2)}) %collective-permute-start.28) | collective-permute-done | bytes 131104 | tf_op jit(solution)/shard_map/ppermute | solution.py:63
  129.5 5.7 %collective-permute-done.31 = bf16[2,128,256]{2,1,0:T(8,128)(2,1)S(1)} collective-permute-done((bf16[2,128,256]{2,1,0:T(8,128)(2,1)S(1)}, bf16[2,128,256]{2,1,0:T(8,128)(2,1)S(1)}, u32[]{:S(2)}, u32[]{:S(2)}) %collective-permute-start.31) | collective-permute-done | bytes 131104 | tf_op jit(solution)/shard_map/ppermute | solution.py:63
  135.2 3.6 %collective-permute-done.32 = bf16[2,128,512]{2,1,0:T(8,128)(2,1)S(1)} collective-permute-done((bf16[2,128,512]{2,1,0:T(8,128)(2,1)S(1)}, bf16[2,128,512]{2,1,0:T(8,128)(2,1)S(1)}, u32[]{:S(2)}, u32[]{:S(2)}) %collective-permute-start.32) | collective-permute-done | bytes 262176 | tf_op jit(solution)/shard_map/ppermute | solution.py:63
  138.9 2.7 %collective-permute-start.33 = (bf16[1,128,256]{2,1,0:T(8,128)(2,1)S(1)}, bf16[1,128,256]{2,1,0:T(8,128)(2,1)S(1)}, u32[]{:S(2)}, u32[]{:S(2)}) collective-permute-start(bf16[1,128,256]{2,1,0:T(8,128)(2,1)S(1)} %fusion.7), channel_id=1, source_target_pairs={{0,8},{1,9},{2,10},{3,11},{4,12},{5,13},{6,14},{7,15},{8,0},{9,1},... | collective-permute-start | bytes 196616 | tf_op jit(solution)/shard_map/ppermute | solution.py:63
  141.9 4.3 %collective-permute-done.33 = bf16[1,128,256]{2,1,0:T(8,128)(2,1)S(1)} collective-permute-done((bf16[1,128,256]{2,1,0:T(8,128)(2,1)S(1)}, bf16[1,128,256]{2,1,0:T(8,128)(2,1)S(1)}, u32[]{:S(2)}, u32[]{:S(2)}) %collective-permute-start.33) | collective-permute-done | bytes 65568 | tf_op jit(solution)/shard_map/ppermute | solution.py:63
  (101 shorter events, 45.0 us)
Async XLA Ops:
  3.8 10.9 %collective-permute-start.2 = (bf16[1280,128]{1,0:T(8,128)(2,1)}, bf16[1280,128]{1,0:T(8,128)(2,1)S(1)}, u32[]{:S(2)}, u32[]{:S(2)}) collective-permute-start(bf16[1280,128]{1,0:T(8,128)(2,1)} %shard_map.85.refs_0_.own_ref), channel_id=1, source_target_pairs={{0,2},{1,3},{2,0},{3,1},{4,6},{5,7},{6,4},{7,5},{8,10},{9,11},{10,... | collective-permute-start | bytes 983048 | tf_op jit(solution)/shard_map/ppermute | solution.py:63
  6.8 9.4 %collective-permute-start = (bf16[1280,128]{1,0:T(8,128)(2,1)}, bf16[1280,128]{1,0:T(8,128)(2,1)S(1)}, u32[]{:S(2)}, u32[]{:S(2)}) collective-permute-start(bf16[1280,128]{1,0:T(8,128)(2,1)} %shard_map.85.refs_0_.own_ref), channel_id=1, source_target_pairs={{0,4},{1,5},{2,6},{3,7},{4,0},{5,1},{6,2},{7,3},{8,12},{9,13},{10,... | collective-permute-start | bytes 983048 | tf_op jit(solution)/shard_map/ppermute | solution.py:63
  16.2 8.3 %collective-permute-start.3 = (bf16[1280,128]{1,0:T(8,128)(2,1)S(1)}, bf16[1280,128]{1,0:T(8,128)(2,1)S(1)}, u32[]{:S(2)}, u32[]{:S(2)}) collective-permute-start(bf16[1280,128]{1,0:T(8,128)(2,1)S(1)} %collective-permute-done.refs_2_), channel_id=1, source_target_pairs={{0,2},{1,3},{2,0},{3,1},{4,6},{5,7},{6,4},{7,5},{8,10},{9,11},{10,... | collective-permute-start | bytes 983048 | tf_op jit(solution)/shard_map/ppermute | solution.py:63
  16.6 16.4 %collective-permute-start.1 = (bf16[1280,128]{1,0:T(8,128)(2,1)}, bf16[1280,128]{1,0:T(8,128)(2,1)S(1)}, u32[]{:S(2)}, u32[]{:S(2)}) collective-permute-start(bf16[1280,128]{1,0:T(8,128)(2,1)} %shard_map.85.refs_0_.own_ref), channel_id=1, source_target_pairs={{0,8},{1,9},{2,10},{3,11},{4,12},{5,13},{6,14},{7,15},{8,0},{9,1},... | collective-permute-start | bytes 983048 | tf_op jit(solution)/shard_map/ppermute | solution.py:63
  27.6 9.8 %collective-permute-start.7 = (bf16[1280,128]{1,0:T(8,128)(2,1)}, bf16[1280,128]{1,0:T(8,128)(2,1)S(1)}, u32[]{:S(2)}, u32[]{:S(2)}) collective-permute-start(bf16[1280,128]{1,0:T(8,128)(2,1)} %shard_map.85.refs_0_.own_ref), channel_id=1, source_target_pairs={{0,1},{1,0},{2,3},{3,2},{4,5},{5,4},{6,7},{7,6},{8,9},{9,8},{10,11... | collective-permute-start | bytes 983048 | tf_op jit(solution)/shard_map/ppermute | solution.py:63
  28.1 9.3 %collective-permute-start.8 = (bf16[1280,128]{1,0:T(8,128)(2,1)S(1)}, bf16[1280,128]{1,0:T(8,128)(2,1)S(1)}, u32[]{:S(2)}, u32[]{:S(2)}) collective-permute-start(bf16[1280,128]{1,0:T(8,128)(2,1)S(1)} %collective-permute-done.2.refs_1_), channel_id=1, source_target_pairs={{0,1},{1,0},{2,3},{3,2},{4,5},{5,4},{6,7},{7,6},{8,9},{9,8},{10,11... | collective-permute-start | bytes 983048 | tf_op jit(solution)/shard_map/ppermute | solution.py:63
  33.0 8.7 %collective-permute-start.5 = (bf16[1280,128]{1,0:T(8,128)(2,1)S(1)}, bf16[1280,128]{1,0:T(8,128)(2,1)S(1)}, u32[]{:S(2)}, u32[]{:S(2)}) collective-permute-start(bf16[1280,128]{1,0:T(8,128)(2,1)S(1)} %collective-permute-done.1.refs_4_), channel_id=1, source_target_pairs={{0,2},{1,3},{2,0},{3,1},{4,6},{5,7},{6,4},{7,5},{8,10},{9,11},{10,... | collective-permute-start | bytes 983048 | tf_op jit(solution)/shard_map/ppermute | solution.py:63
  34.3 10.5 %collective-permute-start.4 = (bf16[1280,128]{1,0:T(8,128)(2,1)S(1)}, bf16[1280,128]{1,0:T(8,128)(2,1)S(1)}, u32[]{:S(2)}, u32[]{:S(2)}) collective-permute-start(bf16[1280,128]{1,0:T(8,128)(2,1)S(1)} %collective-permute-done.1.refs_4_), channel_id=1, source_target_pairs={{0,4},{1,5},{2,6},{3,7},{4,0},{5,1},{6,2},{7,3},{8,12},{9,13},{10,... | collective-permute-start | bytes 983048 | tf_op jit(solution)/shard_map/ppermute | solution.py:63
  36.0 10.9 %collective-permute-start.17 = (f32[192,256]{1,0:T(8,128)S(1)}, f32[192,256]{1,0:T(8,128)S(1)}, u32[]{:S(2)}, u32[]{:S(2)}) collective-permute-start(f32[192,256]{1,0:T(8,128)S(1)} %add.117), channel_id=1, source_target_pairs={{0,4},{1,5},{2,6},{3,7},{4,0},{5,1},{6,2},{7,3},{8,12},{9,13},{10,... | collective-permute-start | bytes 589832 | tf_op jit(solution)/shard_map/ppermute | solution.py:63
  37.4 11.3 %collective-permute-start.9 = (bf16[1280,128]{1,0:T(8,128)(2,1)S(1)}, bf16[1280,128]{1,0:T(8,128)(2,1)S(1)}, u32[]{:S(2)}, u32[]{:S(2)}) collective-permute-start(bf16[1280,128]{1,0:T(8,128)(2,1)S(1)} %collective-permute-done.refs_2_), channel_id=1, source_target_pairs={{0,1},{1,0},{2,3},{3,2},{4,5},{5,4},{6,7},{7,6},{8,9},{9,8},{10,11... | collective-permute-start | bytes 983048 | tf_op jit(solution)/shard_map/ppermute | solution.py:63
  37.4 12.1 %collective-permute-start.11 = (bf16[1280,128]{1,0:T(8,128)(2,1)S(1)}, bf16[1280,128]{1,0:T(8,128)(2,1)S(1)}, u32[]{:S(2)}, u32[]{:S(2)}) collective-permute-start(bf16[1280,128]{1,0:T(8,128)(2,1)S(1)} %collective-permute-done.1.refs_4_), channel_id=1, source_target_pairs={{0,1},{1,0},{2,3},{3,2},{4,5},{5,4},{6,7},{7,6},{8,9},{9,8},{10,11... | collective-permute-start | bytes 983048 | tf_op jit(solution)/shard_map/ppermute | solution.py:63
  41.7 10.9 %collective-permute-start.10 = (bf16[1280,128]{1,0:T(8,128)(2,1)S(1)}, bf16[1280,128]{1,0:T(8,128)(2,1)}, u32[]{:S(2)}, u32[]{:S(2)}) collective-permute-start(bf16[1280,128]{1,0:T(8,128)(2,1)S(1)} %collective-permute-done.3.refs_3_), channel_id=1, source_target_pairs={{0,1},{1,0},{2,3},{3,2},{4,5},{5,4},{6,7},{7,6},{8,9},{9,8},{10,11... | collective-permute-start | bytes 983048 | tf_op jit(solution)/shard_map/ppermute | solution.py:63
  44.8 7.8 %collective-permute-start.12 = (bf16[1280,128]{1,0:T(8,128)(2,1)S(1)}, bf16[1280,128]{1,0:T(8,128)(2,1)}, u32[]{:S(2)}, u32[]{:S(2)}) collective-permute-start(bf16[1280,128]{1,0:T(8,128)(2,1)S(1)} %collective-permute-done.5.refs_5_), channel_id=1, source_target_pairs={{0,1},{1,0},{2,3},{3,2},{4,5},{5,4},{6,7},{7,6},{8,9},{9,8},{10,11... | collective-permute-start | bytes 983048 | tf_op jit(solution)/shard_map/ppermute | solution.py:63
  48.7 16.3 %collective-permute-start.6 = (bf16[1280,128]{1,0:T(8,128)(2,1)S(1)}, bf16[1280,128]{1,0:T(8,128)(2,1)S(1)}, u32[]{:S(2)}, u32[]{:S(2)}) collective-permute-start(bf16[1280,128]{1,0:T(8,128)(2,1)S(1)} %collective-permute-done.4.refs_6_), channel_id=1, source_target_pairs={{0,2},{1,3},{2,0},{3,1},{4,6},{5,7},{6,4},{7,5},{8,10},{9,11},{10,... | collective-permute-start | bytes 983048 | tf_op jit(solution)/shard_map/ppermute | solution.py:63
  49.4 15.6 %collective-permute-start.18 = (f32[192,256]{1,0:T(8,128)S(1)}, f32[192,256]{1,0:T(8,128)S(1)}, u32[]{:S(2)}, u32[]{:S(2)}) collective-permute-start(f32[192,256]{1,0:T(8,128)S(1)} %add.118), channel_id=1, source_target_pairs={{0,8},{1,9},{2,10},{3,11},{4,12},{5,13},{6,14},{7,15},{8,0},{9,1},... | collective-permute-start | bytes 589832 | tf_op jit(solution)/shard_map/ppermute | solution.py:63
  68.0 17.6 %collective-permute-start.15 = (bf16[384,640]{1,0:T(8,128)(2,1)S(1)}, bf16[384,640]{1,0:T(8,128)(2,1)S(1)}, u32[]{:S(2)}, u32[]{:S(2)}) collective-permute-start(bf16[384,640]{1,0:T(8,128)(2,1)S(1)} %get-tuple-element.32), channel_id=1, source_target_pairs={{0,16},{16,0},{1,17},{17,1},{2,18},{18,2},{3,19},{19,3},{4,20},{20... | collective-permute-start | bytes 1474568 | tf_op jit(solution)/shard_map/ppermute | solution.py:63
  70.5 13.8 %collective-permute-start.20 = (bf16[192,256]{1,0:T(8,128)(2,1)S(1)}, bf16[192,256]{1,0:T(8,128)(2,1)S(1)}, u32[]{:S(2)}, u32[]{:S(2)}) collective-permute-start(bf16[192,256]{1,0:T(8,128)(2,1)S(1)} %get-tuple-element.49), channel_id=1, source_target_pairs={{0,16},{16,0},{1,17},{17,1},{2,18},{18,2},{3,19},{19,3},{4,20},{20... | collective-permute-start | bytes 294920 | tf_op jit(solution)/shard_map/ppermute | solution.py:63
  72.3 13.4 %collective-permute-start.22 = (bf16[192,256]{1,0:T(8,128)(2,1)S(1)}, bf16[192,256]{1,0:T(8,128)(2,1)S(1)}, u32[]{:S(2)}, u32[]{:S(2)}) collective-permute-start(bf16[192,256]{1,0:T(8,128)(2,1)S(1)} %convert_element_type.99), channel_id=1, source_target_pairs={{0,16},{16,0},{1,17},{17,1},{2,18},{18,2},{3,19},{19,3},{4,20},{20... | collective-permute-start | bytes 294920 | tf_op jit(solution)/shard_map/ppermute | solution.py:63
  99.1 9.2 %collective-permute-start.27 = (bf16[4,128,256]{2,1,0:T(8,128)(2,1)S(1)}, bf16[4,128,256]{2,1,0:T(8,128)(2,1)S(1)}, u32[]{:S(2)}, u32[]{:S(2)}) collective-permute-start(bf16[4,128,256]{2,1,0:T(8,128)(2,1)S(1)} %add_convert_fusion.1), channel_id=1, source_target_pairs={{0,2},{1,3},{2,0},{3,1},{4,6},{5,7},{6,4},{7,5},{8,10},{9,11},{10,... | collective-permute-start | bytes 786440 | tf_op jit(solution)/shard_map/ppermute | solution.py:63
  100.7 26.1 %collective-permute-start.30 = (bf16[4,128,512]{2,1,0:T(8,128)(2,1)S(1)}, bf16[4,128,512]{2,1,0:T(8,128)(2,1)S(1)}, u32[]{:S(2)}, u32[]{:S(2)}) collective-permute-start(bf16[4,128,512]{2,1,0:T(8,128)(2,1)S(1)} %add_convert_fusion), channel_id=1, source_target_pairs={{0,2},{1,3},{2,0},{3,1},{4,6},{5,7},{6,4},{7,5},{8,10},{9,11},{10,... | collective-permute-start | bytes 1572872 | tf_op jit(solution)/shard_map/ppermute | solution.py:63
  101.4 20.1 %collective-permute-start.25 = (f32[128,256]{1,0:T(8,128)S(1)}, f32[128,256]{1,0:T(8,128)S(1)}, u32[]{:S(2)}, u32[]{:S(2)}) collective-permute-start(f32[128,256]{1,0:T(8,128)S(1)} %add.121), channel_id=1, source_target_pairs={{0,2},{1,3},{2,0},{3,1},{4,6},{5,7},{6,4},{7,5},{8,10},{9,11},{10,... | collective-permute-start | bytes 393224 | tf_op jit(solution)/shard_map/ppermute | solution.py:63
  126.6 21.4 %collective-permute-start.29 = (f32[128,256]{1,0:T(8,128)S(1)}, f32[128,256]{1,0:T(8,128)S(1)}, u32[]{:S(2)}, u32[]{:S(2)}) collective-permute-start(f32[128,256]{1,0:T(8,128)S(1)} %add.124.refs_0_), channel_id=1, source_target_pairs={{0,8},{1,9},{2,10},{3,11},{4,12},{5,13},{6,14},{7,15},{8,0},{9,1},... | collective-permute-start | bytes 393224 | tf_op jit(solution)/shard_map/ppermute | solution.py:63
  126.7 8.4 %collective-permute-start.31 = (bf16[2,128,256]{2,1,0:T(8,128)(2,1)S(1)}, bf16[2,128,256]{2,1,0:T(8,128)(2,1)S(1)}, u32[]{:S(2)}, u32[]{:S(2)}) collective-permute-start(bf16[2,128,256]{2,1,0:T(8,128)(2,1)S(1)} %fusion.5), channel_id=1, source_target_pairs={{0,4},{1,5},{2,6},{3,7},{4,0},{5,1},{6,2},{7,3},{8,12},{9,13},{10,... | collective-permute-start | bytes 393224 | tf_op jit(solution)/shard_map/ppermute | solution.py:63
  129.4 9.4 %collective-permute-start.32 = (bf16[2,128,512]{2,1,0:T(8,128)(2,1)S(1)}, bf16[2,128,512]{2,1,0:T(8,128)(2,1)S(1)}, u32[]{:S(2)}, u32[]{:S(2)}) collective-permute-start(bf16[2,128,512]{2,1,0:T(8,128)(2,1)S(1)} %fusion.1), channel_id=1, source_target_pairs={{0,4},{1,5},{2,6},{3,7},{4,0},{5,1},{6,2},{7,3},{8,12},{9,13},{10,... | collective-permute-start | bytes 786440 | tf_op jit(solution)/shard_map/ppermute | solution.py:63
  (23 other events, 254.6 us)

commit v12 on v9

--- a/solution.py
+++ b/solution.py
@@ -428,7 +428,7 @@
     ends_out = [sum_out]
     if sections == 2:
         ends_out = [swap(sum_out, 1, "section"), sum_out]
-    waits = [got[1], out_x, in_x]
+    waits = [got[1], out_x, None]
     terms = [term for thin in thins for term in sum_thin(thin, waits)]
     grad_in, grad_out = call(
         functools.partial(end_kernel, sections),

time: 143 us -> 143 us (level)
  no operation moved by 1% of the time
where the time goes in v12:
time: 143 us
  waiting for transfers between devices  70.5 us (49%)
  starting transfers between devices  35.8 us (25%)
  Pallas kernels  18.9 us (13%)
  local copies, waits for them, and re-layouts  13.1 us (9%)
  other arithmetic  3.91 us (3%)
    ppermute x36, waiting for transfers between devices, swap(): return lax.ppermute(value, axis, [(i, i ^ bits) for i in range(peers)])  70.5 us
    ppermute x36, starting transfers between devices, swap(): return lax.ppermute(value, axis, [(i, i ^ bits) for i in range(peers)])  35.8 us
    pallas_call x6, Pallas kernels, call(): pl.pallas_call(kernel, in_specs=[IN_SMEM] + [IN_HBM] * len(far) + [IN_VME...  18.9 us
    unnamed x22, local copies, waits for them, and re-layouts  12.8 us
  transfers between devices with their start and end apart: 36, of which 18 were waited for; matrix products, arithmetic and copies ran while one was open for 3% of the time, Pallas kernels for 7%

profile of v12, /device:TPU:0, one launch (start us, length us, event | category | flops | bytes accessed | tf_op | source)
XLA Modules:
  0.0 143.1 jit_solution(12945495259359298881)
XLA Ops:
  1.2 2.5 %shard_map.85.own_ref.refs_0_ = bf16[1280,128]{1,0:T(8,128)(2,1)} custom-call(s32[2]{0:T(128)} %pad_add_fusion.1.scalars, bf16[512,128]{1,0:T(8,128)(2,1)} %bitcast.90, bf16[512,128]{1,0:T(8,128)(2,1)} %bitcast.88, bf16[512,256]{1,0:T(8,128)(2,1)} %space_ref.3, f32[1,8192]{1,0:T(1,128)} %gain_ref.1), custom_call_target="tpu_custom_call" | custom-call | tf_op jit(solution)/shard_map/pallas_call | solution.py:43
  3.8 3.0 %collective-permute-start.2 = (bf16[1280,128]{1,0:T(8,128)(2,1)}, bf16[1280,128]{1,0:T(8,128)(2,1)S(1)}, u32[]{:S(2)}, u32[]{:S(2)}) collective-permute-start(bf16[1280,128]{1,0:T(8,128)(2,1)} %shard_map.85.own_ref.refs_0_), channel_id=1, source_target_pairs={{0,2},{1,3},{2,0},{3,1},{4,6},{5,7},{6,4},{7,5},{8,10},{9,11},{10,... | collective-permute-start | bytes 983048 | tf_op jit(solution)/shard_map/ppermute | solution.py:63
  8.4 6.3 %collective-permute-done.2.refs_1_ = bf16[1280,128]{1,0:T(8,128)(2,1)S(1)} collective-permute-done((bf16[1280,128]{1,0:T(8,128)(2,1)}, bf16[1280,128]{1,0:T(8,128)(2,1)S(1)}, u32[]{:S(2)}, u32[]{:S(2)}) %collective-permute-start.2) | collective-permute-done | bytes 327712 | tf_op jit(solution)/shard_map/ppermute | solution.py:63
  16.6 2.7 %collective-permute-start.1 = (bf16[1280,128]{1,0:T(8,128)(2,1)}, bf16[1280,128]{1,0:T(8,128)(2,1)S(1)}, u32[]{:S(2)}, u32[]{:S(2)}) collective-permute-start(bf16[1280,128]{1,0:T(8,128)(2,1)} %shard_map.85.own_ref.refs_0_), channel_id=1, source_target_pairs={{0,8},{1,9},{2,10},{3,11},{4,12},{5,13},{6,14},{7,15},{8,0},{9,1},... | collective-permute-start | bytes 983048 | tf_op jit(solution)/shard_map/ppermute | solution.py:63
  19.9 4.5 %collective-permute-done.3.refs_3_ = bf16[1280,128]{1,0:T(8,128)(2,1)S(1)} collective-permute-done((bf16[1280,128]{1,0:T(8,128)(2,1)S(1)}, bf16[1280,128]{1,0:T(8,128)(2,1)S(1)}, u32[]{:S(2)}, u32[]{:S(2)}) %collective-permute-start.3) | collective-permute-done | bytes 327712 | tf_op jit(solution)/shard_map/ppermute | solution.py:63
  24.4 3.0 %shard_map.86 = (f32[192,256]{1,0:T(8,128)}, f32[192,256]{1,0:T(8,128)}) custom-call(s32[2]{0:T(128)} %pad_add_fusion.2.scalars, bf16[512,128]{1,0:T(8,128)(2,1)} %bitcast.89, bf16[512,256]{1,0:T(8,128)(2,1)} %space_ref.3, bf16[1280,128]{1,0:T(8,128)(2,1)} %shard_map.85.own_ref.refs_0_), custom_call_target="tpu_custom_call" | custom-call | tf_op jit(solution)/shard_map/pallas_call | solution.py:43
  28.1 4.9 %collective-permute-done.1.refs_4_ = bf16[1280,128]{1,0:T(8,128)(2,1)S(1)} collective-permute-done((bf16[1280,128]{1,0:T(8,128)(2,1)}, bf16[1280,128]{1,0:T(8,128)(2,1)S(1)}, u32[]{:S(2)}, u32[]{:S(2)}) %collective-permute-start.1) | collective-permute-done | bytes 327712 | tf_op jit(solution)/shard_map/ppermute | solution.py:63
  37.9 3.8 %collective-permute-done.5.refs_5_ = bf16[1280,128]{1,0:T(8,128)(2,1)S(1)} collective-permute-done((bf16[1280,128]{1,0:T(8,128)(2,1)S(1)}, bf16[1280,128]{1,0:T(8,128)(2,1)S(1)}, u32[]{:S(2)}, u32[]{:S(2)}) %collective-permute-start.5) | collective-permute-done | bytes 327712 | tf_op jit(solution)/shard_map/ppermute | solution.py:63
  41.7 3.1 %collective-permute-done.4.refs_6_ = bf16[1280,128]{1,0:T(8,128)(2,1)S(1)} collective-permute-done((bf16[1280,128]{1,0:T(8,128)(2,1)S(1)}, bf16[1280,128]{1,0:T(8,128)(2,1)S(1)}, u32[]{:S(2)}, u32[]{:S(2)}) %collective-permute-start.4) | collective-permute-done | bytes 327712 | tf_op jit(solution)/shard_map/ppermute | solution.py:63
  44.8 2.1 %collective-permute-done.7 = f32[192,256]{1,0:T(8,128)S(1)} collective-permute-done((f32[192,256]{1,0:T(8,128)S(1)}, f32[192,256]{1,0:T(8,128)S(1)}, u32[]{:S(2)}, u32[]{:S(2)}) %collective-permute-start.7) | collective-permute-done | bytes 196640 | tf_op jit(solution)/shard_map/ppermute | solution.py:63
  48.7 3.3 %collective-permute-start.18 = (f32[192,256]{1,0:T(8,128)S(1)}, f32[192,256]{1,0:T(8,128)S(1)}, u32[]{:S(2)}, u32[]{:S(2)}) collective-permute-start(f32[192,256]{1,0:T(8,128)S(1)} %add.118), channel_id=1, source_target_pairs={{0,8},{1,9},{2,10},{3,11},{4,12},{5,13},{6,14},{7,15},{8,0},{9,1},... | collective-permute-start | bytes 589832 | tf_op jit(solution)/shard_map/ppermute | solution.py:63
  52.6 2.8 %copy-done = bf16[384,8192]{1,0:T(8,128)(2,1)S(1)} copy-done((bf16[384,8192]{1,0:T(8,128)(2,1)S(1)}, bf16[384,8192]{1,0:T(8,128)(2,1)}, u32[]{:S(2)}) %copy-start) | copy-done | bytes 6291480
  55.4 2.8 %copy-done.3 = bf16[384,8192]{1,0:T(8,128)(2,1)S(1)} copy-done((bf16[384,8192]{1,0:T(8,128)(2,1)S(1)}, bf16[384,8192]{1,0:T(8,128)(2,1)}, u32[]{:S(2)}) %copy-start.3) | copy-done | bytes 6291480
  59.2 5.8 %shard_map.87.refs_2_ = f32[384,768]{1,0:T(8,128)S(1)} custom-call(s32[15]{0:T(128)S(1)} %stack.204.scalars, bf16[384,8192]{1,0:T(8,128)(2,1)S(1)} %copy-done, bf16[384,8192]{1,0:T(8,128)(2,1)S(1)} %copy-done.3, bf16[1280,128]{1,0:T(8,128)(2,1)S(1)} %copy-done.6, bf16[1280,128]{1,0:T(8,128)(2,1)S(1)} %collective-permute-done.2.refs_1_, ...), custom_call_target="tpu_custom_call" | custom-call | flops 3523215360 | tf_op jit(solution)/shard_map/pallas_call | solution.py:43
  73.8 10.4 %collective-permute-done.20.refs_2_ = bf16[192,256]{1,0:T(8,128)(2,1)S(1)} collective-permute-done((bf16[192,256]{1,0:T(8,128)(2,1)S(1)}, bf16[192,256]{1,0:T(8,128)(2,1)S(1)}, u32[]{:S(2)}, u32[]{:S(2)}) %collective-permute-start.20) | collective-permute-done | bytes 98336 | tf_op jit(solution)/shard_map/ppermute | solution.py:63
  85.6 2.8 %copy-done.2 = bf16[384,8192]{1,0:T(8,128)(2,1)S(1)} copy-done((bf16[384,8192]{1,0:T(8,128)(2,1)S(1)}, bf16[384,8192]{1,0:T(8,128)(2,1)}, u32[]{:S(2)}) %copy-start.2) | copy-done | bytes 6291480
  88.4 2.8 %copy-done.5 = bf16[384,8192]{1,0:T(8,128)(2,1)S(1)} copy-done((bf16[384,8192]{1,0:T(8,128)(2,1)S(1)}, bf16[384,8192]{1,0:T(8,128)(2,1)}, u32[]{:S(2)}) %copy-start.5) | copy-done | bytes 6291480
  91.2 4.4 %shard_map.89 = (bf16[384,256]{1,0:T(8,128)(2,1)}, f32[128,256]{1,0:T(8,128)S(1)}, bf16[8,128,256]{2,1,0:T(8,128)(2,1)S(1)}, bf16[8,128,256]{2,1,0:T(8,128)(2,1)...) custom-call(s32[34]{0:T(128)S(1)} %stack.192.scalars, bf16[384,8192]{1,0:T(8,128)(2,1)S(1)} %copy-done.2, ...), custom_call_target="tpu_custom_call" | custom-call | tf_op jit(solution)/shard_map/pallas_call | solution.py:43
  99.0 7.0 %collective-permute-done.27 = bf16[4,128,256]{2,1,0:T(8,128)(2,1)S(1)} collective-permute-done((bf16[4,128,256]{2,1,0:T(8,128)(2,1)S(1)}, bf16[4,128,256]{2,1,0:T(8,128)(2,1)S(1)}, u32[]{:S(2)}, u32[]{:S(2)}) %collective-permute-start.27) | collective-permute-done | bytes 262176 | tf_op jit(solution)/shard_map/ppermute | solution.py:63
  106.1 1.8 %collective-permute-start.30 = (bf16[2,128,256]{2,1,0:T(8,128)(2,1)S(1)}, bf16[2,128,256]{2,1,0:T(8,128)(2,1)S(1)}, u32[]{:S(2)}, u32[]{:S(2)}) collective-permute-start(bf16[2,128,256]{2,1,0:T(8,128)(2,1)S(1)} %fusion.6), channel_id=1, source_target_pairs={{0,4},{1,5},{2,6},{3,7},{4,0},{5,1},{6,2},{7,3},{8,12},{9,13},{10,... | collective-permute-start | bytes 393224 | tf_op jit(solution)/shard_map/ppermute | solution.py:63
  112.8 9.6 %collective-permute-done.33 = bf16[4,128,512]{2,1,0:T(8,128)(2,1)S(1)} collective-permute-done((bf16[4,128,512]{2,1,0:T(8,128)(2,1)S(1)}, bf16[4,128,512]{2,1,0:T(8,128)(2,1)S(1)}, u32[]{:S(2)}, u32[]{:S(2)}) %collective-permute-start.33) | collective-permute-done | bytes 524320 | tf_op jit(solution)/shard_map/ppermute | solution.py:63
  126.6 4.5 %collective-permute-done.28 = f32[128,256]{1,0:T(8,128)S(1)} collective-permute-done((f32[128,256]{1,0:T(8,128)S(1)}, f32[128,256]{1,0:T(8,128)S(1)}, u32[]{:S(2)}, u32[]{:S(2)}) %collective-permute-start.28) | collective-permute-done | bytes 131104 | tf_op jit(solution)/shard_map/ppermute | solution.py:63
  131.4 2.9 %collective-permute-start.35 = (bf16[1,128,512]{2,1,0:T(8,128)(2,1)S(1)}, bf16[1,128,512]{2,1,0:T(8,128)(2,1)S(1)}, u32[]{:S(2)}, u32[]{:S(2)}) collective-permute-start(bf16[1,128,512]{2,1,0:T(8,128)(2,1)S(1)} %fusion.5), channel_id=1, source_target_pairs={{0,8},{1,9},{2,10},{3,11},{4,12},{5,13},{6,14},{7,15},{8,0},{9,1},... | collective-permute-start | bytes 393224 | tf_op jit(solution)/shard_map/ppermute | solution.py:63
  134.3 5.5 %collective-permute-done.29.refs_1_ = f32[128,256]{1,0:T(8,128)S(1)} collective-permute-done((f32[128,256]{1,0:T(8,128)S(1)}, f32[128,256]{1,0:T(8,128)S(1)}, u32[]{:S(2)}, u32[]{:S(2)}) %collective-permute-start.29) | collective-permute-done | bytes 131104 | tf_op jit(solution)/shard_map/ppermute | solution.py:63
  (101 shorter events, 39.7 us)
Async XLA Ops:
  3.8 10.9 %collective-permute-start.2 = (bf16[1280,128]{1,0:T(8,128)(2,1)}, bf16[1280,128]{1,0:T(8,128)(2,1)S(1)}, u32[]{:S(2)}, u32[]{:S(2)}) collective-permute-start(bf16[1280,128]{1,0:T(8,128)(2,1)} %shard_map.85.own_ref.refs_0_), channel_id=1, source_target_pairs={{0,2},{1,3},{2,0},{3,1},{4,6},{5,7},{6,4},{7,5},{8,10},{9,11},{10,... | collective-permute-start | bytes 983048 | tf_op jit(solution)/shard_map/ppermute | solution.py:63
  6.8 9.4 %collective-permute-start = (bf16[1280,128]{1,0:T(8,128)(2,1)}, bf16[1280,128]{1,0:T(8,128)(2,1)S(1)}, u32[]{:S(2)}, u32[]{:S(2)}) collective-permute-start(bf16[1280,128]{1,0:T(8,128)(2,1)} %shard_map.85.own_ref.refs_0_), channel_id=1, source_target_pairs={{0,4},{1,5},{2,6},{3,7},{4,0},{5,1},{6,2},{7,3},{8,12},{9,13},{10,... | collective-permute-start | bytes 983048 | tf_op jit(solution)/shard_map/ppermute | solution.py:63
  16.6 16.4 %collective-permute-start.1 = (bf16[1280,128]{1,0:T(8,128)(2,1)}, bf16[1280,128]{1,0:T(8,128)(2,1)S(1)}, u32[]{:S(2)}, u32[]{:S(2)}) collective-permute-start(bf16[1280,128]{1,0:T(8,128)(2,1)} %shard_map.85.own_ref.refs_0_), channel_id=1, source_target_pairs={{0,8},{1,9},{2,10},{3,11},{4,12},{5,13},{6,14},{7,15},{8,0},{9,1},... | collective-permute-start | bytes 983048 | tf_op jit(solution)/shard_map/ppermute | solution.py:63
  27.6 9.8 %collective-permute-start.9 = (bf16[1280,128]{1,0:T(8,128)(2,1)}, bf16[1280,128]{1,0:T(8,128)(2,1)S(1)}, u32[]{:S(2)}, u32[]{:S(2)}) collective-permute-start(bf16[1280,128]{1,0:T(8,128)(2,1)} %shard_map.85.own_ref.refs_0_), channel_id=1, source_target_pairs={{0,1},{1,0},{2,3},{3,2},{4,5},{5,4},{6,7},{7,6},{8,9},{9,8},{10,11... | collective-permute-start | bytes 983048 | tf_op jit(solution)/shard_map/ppermute | solution.py:63
  28.1 9.3 %collective-permute-start.10 = (bf16[1280,128]{1,0:T(8,128)(2,1)S(1)}, bf16[1280,128]{1,0:T(8,128)(2,1)S(1)}, u32[]{:S(2)}, u32[]{:S(2)}) collective-permute-start(bf16[1280,128]{1,0:T(8,128)(2,1)S(1)} %collective-permute-done.2.refs_1_), channel_id=1, source_target_pairs={{0,1},{1,0},{2,3},{3,2},{4,5},{5,4},{6,7},{7,6},{8,9},{9,8},{10,11... | collective-permute-start | bytes 983048 | tf_op jit(solution)/shard_map/ppermute | solution.py:63
  33.0 8.7 %collective-permute-start.5 = (bf16[1280,128]{1,0:T(8,128)(2,1)S(1)}, bf16[1280,128]{1,0:T(8,128)(2,1)S(1)}, u32[]{:S(2)}, u32[]{:S(2)}) collective-permute-start(bf16[1280,128]{1,0:T(8,128)(2,1)S(1)} %collective-permute-done.1.refs_4_), channel_id=1, source_target_pairs={{0,2},{1,3},{2,0},{3,1},{4,6},{5,7},{6,4},{7,5},{8,10},{9,11},{10,... | collective-permute-start | bytes 983048 | tf_op jit(solution)/shard_map/ppermute | solution.py:63
  34.3 10.5 %collective-permute-start.4 = (bf16[1280,128]{1,0:T(8,128)(2,1)S(1)}, bf16[1280,128]{1,0:T(8,128)(2,1)S(1)}, u32[]{:S(2)}, u32[]{:S(2)}) collective-permute-start(bf16[1280,128]{1,0:T(8,128)(2,1)S(1)} %collective-permute-done.1.refs_4_), channel_id=1, source_target_pairs={{0,4},{1,5},{2,6},{3,7},{4,0},{5,1},{6,2},{7,3},{8,12},{9,13},{10,... | collective-permute-start | bytes 983048 | tf_op jit(solution)/shard_map/ppermute | solution.py:63
  36.0 10.9 %collective-permute-start.7 = (f32[192,256]{1,0:T(8,128)S(1)}, f32[192,256]{1,0:T(8,128)S(1)}, u32[]{:S(2)}, u32[]{:S(2)}) collective-permute-start(f32[192,256]{1,0:T(8,128)S(1)} %add.117), channel_id=1, source_target_pairs={{0,4},{1,5},{2,6},{3,7},{4,0},{5,1},{6,2},{7,3},{8,12},{9,13},{10,... | collective-permute-start | bytes 589832 | tf_op jit(solution)/shard_map/ppermute | solution.py:63
  37.4 11.3 %collective-permute-start.11 = (bf16[1280,128]{1,0:T(8,128)(2,1)S(1)}, bf16[1280,128]{1,0:T(8,128)(2,1)S(1)}, u32[]{:S(2)}, u32[]{:S(2)}) collective-permute-start(bf16[1280,128]{1,0:T(8,128)(2,1)S(1)} %collective-permute-done.refs_2_), channel_id=1, source_target_pairs={{0,1},{1,0},{2,3},{3,2},{4,5},{5,4},{6,7},{7,6},{8,9},{9,8},{10,11... | collective-permute-start | bytes 983048 | tf_op jit(solution)/shard_map/ppermute | solution.py:63
  37.4 14.6 %collective-permute-start.13 = (bf16[1280,128]{1,0:T(8,128)(2,1)S(1)}, bf16[1280,128]{1,0:T(8,128)(2,1)S(1)}, u32[]{:S(2)}, u32[]{:S(2)}) collective-permute-start(bf16[1280,128]{1,0:T(8,128)(2,1)S(1)} %collective-permute-done.1.refs_4_), channel_id=1, source_target_pairs={{0,1},{1,0},{2,3},{3,2},{4,5},{5,4},{6,7},{7,6},{8,9},{9,8},{10,11... | collective-permute-start | bytes 983048 | tf_op jit(solution)/shard_map/ppermute | solution.py:63
  41.7 10.9 %collective-permute-start.12 = (bf16[1280,128]{1,0:T(8,128)(2,1)S(1)}, bf16[1280,128]{1,0:T(8,128)(2,1)}, u32[]{:S(2)}, u32[]{:S(2)}) collective-permute-start(bf16[1280,128]{1,0:T(8,128)(2,1)S(1)} %collective-permute-done.3.refs_3_), channel_id=1, source_target_pairs={{0,1},{1,0},{2,3},{3,2},{4,5},{5,4},{6,7},{7,6},{8,9},{9,8},{10,11... | collective-permute-start | bytes 983048 | tf_op jit(solution)/shard_map/ppermute | solution.py:63
  48.7 16.4 %collective-permute-start.18 = (f32[192,256]{1,0:T(8,128)S(1)}, f32[192,256]{1,0:T(8,128)S(1)}, u32[]{:S(2)}, u32[]{:S(2)}) collective-permute-start(f32[192,256]{1,0:T(8,128)S(1)} %add.118), channel_id=1, source_target_pairs={{0,8},{1,9},{2,10},{3,11},{4,12},{5,13},{6,14},{7,15},{8,0},{9,1},... | collective-permute-start | bytes 589832 | tf_op jit(solution)/shard_map/ppermute | solution.py:63
  52.0 13.0 %collective-permute-start.8 = (bf16[1280,128]{1,0:T(8,128)(2,1)S(1)}, bf16[1280,128]{1,0:T(8,128)(2,1)S(1)}, u32[]{:S(2)}, u32[]{:S(2)}) collective-permute-start(bf16[1280,128]{1,0:T(8,128)(2,1)S(1)} %collective-permute-done.4.refs_6_), channel_id=1, source_target_pairs={{0,2},{1,3},{2,0},{3,1},{4,6},{5,7},{6,4},{7,5},{8,10},{9,11},{10,... | collective-permute-start | bytes 983048 | tf_op jit(solution)/shard_map/ppermute | solution.py:63
  68.0 17.6 %collective-permute-start.17 = (bf16[384,640]{1,0:T(8,128)(2,1)S(1)}, bf16[384,640]{1,0:T(8,128)(2,1)S(1)}, u32[]{:S(2)}, u32[]{:S(2)}) collective-permute-start(bf16[384,640]{1,0:T(8,128)(2,1)S(1)} %get-tuple-element.33), channel_id=1, source_target_pairs={{0,16},{16,0},{1,17},{17,1},{2,18},{18,2},{3,19},{19,3},{4,20},{20... | collective-permute-start | bytes 1474568 | tf_op jit(solution)/shard_map/ppermute | solution.py:63
  70.5 13.8 %collective-permute-start.20 = (bf16[192,256]{1,0:T(8,128)(2,1)S(1)}, bf16[192,256]{1,0:T(8,128)(2,1)S(1)}, u32[]{:S(2)}, u32[]{:S(2)}) collective-permute-start(bf16[192,256]{1,0:T(8,128)(2,1)S(1)} %get-tuple-element.45), channel_id=1, source_target_pairs={{0,16},{16,0},{1,17},{17,1},{2,18},{18,2},{3,19},{19,3},{4,20},{20... | collective-permute-start | bytes 294920 | tf_op jit(solution)/shard_map/ppermute | solution.py:63
  72.3 13.4 %collective-permute-start.22 = (bf16[192,256]{1,0:T(8,128)(2,1)S(1)}, bf16[192,256]{1,0:T(8,128)(2,1)S(1)}, u32[]{:S(2)}, u32[]{:S(2)}) collective-permute-start(bf16[192,256]{1,0:T(8,128)(2,1)S(1)} %convert_element_type.99), channel_id=1, source_target_pairs={{0,16},{16,0},{1,17},{17,1},{2,18},{18,2},{3,19},{19,3},{4,20},{20... | collective-permute-start | bytes 294920 | tf_op jit(solution)/shard_map/ppermute | solution.py:63
  95.6 12.3 %collective-permute-start.24 = (bf16[8,128,512]{2,1,0:T(8,128)(2,1)S(1)}, bf16[8,128,512]{2,1,0:T(8,128)(2,1)S(1)}, u32[]{:S(2)}, u32[]{:S(2)}) collective-permute-start(bf16[8,128,512]{2,1,0:T(8,128)(2,1)S(1)} %get-tuple-element.37), channel_id=1, source_target_pairs={{0,1},{1,0},{2,3},{3,2},{4,5},{5,4},{6,7},{7,6},{8,9},{9,8},{10,11... | collective-permute-start | bytes 3145736 | tf_op jit(solution)/shard_map/ppermute | solution.py:63
  99.0 10.5 %collective-permute-start.23 = (f32[128,256]{1,0:T(8,128)S(1)}, f32[128,256]{1,0:T(8,128)S(1)}, u32[]{:S(2)}, u32[]{:S(2)}) collective-permute-start(f32[128,256]{1,0:T(8,128)S(1)} %get-tuple-element.36), channel_id=1, source_target_pairs={{0,1},{1,0},{2,3},{3,2},{4,5},{5,4},{6,7},{7,6},{8,9},{9,8},{10,11... | collective-permute-start | bytes 393224 | tf_op jit(solution)/shard_map/ppermute | solution.py:63
  108.1 14.3 %collective-permute-start.33 = (bf16[4,128,512]{2,1,0:T(8,128)(2,1)S(1)}, bf16[4,128,512]{2,1,0:T(8,128)(2,1)S(1)}, u32[]{:S(2)}, u32[]{:S(2)}) collective-permute-start(bf16[4,128,512]{2,1,0:T(8,128)(2,1)S(1)} %add_convert_fusion), channel_id=1, source_target_pairs={{0,2},{1,3},{2,0},{3,1},{4,6},{5,7},{6,4},{7,5},{8,10},{9,11},{10,... | collective-permute-start | bytes 1572872 | tf_op jit(solution)/shard_map/ppermute | solution.py:63
  111.2 13.6 %collective-permute-start.31 = (bf16[1,128,256]{2,1,0:T(8,128)(2,1)S(1)}, bf16[1,128,256]{2,1,0:T(8,128)(2,1)S(1)}, u32[]{:S(2)}, u32[]{:S(2)}) collective-permute-start(bf16[1,128,256]{2,1,0:T(8,128)(2,1)S(1)} %fusion.8), channel_id=1, source_target_pairs={{0,8},{1,9},{2,10},{3,11},{4,12},{5,13},{6,14},{7,15},{8,0},{9,1},... | collective-permute-start | bytes 196616 | tf_op jit(solution)/shard_map/ppermute | solution.py:63
  111.4 12.4 %collective-permute-start.25 = (f32[128,256]{1,0:T(8,128)S(1)}, f32[128,256]{1,0:T(8,128)S(1)}, u32[]{:S(2)}, u32[]{:S(2)}) collective-permute-start(f32[128,256]{1,0:T(8,128)S(1)} %add.121), channel_id=1, source_target_pairs={{0,2},{1,3},{2,0},{3,1},{4,6},{5,7},{6,4},{7,5},{8,10},{9,11},{10,... | collective-permute-start | bytes 393224 | tf_op jit(solution)/shard_map/ppermute | solution.py:63
  124.9 9.5 %collective-permute-start.32 = (f32[128,256]{1,0:T(8,128)S(1)}, f32[128,256]{1,0:T(8,128)S(1)}, u32[]{:S(2)}, u32[]{:S(2)}) collective-permute-start(f32[128,256]{1,0:T(8,128)S(1)} %fusion.7.refs_3_), channel_id=1, source_target_pairs={{0,16},{16,0},{1,17},{17,1},{2,18},{18,2},{3,19},{19,3},{4,20},{20... | collective-permute-start | bytes 393224 | tf_op jit(solution)/shard_map/ppermute | solution.py:63
  131.1 8.7 %collective-permute-start.29 = (f32[128,256]{1,0:T(8,128)S(1)}, f32[128,256]{1,0:T(8,128)S(1)}, u32[]{:S(2)}, u32[]{:S(2)}) collective-permute-start(f32[128,256]{1,0:T(8,128)S(1)} %add.124.refs_0_), channel_id=1, source_target_pairs={{0,8},{1,9},{2,10},{3,11},{4,12},{5,13},{6,14},{7,15},{8,0},{9,1},... | collective-permute-start | bytes 393224 | tf_op jit(solution)/shard_map/ppermute | solution.py:63
  131.4 9.9 %collective-permute-start.35 = (bf16[1,128,512]{2,1,0:T(8,128)(2,1)S(1)}, bf16[1,128,512]{2,1,0:T(8,128)(2,1)S(1)}, u32[]{:S(2)}, u32[]{:S(2)}) collective-permute-start(bf16[1,128,512]{2,1,0:T(8,128)(2,1)S(1)} %fusion.5), channel_id=1, source_target_pairs={{0,8},{1,9},{2,10},{3,11},{4,12},{5,13},{6,14},{7,15},{8,0},{9,1},... | collective-permute-start | bytes 393224 | tf_op jit(solution)/shard_map/ppermute | solution.py:63
  (23 other events, 233.6 us)

commit v13 on v12

--- a/solution.py
+++ b/solution.py
@@ -394,7 +394,7 @@
     marks += [m ^ 1 for m in marks]
     acc = project([spot ^ m for m in marks], flag, [shards[m] for m in marks], tokens)[0]
     pair = [shards[ends], swap(after(shards[ends], acc), 1)]
-    acc, send = project([spot ^ ends, spot ^ ends ^ 1], flag, pair, tokens, acc, final=True)
+    acc, send = project([spot ^ ends, spot ^ ends ^ 1], flag, pair, tokens, after(acc, *keeps, *others), final=True)
     sent = from_sections(send)
 
     near = list(range(0, peers, 4))

time: 143 us -> 156 us (1.091)
  local copies, waits for them, and re-layouts: 13.1 us -> 23 us
  starting transfers between devices: 35.8 us -> 37.5 us
    unnamed x22 -> x34, local copies, waits for them, and re-layouts: 12.8 us -> 22.7 us
    ppermute x36, starting transfers between devices: 35.8 us -> 37.5 us  [swap(): return lax.ppermute(value, axis, [(i, i ^ bits) for i in range(peers)])]
  transfers between devices with their start and end apart: 36 -> 36, of which waited for: 18 -> 19; matrix products, arithmetic and copies ran while one was open for 3% -> 2% of each run, Pallas kernels for 7% -> 6%
where the time goes in v13:
time: 156 us; the launch traced here: 155 us
  waiting for transfers between devices  69.9 us (45%)
  starting transfers between devices  37.5 us (24%)
  local copies, waits for them, and re-layouts  23 us (15%)
  Pallas kernels  20 us (13%)
  other arithmetic  3.98 us (3%)
    ppermute x36, waiting for transfers between devices, swap(): return lax.ppermute(value, axis, [(i, i ^ bits) for i in range(peers)])  69.9 us
    ppermute x36, starting transfers between devices, swap(): return lax.ppermute(value, axis, [(i, i ^ bits) for i in range(peers)])  37.5 us
    unnamed x34, local copies, waits for them, and re-layouts  22.7 us
    pallas_call x6, Pallas kernels, call(): pl.pallas_call(kernel, in_specs=[IN_SMEM] + [IN_HBM] * len(far) + [IN_VME...  20 us
  transfers between devices with their start and end apart: 36, of which 19 were waited for; matrix products, arithmetic and copies ran while one was open for 2% of the time, Pallas kernels for 6%

profile of v13, /device:TPU:0, one launch (start us, length us, event | category | flops | bytes accessed | tf_op | source)
XLA Modules:
  0.0 155.3 jit_solution(16078650972968167020)
XLA Ops:
  1.2 2.6 %shard_map.85.own_ref.refs_0_ = bf16[1280,128]{1,0:T(8,128)(2,1)} custom-call(s32[2]{0:T(128)} %pad_add_fusion.1.scalars, bf16[512,128]{1,0:T(8,128)(2,1)} %bitcast.90, bf16[512,128]{1,0:T(8,128)(2,1)} %bitcast.88, bf16[512,256]{1,0:T(8,128)(2,1)} %space_ref.3, f32[1,8192]{1,0:T(1,128)} %gain_ref.1), custom_call_target="tpu_custom_call" | custom-call | tf_op jit(solution)/shard_map/pallas_call | solution.py:43
  3.8 3.0 %collective-permute-start.2 = (bf16[1280,128]{1,0:T(8,128)(2,1)}, bf16[1280,128]{1,0:T(8,128)(2,1)S(1)}, u32[]{:S(2)}, u32[]{:S(2)}) collective-permute-start(bf16[1280,128]{1,0:T(8,128)(2,1)} %shard_map.85.own_ref.refs_0_), channel_id=1, source_target_pairs={{0,2},{1,3},{2,0},{3,1},{4,6},{5,7},{6,4},{7,5},{8,10},{9,11},{10,... | collective-permute-start | bytes 983048 | tf_op jit(solution)/shard_map/ppermute | solution.py:63
  8.4 6.3 %collective-permute-done.2.refs_1_ = bf16[1280,128]{1,0:T(8,128)(2,1)S(1)} collective-permute-done((bf16[1280,128]{1,0:T(8,128)(2,1)}, bf16[1280,128]{1,0:T(8,128)(2,1)S(1)}, u32[]{:S(2)}, u32[]{:S(2)}) %collective-permute-start.2) | collective-permute-done | bytes 327712 | tf_op jit(solution)/shard_map/ppermute | solution.py:63
  16.6 2.7 %collective-permute-start.1 = (bf16[1280,128]{1,0:T(8,128)(2,1)}, bf16[1280,128]{1,0:T(8,128)(2,1)S(1)}, u32[]{:S(2)}, u32[]{:S(2)}) collective-permute-start(bf16[1280,128]{1,0:T(8,128)(2,1)} %shard_map.85.own_ref.refs_0_), channel_id=1, source_target_pairs={{0,8},{1,9},{2,10},{3,11},{4,12},{5,13},{6,14},{7,15},{8,0},{9,1},... | collective-permute-start | bytes 983048 | tf_op jit(solution)/shard_map/ppermute | solution.py:63
  20.0 4.5 %collective-permute-done.3.refs_3_ = bf16[1280,128]{1,0:T(8,128)(2,1)S(1)} collective-permute-done((bf16[1280,128]{1,0:T(8,128)(2,1)S(1)}, bf16[1280,128]{1,0:T(8,128)(2,1)S(1)}, u32[]{:S(2)}, u32[]{:S(2)}) %collective-permute-start.3) | collective-permute-done | bytes 327712 | tf_op jit(solution)/shard_map/ppermute | solution.py:63
  24.5 3.0 %shard_map.86 = (f32[192,256]{1,0:T(8,128)}, f32[192,256]{1,0:T(8,128)}) custom-call(s32[2]{0:T(128)} %pad_add_fusion.2.scalars, bf16[512,128]{1,0:T(8,128)(2,1)} %bitcast.89, bf16[512,256]{1,0:T(8,128)(2,1)} %space_ref.3, bf16[1280,128]{1,0:T(8,128)(2,1)} %shard_map.85.own_ref.refs_0_), custom_call_target="tpu_custom_call" | custom-call | tf_op jit(solution)/shard_map/pallas_call | solution.py:43
  35.1 2.9 %collective-permute-done.7 = f32[192,256]{1,0:T(8,128)S(1)} collective-permute-done((f32[192,256]{1,0:T(8,128)S(1)}, f32[192,256]{1,0:T(8,128)S(1)}, u32[]{:S(2)}, u32[]{:S(2)}) %collective-permute-start.7) | collective-permute-done | bytes 196640 | tf_op jit(solution)/shard_map/ppermute | solution.py:63
  38.0 2.6 %collective-permute-start.17 = (f32[192,256]{1,0:T(8,128)S(1)}, f32[192,256]{1,0:T(8,128)S(1)}, u32[]{:S(2)}, u32[]{:S(2)}) collective-permute-start(f32[192,256]{1,0:T(8,128)S(1)} %add.118), channel_id=1, source_target_pairs={{0,8},{1,9},{2,10},{3,11},{4,12},{5,13},{6,14},{7,15},{8,0},{9,1},... | collective-permute-start | bytes 589832 | tf_op jit(solution)/shard_map/ppermute | solution.py:63
  42.0 6.5 %collective-permute-done.4.refs_6_ = bf16[1280,128]{1,0:T(8,128)(2,1)S(1)} collective-permute-done((bf16[1280,128]{1,0:T(8,128)(2,1)S(1)}, bf16[1280,128]{1,0:T(8,128)(2,1)S(1)}, u32[]{:S(2)}, u32[]{:S(2)}) %collective-permute-start.4) | collective-permute-done | bytes 327712 | tf_op jit(solution)/shard_map/ppermute | solution.py:63
  54.3 2.8 %copy-done = bf16[384,8192]{1,0:T(8,128)(2,1)S(1)} copy-done((bf16[384,8192]{1,0:T(8,128)(2,1)S(1)}, bf16[384,8192]{1,0:T(8,128)(2,1)}, u32[]{:S(2)}) %copy-start) | copy-done | bytes 6291480
  57.0 2.8 %copy-done.3 = bf16[384,8192]{1,0:T(8,128)(2,1)S(1)} copy-done((bf16[384,8192]{1,0:T(8,128)(2,1)S(1)}, bf16[384,8192]{1,0:T(8,128)(2,1)}, u32[]{:S(2)}) %copy-start.3) | copy-done | bytes 6291480
  63.7 5.6 %shard_map.87.refs_2_ = f32[384,768]{1,0:T(8,128)S(1)} custom-call(s32[15]{0:T(128)S(1)} %stack.204.scalars, bf16[384,8192]{1,0:T(8,128)(2,1)S(1)} %copy-done, bf16[384,8192]{1,0:T(8,128)(2,1)S(1)} %copy-done.3, bf16[1280,128]{1,0:T(8,128)(2,1)S(1)} %copy-done.6, bf16[1280,128]{1,0:T(8,128)(2,1)S(1)} %collective-permute-done.2.refs_1_, ...), custom_call_target="tpu_custom_call" | custom-call | flops 3523215360 | tf_op jit(solution)/shard_map/pallas_call | solution.py:43
  76.9 2.8 %copy-done.1 = bf16[384,8192]{1,0:T(8,128)(2,1)S(1)} copy-done((bf16[384,8192]{1,0:T(8,128)(2,1)S(1)}, bf16[384,8192]{1,0:T(8,128)(2,1)}, u32[]{:S(2)}) %copy-start.1) | copy-done | bytes 6291480
  79.7 2.8 %copy-done.4 = bf16[384,8192]{1,0:T(8,128)(2,1)S(1)} copy-done((bf16[384,8192]{1,0:T(8,128)(2,1)S(1)}, bf16[384,8192]{1,0:T(8,128)(2,1)}, u32[]{:S(2)}) %copy-start.4) | copy-done | bytes 6291480
  82.5 2.6 %shard_map.88 = (f32[384,768]{1,0:T(8,128)S(1)}, bf16[384,640]{1,0:T(8,128)(2,1)}) custom-call(s32[3]{0:T(128)S(1)} %pad_add_fusion.scalars, bf16[384,8192]{1,0:T(8,128)(2,1)S(1)} %copy-done.1, bf16[384,8192]{1,0:T(8,128)(2,1)S(1)} %copy-done.4, bf16[1280,128]{1,0:T(8,128)(2,1)} %collective-permute-done.8.refs_0_, ...), custom_call_target="tpu_custom_call" | custom-call | flops 503316480 | tf_op jit(solution)/shard_map/pallas_call | solution.py:43
  86.9 10.9 %collective-permute-done.22.refs_0_ = bf16[384,640]{1,0:T(8,128)(2,1)S(1)} collective-permute-done((bf16[384,640]{1,0:T(8,128)(2,1)}, bf16[384,640]{1,0:T(8,128)(2,1)S(1)}, u32[]{:S(2)}, u32[]{:S(2)}) %collective-permute-start.22) | collective-permute-done | bytes 491552 | tf_op jit(solution)/shard_map/ppermute | solution.py:63
  97.8 2.8 %copy-done.2 = bf16[384,8192]{1,0:T(8,128)(2,1)S(1)} copy-done((bf16[384,8192]{1,0:T(8,128)(2,1)S(1)}, bf16[384,8192]{1,0:T(8,128)(2,1)}, u32[]{:S(2)}) %copy-start.2) | copy-done | bytes 6291480
  100.6 2.8 %copy-done.5 = bf16[384,8192]{1,0:T(8,128)(2,1)S(1)} copy-done((bf16[384,8192]{1,0:T(8,128)(2,1)S(1)}, bf16[384,8192]{1,0:T(8,128)(2,1)}, u32[]{:S(2)}) %copy-start.5) | copy-done | bytes 6291480
  103.4 4.4 %shard_map.89 = (bf16[384,256]{1,0:T(8,128)(2,1)}, f32[128,256]{1,0:T(8,128)S(1)}, bf16[8,128,256]{2,1,0:T(8,128)(2,1)S(1)}, bf16[8,128,256]{2,1,0:T(8,128)(2,1)...) custom-call(s32[34]{0:T(128)S(1)} %stack.192.scalars, bf16[384,8192]{1,0:T(8,128)(2,1)S(1)} %copy-done.2, ...), custom_call_target="tpu_custom_call" | custom-call | tf_op jit(solution)/shard_map/pallas_call | solution.py:43
  111.2 7.0 %collective-permute-done.27 = bf16[4,128,256]{2,1,0:T(8,128)(2,1)S(1)} collective-permute-done((bf16[4,128,256]{2,1,0:T(8,128)(2,1)S(1)}, bf16[4,128,256]{2,1,0:T(8,128)(2,1)S(1)}, u32[]{:S(2)}, u32[]{:S(2)}) %collective-permute-start.27) | collective-permute-done | bytes 262176 | tf_op jit(solution)/shard_map/ppermute | solution.py:63
  127.1 7.8 %collective-permute-done.33 = bf16[4,128,512]{2,1,0:T(8,128)(2,1)S(1)} collective-permute-done((bf16[4,128,512]{2,1,0:T(8,128)(2,1)S(1)}, bf16[4,128,512]{2,1,0:T(8,128)(2,1)S(1)}, u32[]{:S(2)}, u32[]{:S(2)}) %collective-permute-start.33) | collective-permute-done | bytes 524320 | tf_op jit(solution)/shard_map/ppermute | solution.py:63
  139.1 5.4 %collective-permute-done.28 = f32[128,256]{1,0:T(8,128)S(1)} collective-permute-done((f32[128,256]{1,0:T(8,128)S(1)}, f32[128,256]{1,0:T(8,128)S(1)}, u32[]{:S(2)}, u32[]{:S(2)}) %collective-permute-start.28) | collective-permute-done | bytes 131104 | tf_op jit(solution)/shard_map/ppermute | solution.py:63
  147.7 3.0 %collective-permute-done.29.refs_1_ = f32[128,256]{1,0:T(8,128)S(1)} collective-permute-done((f32[128,256]{1,0:T(8,128)S(1)}, f32[128,256]{1,0:T(8,128)S(1)}, u32[]{:S(2)}, u32[]{:S(2)}) %collective-permute-start.29) | collective-permute-done | bytes 131104 | tf_op jit(solution)/shard_map/ppermute | solution.py:63
  150.7 2.8 %collective-permute-done.35 = bf16[1,128,512]{2,1,0:T(8,128)(2,1)S(1)} collective-permute-done((bf16[1,128,512]{2,1,0:T(8,128)(2,1)S(1)}, bf16[1,128,512]{2,1,0:T(8,128)(2,1)S(1)}, u32[]{:S(2)}, u32[]{:S(2)}) %collective-permute-start.35) | collective-permute-done | bytes 131104 | tf_op jit(solution)/shard_map/ppermute | solution.py:63
  (113 shorter events, 54.0 us)
Async XLA Ops:
  3.8 10.9 %collective-permute-start.2 = (bf16[1280,128]{1,0:T(8,128)(2,1)}, bf16[1280,128]{1,0:T(8,128)(2,1)S(1)}, u32[]{:S(2)}, u32[]{:S(2)}) collective-permute-start(bf16[1280,128]{1,0:T(8,128)(2,1)} %shard_map.85.own_ref.refs_0_), channel_id=1, source_target_pairs={{0,2},{1,3},{2,0},{3,1},{4,6},{5,7},{6,4},{7,5},{8,10},{9,11},{10,... | collective-permute-start | bytes 983048 | tf_op jit(solution)/shard_map/ppermute | solution.py:63
  6.8 9.4 %collective-permute-start = (bf16[1280,128]{1,0:T(8,128)(2,1)}, bf16[1280,128]{1,0:T(8,128)(2,1)S(1)}, u32[]{:S(2)}, u32[]{:S(2)}) collective-permute-start(bf16[1280,128]{1,0:T(8,128)(2,1)} %shard_map.85.own_ref.refs_0_), channel_id=1, source_target_pairs={{0,4},{1,5},{2,6},{3,7},{4,0},{5,1},{6,2},{7,3},{8,12},{9,13},{10,... | collective-permute-start | bytes 983048 | tf_op jit(solution)/shard_map/ppermute | solution.py:63
  16.2 8.3 %collective-permute-start.3 = (bf16[1280,128]{1,0:T(8,128)(2,1)S(1)}, bf16[1280,128]{1,0:T(8,128)(2,1)S(1)}, u32[]{:S(2)}, u32[]{:S(2)}) collective-permute-start(bf16[1280,128]{1,0:T(8,128)(2,1)S(1)} %collective-permute-done.refs_2_), channel_id=1, source_target_pairs={{0,2},{1,3},{2,0},{3,1},{4,6},{5,7},{6,4},{7,5},{8,10},{9,11},{10,... | collective-permute-start | bytes 983048 | tf_op jit(solution)/shard_map/ppermute | solution.py:63
  16.6 16.4 %collective-permute-start.1 = (bf16[1280,128]{1,0:T(8,128)(2,1)}, bf16[1280,128]{1,0:T(8,128)(2,1)S(1)}, u32[]{:S(2)}, u32[]{:S(2)}) collective-permute-start(bf16[1280,128]{1,0:T(8,128)(2,1)} %shard_map.85.own_ref.refs_0_), channel_id=1, source_target_pairs={{0,8},{1,9},{2,10},{3,11},{4,12},{5,13},{6,14},{7,15},{8,0},{9,1},... | collective-permute-start | bytes 983048 | tf_op jit(solution)/shard_map/ppermute | solution.py:63
  31.8 8.8 %collective-permute-start.9 = (bf16[1280,128]{1,0:T(8,128)(2,1)}, bf16[1280,128]{1,0:T(8,128)(2,1)S(1)}, u32[]{:S(2)}, u32[]{:S(2)}) collective-permute-start(bf16[1280,128]{1,0:T(8,128)(2,1)} %shard_map.85.own_ref.refs_0_), channel_id=1, source_target_pairs={{0,1},{1,0},{2,3},{3,2},{4,5},{5,4},{6,7},{7,6},{8,9},{9,8},{10,11... | collective-permute-start | bytes 983048 | tf_op jit(solution)/shard_map/ppermute | solution.py:63
  31.8 8.8 %collective-permute-start.10 = (bf16[1280,128]{1,0:T(8,128)(2,1)S(1)}, bf16[1280,128]{1,0:T(8,128)(2,1)S(1)}, u32[]{:S(2)}, u32[]{:S(2)}) collective-permute-start(bf16[1280,128]{1,0:T(8,128)(2,1)S(1)} %collective-permute-done.2.refs_1_), channel_id=1, source_target_pairs={{0,1},{1,0},{2,3},{3,2},{4,5},{5,4},{6,7},{7,6},{8,9},{9,8},{10,11... | collective-permute-start | bytes 983048 | tf_op jit(solution)/shard_map/ppermute | solution.py:63
  33.0 8.9 %collective-permute-start.5 = (bf16[1280,128]{1,0:T(8,128)(2,1)S(1)}, bf16[1280,128]{1,0:T(8,128)(2,1)S(1)}, u32[]{:S(2)}, u32[]{:S(2)}) collective-permute-start(bf16[1280,128]{1,0:T(8,128)(2,1)S(1)} %collective-permute-done.1.refs_4_), channel_id=1, source_target_pairs={{0,2},{1,3},{2,0},{3,1},{4,6},{5,7},{6,4},{7,5},{8,10},{9,11},{10,... | collective-permute-start | bytes 983048 | tf_op jit(solution)/shard_map/ppermute | solution.py:63
  34.4 14.1 %collective-permute-start.4 = (bf16[1280,128]{1,0:T(8,128)(2,1)S(1)}, bf16[1280,128]{1,0:T(8,128)(2,1)S(1)}, u32[]{:S(2)}, u32[]{:S(2)}) collective-permute-start(bf16[1280,128]{1,0:T(8,128)(2,1)S(1)} %collective-permute-done.1.refs_4_), channel_id=1, source_target_pairs={{0,4},{1,5},{2,6},{3,7},{4,0},{5,1},{6,2},{7,3},{8,12},{9,13},{10,... | collective-permute-start | bytes 983048 | tf_op jit(solution)/shard_map/ppermute | solution.py:63
  38.0 10.5 %collective-permute-start.17 = (f32[192,256]{1,0:T(8,128)S(1)}, f32[192,256]{1,0:T(8,128)S(1)}, u32[]{:S(2)}, u32[]{:S(2)}) collective-permute-start(f32[192,256]{1,0:T(8,128)S(1)} %add.118), channel_id=1, source_target_pairs={{0,8},{1,9},{2,10},{3,11},{4,12},{5,13},{6,14},{7,15},{8,0},{9,1},... | collective-permute-start | bytes 589832 | tf_op jit(solution)/shard_map/ppermute | solution.py:63
  40.6 10.1 %collective-permute-start.11 = (bf16[1280,128]{1,0:T(8,128)(2,1)S(1)}, bf16[1280,128]{1,0:T(8,128)(2,1)S(1)}, u32[]{:S(2)}, u32[]{:S(2)}) collective-permute-start(bf16[1280,128]{1,0:T(8,128)(2,1)S(1)} %collective-permute-done.refs_2_), channel_id=1, source_target_pairs={{0,1},{1,0},{2,3},{3,2},{4,5},{5,4},{6,7},{7,6},{8,9},{9,8},{10,11... | collective-permute-start | bytes 983048 | tf_op jit(solution)/shard_map/ppermute | solution.py:63
  40.6 12.2 %collective-permute-start.13 = (bf16[1280,128]{1,0:T(8,128)(2,1)S(1)}, bf16[1280,128]{1,0:T(8,128)(2,1)S(1)}, u32[]{:S(2)}, u32[]{:S(2)}) collective-permute-start(bf16[1280,128]{1,0:T(8,128)(2,1)S(1)} %collective-permute-done.1.refs_4_), channel_id=1, source_target_pairs={{0,1},{1,0},{2,3},{3,2},{4,5},{5,4},{6,7},{7,6},{8,9},{9,8},{10,11... | collective-permute-start | bytes 983048 | tf_op jit(solution)/shard_map/ppermute | solution.py:63
  42.0 12.3 %collective-permute-start.12 = (bf16[1280,128]{1,0:T(8,128)(2,1)S(1)}, bf16[1280,128]{1,0:T(8,128)(2,1)}, u32[]{:S(2)}, u32[]{:S(2)}) collective-permute-start(bf16[1280,128]{1,0:T(8,128)(2,1)S(1)} %collective-permute-done.3.refs_3_), channel_id=1, source_target_pairs={{0,1},{1,0},{2,3},{3,2},{4,5},{5,4},{6,7},{7,6},{8,9},{9,8},{10,11... | collective-permute-start | bytes 983048 | tf_op jit(solution)/shard_map/ppermute | solution.py:63
  51.5 17.9 %collective-permute-start.8 = (bf16[1280,128]{1,0:T(8,128)(2,1)S(1)}, bf16[1280,128]{1,0:T(8,128)(2,1)}, u32[]{:S(2)}, u32[]{:S(2)}) collective-permute-start(bf16[1280,128]{1,0:T(8,128)(2,1)S(1)} %collective-permute-done.4.refs_6_), channel_id=1, source_target_pairs={{0,2},{1,3},{2,0},{3,1},{4,6},{5,7},{6,4},{7,5},{8,10},{9,11},{10,... | collective-permute-start | bytes 983048 | tf_op jit(solution)/shard_map/ppermute | solution.py:63
  53.5 15.9 %collective-permute-start.18 = (bf16[192,256]{1,0:T(8,128)(2,1)S(1)}, bf16[192,256]{1,0:T(8,128)(2,1)S(1)}, u32[]{:S(2)}, u32[]{:S(2)}) collective-permute-start(bf16[192,256]{1,0:T(8,128)(2,1)S(1)} %get-tuple-element.49), channel_id=1, source_target_pairs={{0,2},{1,3},{2,0},{3,1},{4,6},{5,7},{6,4},{7,5},{8,10},{9,11},{10,... | collective-permute-start | bytes 294920 | tf_op jit(solution)/shard_map/ppermute | solution.py:63
  85.1 12.8 %collective-permute-start.22 = (bf16[384,640]{1,0:T(8,128)(2,1)}, bf16[384,640]{1,0:T(8,128)(2,1)S(1)}, u32[]{:S(2)}, u32[]{:S(2)}) collective-permute-start(bf16[384,640]{1,0:T(8,128)(2,1)} %get-tuple-element.36), channel_id=1, source_target_pairs={{0,16},{16,0},{1,17},{17,1},{2,18},{18,2},{3,19},{19,3},{4,20},{20... | collective-permute-start | bytes 1474568 | tf_op jit(solution)/shard_map/ppermute | solution.py:63
  107.8 12.7 %collective-permute-start.24 = (bf16[8,128,512]{2,1,0:T(8,128)(2,1)S(1)}, bf16[8,128,512]{2,1,0:T(8,128)(2,1)S(1)}, u32[]{:S(2)}, u32[]{:S(2)}) collective-permute-start(bf16[8,128,512]{2,1,0:T(8,128)(2,1)S(1)} %get-tuple-element.39), channel_id=1, source_target_pairs={{0,1},{1,0},{2,3},{3,2},{4,5},{5,4},{6,7},{7,6},{8,9},{9,8},{10,11... | collective-permute-start | bytes 3145736 | tf_op jit(solution)/shard_map/ppermute | solution.py:63
  109.8 8.4 %collective-permute-start.27 = (bf16[4,128,256]{2,1,0:T(8,128)(2,1)S(1)}, bf16[4,128,256]{2,1,0:T(8,128)(2,1)S(1)}, u32[]{:S(2)}, u32[]{:S(2)}) collective-permute-start(bf16[4,128,256]{2,1,0:T(8,128)(2,1)S(1)} %add_convert_fusion.1), channel_id=1, source_target_pairs={{0,2},{1,3},{2,0},{3,1},{4,6},{5,7},{6,4},{7,5},{8,10},{9,11},{10,... | collective-permute-start | bytes 786440 | tf_op jit(solution)/shard_map/ppermute | solution.py:63
  111.2 10.1 %collective-permute-start.23 = (f32[128,256]{1,0:T(8,128)S(1)}, f32[128,256]{1,0:T(8,128)S(1)}, u32[]{:S(2)}, u32[]{:S(2)}) collective-permute-start(f32[128,256]{1,0:T(8,128)S(1)} %get-tuple-element.38), channel_id=1, source_target_pairs={{0,1},{1,0},{2,3},{3,2},{4,5},{5,4},{6,7},{7,6},{8,9},{9,8},{10,11... | collective-permute-start | bytes 393224 | tf_op jit(solution)/shard_map/ppermute | solution.py:63
  120.6 14.3 %collective-permute-start.33 = (bf16[4,128,512]{2,1,0:T(8,128)(2,1)S(1)}, bf16[4,128,512]{2,1,0:T(8,128)(2,1)S(1)}, u32[]{:S(2)}, u32[]{:S(2)}) collective-permute-start(bf16[4,128,512]{2,1,0:T(8,128)(2,1)S(1)} %add_convert_fusion), channel_id=1, source_target_pairs={{0,2},{1,3},{2,0},{3,1},{4,6},{5,7},{6,4},{7,5},{8,10},{9,11},{10,... | collective-permute-start | bytes 1572872 | tf_op jit(solution)/shard_map/ppermute | solution.py:63
  123.5 13.9 %collective-permute-start.31 = (bf16[1,128,256]{2,1,0:T(8,128)(2,1)S(1)}, bf16[1,128,256]{2,1,0:T(8,128)(2,1)S(1)}, u32[]{:S(2)}, u32[]{:S(2)}) collective-permute-start(bf16[1,128,256]{2,1,0:T(8,128)(2,1)S(1)} %fusion.8), channel_id=1, source_target_pairs={{0,8},{1,9},{2,10},{3,11},{4,12},{5,13},{6,14},{7,15},{8,0},{9,1},... | collective-permute-start | bytes 196616 | tf_op jit(solution)/shard_map/ppermute | solution.py:63
  125.6 10.8 %collective-permute-start.25 = (f32[128,256]{1,0:T(8,128)S(1)}, f32[128,256]{1,0:T(8,128)S(1)}, u32[]{:S(2)}, u32[]{:S(2)}) collective-permute-start(f32[128,256]{1,0:T(8,128)S(1)} %add.121), channel_id=1, source_target_pairs={{0,2},{1,3},{2,0},{3,1},{4,6},{5,7},{6,4},{7,5},{8,10},{9,11},{10,... | collective-permute-start | bytes 393224 | tf_op jit(solution)/shard_map/ppermute | solution.py:63
  135.2 11.4 %collective-permute-start.34 = (bf16[2,128,512]{2,1,0:T(8,128)(2,1)S(1)}, bf16[2,128,512]{2,1,0:T(8,128)(2,1)S(1)}, u32[]{:S(2)}, u32[]{:S(2)}) collective-permute-start(bf16[2,128,512]{2,1,0:T(8,128)(2,1)S(1)} %fusion.2), channel_id=1, source_target_pairs={{0,4},{1,5},{2,6},{3,7},{4,0},{5,1},{6,2},{7,3},{8,12},{9,13},{10,... | collective-permute-start | bytes 786440 | tf_op jit(solution)/shard_map/ppermute | solution.py:63
  136.4 8.1 %collective-permute-start.28 = (f32[128,256]{1,0:T(8,128)S(1)}, f32[128,256]{1,0:T(8,128)S(1)}, u32[]{:S(2)}, u32[]{:S(2)}) collective-permute-start(f32[128,256]{1,0:T(8,128)S(1)} %add.122), channel_id=1, source_target_pairs={{0,4},{1,5},{2,6},{3,7},{4,0},{5,1},{6,2},{7,3},{8,12},{9,13},{10,... | collective-permute-start | bytes 393224 | tf_op jit(solution)/shard_map/ppermute | solution.py:63
  137.4 10.3 %collective-permute-start.32 = (f32[128,256]{1,0:T(8,128)S(1)}, f32[128,256]{1,0:T(8,128)S(1)}, u32[]{:S(2)}, u32[]{:S(2)}) collective-permute-start(f32[128,256]{1,0:T(8,128)S(1)} %fusion.7.refs_3_), channel_id=1, source_target_pairs={{0,16},{16,0},{1,17},{17,1},{2,18},{18,2},{3,19},{19,3},{4,20},{20... | collective-permute-start | bytes 393224 | tf_op jit(solution)/shard_map/ppermute | solution.py:63
  (29 other events, 232.8 us)
